TPU v7x, 32 devices: a whole 2x2x4 slice. The times are simulated.
32 devices in a mesh: seq: 4 (over z), tensor: 8 (over y, x, core).
Axes of the slice: x: 2, y: 2, z: 4, core: 2. Of those that a mesh axis runs over, the one named last changes fastest.
Arguments:
- tokens: bfloat16 [4096, 1536], P(('seq', 'tensor')), may hold values from -6 to 6
- segment_ids: int32 [4096], P(('seq', 'tensor')), may hold values from 0 to 15, never falling along the last dimension, each value on 1 to 1024 neighbouring positions
- page_table: int32 [4, 64], P('seq'), may hold values from 0 to 63, each once within a row
- attn_gain: float32 [1536], replicated, may hold values from 0.6 to 6
- w_qkv: bfloat16 [1536, 2048], P(None, 'tensor'), may hold values from -0.15625 to 0.15625
- w_out: bfloat16 [1536, 1536], P(None, 'tensor'), may hold values from -0.15625 to 0.15625
- moe_gain: float32 [1536], replicated, may hold values from 0.25 to 1.75
- route_ids: int32 [4096, 4], P(('seq', 'tensor')), may hold values from 0 to 7, all different within a row; in each aligned block of 128 rows (0 to 127, 128 to 255, ...) at most 96 rows name the same one
- route_weight: float32 [4096, 4], P(('seq', 'tensor')), may hold values from 0.05 to 1
- w_gate: bfloat16 [8, 1536, 768], P('tensor'), may hold values from -0.15625 to 0.15625
- w_up: bfloat16 [8, 1536, 768], P('tensor'), may hold values from -0.15625 to 0.15625
- w_down: bfloat16 [8, 768, 1536], P('tensor'), may hold values from -0.21875 to 0.21875
Outputs:
- mixed: bfloat16 [4096, 1536], P(('seq', 'tensor'))
- cache: bfloat16 [256, 16, 512], P(('seq', 'tensor'))
Inputs may be any that keep to these rules, and one draw needn't show every extreme that they name: `segment_ids`: segment numbers never fall along the tokens; every prompt spans 1 to 1024 tokens and one spans exactly 1024. `page_table`: each row is a permutation of the slots of one block. `route_ids`: each token names 4 different experts; among the rows of one device no expert is named more than 96 times, a bound that some block reaches.
All inputs are finite; a program needn't handle non-finite values.
Results may differ from a plain program's by a relative error of at most 0.012.
The roundings to bfloat16 on the way count: a program that leaves them out, or rounds other values in their place, can miss the bound.
Values may be sent and summed in bfloat16 or wider, within the bound.
No kernel may reach another device: no remote copies, remote signals or barrier semaphores. Data moves between devices by JAX's collectives and lax.ppermute only.
A program may use at most 128 MiB of HBM per device.

v0:
```python
import math

import jax
import jax.numpy as jnp
from jax import lax
from jax.sharding import PartitionSpec as P

HEADS = 12
KV_HEADS = 2
HEAD = 128
TOP = 4
PAGE = 16


epsilon = 1e-06


def from_behind(value, axis, by):
    length = lax.axis_size(axis)
    pairs = [(i, i + by) for i in range(length) if 0 <= i + by < length]
    return lax.ppermute(value, axis, pairs)


def rms_scaled(values, scales):
    wide = values.astype(jnp.float32)
    mean_sq = jnp.mean(wide * wide, axis=-1, keepdims=True)
    return (wide * lax.rsqrt(mean_sq + epsilon) * scales).astype(jnp.bfloat16)


def attend(queries, keys_window, values_window, allowed):
    scores = jnp.einsum(
        "qhd,kd->hqk", queries, keys_window, preferred_element_type=jnp.float32
    ) / math.sqrt(queries.shape[-1])
    scores = jnp.where(allowed[None], scores, -jnp.inf)
    highest = jnp.max(scores, axis=-1, keepdims=True)
    weights = jnp.exp(scores - highest)
    totals = jnp.sum(weights, axis=-1, keepdims=True)
    shares = (weights / totals).astype(jnp.bfloat16)
    return jnp.einsum("hqk,kd->qhd", shares, values_window, preferred_element_type=jnp.float32)


def body(
    tokens,
    segment_ids,
    page_table,
    attn_gain,
    w_qkv,
    w_out,
    moe_gain,
    route_ids,
    route_weight,
    w_gate,
    w_up,
    w_down,
):
    tok_rows = tokens.shape[0]
    tensor_size = lax.axis_size("tensor")
    tensor_index = lax.axis_index("tensor")
    seq_index = lax.axis_index("seq")
    block_rows = tok_rows * tensor_size
    normed = rms_scaled(tokens, attn_gain)
    block_normed = lax.all_gather(normed, "tensor", axis=0, tiled=True)
    own_columns = jnp.dot(block_normed, w_qkv, preferred_element_type=jnp.float32).astype(
        jnp.bfloat16
    )
    projected = lax.all_to_all(own_columns, "tensor", split_axis=0, concat_axis=1, tiled=True)
    query_width = HEADS * HEAD
    queries = projected[:, :query_width].reshape(tok_rows, HEADS, HEAD)
    own_kv = projected[:, query_width:]
    block_kv, block_segs = (
        lax.all_gather(own_kv, "tensor", axis=0, tiled=True),
        lax.all_gather(segment_ids, "tensor", axis=0, tiled=True),
    )
    earlier_kv, earlier_seg_block = from_behind((block_kv, block_segs), "seq", 1)
    pages_here = tok_rows // PAGE
    pages_block = block_rows // PAGE
    slot_ids = tensor_index * pages_here + jnp.arange(pages_here, dtype=jnp.int32)
    matches = page_table[0][None, :] == slot_ids[:, None]
    logical = jnp.sum(
        jnp.where(matches, jnp.arange(pages_block, dtype=jnp.int32)[None, :], 0), axis=1
    )
    cache_pages = block_kv.reshape(pages_block, PAGE, block_kv.shape[1])[logical]
    all_kv = jnp.concatenate([earlier_kv, block_kv], axis=0)
    all_segs = jnp.concatenate([earlier_seg_block, block_segs], axis=0)
    window = block_rows + tok_rows
    first_key = tensor_index * tok_rows
    keys_window = lax.dynamic_slice_in_dim(all_kv, first_key, window, 0)
    segs_window = lax.dynamic_slice_in_dim(all_segs, first_key, window, 0)
    key_pos = (seq_index - 1) * block_rows + first_key + jnp.arange(window, dtype=jnp.int32)
    query_pos = seq_index * block_rows + first_key + jnp.arange(tok_rows, dtype=jnp.int32)
    allowed = (
        (segs_window[None, :] == segment_ids[:, None])
        & (key_pos[None, :] <= query_pos[:, None])
        & (key_pos[None, :] >= 0)
    )
    per_group = HEADS // KV_HEADS
    contexts = []
    for kv_group in range(KV_HEADS):
        key_cols = keys_window[:, kv_group * HEAD : (kv_group + 1) * HEAD]
        value_cols = keys_window[:, (KV_HEADS + kv_group) * HEAD : (KV_HEADS + kv_group + 1) * HEAD]
        contexts.append(
            attend(
                queries[:, kv_group * per_group : (kv_group + 1) * per_group],
                key_cols,
                value_cols,
                allowed,
            )
        )
    context = jnp.concatenate(contexts, axis=1).reshape(tok_rows, query_width).astype(jnp.bfloat16)
    attn_out = jnp.dot(
        context,
        lax.all_gather(w_out, "tensor", axis=1, tiled=True),
        preferred_element_type=jnp.float32,
    )
    residual = (tokens.astype(jnp.float32) + attn_out).astype(jnp.bfloat16)
    expert_input = rms_scaled(residual, moe_gain)
    experts_all = w_gate.shape[0] * tensor_size
    capacity = max(2, 3 * tok_rows * TOP // (2 * experts_all))
    flat_routes = route_ids.reshape(-1)
    expert_hits = (
        flat_routes[:, None] == jnp.arange(experts_all, dtype=jnp.int32)[None, :]
    ).astype(jnp.int32)
    earlier_hits = jnp.cumsum(expert_hits, axis=0) - expert_hits
    slot_rank = jnp.sum(earlier_hits * expert_hits, axis=1)
    dest_slot = flat_routes * capacity + slot_rank
    slot_table = (
        jnp.arange(experts_all * capacity, dtype=jnp.int32)[:, None, None]
        == dest_slot.reshape(tok_rows, TOP)[None]
    )
    dispatch = jnp.any(slot_table, axis=2).astype(jnp.bfloat16)
    outgoing = jnp.dot(dispatch, expert_input, preferred_element_type=jnp.float32).astype(
        jnp.bfloat16
    )
    outgoing = outgoing.reshape(experts_all, capacity, expert_input.shape[1])
    arrived = lax.all_to_all(outgoing, "tensor", split_axis=0, concat_axis=0, tiled=True)
    rows_flat = arrived.reshape(-1, arrived.shape[-1])
    gate_out = jnp.dot(rows_flat, w_gate[0], preferred_element_type=jnp.float32)
    up_out = jnp.dot(rows_flat, w_up[0], preferred_element_type=jnp.float32)
    hidden = (jnp.maximum(gate_out, 0.0) * up_out).astype(jnp.bfloat16)
    produced = jnp.dot(hidden, w_down[0], preferred_element_type=jnp.float32).astype(jnp.bfloat16)
    returned = lax.all_to_all(
        produced.reshape(arrived.shape), "tensor", split_axis=0, concat_axis=0, tiled=True
    )
    picked = returned.reshape(-1, returned.shape[-1])[dest_slot].reshape(
        tok_rows, TOP, returned.shape[-1]
    )
    routed_sum = jnp.einsum("tk,tkd->td", route_weight, picked.astype(jnp.float32))
    mixed = (residual.astype(jnp.float32) + routed_sum).astype(jnp.bfloat16)
    return (mixed, cache_pages)


def solution(mesh):
    return jax.shard_map(
        body,
        mesh=mesh,
        in_specs=(
            P(("seq", "tensor"), None),
            P(("seq", "tensor")),
            P("seq", None),
            P(),
            P(None, "tensor"),
            P(None, "tensor"),
            P(),
            P(("seq", "tensor"), None),
            P(("seq", "tensor"), None),
            P("tensor", None, None),
            P("tensor", None, None),
            P("tensor", None, None),
        ),
        out_specs=(P(("seq", "tensor"), None), P(("seq", "tensor"), None, None)),
        check_vma=False,
    )
```

profile of v0, /device:TPU:0, one launch (start us, length us, event | category | flops | bytes accessed | tf_op | source)
XLA Modules:
  0.0 230.4 jit_solution(14918673595110196278)
XLA Ops:
  7.2 0.0 copy-start
  7.2 0.0 all-gather.5.cloned.1.call-start
  7.2 1.3 fusion.27
  8.5 1.9 fusion.29
  10.4 0.0 all-gather.5.cloned.1.call-update
  10.5 0.0 all-gather.7.cloned.1.call-start
  10.5 35.1 %all-gather.5.cloned.1.call-done = bf16[1024,1536]{1,0:T(8,128)(2,1)} async-done(((bf16[128,1536]{1,0:T(8,128)(2,1)}), bf16[1024,1536]{1,0:T(8,128)(2,1)}) %all-gather.5.cloned.1.call-update) | async-done | bytes 3145744 | tf_op jit(solution)/shard_map/all_gather | solution.py:62
  45.6 3.1 %convolution_convert_fusion.2 = bf16[1024,256]{1,0:T(8,128)(2,1)S(1)} fusion(bf16[1024,1536]{1,0:T(8,128)(2,1)} %all-gather.5.cloned.1.call-done, bf16[1536,256]{1,0:T(8,128)(2,1)} %param.16), kind=kOutput, calls=%fused_computation.33 | convolution fusion | flops 805568512 | bytes 4456448 | tf_op jit(solution)/shard_map/dot_general | solution.py:63
  48.7 0.0 copy-start.8
  48.7 0.0 copy-start.9
  48.7 12.3 %all_to_all.29 = bf16[8,128,256]{2,1,0:T(8,128)(2,1)S(1)} all-to-all(bf16[8,128,256]{2,1,0:T(8,128)(2,1)S(1)} %bitcast.128), channel_id=1, replica_groups=mesh['seq'=4,'tensor'=8] {'tensor'}, dimensions={0} | all-to-all | bytes 1048576 | tf_op jit(solution)/shard_map/all_to_all | solution.py:66
  61.1 0.7 slice.44
  61.7 0.0 all-gather.7.cloned.1.call-update
  61.8 0.0 all-gather.9.cloned.1.call-start
  61.8 0.7 all-gather.9.cloned.1.call-update
  62.5 0.0 copy-done.8
  62.5 7.8 %all-gather = s32[8,1,128]{2,1,0:T(1,128)S(1)} all-gather(s32[1,1,128]{2,1,0:T(1,128)S(1)} %bitcast.137), channel_id=1, replica_groups=mesh['seq'=4,'tensor'=8] {'tensor'}, dimensions={0}, use_global_device_ids=true | all-gather | bytes 4608 | tf_op jit(solution)/shard_map/all_gather | solution.py:72
  70.3 3.4 %collective-permute-start.1 = (s32[1024]{0:T(1024)S(1)}, s32[1024]{0:T(1024)S(1)}, u32[]{:S(2)}, u32[]{:S(2)}) collective-permute-start(s32[1024]{0:T(1024)S(1)} %bitcast.134), channel_id=1, source_target_pairs={{0,8},{8,16},{16,24},{1,9},{9,17},{17,25},{2,10},{10,18},{18,26},{... | collective-permute-start | bytes 12296 | tf_op jit(solution)/shard_map/ppermute | solution.py:21
  73.7 0.0 copy-done.9
  73.7 0.1 copy.50
  73.8 0.1 eq.78
  73.9 0.1 eq.74
  74.0 1.1 reduce-window.6
  75.2 0.2 slice_reduce_fusion
  75.5 0.1 fusion.52
  75.5 0.1 reduce_sum.64
  75.7 8.9 %all-gather.7.cloned.1.call-done = bf16[1024,512]{1,0:T(8,128)(2,1)} async-done(((bf16[128,512]{1,0:T(8,128)(2,1)}), bf16[1024,512]{1,0:T(8,128)(2,1)}) %all-gather.7.cloned.1.call-update) | async-done | bytes 1048592 | tf_op jit(solution)/shard_map/all_gather | solution.py:71
  84.5 4.4 %collective-permute-start = (bf16[1024,512]{1,0:T(8,128)(2,1)}, bf16[1024,512]{1,0:T(8,128)(2,1)}, u32[]{:S(2)}, u32[]{:S(2)}) collective-permute-start(bf16[1024,512]{1,0:T(8,128)(2,1)} %all-gather.7.cloned.1.call-done), channel_id=1, source_target_pairs={{0,8},{8,16},{16,24},{1,9},{9,17},{17,25},{2,10},{10,18},{18,26},{... | collective-permute-start | bytes 3145736 | tf_op jit(solution)/shard_map/ppermute | solution.py:21
  88.9 0.6 broadcast_multiply_fusion
  89.6 0.1 copy.53
  89.7 0.9 fusion.21
  90.5 0.0 collective-permute-done.1
  90.5 0.1 dynamic-slice_add_fusion
  90.6 1.9 and_and_fusion
  92.5 0.9 copy.43
  93.5 17.6 %collective-permute-done = bf16[1024,512]{1,0:T(8,128)(2,1)} collective-permute-done((bf16[1024,512]{1,0:T(8,128)(2,1)}, bf16[1024,512]{1,0:T(8,128)(2,1)}, u32[]{:S(2)}, u32[]{:S(2)}) %collective-permute-start) | collective-permute-done | bytes 1048608 | tf_op jit(solution)/shard_map/ppermute | solution.py:21
  111.1 2.0 fusion.22
  113.0 0.0 copy-start.3
  113.1 2.6 %fusion.69 = f32[6,128]{1,0:T(8,128)S(1)} fusion(pred[128,1152]{0,1:T(8,128)(4,1)} %and_and_fusion, bf16[1152,512]{1,0:T(8,128)(2,1)S(1)} %fusion.22, bf16[128,12,128]{0,2,1:T(8,128)(2,1)} %bitcast.129), kind=kOutput, calls=%fused_computation.93 | convolution fusion | flops 230032512 | bytes 642048 | tf_op jit(solution)/shard_map/sub | solution.py:36
  115.7 3.5 %fusion.26 = bf16[128,6,128]{0,2,1:T(8,128)(2,1)} fusion(f32[6,128]{1,0:T(8,128)S(1)} %fusion.69, bf16[1152,512]{1,0:T(8,128)(2,1)S(1)} %fusion.22, pred[128,1152]{0,1:T(8,128)(4,1)} %and_and_fusion, bf16[128,12,128]{0,2,1:T(8,128)(2,1)} %bitcast.130), kind=kOutput, calls=%fused_computation.40 | convolution fusion | flops 457508736 | bytes 1134592 | tf_op jit(solution)/shard_map/hqk,kd->qhd/dot_general | solution.py:39
  119.2 2.2 fusion.72
  121.4 0.0 copy-start.1
  121.4 3.0 %fusion.25 = bf16[128,6,128]{0,2,1:T(8,128)(2,1)S(1)} fusion(f32[6,128]{1,0:T(8,128)S(1)} %fusion.72, bf16[1152,512]{1,0:T(8,128)(2,1)} %copy-done.3, pred[128,1152]{0,1:T(8,128)(4,1)} %and_and_fusion, bf16[128,12,128]{0,2,1:T(8,128)(2,1)} %bitcast.132), kind=kOutput, calls=%fused_computation.39 | convolution fusion | flops 457508736 | bytes 1133568 | tf_op jit(solution)/shard_map/hqk,kd->qhd/dot_general | solution.py:39
  124.4 0.8 pad_maximum_fusion
  125.2 0.1 all-gather.9.cloned.1.call-done
  125.4 4.2 %multiply_reduce_fusion = (f32[128]{0:T(128)S(1)}, f32[128,1536]{1,0:T(8,128)S(1)}) fusion(bf16[128,1536]{0,1:T(8,128)(2,1)} %bitcast.126, bf16[1536,1536]{0,1:T(8,128)(2,1)} %all-gather.9.cloned.1.call-done, bf16[128,1536]{1,0:T(8,128)(2,1)S(1)} %copy-done.1), kind=kOutput, calls=%fused_computation.47 | convolution fusion | flops 605159296 | bytes 6291968 | tf_op jit(solution)/shard_map/dot_general | solution.py:110
  129.6 0.8 convolution_convert_fusion.1
  130.5 0.0 copy-start.11
  130.5 32.1 %all_to_all.30 = bf16[8,96,1536]{2,1,0:T(8,128)(2,1)S(1)} all-to-all(bf16[8,96,1536]{2,1,0:T(8,128)(2,1)S(1)} %bitcast.119), channel_id=1, replica_groups=mesh['seq'=4,'tensor'=8] {'tensor'}, dimensions={0} | all-to-all | bytes 4718592 | tf_op jit(solution)/shard_map/all_to_all | solution.py:135
  162.6 1.4 copy-done.2
  164.0 0.0 copy-done.11
  164.0 3.4 %fusion.13 = f32[768,768]{1,0:T(8,128)} fusion(bf16[768,1536]{1,0:T(8,128)(2,1)S(1)} %bitcast.121, bf16[1,1536,768]{2,1,0:T(8,128)(2,1)S(1)} %copy-done.11), kind=kOutput, calls=%fused_computation.22 | convolution fusion | flops 1811939328 | bytes 7077888 | tf_op jit(solution)/shard_map/dot_general | solution.py:138
  167.4 9.1 %convolution_convert_fusion = bf16[768,1536]{1,0:T(8,128)(2,1)} fusion(bf16[1,768,1536]{2,1,0:T(8,128)(2,1)S(1)} %copy-done, f32[768,768]{1,0:T(8,128)} %fusion.13, bf16[768,1536]{1,0:T(8,128)(2,1)} %bitcast.122, bf16[1,1536,768]{2,1,0:T(8,128)(2,1)} %param.21), kind=kOutput, calls=%fused_computation.16 | convolution fusion | flops 3626827776 | bytes 11796480 | tf_op jit(solution)/shard_map/dot_general | solution.py:140
  176.5 4.5 %all-to-all-start.2 = ((bf16[8,96,1536]{2,1,0:T(8,128)(2,1)}), bf16[8,96,1536]{2,1,0:T(8,128)(2,1)}, u32[]{:S(2)}, u32[]{:S(2)}) async-start(bf16[8,96,1536]{2,1,0:T(8,128)(2,1)} %bitcast.120), calls=%async_computation.2 | async-start | bytes 4718592 | tf_op jit(solution)/shard_map/all_to_all | solution.py:141
  181.0 0.0 copy-done.5
  181.0 0.1 mul.91
  181.1 0.2 copy.58
  181.3 0.2 select_reduce_fusion
  181.5 2.4 %gather_fusion.1 = bf16[8,16,512]{2,1,0:T(8,128)(2,1)} fusion(bf16[64,16,512]{2,1,0:T(8,128)(2,1)} %bitcast.127, s32[1024]{0:T(1024)S(1)} %pad_clamp_fusion), kind=kCustom, calls=%fused_computation.1 | custom fusion | bytes 262176 | tf_op jit(solution)/shard_map/gather | solution.py:82
  184.0 26.5 %all-to-all-done.2 = bf16[8,96,1536]{2,1,0:T(8,128)(2,1)} async-done(((bf16[8,96,1536]{2,1,0:T(8,128)(2,1)}), bf16[8,96,1536]{2,1,0:T(8,128)(2,1)}, u32[]{:S(2)}, u32[]{:S(2)}) %all-to-all-start.2) | async-done | bytes 2359328 | tf_op jit(solution)/shard_map/all_to_all | solution.py:141
  210.4 6.4 %gather_fusion = bf16[512,1536]{1,0:T(8,128)(2,1)} fusion(bf16[768,1536]{1,0:T(8,128)(2,1)} %bitcast.22, s32[1024]{0:T(1024)S(1)} %pad_clamp_fusion.1), kind=kCustom, calls=%fused_computation | custom fusion | bytes 3147776 | tf_op jit(solution)/shard_map/gather | solution.py:144
  216.8 3.9 %reshape.209 = bf16[128,4,1536]{2,1,0:T(4,128)(2,1)} reshape(bf16[512,1536]{1,0:T(8,128)(2,1)} %gather_fusion) | data formatting | bytes 3145728 | tf_op jit(solution)/shard_map/reshape | solution.py:144
  220.7 2.4 %fusion.75 = f32[128,1,1536]{2,1,0:T(1,128)S(1)} fusion(bf16[128,4,1536]{2,1,0:T(4,128)(2,1)} %reshape.209, bf16[128,4,1]{1,2,0:T(2,128)(2,1)S(1)} %copy.58), kind=kOutput, calls=%fused_computation.95 | convolution fusion | flops 1572864 | bytes 2360320 | tf_op jit(solution)/shard_map/tk,tkd->td/dot_general | solution.py:147
  223.1 0.8 fusion.30
  (30 shorter events, 0.2 us)
Async XLA Ops:
  7.2 160.2 %copy-start = (bf16[1,768,1536]{2,1,0:T(8,128)(2,1)S(1)}, bf16[1,768,1536]{2,1,0:T(8,128)(2,1)}, u32[]{:S(2)}) copy-start(bf16[1,768,1536]{2,1,0:T(8,128)(2,1)} %param.23) | copy-start | bytes 7077892
  7.2 38.5 %all-gather.5.cloned.1.call-start = ((), (), s32[]{:S(2)}) async-start(), calls=%async_computation.3 | async-start | bytes 3538944 | tf_op jit(solution)/shard_map/all_gather | solution.py:62
  10.5 74.0 %all-gather.7.cloned.1.call-start = ((), (), s32[]{:S(2)}) async-start(), calls=%async_computation.4 | async-start | bytes 1179648 | tf_op jit(solution)/shard_map/all_gather | solution.py:71
  48.7 13.8 %copy-start.8 = (s32[128]{0:T(128)S(1)}, s32[128]{0:T(128)}, u32[]{:S(2)}) copy-start(s32[128]{0:T(128)} %param.13) | copy-start | bytes 1540
  48.7 25.0 %copy-start.9 = (s32[128,4]{0,1:T(4,128)S(1)}, s32[128,4]{0,1:T(4,128)}, u32[]{:S(2)}) copy-start(s32[128,4]{0,1:T(4,128)} %param.19) | copy-start | bytes 6148
  61.8 63.6 %all-gather.9.cloned.1.call-start = ((), (), s32[]{:S(2)}) async-start(), calls=%async_computation.5 | async-start | bytes 5308416 | tf_op jit(solution)/shard_map/all_gather | solution.py:112
  70.3 20.2 %collective-permute-start.1 = (s32[1024]{0:T(1024)S(1)}, s32[1024]{0:T(1024)S(1)}, u32[]{:S(2)}, u32[]{:S(2)}) collective-permute-start(s32[1024]{0:T(1024)S(1)} %bitcast.134), channel_id=1, source_target_pairs={{0,8},{8,16},{16,24},{1,9},{9,17},{17,25},{2,10},{10,18},{18,26},{... | collective-permute-start | bytes 12296 | tf_op jit(solution)/shard_map/ppermute | solution.py:21
  84.5 26.5 %collective-permute-start = (bf16[1024,512]{1,0:T(8,128)(2,1)}, bf16[1024,512]{1,0:T(8,128)(2,1)}, u32[]{:S(2)}, u32[]{:S(2)}) collective-permute-start(bf16[1024,512]{1,0:T(8,128)(2,1)} %all-gather.7.cloned.1.call-done), channel_id=1, source_target_pairs={{0,8},{8,16},{16,24},{1,9},{9,17},{17,25},{2,10},{10,18},{18,26},{... | collective-permute-start | bytes 3145736 | tf_op jit(solution)/shard_map/ppermute | solution.py:21
  113.0 6.1 %copy-start.3 = (bf16[1152,512]{1,0:T(8,128)(2,1)}, bf16[1152,512]{1,0:T(8,128)(2,1)S(1)}, u32[]{:S(2)}) copy-start(bf16[1152,512]{1,0:T(8,128)(2,1)S(1)} %fusion.22) | copy-start | bytes 3538948
  121.4 3.0 %copy-start.6 = (bf16[128,6,128]{0,2,1:T(8,128)(2,1)S(1)}, bf16[128,6,128]{0,2,1:T(8,128)(2,1)}, u32[]{:S(2)}) copy-start(bf16[128,6,128]{0,2,1:T(8,128)(2,1)} %fusion.26) | copy-start | bytes 589828
  121.4 4.0 %copy-start.1 = (bf16[128,1536]{1,0:T(8,128)(2,1)S(1)}, bf16[128,1536]{1,0:T(8,128)(2,1)}, u32[]{:S(2)}) copy-start(bf16[128,1536]{1,0:T(8,128)(2,1)} %param.12) | copy-start | bytes 1179652
  125.4 4.3 %copy-start.4 = (pred[768,128]{1,0:T(8,128)(4,1)S(1)}, pred[768,128]{1,0:T(8,128)(4,1)}, u32[]{:S(2)}) copy-start(pred[768,128]{1,0:T(8,128)(4,1)} %fusion.21) | copy-start | bytes 294916
  125.4 4.3 %copy-start.7 = (f32[1536]{0:T(1024)S(1)}, f32[1536]{0:T(1024)}, u32[]{:S(2)}) copy-start(f32[1536]{0:T(1024)} %param.18) | copy-start | bytes 18436
  130.5 33.5 %copy-start.11 = (bf16[1,1536,768]{2,1,0:T(8,128)(2,1)S(1)}, bf16[1,1536,768]{2,1,0:T(8,128)(2,1)}, u32[]{:S(2)}) copy-start(bf16[1,1536,768]{2,1,0:T(8,128)(2,1)} %param.22) | copy-start | bytes 7077892
  162.6 1.4 copy-start.2
  176.5 4.5 %copy-start.5 = (s32[128,4]{1,0:T(8,128)S(1)}, s32[128,4]{1,0:T(8,128)}, u32[]{:S(2)}) copy-start(s32[128,4]{1,0:T(8,128)} %get-tuple-element.2) | copy-start | bytes 6148
  176.5 4.6 %copy-start.10 = (f32[128,4]{0,1:T(4,128)S(1)}, f32[128,4]{0,1:T(4,128)}, u32[]{:S(2)}) copy-start(f32[128,4]{0,1:T(4,128)} %param.20) | copy-start | bytes 6148
  176.5 4.8 %copy-start.12 = (s32[1,64]{1,0:T(1,128)S(1)}, s32[1,64]{1,0:T(1,128)}, u32[]{:S(2)}) copy-start(s32[1,64]{1,0:T(1,128)} %param.14) | copy-start | bytes 772
  176.5 34.0 %all-to-all-start.2 = ((bf16[8,96,1536]{2,1,0:T(8,128)(2,1)}), bf16[8,96,1536]{2,1,0:T(8,128)(2,1)}, u32[]{:S(2)}, u32[]{:S(2)}) async-start(bf16[8,96,1536]{2,1,0:T(8,128)(2,1)} %bitcast.120), calls=%async_computation.2 | async-start | bytes 4718592 | tf_op jit(solution)/shard_map/all_to_all | solution.py:141
Sparse Core Ops, SparseCore 0:
  10.6 35.0 all-gather.4
  61.9 22.5 all-gather.6
  86.4 38.8 all-gather.8
where the time goes:
time: 231 us; the launch traced here: 230 us
  waiting for transfers between devices  88.9 us (38%)
  blocking collectives  52.2 us (23%)
  matrix products  34.3 us (15%)
  local copies, waits for them, and re-layouts  16.8 us (7%)
  between operations  14 us (6%)
  starting transfers between devices  12.4 us (5%)
  other arithmetic  11.8 us (5%)
    all_gather x1, waiting for transfers between devices, body(): block_normed = lax.all_gather(normed, 'tensor', axis=0, tiled=True)  35.1 us
    all_to_all x1, blocking collectives, body(): lax.all_to_all(outgoing, 'tensor', split_axis=0, concat_axis=0, tiled=True)  32.1 us
    all_to_all x1, waiting for transfers between devices, body(): lax.all_to_all(produced.reshape(arrived.shape), 'tensor', split_axis=0, c...  26.5 us
    ppermute x2, waiting for transfers between devices, from_behind(): return lax.ppermute(value, axis, pairs)  17.6 us
    all_to_all x1, blocking collectives, body(): lax.all_to_all(own_columns, 'tensor', split_axis=0, concat_axis=1, tiled=...  12.3 us
    dot_general x1, matrix products, body(): jnp.dot(hidden, w_down[0], preferred_element_type=jnp.float32)  9.06 us
    all_gather x1, waiting for transfers between devices, body(): lax.all_gather(own_kv, 'tensor', axis=0, tiled=True)  8.85 us
    all_gather x1, blocking collectives, body(): lax.all_gather(segment_ids, 'tensor', axis=0, tiled=True)  7.8 us
  transfers between devices with their start and end apart: 6, of which 5 were waited for; matrix products, arithmetic and copies ran while one was open for 10% of the time, Pallas kernels for 0%

commit v1 on v0

--- a/solution.py
+++ b/solution.py
@@ -1,8 +1,11 @@
+import functools
 import math
 
 import jax
 import jax.numpy as jnp
 from jax import lax
+from jax.experimental import pallas as pl
+from jax.experimental.pallas import tpu as pltpu
 from jax.sharding import PartitionSpec as P
 
 HEADS = 12
@@ -10,9 +13,455 @@
 HEAD = 128
 TOP = 4
 PAGE = 16
+CORES = 2
+CHIPS = 4
 
 
 epsilon = 1e-06
+MIB = 1024 * 1024
+
+
+def vmem():
+    return pl.BlockSpec(memory_space=pltpu.VMEM)
+
+
+def anywhere():
+    return pl.BlockSpec(memory_space=pl.ANY)
+
+
+def params(mib):
+    return pltpu.CompilerParams(vmem_limit_bytes=mib * MIB)
+
+
+def place():
+    index = lax.axis_index("tensor")
+    return index // CORES, lax.rem(index, CORES)
+
+
+def hop(value, by):
+    length = lax.axis_size("tensor")
+    return lax.ppermute(value, "tensor", [(i, i ^ by) for i in range(length)])
+
+
+def chip_exchange(value):
+    length = lax.axis_size("tensor")
+    groups = [[i for i in range(length) if i % CORES == core] for core in range(CORES)]
+    return lax.all_to_all(
+        value, "tensor", split_axis=0, concat_axis=0, tiled=True, axis_index_groups=groups
+    )
+
+
+def norm_kernel(tokens_ref, gain_ref, out_ref):
+    wide = tokens_ref[...].astype(jnp.float32)
+    mean_sq = jnp.mean(wide * wide, axis=-1, keepdims=True)
+    out_ref[...] = (wide * lax.rsqrt(mean_sq + epsilon) * gain_ref[...]).astype(jnp.bfloat16)
+
+
+def norm_call(tokens, gain):
+    return pl.pallas_call(
+        norm_kernel,
+        out_shape=jax.ShapeDtypeStruct(tokens.shape, jnp.bfloat16),
+        in_specs=[vmem()] * 2,
+        out_specs=vmem(),
+        compiler_params=params(16),
+        name="norm_tokens",
+    )(tokens, gain.reshape(1, -1))
+
+
+def transpose_kernel(in_ref, out_ref):
+    out_ref[...] = in_ref[...].T
+
+
+def transpose_call(value):
+    return pl.pallas_call(
+        transpose_kernel,
+        out_shape=jax.ShapeDtypeStruct(value.shape[::-1], value.dtype),
+        in_specs=[vmem()],
+        out_specs=vmem(),
+        compiler_params=params(16),
+        name="transpose_w_out",
+    )(value)
+
+
+def project_kernel(own, by_x, by_y, by_xy, w_own, w_other, out_ref, rows_ref):
+    chip, core = place()
+    rows, cols = own.shape[0], w_own.shape[1]
+    for hop_by, piece in enumerate((own, by_x, by_y, by_xy)):
+        start = pl.multiple_of((chip ^ hop_by) * rows, rows)
+        rows_ref[pl.ds(start, rows), :] = piece[...]
+    for which, weights in ((core, w_own), (1 - core, w_other)):
+        start = pl.multiple_of(which * cols, cols)
+        out_ref[:, pl.ds(start, cols)] = jnp.dot(
+            rows_ref[...], weights[...], preferred_element_type=jnp.float32
+        ).astype(jnp.bfloat16)
+
+
+def project_call(pieces, w_own, w_other):
+    rows, width = pieces[0].shape
+    return pl.pallas_call(
+        project_kernel,
+        out_shape=jax.ShapeDtypeStruct((CHIPS * rows, CORES * w_own.shape[1]), jnp.bfloat16),
+        in_specs=[vmem()] * 6,
+        out_specs=vmem(),
+        scratch_shapes=[pltpu.VMEM((CHIPS * rows, width), jnp.bfloat16)],
+        compiler_params=params(24),
+        name="project",
+    )(*pieces, w_own, w_other)
+
+
+def attend_kernel(
+    proj_ref, same_ref, other_ref, prev_ref, prev_other_ref, table_ref, out_ref,
+    q_ref, s_ref, top_ref, sum_ref, acc_ref,
+):
+    chip, core = place()
+    seq = lax.axis_index("seq")
+    rows = prev_ref.shape[0]
+    per_group = HEADS // KV_HEADS
+    per_chip = HEADS // (CHIPS - 1)
+    block_rows = rows * CORES * CHIPS
+    n_table = table_ref.shape[0]
+    experts = table_ref.shape[1] // 2
+    me = seq * CORES * CHIPS + chip * CORES + core
+    own_first = me * rows
+
+    own_seg = jnp.broadcast_to(table_ref[me][experts : experts + 1, :], (rows, rows)).T
+    before = jnp.zeros((rows, rows), jnp.float32)
+    for i in range(n_table):
+        row = table_ref[i][experts : experts + 1, :]
+        before = before + jnp.where(row < own_seg, 1.0, 0.0)
+    first_key = jnp.sum(before, axis=1, keepdims=True).astype(jnp.int32)
+    query_pos = own_first + lax.broadcasted_iota(jnp.int32, (rows, 1), 0)
+    lowest = jnp.min(first_key)
+    lane = lax.broadcasted_iota(jnp.int32, (rows, rows), 1)
+
+    for head in range(HEADS):
+        j, i = head // per_chip, head % per_chip
+        q_ref[head * rows : (head + 1) * rows, :] = proj_ref[
+            j * rows : (j + 1) * rows, i * HEAD : (i + 1) * HEAD
+        ]
+
+    blocks = []
+    for ref, which in ((same_ref, core), (other_ref, 1 - core)):
+        for j in range(CHIPS):
+            base = jnp.where(j <= chip, seq, seq - 1) * block_rows
+            blocks.append((ref, j * rows, base + (j * CORES + which) * rows))
+    for ref, which in ((prev_ref, core), (prev_other_ref, 1 - core)):
+        blocks.append((ref, 0, (seq - 1) * block_rows + (chip * CORES + which) * rows))
+
+    scale = math.log2(math.e) / math.sqrt(HEAD)
+    group_rows = per_group * rows
+    top_ref[...] = jnp.full(top_ref.shape, -jnp.inf, jnp.float32)
+    sum_ref[...] = jnp.zeros(sum_ref.shape, jnp.float32)
+    acc_ref[...] = jnp.zeros(acc_ref.shape, jnp.float32)
+    used = []
+    for n, (ref, row0, first) in enumerate(blocks):
+        use = (first <= own_first) & (first + rows > lowest)
+        used.append(use)
+
+        @pl.when(use)
+        def _(n=n, ref=ref, row0=row0, first=first):
+            key_pos = first + lane
+            bias = jnp.where((key_pos >= first_key) & (key_pos <= query_pos), 0.0, -jnp.inf)
+            for g in range(KV_HEADS):
+                keys = ref[row0 : row0 + rows, g * HEAD : (g + 1) * HEAD]
+                scores = lax.dot_general(
+                    q_ref[g * group_rows : (g + 1) * group_rows, :], keys,
+                    (((1,), (1,)), ((), ())), preferred_element_type=jnp.float32,
+                )
+                scores = (scores.reshape(per_group, rows, rows) * scale + bias[None]).reshape(
+                    group_rows, rows
+                )
+                s_ref[n, g * group_rows : (g + 1) * group_rows, :] = scores
+                part = top_ref.at[g * group_rows : (g + 1) * group_rows, :]
+                part[...] = jnp.maximum(part[...], scores)
+
+    top_ref[...] = jnp.broadcast_to(
+        jnp.max(top_ref[...], axis=1, keepdims=True), top_ref.shape
+    )
+    for n, (ref, row0, first) in enumerate(blocks):
+
+        @pl.when(used[n])
+        def _(n=n, ref=ref, row0=row0):
+            for g in range(KV_HEADS):
+                part = slice(g * group_rows, (g + 1) * group_rows)
+                weights = jnp.exp2(s_ref[n, part, :] - top_ref[part, :])
+                sum_ref[part, :] += weights
+                values = ref[row0 : row0 + rows, (KV_HEADS + g) * HEAD : (KV_HEADS + g + 1) * HEAD]
+                acc_ref[part, :] += jnp.dot(
+                    weights.astype(jnp.bfloat16), values, preferred_element_type=jnp.float32
+                )
+
+    for head in range(HEADS):
+        part = slice(head * rows, (head + 1) * rows)
+        total = jnp.sum(sum_ref[part, :], axis=1, keepdims=True)
+        out_ref[:, head * HEAD : (head + 1) * HEAD] = (acc_ref[part, :] / total).astype(
+            jnp.bfloat16
+        )
+
+
+def attend_call(projected, same, other, prev, prev_other, table):
+    rows = prev.shape[0]
+    wide = HEADS * rows
+    return pl.pallas_call(
+        attend_kernel,
+        out_shape=jax.ShapeDtypeStruct((rows, HEADS * HEAD), jnp.bfloat16),
+        in_specs=[vmem()] * 6,
+        out_specs=vmem(),
+        scratch_shapes=[
+            pltpu.VMEM((wide, HEAD), jnp.bfloat16),
+            pltpu.VMEM((2 * CHIPS + 2, wide, rows), jnp.float32),
+            pltpu.VMEM((wide, rows), jnp.float32),
+            pltpu.VMEM((wide, rows), jnp.float32),
+            pltpu.VMEM((wide, HEAD), jnp.float32),
+        ],
+        compiler_params=params(32),
+        name="attend",
+    )(projected, same, other, prev, prev_other, table)
+
+
+def residual_kernel(*refs):
+    same, other = refs[:CHIPS], refs[CHIPS : 2 * CHIPS]
+    context_ref, tokens_ref, gain_ref, residual_ref, out_ref, w_ref, sem = refs[2 * CHIPS :]
+    chip, core = place()
+    cols = same[0].shape[0]
+    copies = []
+    for pieces, which in ((same, core), (other, 1 - core)):
+        for hop_by, piece in enumerate(pieces):
+            start = pl.multiple_of(((chip ^ hop_by) * CORES + which) * cols, cols)
+            copies.append(
+                pltpu.make_async_copy(
+                    piece, w_ref.at[pl.ds(start, cols), :], sem.at[len(copies)]
+                )
+            )
+    for copy in copies:
+        copy.start()
+    for copy in copies:
+        copy.wait()
+    added = lax.dot_general(
+        context_ref[...], w_ref[...], (((1,), (1,)), ((), ())), preferred_element_type=jnp.float32
+    )
+    residual = (tokens_ref[...].astype(jnp.float32) + added).astype(jnp.bfloat16)
+    residual_ref[...] = residual
+    wide = residual.astype(jnp.float32)
+    mean_sq = jnp.mean(wide * wide, axis=-1, keepdims=True)
+    out_ref[...] = (wide * lax.rsqrt(mean_sq + epsilon) * gain_ref[...]).astype(jnp.bfloat16)
+
+
+def residual_call(w_same, w_other, context, tokens, gain):
+    cols, depth = w_same[0].shape
+    shape = jax.ShapeDtypeStruct(tokens.shape, jnp.bfloat16)
+    return pl.pallas_call(
+        residual_kernel,
+        out_shape=(shape, shape),
+        in_specs=[anywhere()] * (2 * CHIPS) + [vmem()] * 3,
+        out_specs=(vmem(), vmem()),
+        scratch_shapes=[
+            pltpu.VMEM((2 * CHIPS * cols, depth), jnp.bfloat16),
+            pltpu.SemaphoreType.DMA((2 * CHIPS,)),
+        ],
+        compiler_params=params(24),
+        name="residual",
+    )(*w_same, *w_other, context, tokens, gain.reshape(1, -1))
+
+
+def expert_kernel(
+    steps, own, by_x, by_y, by_xy, table_ref,
+    gate_own, up_own, down_own, gate_other, up_other, down_other,
+    out_own, out_x, out_y, out_xy, rows_ref, acc_ref, total_ref,
+):
+    chip, core = place()
+    seq = lax.axis_index("seq")
+    rows = own.shape[0]
+    experts = table_ref.shape[1] // 2
+    step = pl.program_id(0)
+
+    @pl.when(step == 0)
+    def _():
+        for hop_by, piece in enumerate((own, by_x, by_y, by_xy)):
+            rows_ref[hop_by * rows : (hop_by + 1) * rows, :] = piece[...]
+
+    def part(gate, up, down, first):
+        gate_out = jnp.dot(rows_ref[...], gate[...], preferred_element_type=jnp.float32)
+        up_out = jnp.dot(rows_ref[...], up[...], preferred_element_type=jnp.float32)
+        hidden = (jnp.maximum(gate_out, 0.0) * up_out).astype(jnp.bfloat16)
+        made = jnp.dot(hidden, down[...], preferred_element_type=jnp.float32)
+
+        @pl.when(step == first)
+        def _():
+            acc_ref[...] = made
+
+        @pl.when(step != first)
+        def _():
+            acc_ref[...] += made
+
+    def weight_of(hop_by, which):
+        expert = chip * CORES + which
+        block = table_ref[(seq * CHIPS + (chip ^ hop_by)) * CORES + core]
+        row_id = lax.broadcasted_iota(jnp.int32, block.shape, 0)
+        row = jnp.sum(jnp.where(row_id == expert, block, 0.0), axis=0, keepdims=True)
+        return jnp.broadcast_to(row, (rows, rows)).T[:, :1]
+
+    @pl.when(step < steps)
+    def _():
+        part(gate_own, up_own, down_own, 0)
+
+    @pl.when(step >= steps)
+    def _():
+        part(gate_other, up_other, down_other, steps)
+
+    @pl.when(step == steps - 1)
+    def _():
+        for hop_by in range(CHIPS):
+            span = slice(hop_by * rows, (hop_by + 1) * rows)
+            made = acc_ref[span, :].astype(jnp.bfloat16).astype(jnp.float32)
+            total_ref[span, :] = weight_of(hop_by, core) * made
+
+    @pl.when(step == 2 * steps - 1)
+    def _():
+        for hop_by, out_ref in enumerate((out_own, out_x, out_y, out_xy)):
+            span = slice(hop_by * rows, (hop_by + 1) * rows)
+            made = acc_ref[span, :].astype(jnp.bfloat16).astype(jnp.float32)
+            out_ref[...] = (total_ref[span, :] + weight_of(hop_by, 1 - core) * made).astype(
+                out_ref.dtype
+            )
+
+
+def expert_call(pieces, table, own_weights, other_weights):
+    rows, width = pieces[0].shape
+    hidden = own_weights[0].shape[1]
+    tile = 256
+    steps = hidden // tile
+
+    def own_tile(i):
+        return jnp.minimum(i, steps - 1)
+
+    def other_tile(i):
+        return jnp.maximum(i - steps, 0)
+
+    def weight_specs(tile_of):
+        return [
+            pl.BlockSpec((width, tile), lambda i: (0, tile_of(i))),
+            pl.BlockSpec((width, tile), lambda i: (0, tile_of(i))),
+            pl.BlockSpec((tile, width), lambda i: (tile_of(i), 0)),
+        ]
+
+    whole = pl.BlockSpec((rows, width), lambda i: (0, 0))
+    return pl.pallas_call(
+        functools.partial(expert_kernel, steps),
+        grid=(2 * steps,),
+        out_shape=tuple(
+            jax.ShapeDtypeStruct((rows, width), kind)
+            for kind in (jnp.float32, jnp.bfloat16, jnp.bfloat16, jnp.bfloat16)
+        ),
+        in_specs=[whole] * CHIPS
+        + [pl.BlockSpec(table.shape, lambda i: (0, 0, 0))]
+        + weight_specs(own_tile)
+        + weight_specs(other_tile),
+        out_specs=(whole,) * CHIPS,
+        scratch_shapes=[
+            pltpu.VMEM((CHIPS * rows, width), jnp.bfloat16),
+            pltpu.VMEM((CHIPS * rows, width), jnp.float32),
+            pltpu.VMEM((CHIPS * rows, width), jnp.float32),
+        ],
+        compiler_params=params(40),
+        name="experts",
+    )(*pieces, table, *own_weights, *other_weights)
+
+
+def mix_kernel(residual_ref, own, by_x, by_y, by_xy, out_ref):
+    total = own[...] + by_x[...].astype(jnp.float32)
+    total = total + by_y[...].astype(jnp.float32) + by_xy[...].astype(jnp.float32)
+    out_ref[...] = (residual_ref[...].astype(jnp.float32) + total).astype(jnp.bfloat16)
+
+
+def mix_call(residual, pieces):
+    return pl.pallas_call(
+        mix_kernel,
+        out_shape=jax.ShapeDtypeStruct(residual.shape, jnp.bfloat16),
+        in_specs=[vmem()] * 5,
+        out_specs=vmem(),
+        compiler_params=params(16),
+        name="mix",
+    )(residual, *pieces)
+
+
+def cache_kernel(table_ref, kv_ref, out_ref):
+    pages = out_ref.shape[0]
+    index = lax.axis_index("tensor")
+
+    def one(logical, carry):
+        slot = table_ref[0, logical]
+
+        @pl.when(slot // pages == index)
+        def _():
+            start = pl.multiple_of(logical * PAGE, PAGE)
+            out_ref[lax.rem(slot, pages)] = kv_ref[pl.ds(start, PAGE), :]
+
+        return carry
+
+    lax.fori_loop(0, table_ref.shape[1], one, 0)
+
+
+def cache_call(page_table, block_kv, pages):
+    return pl.pallas_call(
+        cache_kernel,
+        out_shape=jax.ShapeDtypeStruct((pages, PAGE, block_kv.shape[1]), jnp.bfloat16),
+        in_specs=[pl.BlockSpec(memory_space=pltpu.SMEM), vmem()],
+        out_specs=vmem(),
+        compiler_params=params(16),
+        name="cache_pages",
+    )(page_table, block_kv)
+
+
+def chip_body(
+    tokens, segment_ids, page_table, attn_gain, w_qkv, w_out, moe_gain,
+    route_ids, route_weight, w_gate, w_up, w_down,
+):
+    rows = tokens.shape[0]
+    seq_size = lax.axis_size("seq")
+    experts = lax.axis_size("tensor") * w_gate.shape[0]
+    chip, core = place()
+
+    normed = norm_call(tokens, attn_gain)
+    pieces = [normed] + [hop(normed, CORES * by) for by in (1, 2, 3)]
+    w_qkv_other = hop(w_qkv, 1)
+    expert_own = [w_gate[0], w_up[0], w_down[0]]
+    expert_other = [hop(w, 1) for w in expert_own]
+
+    routes, weights, segs, _ = lax.optimization_barrier(
+        (route_ids, route_weight, segment_ids, normed)
+    )
+    named = routes.T[:, None, :] == jnp.arange(experts, dtype=jnp.int32)[None, :, None]
+    spread = jnp.sum(jnp.where(named, weights.T[:, None, :], 0.0), axis=0)
+    seg_rows = jnp.broadcast_to(segs.astype(jnp.float32)[None, :], (experts, rows))
+    table = lax.all_gather(
+        jnp.concatenate([spread, seg_rows], axis=0), ("seq", "tensor"), axis=0, tiled=False
+    )
+
+    projected = chip_exchange(project_call(pieces, w_qkv, w_qkv_other))
+    own_kv = projected[(CHIPS - 1) * rows :]
+    prev_kv = lax.ppermute(own_kv, "seq", [(i, i + 1) for i in range(seq_size - 1)])
+    going = jnp.where(
+        (jnp.arange(CHIPS, dtype=jnp.int32) < chip)[:, None, None], prev_kv[None], own_kv[None]
+    ).reshape(CHIPS * rows, own_kv.shape[1])
+    same_kv = chip_exchange(going)
+    other_kv = hop(same_kv, 1)
+    prev_other = hop(prev_kv, 1)
+    context = attend_call(projected, same_kv, other_kv, prev_kv, prev_other, table)
+
+    w_out_own, _ = lax.optimization_barrier((transpose_call(w_out), projected))
+    w_out_same = [w_out_own] + [hop(w_out_own, CORES * by) for by in (1, 2, 3)]
+    w_out_other = [hop(w, 1) for w in w_out_same]
+    residual, expert_input = residual_call(w_out_same, w_out_other, context, tokens, moe_gain)
+
+    inputs = [expert_input] + [hop(expert_input, CORES * by) for by in (1, 2, 3)]
+    made = expert_call(inputs, table, expert_own, expert_other)
+    returned = [made[0]] + [hop(made[by], CORES * by) for by in (1, 2, 3)]
+    mixed = mix_call(residual, returned)
+
+    block_kv = lax.all_gather(own_kv, "tensor", axis=0, tiled=True)
+    cache = cache_call(page_table, block_kv, rows // PAGE)
+    return (mixed, cache)
 
 
 def from_behind(value, axis, by):
@@ -39,7 +488,7 @@
     return jnp.einsum("hqk,kd->qhd", shares, values_window, preferred_element_type=jnp.float32)
 
 
-def body(
+def block_body(
     tokens,
     segment_ids,
     page_table,
@@ -149,9 +598,14 @@
     return (mixed, cache_pages)
 
 
+def by_chips(mesh):
+    size = mesh.shape["tensor"]
+    return size == CORES * CHIPS and (HEADS + 2 * KV_HEADS) % size == 0
+
+
 def solution(mesh):
     return jax.shard_map(
-        body,
+        chip_body if by_chips(mesh) else block_body,
         mesh=mesh,
         in_specs=(
             P(("seq", "tensor"), None),

time: 231 us -> 201 us (0.87)
  matrix products: 34.3 us -> 0 us
  Pallas kernels: 0 us -> 27 us
  starting transfers between devices: 12.4 us -> 27.9 us
  other arithmetic: 11.8 us -> 0.94 us
  local copies, waits for them, and re-layouts: 16.8 us -> 6.06 us
  blocking collectives: 52.2 us -> 42.7 us
  waiting for transfers between devices: 88.9 us -> 81.1 us
    ppermute x2 -> x23, waiting for transfers between devices: 17.6 us -> 65.8 us  [the longest x22 62.7 us: hop(): return lax.ppermute(value, 'tensor', [(i, i ^ by) for i in range(length)])]
    all_to_all x2 -> x0, blocking collectives: 44.4 us -> none  [the longest x1 32.1 us: body(): lax.all_to_all(outgoing, 'tensor', split_axis=0, concat_axis=0, tiled=True)]
    all_gather x3 -> x1, waiting for transfers between devices: 44.1 us -> 0.01 us  [chip_body(): block_kv = lax.all_gather(own_kv, 'tensor', axis=0, tiled=True)]
    all_gather x1, blocking collectives: 7.8 us -> 42.7 us  [chip_body(): lax.all_gather(jnp.concatenate([spread, seg_rows], axis=0), ('seq', 'tens...]
    dot_general x8 -> x0, matrix products: 29.4 us -> none  [the longest x1 9.06 us: body(): jnp.dot(hidden, w_down[0], preferred_element_type=jnp.float32)]
    pallas_call x0 -> x8, Pallas kernels: none -> 27 us  [the longest x1 14.3 us: expert_call(): pl.pallas_call(functools.partial(expert_kernel, steps), grid=(2 * steps,)...]
    ppermute x2 -> x23, starting transfers between devices: 7.78 us -> 20.9 us  [the longest x22 17.3 us: hop(): return lax.ppermute(value, 'tensor', [(i, i ^ by) for i in range(length)])]
    all_to_all x1 -> x2, waiting for transfers between devices: 26.5 us -> 15.3 us  [chip_exchange(): lax.all_to_all(value, 'tensor', split_axis=0, concat_axis=0, tiled=True,...]
  transfers between devices with their start and end apart: 6 -> 26, of which waited for: 5 -> 14; matrix products, arithmetic and copies ran while one was open for 10% -> 1% of each run, Pallas kernels for 0% -> 12%
where the time goes in v1:
time: 201 us; the launch traced here: 200 us
  waiting for transfers between devices  81.1 us (40%)
  blocking collectives  42.7 us (21%)
  starting transfers between devices  27.9 us (14%)
  Pallas kernels  27 us (13%)
  between operations  14.3 us (7%)
  local copies, waits for them, and re-layouts  6.06 us (3%)
    ppermute x22, waiting for transfers between devices, hop(): return lax.ppermute(value, 'tensor', [(i, i ^ by) for i in range(length)])  62.7 us
    all_gather x1, blocking collectives, chip_body(): lax.all_gather(jnp.concatenate([spread, seg_rows], axis=0), ('seq', 'tens...  42.7 us
    ppermute x22, starting transfers between devices, hop(): return lax.ppermute(value, 'tensor', [(i, i ^ by) for i in range(length)])  17.3 us
    all_to_all x2, waiting for transfers between devices, chip_exchange(): lax.all_to_all(value, 'tensor', split_axis=0, concat_axis=0, tiled=True,...  15.3 us
    pallas_call x1, Pallas kernels, expert_call(): pl.pallas_call(functools.partial(expert_kernel, steps), grid=(2 * steps,)...  14.3 us
    all_to_all x2, starting transfers between devices, chip_exchange(): lax.all_to_all(value, 'tensor', split_axis=0, concat_axis=0, tiled=True,...  6.94 us
    unnamed x29, local copies, waits for them, and re-layouts  4.68 us
  transfers between devices with their start and end apart: 26, of which 14 were waited for; matrix products, arithmetic and copies ran while one was open for 1% of the time, Pallas kernels for 12%

profile of v1, /device:TPU:0, one launch (start us, length us, event | category | flops | bytes accessed | tf_op | source)
XLA Modules:
  0.0 200.0 jit_solution(13882892734289930073)
XLA Ops:
  7.2 0.5 collective-permute-start.3
  7.7 0.7 reshape.34.gain_ref
  8.4 1.0 copy-done.2
  9.4 0.2 norm_tokens.1.own
  9.6 3.5 %collective-permute-start.2 = (bf16[128,1536]{1,0:T(8,128)(2,1)S(1)}, bf16[128,1536]{1,0:T(8,128)(2,1)S(1)}, u32[]{:S(2)}, u32[]{:S(2)}) collective-permute-start(bf16[128,1536]{1,0:T(8,128)(2,1)S(1)} %norm_tokens.1.own), channel_id=1, source_target_pairs={{0,6},{1,7},{2,4},{3,5},{4,2},{5,3},{6,0},{7,1},{8,14},{9,15},{10,... | collective-permute-start | bytes 1179656 | tf_op jit(solution)/shard_map/ppermute | solution.py:43
  13.1 0.5 collective-permute-start.1
  13.6 0.1 collective-permute-start
  13.7 9.4 %collective-permute-done.2.by_xy = bf16[128,1536]{1,0:T(8,128)(2,1)S(1)} collective-permute-done((bf16[128,1536]{1,0:T(8,128)(2,1)S(1)}, bf16[128,1536]{1,0:T(8,128)(2,1)S(1)}, u32[]{:S(2)}, u32[]{:S(2)}) %collective-permute-start.2) | collective-permute-done | bytes 393248 | tf_op jit(solution)/shard_map/ppermute | solution.py:43
  23.1 8.2 %collective-permute-done.1.by_y = bf16[128,1536]{1,0:T(8,128)(2,1)S(1)} collective-permute-done((bf16[128,1536]{1,0:T(8,128)(2,1)S(1)}, bf16[128,1536]{1,0:T(8,128)(2,1)S(1)}, u32[]{:S(2)}, u32[]{:S(2)}) %collective-permute-start.1) | collective-permute-done | bytes 393248 | tf_op jit(solution)/shard_map/ppermute | solution.py:43
  31.3 0.3 collective-permute-done.by_x
  31.6 1.1 copy-done.5
  32.7 1.9 project.1
  34.6 3.5 %all-to-all-start = ((bf16[4,128,512]{2,1,0:T(8,128)(2,1)}), bf16[4,128,512]{2,1,0:T(8,128)(2,1)S(1)}, u32[]{:S(2)}, u32[]{:S(2)}) async-start(bf16[4,128,512]{2,1,0:T(8,128)(2,1)} %bitcast), calls=%async_computation | async-start | bytes 1048576 | tf_op jit(solution)/shard_map/all_to_all | solution.py:49
  38.1 0.0 copy-start.10
  38.1 0.0 copy-start.13
  38.1 0.0 copy-start.11
  38.1 0.0 copy-start.12
  38.1 0.1 collective-permute-start.17
  38.2 0.3 copy.15.in_ref
  38.5 0.2 transpose_w_out.1.refs_0_
  38.7 7.5 %all-to-all-done = bf16[4,128,512]{2,1,0:T(8,128)(2,1)S(1)} async-done(((bf16[4,128,512]{2,1,0:T(8,128)(2,1)}), bf16[4,128,512]{2,1,0:T(8,128)(2,1)S(1)}, u32[]{:S(2)}, u32[]{:S(2)}) %all-to-all-start) | async-done | bytes 524320 | tf_op jit(solution)/shard_map/all_to_all | solution.py:49
  46.3 0.0 collective-permute-start.7
  46.3 1.4 collective-permute-start.6
  47.7 0.7 fusion
  48.4 3.7 %collective-permute-start.11 = (bf16[128,512]{1,0:T(8,128)(2,1)S(1)}, bf16[128,512]{1,0:T(8,128)(2,1)S(1)}, u32[]{:S(2)}, u32[]{:S(2)}) collective-permute-start(bf16[128,512]{1,0:T(8,128)(2,1)S(1)} %get-tuple-element.23), channel_id=1, source_target_pairs={{0,8},{8,16},{16,24},{1,9},{9,17},{17,25},{2,10},{10,18},{18,26},{... | collective-permute-start | bytes 393224 | tf_op jit(solution)/shard_map/ppermute | solution.py:443
  52.0 3.1 %collective-permute-done.11.prev_ref = bf16[128,512]{1,0:T(8,128)(2,1)S(1)} collective-permute-done((bf16[128,512]{1,0:T(8,128)(2,1)S(1)}, bf16[128,512]{1,0:T(8,128)(2,1)S(1)}, u32[]{:S(2)}, u32[]{:S(2)}) %collective-permute-start.11) | collective-permute-done | bytes 131104 | tf_op jit(solution)/shard_map/ppermute | solution.py:443
  55.2 0.5 collective-permute-start.18
  55.7 1.0 collective-permute-done.13.prev_other_ref
  56.7 0.1 collective-permute-start.19
  56.8 1.5 collective-permute-start.5
  58.3 4.7 %collective-permute-done.6.refs_3_ = bf16[192,1536]{1,0:T(8,128)(2,1)S(1)} collective-permute-done((bf16[192,1536]{1,0:T(8,128)(2,1)S(1)}, bf16[192,1536]{1,0:T(8,128)(2,1)S(1)}, u32[]{:S(2)}, u32[]{:S(2)}) %collective-permute-start.6) | collective-permute-done | bytes 589856 | tf_op jit(solution)/shard_map/ppermute | solution.py:43
  63.0 1.4 collective-permute-start.4
  64.4 0.9 broadcast_select_fusion
  65.4 3.5 %all-to-all-start.1 = ((bf16[4,128,512]{2,1,0:T(8,128)(2,1)}), bf16[4,128,512]{2,1,0:T(8,128)(2,1)S(1)}, u32[]{:S(2)}, u32[]{:S(2)}) async-start(bf16[4,128,512]{2,1,0:T(8,128)(2,1)} %broadcast_select_fusion), calls=%async_computation.1 | async-start | bytes 1048576 | tf_op jit(solution)/shard_map/all_to_all | solution.py:49
  68.8 0.0 all-gather.4.cloned.1.call-start
  68.9 6.8 %collective-permute-done.5.refs_2_ = bf16[192,1536]{1,0:T(8,128)(2,1)} collective-permute-done((bf16[192,1536]{1,0:T(8,128)(2,1)S(1)}, bf16[192,1536]{1,0:T(8,128)(2,1)}, u32[]{:S(2)}, u32[]{:S(2)}) %collective-permute-start.5) | collective-permute-done | bytes 589856 | tf_op jit(solution)/shard_map/ppermute | solution.py:43
  75.7 0.0 collective-permute-start.10
  75.7 7.8 %all-to-all-done.1 = bf16[4,128,512]{2,1,0:T(8,128)(2,1)S(1)} async-done(((bf16[4,128,512]{2,1,0:T(8,128)(2,1)}), bf16[4,128,512]{2,1,0:T(8,128)(2,1)S(1)}, u32[]{:S(2)}, u32[]{:S(2)}) %all-to-all-start.1) | async-done | bytes 524320 | tf_op jit(solution)/shard_map/all_to_all | solution.py:49
  83.5 0.0 collective-permute-done.4.refs_1_
  83.5 0.0 all-gather.4.cloned.1.call-update
  83.6 2.0 %collective-permute-done.12.other_ref = bf16[512,512]{1,0:T(8,128)(2,1)} collective-permute-done((bf16[512,512]{1,0:T(8,128)(2,1)S(1)}, bf16[512,512]{1,0:T(8,128)(2,1)}, u32[]{:S(2)}, u32[]{:S(2)}) %collective-permute-start.12) | collective-permute-done | bytes 524320 | tf_op jit(solution)/shard_map/ppermute | solution.py:43
  85.6 0.1 collective-permute-start.9
  85.7 0.4 collective-permute-start.8
  86.2 42.7 %all-gather = f32[512,128]{1,0:T(8,128)S(1)} all-gather(f32[16,128]{1,0:T(8,128)S(1)} %pad_maximum_fusion), channel_id=2, replica_groups=mesh['seq'=4,'tensor'=8] {'seq','tensor'}, dimensions={0}, use_global_device_ids=true | all-gather | bytes 270336 | tf_op jit(solution)/shard_map/all_gather | solution.py:437
  128.8 3.0 %attend.1.refs_8_ = bf16[128,1536]{1,0:T(8,128)(2,1)S(1)} custom-call(bf16[512,512]{1,0:T(8,128)(2,1)S(1)} %bitcast.12, bf16[512,512]{1,0:T(8,128)(2,1)S(1)} %bitcast.20, bf16[512,512]{1,0:T(8,128)(2,1)} %collective-permute-done.12.other_ref, bf16[128,512]{1,0:T(8,128)(2,1)S(1)} %collective-permute-done.11.prev_ref, ...), custom_call_target="tpu_custom_call" | custom-call | tf_op jit(solution)/shard_map/attend/pallas_call | solution.py:205
  131.8 0.0 copy-start
  131.8 0.0 copy-start.1
  131.9 4.0 %residual.1 = (bf16[128,1536]{1,0:T(8,128)(2,1)S(1)}, bf16[128,1536]{1,0:T(8,128)(2,1)S(1)}) custom-call(bf16[192,1536]{1,0:T(8,128)(2,1)S(1)} %transpose_w_out.1.refs_0_, bf16[192,1536]{1,0:T(8,128)(2,1)} %collective-permute-done.4.refs_1_, bf16[192,1536]{1,0:T(8,128)(2,1)} %collective-permute-done.5.refs_2_, ...), custom_call_target="tpu_custom_call" | custom-call | tf_op jit(solution)/shard_map/residual/pallas_call | solution.py:253
  135.9 0.0 copy-start.6
  135.9 0.0 copy-start.8
  135.9 0.1 collective-permute-start.16
  136.0 0.1 collective-permute-start.15
  136.1 3.4 %collective-permute-start.14 = (bf16[128,1536]{1,0:T(8,128)(2,1)S(1)}, bf16[128,1536]{1,0:T(8,128)(2,1)S(1)}, u32[]{:S(2)}, u32[]{:S(2)}) collective-permute-start(bf16[128,1536]{1,0:T(8,128)(2,1)S(1)} %get-tuple-element.17.own), channel_id=1, source_target_pairs={{0,2},{1,3},{2,0},{3,1},{4,6},{5,7},{6,4},{7,5},{8,10},{9,11},{10,... | collective-permute-start | bytes 1179656 | tf_op jit(solution)/shard_map/ppermute | solution.py:43
  139.5 9.4 %collective-permute-done.16.by_xy = bf16[128,1536]{1,0:T(8,128)(2,1)S(1)} collective-permute-done((bf16[128,1536]{1,0:T(8,128)(2,1)S(1)}, bf16[128,1536]{1,0:T(8,128)(2,1)S(1)}, u32[]{:S(2)}, u32[]{:S(2)}) %collective-permute-start.16) | collective-permute-done | bytes 393248 | tf_op jit(solution)/shard_map/ppermute | solution.py:43
  148.9 7.5 %collective-permute-done.15.by_y = bf16[128,1536]{1,0:T(8,128)(2,1)S(1)} collective-permute-done((bf16[128,1536]{1,0:T(8,128)(2,1)S(1)}, bf16[128,1536]{1,0:T(8,128)(2,1)S(1)}, u32[]{:S(2)}, u32[]{:S(2)}) %collective-permute-start.15) | collective-permute-done | bytes 393248 | tf_op jit(solution)/shard_map/ppermute | solution.py:43
  156.4 14.3 %experts.1 = (f32[128,1536]{1,0:T(8,128)S(1)}, bf16[128,1536]{1,0:T(8,128)(2,1)}, bf16[128,1536]{1,0:T(8,128)(2,1)}, bf16[128,1536]{1,0:T(8,128)(2,1)S(1)}) custom-call(bf16[128,1536]{1,0:T(8,128)(2,1)S(1)} %get-tuple-element.17.own, bf16[128,1536]{1,0:T(8,128)(2,1)S(1)} %collective-permute-done.14.by_x, bf16[128,1536]{1,0:T(8,128)(2,1)S(1)} %collective-permute-done.15.by_y, ...), custom_call_target="tpu_custom_call" | custom-call | tf_op jit(solution)/shard_map/experts/pallas_call | solution.py:349
  170.7 1.5 collective-permute-start.21
  172.2 2.0 %collective-permute-start.22 = (bf16[128,1536]{1,0:T(8,128)(2,1)S(1)}, bf16[128,1536]{1,0:T(8,128)(2,1)S(1)}, u32[]{:S(2)}, u32[]{:S(2)}) collective-permute-start(bf16[128,1536]{1,0:T(8,128)(2,1)S(1)} %get-tuple-element.21), channel_id=1, source_target_pairs={{0,6},{1,7},{2,4},{3,5},{4,2},{5,3},{6,0},{7,1},{8,14},{9,15},{10,... | collective-permute-start | bytes 1179656 | tf_op jit(solution)/shard_map/ppermute | solution.py:43
  174.2 1.2 copy-done.4
  175.4 2.5 %cache_pages.1 = bf16[8,16,512]{2,1,0:T(8,128)(2,1)} custom-call(s32[1,64]{1,0:T(1,128)S(1)} %copy-done.8, bf16[1024,512]{1,0:T(8,128)(2,1)S(1)} %bitcast.21), custom_call_target="tpu_custom_call" | custom-call | tf_op jit(solution)/shard_map/cache_pages/pallas_call | solution.py:406
  177.9 5.0 %collective-permute-done.20.by_x = bf16[128,1536]{1,0:T(8,128)(2,1)S(1)} collective-permute-done((bf16[128,1536]{1,0:T(8,128)(2,1)}, bf16[128,1536]{1,0:T(8,128)(2,1)S(1)}, u32[]{:S(2)}, u32[]{:S(2)}) %collective-permute-start.20) | collective-permute-done | bytes 393248 | tf_op jit(solution)/shard_map/ppermute | solution.py:43
  182.9 8.3 %collective-permute-done.22.by_xy = bf16[128,1536]{1,0:T(8,128)(2,1)S(1)} collective-permute-done((bf16[128,1536]{1,0:T(8,128)(2,1)S(1)}, bf16[128,1536]{1,0:T(8,128)(2,1)S(1)}, u32[]{:S(2)}, u32[]{:S(2)}) %collective-permute-start.22) | collective-permute-done | bytes 393248 | tf_op jit(solution)/shard_map/ppermute | solution.py:43
  191.2 1.0 copy-done.7
  192.2 1.0 mix.1
  (36 shorter events, 0.1 us)
Async XLA Ops:
  7.2 24.4 %collective-permute-start.3 = (bf16[1536,256]{1,0:T(8,128)(2,1)}, bf16[1536,256]{1,0:T(8,128)(2,1)S(1)}, u32[]{:S(2)}, u32[]{:S(2)}) collective-permute-start(bf16[1536,256]{1,0:T(8,128)(2,1)} %w_own.1), channel_id=1, source_target_pairs={{0,1},{1,0},{2,3},{3,2},{4,5},{5,4},{6,7},{7,6},{8,9},{9,8},{10,11... | collective-permute-start | bytes 2359304 | tf_op jit(solution)/shard_map/ppermute | solution.py:43
  8.4 1.0 copy-start.2
  9.4 28.8 %copy-start.9 = (bf16[1536,192]{0,1:T(8,128)(2,1)S(1)}, bf16[1536,192]{0,1:T(8,128)(2,1)}, u32[]{:S(2)}) copy-start(bf16[1536,192]{0,1:T(8,128)(2,1)} %param.17) | copy-start | bytes 1769476
  9.6 13.5 %collective-permute-start.2 = (bf16[128,1536]{1,0:T(8,128)(2,1)S(1)}, bf16[128,1536]{1,0:T(8,128)(2,1)S(1)}, u32[]{:S(2)}, u32[]{:S(2)}) collective-permute-start(bf16[128,1536]{1,0:T(8,128)(2,1)S(1)} %norm_tokens.1.own), channel_id=1, source_target_pairs={{0,6},{1,7},{2,4},{3,5},{4,2},{5,3},{6,0},{7,1},{8,14},{9,15},{10,... | collective-permute-start | bytes 1179656 | tf_op jit(solution)/shard_map/ppermute | solution.py:43
  13.1 18.2 %collective-permute-start.1 = (bf16[128,1536]{1,0:T(8,128)(2,1)S(1)}, bf16[128,1536]{1,0:T(8,128)(2,1)S(1)}, u32[]{:S(2)}, u32[]{:S(2)}) collective-permute-start(bf16[128,1536]{1,0:T(8,128)(2,1)S(1)} %norm_tokens.1.own), channel_id=1, source_target_pairs={{0,4},{1,5},{2,6},{3,7},{4,0},{5,1},{6,2},{7,3},{8,12},{9,13},{10,... | collective-permute-start | bytes 1179656 | tf_op jit(solution)/shard_map/ppermute | solution.py:43
  13.6 18.0 %collective-permute-start = (bf16[128,1536]{1,0:T(8,128)(2,1)S(1)}, bf16[128,1536]{1,0:T(8,128)(2,1)S(1)}, u32[]{:S(2)}, u32[]{:S(2)}) collective-permute-start(bf16[128,1536]{1,0:T(8,128)(2,1)S(1)} %norm_tokens.1.own), channel_id=1, source_target_pairs={{0,2},{1,3},{2,0},{3,1},{4,6},{5,7},{6,4},{7,5},{8,10},{9,11},{10,... | collective-permute-start | bytes 1179656 | tf_op jit(solution)/shard_map/ppermute | solution.py:43
  31.6 1.1 copy-start.5
  34.6 11.7 %all-to-all-start = ((bf16[4,128,512]{2,1,0:T(8,128)(2,1)}), bf16[4,128,512]{2,1,0:T(8,128)(2,1)S(1)}, u32[]{:S(2)}, u32[]{:S(2)}) async-start(bf16[4,128,512]{2,1,0:T(8,128)(2,1)} %bitcast), calls=%async_computation | async-start | bytes 1048576 | tf_op jit(solution)/shard_map/all_to_all | solution.py:49
  38.1 48.0 %copy-start.10 = (f32[1536]{0:T(1024)S(1)}, f32[1536]{0:T(1024)}, u32[]{:S(2)}) copy-start(f32[1536]{0:T(1024)} %param.18) | copy-start | bytes 18436
  38.1 48.0 %copy-start.13 = (s32[128]{0:T(128)S(1)}, s32[128]{0:T(128)}, u32[]{:S(2)}) copy-start(s32[128]{0:T(128)} %param.13) | copy-start | bytes 1540
  38.1 48.0 %copy-start.11 = (f32[128,4]{0,1:T(4,128)S(1)}, f32[128,4]{0,1:T(4,128)}, u32[]{:S(2)}) copy-start(f32[128,4]{0,1:T(4,128)} %param.20) | copy-start | bytes 6148
  38.1 48.0 %copy-start.12 = (s32[128,4]{0,1:T(4,128)S(1)}, s32[128,4]{0,1:T(4,128)}, u32[]{:S(2)}) copy-start(s32[128,4]{0,1:T(4,128)} %param.19) | copy-start | bytes 6148
  38.1 97.9 %collective-permute-start.17 = (bf16[1536,768]{1,0:T(8,128)(2,1)}, bf16[1536,768]{1,0:T(8,128)(2,1)}, u32[]{:S(2)}, u32[]{:S(2)}) collective-permute-start(bf16[1536,768]{1,0:T(8,128)(2,1)} %bitcast.7.gate_own), channel_id=1, source_target_pairs={{0,1},{1,0},{2,3},{3,2},{4,5},{5,4},{6,7},{7,6},{8,9},{9,8},{10,11... | collective-permute-start | bytes 7077896 | tf_op jit(solution)/shard_map/ppermute | solution.py:43
  46.3 10.5 %collective-permute-start.7 = (bf16[192,1536]{1,0:T(8,128)(2,1)S(1)}, bf16[192,1536]{1,0:T(8,128)(2,1)S(1)}, u32[]{:S(2)}, u32[]{:S(2)}) collective-permute-start(bf16[192,1536]{1,0:T(8,128)(2,1)S(1)} %transpose_w_out.1.refs_0_), channel_id=1, source_target_pairs={{0,1},{1,0},{2,3},{3,2},{4,5},{5,4},{6,7},{7,6},{8,9},{9,8},{10,11... | collective-permute-start | bytes 1769480 | tf_op jit(solution)/shard_map/ppermute | solution.py:43
  46.3 16.7 %collective-permute-start.6 = (bf16[192,1536]{1,0:T(8,128)(2,1)S(1)}, bf16[192,1536]{1,0:T(8,128)(2,1)S(1)}, u32[]{:S(2)}, u32[]{:S(2)}) collective-permute-start(bf16[192,1536]{1,0:T(8,128)(2,1)S(1)} %transpose_w_out.1.refs_0_), channel_id=1, source_target_pairs={{0,6},{1,7},{2,4},{3,5},{4,2},{5,3},{6,0},{7,1},{8,14},{9,15},{10,... | collective-permute-start | bytes 1769480 | tf_op jit(solution)/shard_map/ppermute | solution.py:43
  48.4 6.8 %collective-permute-start.11 = (bf16[128,512]{1,0:T(8,128)(2,1)S(1)}, bf16[128,512]{1,0:T(8,128)(2,1)S(1)}, u32[]{:S(2)}, u32[]{:S(2)}) collective-permute-start(bf16[128,512]{1,0:T(8,128)(2,1)S(1)} %get-tuple-element.23), channel_id=1, source_target_pairs={{0,8},{8,16},{16,24},{1,9},{9,17},{17,25},{2,10},{10,18},{18,26},{... | collective-permute-start | bytes 393224 | tf_op jit(solution)/shard_map/ppermute | solution.py:443
  55.2 1.5 collective-permute-start.13
  55.2 84.3 %collective-permute-start.18 = (bf16[1536,768]{1,0:T(8,128)(2,1)}, bf16[1536,768]{1,0:T(8,128)(2,1)}, u32[]{:S(2)}, u32[]{:S(2)}) collective-permute-start(bf16[1536,768]{1,0:T(8,128)(2,1)} %bitcast.15), channel_id=1, source_target_pairs={{0,1},{1,0},{2,3},{3,2},{4,5},{5,4},{6,7},{7,6},{8,9},{9,8},{10,11... | collective-permute-start | bytes 7077896 | tf_op jit(solution)/shard_map/ppermute | solution.py:43
  56.7 82.8 %collective-permute-start.19 = (bf16[768,1536]{1,0:T(8,128)(2,1)}, bf16[768,1536]{1,0:T(8,128)(2,1)}, u32[]{:S(2)}, u32[]{:S(2)}) collective-permute-start(bf16[768,1536]{1,0:T(8,128)(2,1)} %bitcast.17), channel_id=1, source_target_pairs={{0,1},{1,0},{2,3},{3,2},{4,5},{5,4},{6,7},{7,6},{8,9},{9,8},{10,11... | collective-permute-start | bytes 7077896 | tf_op jit(solution)/shard_map/ppermute | solution.py:43
  56.8 18.9 %collective-permute-start.5 = (bf16[192,1536]{1,0:T(8,128)(2,1)S(1)}, bf16[192,1536]{1,0:T(8,128)(2,1)}, u32[]{:S(2)}, u32[]{:S(2)}) collective-permute-start(bf16[192,1536]{1,0:T(8,128)(2,1)S(1)} %transpose_w_out.1.refs_0_), channel_id=1, source_target_pairs={{0,4},{1,5},{2,6},{3,7},{4,0},{5,1},{6,2},{7,3},{8,12},{9,13},{10,... | collective-permute-start | bytes 1769480 | tf_op jit(solution)/shard_map/ppermute | solution.py:43
  58.3 73.6 %copy-start.3 = (bf16[128,1536]{1,0:T(8,128)(2,1)S(1)}, bf16[128,1536]{1,0:T(8,128)(2,1)}, u32[]{:S(2)}) copy-start(bf16[128,1536]{1,0:T(8,128)(2,1)} %refs_9_.1) | copy-start | bytes 1179652
  63.0 20.5 %collective-permute-start.4 = (bf16[192,1536]{1,0:T(8,128)(2,1)S(1)}, bf16[192,1536]{1,0:T(8,128)(2,1)}, u32[]{:S(2)}, u32[]{:S(2)}) collective-permute-start(bf16[192,1536]{1,0:T(8,128)(2,1)S(1)} %transpose_w_out.1.refs_0_), channel_id=1, source_target_pairs={{0,2},{1,3},{2,0},{3,1},{4,6},{5,7},{6,4},{7,5},{8,10},{9,11},{10,... | collective-permute-start | bytes 1769480 | tf_op jit(solution)/shard_map/ppermute | solution.py:43
  65.4 18.2 %all-to-all-start.1 = ((bf16[4,128,512]{2,1,0:T(8,128)(2,1)}), bf16[4,128,512]{2,1,0:T(8,128)(2,1)S(1)}, u32[]{:S(2)}, u32[]{:S(2)}) async-start(bf16[4,128,512]{2,1,0:T(8,128)(2,1)} %broadcast_select_fusion), calls=%async_computation.1 | async-start | bytes 1048576 | tf_op jit(solution)/shard_map/all_to_all | solution.py:49
  68.8 105.4 %all-gather.4.cloned.1.call-start = ((), (), s32[]{:S(2)}) async-start(), calls=%async_computation.2 | async-start | bytes 1179648 | tf_op jit(solution)/shard_map/all_gather | solution.py:462
  75.7 10.0 %collective-permute-start.10 = (bf16[192,1536]{1,0:T(8,128)(2,1)S(1)}, bf16[192,1536]{1,0:T(8,128)(2,1)}, u32[]{:S(2)}, u32[]{:S(2)}) collective-permute-start(bf16[192,1536]{1,0:T(8,128)(2,1)S(1)} %collective-permute-done.6.refs_3_), channel_id=1, source_target_pairs={{0,1},{1,0},{2,3},{3,2},{4,5},{5,4},{6,7},{7,6},{8,9},{9,8},{10,11... | collective-permute-start | bytes 1769480 | tf_op jit(solution)/shard_map/ppermute | solution.py:43
  83.5 2.0 %collective-permute-start.12 = (bf16[512,512]{1,0:T(8,128)(2,1)S(1)}, bf16[512,512]{1,0:T(8,128)(2,1)}, u32[]{:S(2)}, u32[]{:S(2)}) collective-permute-start(bf16[512,512]{1,0:T(8,128)(2,1)S(1)} %bitcast.19), channel_id=1, source_target_pairs={{0,1},{1,0},{2,3},{3,2},{4,5},{5,4},{6,7},{7,6},{8,9},{9,8},{10,11... | collective-permute-start | bytes 1572872 | tf_op jit(solution)/shard_map/ppermute | solution.py:43
  85.6 46.3 %collective-permute-start.9 = (bf16[192,1536]{1,0:T(8,128)(2,1)}, bf16[192,1536]{1,0:T(8,128)(2,1)S(1)}, u32[]{:S(2)}, u32[]{:S(2)}) collective-permute-start(bf16[192,1536]{1,0:T(8,128)(2,1)} %collective-permute-done.5.refs_2_), channel_id=1, source_target_pairs={{0,1},{1,0},{2,3},{3,2},{4,5},{5,4},{6,7},{7,6},{8,9},{9,8},{10,11... | collective-permute-start | bytes 1769480 | tf_op jit(solution)/shard_map/ppermute | solution.py:43
  85.7 46.1 %collective-permute-start.8 = (bf16[192,1536]{1,0:T(8,128)(2,1)}, bf16[192,1536]{1,0:T(8,128)(2,1)S(1)}, u32[]{:S(2)}, u32[]{:S(2)}) collective-permute-start(bf16[192,1536]{1,0:T(8,128)(2,1)} %collective-permute-done.4.refs_1_), channel_id=1, source_target_pairs={{0,1},{1,0},{2,3},{3,2},{4,5},{5,4},{6,7},{7,6},{8,9},{9,8},{10,11... | collective-permute-start | bytes 1769480 | tf_op jit(solution)/shard_map/ppermute | solution.py:43
  131.8 24.6 %copy-start = (bf16[1,1536,768]{2,1,0:T(8,128)(2,1)S(1)}, bf16[1,1536,768]{2,1,0:T(8,128)(2,1)}, u32[]{:S(2)}) copy-start(bf16[1,1536,768]{2,1,0:T(8,128)(2,1)} %param.22) | copy-start | bytes 7077892
  131.8 24.6 %copy-start.1 = (bf16[1,768,1536]{2,1,0:T(8,128)(2,1)S(1)}, bf16[1,768,1536]{2,1,0:T(8,128)(2,1)}, u32[]{:S(2)}) copy-start(bf16[1,768,1536]{2,1,0:T(8,128)(2,1)} %param.23) | copy-start | bytes 7077892
  135.9 34.8 %copy-start.6 = (bf16[128,1536]{1,0:T(8,128)(2,1)}, bf16[128,1536]{1,0:T(8,128)(2,1)S(1)}, u32[]{:S(2)}) copy-start(bf16[128,1536]{1,0:T(8,128)(2,1)S(1)} %get-tuple-element.16.residual_ref) | copy-start | bytes 1179652
  135.9 38.3 %copy-start.8 = (s32[1,64]{1,0:T(1,128)S(1)}, s32[1,64]{1,0:T(1,128)}, u32[]{:S(2)}) copy-start(s32[1,64]{1,0:T(1,128)} %table_ref.1) | copy-start | bytes 772
  135.9 13.0 %collective-permute-start.16 = (bf16[128,1536]{1,0:T(8,128)(2,1)S(1)}, bf16[128,1536]{1,0:T(8,128)(2,1)S(1)}, u32[]{:S(2)}, u32[]{:S(2)}) collective-permute-start(bf16[128,1536]{1,0:T(8,128)(2,1)S(1)} %get-tuple-element.17.own), channel_id=1, source_target_pairs={{0,6},{1,7},{2,4},{3,5},{4,2},{5,3},{6,0},{7,1},{8,14},{9,15},{10,... | collective-permute-start | bytes 1179656 | tf_op jit(solution)/shard_map/ppermute | solution.py:43
  136.0 20.4 %collective-permute-start.15 = (bf16[128,1536]{1,0:T(8,128)(2,1)S(1)}, bf16[128,1536]{1,0:T(8,128)(2,1)S(1)}, u32[]{:S(2)}, u32[]{:S(2)}) collective-permute-start(bf16[128,1536]{1,0:T(8,128)(2,1)S(1)} %get-tuple-element.17.own), channel_id=1, source_target_pairs={{0,4},{1,5},{2,6},{3,7},{4,0},{5,1},{6,2},{7,3},{8,12},{9,13},{10,... | collective-permute-start | bytes 1179656 | tf_op jit(solution)/shard_map/ppermute | solution.py:43
  136.1 20.3 %collective-permute-start.14 = (bf16[128,1536]{1,0:T(8,128)(2,1)S(1)}, bf16[128,1536]{1,0:T(8,128)(2,1)S(1)}, u32[]{:S(2)}, u32[]{:S(2)}) collective-permute-start(bf16[128,1536]{1,0:T(8,128)(2,1)S(1)} %get-tuple-element.17.own), channel_id=1, source_target_pairs={{0,2},{1,3},{2,0},{3,1},{4,6},{5,7},{6,4},{7,5},{8,10},{9,11},{10,... | collective-permute-start | bytes 1179656 | tf_op jit(solution)/shard_map/ppermute | solution.py:43
  170.7 12.2 %collective-permute-start.20 = (bf16[128,1536]{1,0:T(8,128)(2,1)}, bf16[128,1536]{1,0:T(8,128)(2,1)S(1)}, u32[]{:S(2)}, u32[]{:S(2)}) collective-permute-start(bf16[128,1536]{1,0:T(8,128)(2,1)} %get-tuple-element.19), channel_id=1, source_target_pairs={{0,2},{1,3},{2,0},{3,1},{4,6},{5,7},{6,4},{7,5},{8,10},{9,11},{10,... | collective-permute-start | bytes 1179656 | tf_op jit(solution)/shard_map/ppermute | solution.py:43
  170.7 12.2 %collective-permute-start.21 = (bf16[128,1536]{1,0:T(8,128)(2,1)}, bf16[128,1536]{1,0:T(8,128)(2,1)S(1)}, u32[]{:S(2)}, u32[]{:S(2)}) collective-permute-start(bf16[128,1536]{1,0:T(8,128)(2,1)} %get-tuple-element.20), channel_id=1, source_target_pairs={{0,4},{1,5},{2,6},{3,7},{4,0},{5,1},{6,2},{7,3},{8,12},{9,13},{10,... | collective-permute-start | bytes 1179656 | tf_op jit(solution)/shard_map/ppermute | solution.py:43
  172.2 19.0 %collective-permute-start.22 = (bf16[128,1536]{1,0:T(8,128)(2,1)S(1)}, bf16[128,1536]{1,0:T(8,128)(2,1)S(1)}, u32[]{:S(2)}, u32[]{:S(2)}) collective-permute-start(bf16[128,1536]{1,0:T(8,128)(2,1)S(1)} %get-tuple-element.21), channel_id=1, source_target_pairs={{0,6},{1,7},{2,4},{3,5},{4,2},{5,3},{6,0},{7,1},{8,14},{9,15},{10,... | collective-permute-start | bytes 1179656 | tf_op jit(solution)/shard_map/ppermute | solution.py:43
  174.2 1.2 copy-start.4
  191.2 1.0 copy-start.7
Sparse Core Ops, SparseCore 0:
  83.7 25.4 all-gather.3

commit v2 on v0

--- a/solution.py
+++ b/solution.py
@@ -1,8 +1,11 @@
+import functools
 import math
 
 import jax
 import jax.numpy as jnp
 from jax import lax
+from jax.experimental import pallas as pl
+from jax.experimental.pallas import tpu as pltpu
 from jax.sharding import PartitionSpec as P
 
 HEADS = 12
@@ -10,9 +13,526 @@
 HEAD = 128
 TOP = 4
 PAGE = 16
+CORES = 2
+CHIPS = 4
 
 
 epsilon = 1e-06
+MIB = 1024 * 1024
+
+
+LONG = pl.CostEstimate(flops=20 * 10**9, bytes_accessed=1, transcendentals=0)
+
+
+ORDER = (0, 3, 1, 2)
+
+
+def vmem():
+    return pl.BlockSpec(memory_space=pltpu.VMEM)
+
+
+def anywhere():
+    return pl.BlockSpec(memory_space=pl.ANY)
+
+
+def params(mib):
+    return pltpu.CompilerParams(vmem_limit_bytes=mib * MIB)
+
+
+def place():
+    index = lax.axis_index("tensor")
+    return index // CORES, lax.rem(index, CORES)
+
+
+def hop(value, by):
+    length = lax.axis_size("tensor")
+    return lax.ppermute(value, "tensor", [(i, i ^ by) for i in range(length)])
+
+
+def rms_rows(wide, gain_ref):
+    mean_sq = jnp.mean(wide * wide, axis=-1, keepdims=True)
+    return (wide * lax.rsqrt(mean_sq + epsilon) * gain_ref[...]).astype(jnp.bfloat16)
+
+
+def project_kernel(first, second, gain_ref, w_own, w_other, out_ref, rows_ref):
+    core = place()[1]
+    rows, cols = first.shape[0], w_own.shape[1]
+    rows_ref[:rows, :] = rms_rows(first[...].astype(jnp.float32), gain_ref)
+    rows_ref[rows:, :] = rms_rows(second[...].astype(jnp.float32), gain_ref)
+    for which, weights in ((core, w_own), (1 - core, w_other)):
+        span = pl.ds(pl.multiple_of(which * cols, cols), cols)
+        out_ref[:, span] = jnp.dot(
+            rows_ref[...], weights[...], preferred_element_type=jnp.float32
+        ).astype(jnp.bfloat16)
+
+
+def project_call(first, second, gain, w_own, w_other):
+    rows, width = first.shape
+    return pl.pallas_call(
+        project_kernel,
+        out_shape=jax.ShapeDtypeStruct((2 * rows, CORES * w_own.shape[1]), jnp.bfloat16),
+        in_specs=[vmem()] * 5,
+        out_specs=vmem(),
+        scratch_shapes=[pltpu.VMEM((2 * rows, width), jnp.bfloat16)],
+        cost_estimate=LONG,
+        compiler_params=params(16),
+        name="project",
+    )(first, second, gain, w_own, w_other)
+
+
+def pack_kernel(own, by_x, by_y, by_xy, segs_ref, routes_ref, shares_ref, out_ref):
+    chip = place()[0]
+    rows, width = own.shape
+    for hop_by, piece in enumerate((own, by_x, by_y, by_xy)):
+
+        @pl.when(chip ^ hop_by == CHIPS - 1)
+        def _(piece=piece):
+            out_ref[:rows, :] = piece[...]
+
+    experts = PAGE // 2
+    named = lax.broadcasted_iota(jnp.int32, (experts, rows), 0)
+    table = jnp.zeros((experts, rows), jnp.float32)
+    for k in range(TOP):
+        routed = jnp.broadcast_to(routes_ref[k : k + 1, :], (experts, rows)) == named
+        table = table + jnp.where(routed, shares_ref[k : k + 1, :], 0.0)
+    segs = jnp.broadcast_to(segs_ref[...].astype(jnp.float32), (experts, rows))
+    out_ref[rows:, :rows] = jnp.concatenate([segs, table], axis=0).astype(jnp.bfloat16)
+    for part in (1, 2):
+        table = table - table.astype(jnp.bfloat16).astype(jnp.float32)
+        out_ref[rows:, part * rows : (part + 1) * rows] = jnp.concatenate(
+            [segs, table], axis=0
+        ).astype(jnp.bfloat16)
+    out_ref[rows:, 3 * rows :] = jnp.zeros((PAGE, width - 3 * rows), jnp.bfloat16)
+
+
+def pack_call(pieces, segment_ids, routes, shares):
+    rows, width = pieces[0].shape
+    return pl.pallas_call(
+        pack_kernel,
+        out_shape=jax.ShapeDtypeStruct((rows + PAGE, width), jnp.bfloat16),
+        in_specs=[vmem()] * (CHIPS + 3),
+        out_specs=vmem(),
+        compiler_params=params(16),
+        name="pack_kv",
+    )(*pieces, segment_ids.reshape(1, rows), routes.T, shares.T)
+
+
+def choose_kernel(own, prev, *out_refs):
+    chip = place()[0]
+    rows = own.shape[0] - PAGE
+    row_id = lax.broadcasted_iota(jnp.int32, (PAGE, own.shape[1]), 0)
+    for hop_by, out_ref in enumerate(out_refs, 1):
+        later = (chip ^ hop_by) > chip
+
+        @pl.when(later)
+        def _(out_ref=out_ref):
+            out_ref[...] = own[...]
+
+        @pl.when(jnp.logical_not(later))
+        def _(out_ref=out_ref):
+            out_ref[:rows, :] = prev[:rows, :]
+            below, mine = prev[rows:, :].astype(jnp.float32), own[rows:, :].astype(jnp.float32)
+            out_ref[rows:, :] = jnp.where(row_id < PAGE // 2, below, mine).astype(jnp.bfloat16)
+
+
+def choose_call(own, prev):
+    return pl.pallas_call(
+        choose_kernel,
+        out_shape=(jax.ShapeDtypeStruct(own.shape, own.dtype),) * (CHIPS - 1),
+        in_specs=[vmem()] * 2,
+        out_specs=(vmem(),) * (CHIPS - 1),
+        compiler_params=params(16),
+        name="choose_kv",
+    )(own, prev)
+
+
+def attend_kernel(*refs):
+    projected, refs = refs[:CHIPS], refs[CHIPS:]
+    windows, refs = refs[: 2 * (CHIPS + 1)], refs[2 * (CHIPS + 1) :]
+    out_ref, q_ref, s_ref, top_ref, sum_ref, acc_ref = refs
+    chip, core = place()
+    seq = lax.axis_index("seq")
+    rows = out_ref.shape[0]
+    per_group = HEADS // KV_HEADS
+    per_chip = HEADS // (CHIPS - 1)
+    block_rows = rows * CORES * CHIPS
+    own_first = seq * block_rows + (chip * CORES + core) * rows
+
+    def segs_of(ref):
+        return ref[rows : rows + 1, :rows].astype(jnp.float32)
+
+    own_segs = segs_of(windows[0])
+    query_seg = jnp.broadcast_to(own_segs, (rows, rows)).T
+    query_pos = lax.broadcasted_iota(jnp.int32, (rows, rows), 0) + own_first
+    lane = lax.broadcasted_iota(jnp.int32, (rows, rows), 1)
+    lowest = jnp.min(own_segs)
+
+    for hop_by, piece in enumerate(projected):
+        source = chip ^ hop_by
+
+        @pl.when(source < CHIPS - 1)
+        def _(source=source, piece=piece):
+            for i in range(per_chip):
+                start = pl.multiple_of((source * per_chip + i) * rows, rows)
+                q_ref[pl.ds(start, rows), :] = piece[:, i * HEAD : (i + 1) * HEAD]
+
+    pairs = []
+    for n in range(CHIPS + 1):
+        if n == 0:
+            base, source = seq, chip
+        elif n == CHIPS:
+            base, source = seq - 1, chip
+        else:
+            source = chip ^ n
+            base = jnp.where(source < chip, seq, seq - 1)
+        first = base * block_rows + source * CORES * rows
+        refs = (windows[n], windows[n + CHIPS + 1])
+        pairs.append((refs, (first + core * rows, first + (1 - core) * rows)))
+
+    scale = math.log2(math.e) / math.sqrt(HEAD)
+    group_rows = per_group * rows
+    used = []
+    for n, (refs, firsts) in enumerate(pairs):
+        use = (firsts[0] >= 0) & (firsts[0] <= own_first)
+        last_seg = jnp.max(jnp.maximum(segs_of(refs[0]), segs_of(refs[1])))
+        used.append(use & (last_seg >= lowest))
+
+        def scores_of(n=n, refs=refs, firsts=firsts):
+            bias = []
+            for ref, first in zip(refs, firsts):
+                allowed = (segs_of(ref) == query_seg) & (first + lane <= query_pos)
+                bias.append(jnp.where(allowed, 0.0, -jnp.inf))
+            bias = jnp.concatenate(bias, axis=1)
+            for g in range(KV_HEADS):
+                span = slice(g * HEAD, (g + 1) * HEAD)
+                keys = jnp.concatenate([ref[:rows, span] for ref in refs], axis=0)
+                part = slice(g * group_rows, (g + 1) * group_rows)
+                scores = lax.dot_general(
+                    q_ref[part, :], keys, (((1,), (1,)), ((), ())),
+                    preferred_element_type=jnp.float32,
+                )
+                scores = scores.reshape(per_group, rows, 2 * rows) * scale + bias[None]
+                scores = scores.reshape(group_rows, 2 * rows)
+                s_ref[n, part, :] = scores
+                high = jnp.maximum(scores[:, :rows], scores[:, rows:])
+                top_ref[part, :] = high if n == 0 else jnp.maximum(top_ref[part, :], high)
+
+        if n == 0:
+            scores_of()
+        else:
+            pl.when(used[n])(scores_of)
+
+    top_ref[...] = jnp.broadcast_to(jnp.max(top_ref[...], axis=1, keepdims=True), top_ref.shape)
+    for n, (refs, firsts) in enumerate(pairs):
+
+        def weigh(n=n, refs=refs):
+            for g in range(KV_HEADS):
+                part = slice(g * group_rows, (g + 1) * group_rows)
+                top = top_ref[part, :]
+                weights = jnp.exp2(s_ref[n, part, :] - jnp.concatenate([top, top], axis=1))
+                span = slice((KV_HEADS + g) * HEAD, (KV_HEADS + g + 1) * HEAD)
+                values = jnp.concatenate([ref[:rows, span] for ref in refs], axis=0)
+                made = jnp.dot(
+                    weights.astype(jnp.bfloat16), values, preferred_element_type=jnp.float32
+                )
+                sums = weights[:, :rows] + weights[:, rows:]
+                if n == 0:
+                    sum_ref[part, :] = sums
+                    acc_ref[part, :] = made
+                else:
+                    sum_ref[part, :] += sums
+                    acc_ref[part, :] += made
+
+        if n == 0:
+            weigh()
+        else:
+            pl.when(used[n])(weigh)
+
+    for head in range(HEADS):
+        part = slice(head * rows, (head + 1) * rows)
+        total = jnp.sum(sum_ref[part, :], axis=1, keepdims=True)
+        out_ref[:, head * HEAD : (head + 1) * HEAD] = (acc_ref[part, :] / total).astype(
+            jnp.bfloat16
+        )
+
+
+def attend_call(projected, windows):
+    rows = projected[0].shape[0]
+    wide = HEADS * rows
+    return pl.pallas_call(
+        attend_kernel,
+        out_shape=jax.ShapeDtypeStruct((rows, HEADS * HEAD), jnp.bfloat16),
+        in_specs=[vmem()] * (len(projected) + len(windows)),
+        out_specs=vmem(),
+        scratch_shapes=[
+            pltpu.VMEM((wide, HEAD), jnp.bfloat16),
+            pltpu.VMEM((CHIPS + 1, wide, 2 * rows), jnp.float32),
+            pltpu.VMEM((wide, rows), jnp.float32),
+            pltpu.VMEM((wide, rows), jnp.float32),
+            pltpu.VMEM((wide, HEAD), jnp.float32),
+        ],
+        cost_estimate=LONG,
+        compiler_params=params(32),
+        name="attend",
+    )(*projected, *windows)
+
+
+def assemble_kernel(same, other, out_ref):
+    chip, core = place()
+    cols = same[0].shape[0]
+    for pieces, which in ((same, core), (other, 1 - core)):
+        done = 0
+        for piece in pieces:
+            count = piece.shape[0]
+            start = ((chip ^ (done // cols)) * CORES + which) * cols + done % cols
+            out_ref[pl.ds(pl.multiple_of(start, PAGE), count), :] = piece[...]
+            done += count
+
+
+def assemble_call(same, other):
+    shape = (CORES * CHIPS * same[0].shape[0], same[0].shape[1])
+    count = len(same)
+    return pl.pallas_call(
+        lambda *refs: assemble_kernel(refs[:count], refs[count:-1], refs[-1]),
+        out_shape=jax.ShapeDtypeStruct(shape, jnp.bfloat16),
+        in_specs=[vmem()] * (2 * count),
+        out_specs=vmem(),
+        compiler_params=params(16),
+        name="assemble_w_out",
+    )(*same, *other)
+
+
+def expert_kernel(tile, *refs):
+    context, tokens, tables = refs[:2], refs[2:4], refs[4:6]
+    w_ref, gain_ref = refs[6:8]
+    held, outs, (rows_ref, hidden_ref, total_ref) = refs[8:14], refs[-5:-3], refs[-3:]
+    chip, core = place()
+    rows, width = context[0].shape
+    hidden = hidden_ref.shape[1]
+    spans = [slice(i * rows, (i + 1) * rows) for i in range(2)]
+    for span, piece in zip(spans, context):
+        rows_ref[span, :] = piece[...]
+    added = lax.dot_general(
+        rows_ref[...], w_ref[...], (((1,), (1,)), ((), ())), preferred_element_type=jnp.float32
+    )
+    for span, piece in zip(spans, tokens):
+        residual = (piece[...].astype(jnp.float32) + added[span]).astype(jnp.bfloat16)
+        wide = residual.astype(jnp.float32)
+        if outs[0].dtype == jnp.float32 and span.start == 0:
+            total_ref[span, :] = wide
+        else:
+            total_ref[span, :] = jnp.zeros_like(wide)
+        rows_ref[span, :] = rms_rows(wide, gain_ref)
+
+    for which in range(CORES):
+        expert = chip * CORES + (core if which == 0 else 1 - core)
+        gate, up, down = held[3 * which : 3 * which + 3]
+        shares = []
+        for table in tables:
+            below = table[rows:, :].astype(jnp.float32)
+            row_id = lax.broadcasted_iota(jnp.int32, below.shape, 0)
+            row = jnp.sum(
+                jnp.where(row_id == PAGE // 2 + expert, below, 0.0), axis=0, keepdims=True
+            )
+            row = row[:, :rows] + row[:, rows : 2 * rows] + row[:, 2 * rows : 3 * rows]
+            shares.append(jnp.broadcast_to(row, (rows, rows)).T[:, :1])
+        for column in range(0, hidden, tile):
+            span = slice(column, column + tile)
+            gate_out = jnp.dot(rows_ref[...], gate[:, span], preferred_element_type=jnp.float32)
+            up_out = jnp.dot(rows_ref[...], up[:, span], preferred_element_type=jnp.float32)
+            hidden_ref[:, span] = (jnp.maximum(gate_out, 0.0) * up_out).astype(jnp.bfloat16)
+        for column in range(0, width, 2 * tile):
+            cols = slice(column, column + 2 * tile)
+            made = jnp.dot(hidden_ref[...], down[:, cols], preferred_element_type=jnp.float32)
+            made = made.astype(jnp.bfloat16).astype(jnp.float32)
+            for span, share, out_ref in zip(spans, shares, outs):
+                total = total_ref[span, cols] + share * made[span]
+                if which == 0:
+                    total_ref[span, cols] = total
+                else:
+                    out_ref[:, cols] = total.astype(out_ref.dtype)
+
+
+def expert_call(context, tokens, tables, w_all, gain, weights, kinds, *earlier):
+    rows, width = tokens[0].shape
+    hidden = weights[0].shape[1]
+    return pl.pallas_call(
+        functools.partial(expert_kernel, 256),
+        out_shape=tuple(jax.ShapeDtypeStruct((rows, width), kind) for kind in kinds),
+        in_specs=[vmem()] * 14 + [anywhere()] * len(earlier),
+        out_specs=(vmem(), vmem()),
+        scratch_shapes=[
+            pltpu.VMEM((2 * rows, width), jnp.bfloat16),
+            pltpu.VMEM((2 * rows, hidden), jnp.bfloat16),
+            pltpu.VMEM((2 * rows, width), jnp.float32),
+        ],
+        cost_estimate=LONG,
+        compiler_params=params(32),
+        name="experts",
+    )(*context, *tokens, *tables, w_all, gain, *weights, *earlier)
+
+
+def mix_kernel(own, by_x, by_y, by_xy, out_ref):
+    total = by_x[...].astype(jnp.float32) + by_y[...].astype(jnp.float32)
+    total = total + by_xy[...].astype(jnp.float32)
+    out_ref[...] = (own[...] + total).astype(jnp.bfloat16)
+
+
+def mix_call(pieces):
+    return pl.pallas_call(
+        mix_kernel,
+        out_shape=jax.ShapeDtypeStruct(pieces[0].shape, jnp.bfloat16),
+        in_specs=[vmem()] * CHIPS,
+        out_specs=vmem(),
+        compiler_params=params(16),
+        name="mix",
+    )(*pieces)
+
+
+def cache_kernel(table_ref, *refs):
+    same, other, (out_ref, held) = refs[:2], refs[2:4], refs[4:]
+    core = place()[1]
+    page_rows = held.shape[1]
+    pages = page_rows // PAGE
+    for i, hop_by in enumerate(ORDER):
+        source = (CHIPS - 1 ^ hop_by) * CORES
+        span = slice(i % 2 * page_rows, (i % 2 + 1) * page_rows)
+        held[source + core] = same[i // 2][span, :]
+        held[source + 1 - core] = other[i // 2][span, :]
+
+    def one(logical, carry):
+        slot = table_ref[0, logical]
+        to = slot // pages
+
+        @pl.when(lax.rem(to, CORES) == core)
+        def _():
+            from_row = pl.multiple_of(lax.rem(logical, pages) * PAGE, PAGE)
+            to_row = pl.multiple_of(lax.rem(slot, pages) * PAGE, PAGE)
+            out_ref[to // CORES, pl.ds(to_row, PAGE), :] = held[
+                logical // pages, pl.ds(from_row, PAGE), :
+            ]
+
+        return carry
+
+    lax.fori_loop(0, table_ref.shape[1], one, 0, unroll=8)
+
+
+def cache_call(page_table, same, other):
+    rows, width = same[0].shape[0] // 2, same[0].shape[1]
+    return pl.pallas_call(
+        cache_kernel,
+        out_shape=jax.ShapeDtypeStruct((CHIPS, rows, width), jnp.bfloat16),
+        in_specs=[pl.BlockSpec(memory_space=pltpu.SMEM)] + [vmem()] * 4,
+        out_specs=vmem(),
+        scratch_shapes=[pltpu.VMEM((CORES * CHIPS, rows, width), jnp.bfloat16)],
+        compiler_params=params(16),
+        name="cache_pages",
+    )(page_table, *same, *other)
+
+
+def join_kernel(*refs):
+    pieces, out_ref = refs[:CHIPS], refs[CHIPS]
+    for hop_by, piece in enumerate(pieces):
+
+        @pl.when(place()[0] ^ hop_by == CHIPS - 1)
+        def _(piece=piece):
+            out_ref[...] = piece[...]
+
+
+def join_call(pieces):
+    return pl.pallas_call(
+        join_kernel,
+        out_shape=jax.ShapeDtypeStruct(pieces[0].shape, pieces[0].dtype),
+        in_specs=[vmem()] * CHIPS,
+        out_specs=vmem(),
+        compiler_params=params(16),
+        name="join_pages",
+    )(*pieces)
+
+
+def hold_kernel(in_ref, *refs):
+    refs[-1][...] = in_ref[...]
+
+
+def hold_call(value, *earlier):
+    return pl.pallas_call(
+        hold_kernel,
+        out_shape=jax.ShapeDtypeStruct(value.shape, value.dtype),
+        in_specs=[vmem()] + [anywhere()] * len(earlier),
+        out_specs=vmem(),
+        cost_estimate=LONG,
+        compiler_params=params(16),
+        name="hold",
+    )(value, *earlier)
+
+
+def after(value, other):
+    return lax.optimization_barrier((value, other))[0]
+
+
+def chip_body(
+    tokens, segment_ids, page_table, attn_gain, w_qkv, w_out, moe_gain,
+    route_ids, route_weight, w_gate, w_up, w_down,
+):
+    rows = tokens.shape[0]
+    seq_size = lax.axis_size("seq")
+
+    def chips(value, by):
+        return hop(value, CORES * by)
+
+    gate, up, down = w_gate[0], w_up[0], w_down[0]
+    w_own = w_out.T
+
+    tokens_xy, tokens_x, tokens_y = chips(tokens, 3), chips(tokens, 1), chips(tokens, 2)
+    w_qkv_other = hop(w_qkv, 1)
+    made = project_call(tokens, tokens_xy, attn_gain, w_qkv, w_qkv_other)
+    late = project_call(tokens_x, tokens_y, attn_gain, w_qkv, w_qkv_other)
+    projected = [made[:rows], chips(late[:rows], 1), chips(late[rows:], 2), chips(made[rows:], 3)]
+    gate_other, up_other = hop(after(gate, tokens_xy), 1), hop(after(up, made), 1)
+
+    paged = cache_call(page_table, (made, late), (hop(after(made, late), 1), hop(late, 1)))
+    own_kv = pack_call(
+        after(projected, (paged, gate_other, up_other)), segment_ids, route_ids, route_weight
+    )
+    prev_kv = lax.ppermute(own_kv, "seq", [(i, i + 1) for i in range(seq_size - 1)])
+    w_going, down_going = after((w_own, down), late)
+    w_x, w_y = chips(w_going, 1), chips(w_going, 2)
+    down_other, w_own_other = hop(down_going, 1), hop(w_going, 1)
+
+    sent = choose_call(own_kv, after(prev_kv, (w_x, w_y, down_other, w_own_other)))
+    kv_xy, kv_x, kv_y = chips(sent[2], 3), chips(sent[0], 1), chips(sent[1], 2)
+    half = w_own.shape[0] // 2
+    w_relayed = [hold_call(w_y[:half], *sent), hold_call(w_x[half:], *sent)]
+    w_diagonal = [chips(w_relayed[0], 1), chips(w_relayed[1], 2)]
+    windows = [own_kv, kv_x, kv_y, kv_xy, prev_kv]
+    windows_other = [hop(w, 1) for w in windows]
+    w_other = [w_own_other] + [hop(after(w, sent), 1) for w in (w_x, w_y)]
+    windows_other = after(windows_other, (w_other, w_relayed))
+    context = after(attend_call(projected, windows + windows_other), w_diagonal)
+    context_xy, context_x, context_y = chips(context, 3), chips(context, 1), chips(context, 2)
+    last = CHIPS - 1
+    paged = after(paged, context)
+    pages = [paged[last]]
+    for by in (1, 2, 3):
+        pairs = [(last * CORES + k, (last ^ by) * CORES + k) for k in range(CORES)]
+        pages.append(lax.ppermute(paged[last ^ by], "tensor", pairs))
+    pages = join_call(pages)
+    w_other += [hop(w, 1) for w in w_diagonal]
+    w_all = assemble_call([w_own, w_x, w_y] + w_diagonal, w_other)
+
+    weights = [gate, up, down, gate_other, up_other, down_other]
+    out, out_xy = expert_call(
+        (context, context_xy), (tokens, tokens_xy), (own_kv, kv_xy), w_all, moe_gain, weights,
+        (jnp.float32, jnp.bfloat16),
+    )
+    back_xy = chips(out_xy, 3)
+    out_x, out_y = expert_call(
+        (context_x, context_y), (tokens_x, tokens_y), (kv_x, kv_y), w_all, moe_gain, weights,
+        (jnp.bfloat16, jnp.bfloat16), out_xy,
+    )
+    back_x, back_y = chips(out_x, 1), chips(out_y, 2)
+    mixed = mix_call((out, back_x, back_y, back_xy))
+    return (mixed, pages.reshape(rows // PAGE, PAGE, pages.shape[1]))
 
 
 def from_behind(value, axis, by):
@@ -39,7 +559,7 @@
     return jnp.einsum("hqk,kd->qhd", shares, values_window, preferred_element_type=jnp.float32)
 
 
-def body(
+def block_body(
     tokens,
     segment_ids,
     page_table,
@@ -149,9 +669,14 @@
     return (mixed, cache_pages)
 
 
+def by_chips(mesh):
+    size = mesh.shape["tensor"]
+    return size == CORES * CHIPS and (HEADS + 2 * KV_HEADS) % size == 0
+
+
 def solution(mesh):
     return jax.shard_map(
-        body,
+        chip_body if by_chips(mesh) else block_body,
         mesh=mesh,
         in_specs=(
             P(("seq", "tensor"), None),

time: 231 us -> 121 us (0.52)
  blocking collectives: 52.2 us -> 0 us
  matrix products: 34.3 us -> 0 us
  waiting for transfers between devices: 88.9 us -> 66 us
  starting transfers between devices: 12.4 us -> 32.5 us
  Pallas kernels: 0 us -> 18.2 us
  local copies, waits for them, and re-layouts: 16.8 us -> 3.14 us
  between operations: 14 us -> 1 us
  other arithmetic: 11.8 us -> 0 us
    ppermute x2 -> x39, waiting for transfers between devices: 17.6 us -> 66 us  [the longest x35 52.4 us: hop(): return lax.ppermute(value, 'tensor', [(i, i ^ by) for i in range(length)])]
    all_to_all x2 -> x0, blocking collectives: 44.4 us -> none  [the longest x1 32.1 us: body(): lax.all_to_all(outgoing, 'tensor', split_axis=0, concat_axis=0, tiled=True)]
    all_gather x3 -> x0, waiting for transfers between devices: 44.1 us -> none  [the longest x1 35.1 us: body(): block_normed = lax.all_gather(normed, 'tensor', axis=0, tiled=True)]
    dot_general x8 -> x0, matrix products: 29.4 us -> none  [the longest x1 9.06 us: body(): jnp.dot(hidden, w_down[0], preferred_element_type=jnp.float32)]
    all_to_all x1 -> x0, waiting for transfers between devices: 26.5 us -> none  [body(): lax.all_to_all(produced.reshape(arrived.shape), 'tensor', split_axis=0, c...]
    ppermute x2 -> x39, starting transfers between devices: 7.78 us -> 32.5 us  [the longest x35 26.4 us: hop(): return lax.ppermute(value, 'tensor', [(i, i ^ by) for i in range(length)])]
    pallas_call x0 -> x13, Pallas kernels: none -> 18.2 us  [the longest x2 10.7 us: expert_call(): pl.pallas_call(functools.partial(expert_kernel, 256), out_shape=tuple((ja...]
    gather x2 -> x0, local copies, waits for them, and re-layouts: 8.82 us -> none  [the longest x1 6.39 us: body(): returned.reshape(-1, returned.shape[-1])[dest_slot]]
  transfers between devices with their start and end apart: 6 -> 39, of which waited for: 5 -> 15; matrix products, arithmetic and copies ran while one was open for 10% -> 0% of each run, Pallas kernels for 0% -> 14%
where the time goes in v2:
time: 121 us
  waiting for transfers between devices  66 us (55%)
  starting transfers between devices  32.5 us (27%)
  Pallas kernels  18.2 us (15%)
  local copies, waits for them, and re-layouts  3.14 us (3%)
    ppermute x35, waiting for transfers between devices, hop(): return lax.ppermute(value, 'tensor', [(i, i ^ by) for i in range(length)])  52.4 us
    ppermute x35, starting transfers between devices, hop(): return lax.ppermute(value, 'tensor', [(i, i ^ by) for i in range(length)])  26.4 us
    ppermute x3, waiting for transfers between devices, chip_body(): pages.append(lax.ppermute(paged[last ^ by], 'tensor', pairs))  13.6 us
    pallas_call x2, Pallas kernels, expert_call(): pl.pallas_call(functools.partial(expert_kernel, 256), out_shape=tuple((ja...  10.7 us
    ppermute x1, starting transfers between devices, chip_body(): lax.ppermute(own_kv, 'seq', [(i, i + 1) for i in range(seq_size - 1)])  3.47 us
    unnamed x28, local copies, waits for them, and re-layouts  3.03 us
    ppermute x3, starting transfers between devices, chip_body(): pages.append(lax.ppermute(paged[last ^ by], 'tensor', pairs))  2.63 us
  transfers between devices with their start and end apart: 39, of which 15 were waited for; matrix products, arithmetic and copies ran while one was open for 0% of the time, Pallas kernels for 14%

profile of v2, /device:TPU:0, one launch (start us, length us, event | category | flops | bytes accessed | tf_op | source)
XLA Modules:
  0.0 120.8 jit_solution(11149765420973323797)
XLA Ops:
  0.6 0.5 collective-permute-start.1
  1.1 3.5 %collective-permute-start = (bf16[128,1536]{1,0:T(8,128)(2,1)}, bf16[128,1536]{1,0:T(8,128)(2,1)S(1)}, u32[]{:S(2)}, u32[]{:S(2)}) collective-permute-start(bf16[128,1536]{1,0:T(8,128)(2,1)} %refs_2_.1), channel_id=1, source_target_pairs={{0,6},{1,7},{2,4},{3,5},{4,2},{5,3},{6,0},{7,1},{8,14},{9,15},{10,... | collective-permute-start | bytes 1179656 | tf_op jit(solution)/shard_map/ppermute | solution.py:49
  4.7 0.5 collective-permute-start.2
  5.2 0.1 collective-permute-start.3
  5.3 9.6 %collective-permute-done.second.refs_3_ = bf16[128,1536]{1,0:T(8,128)(2,1)S(1)} collective-permute-done((bf16[128,1536]{1,0:T(8,128)(2,1)}, bf16[128,1536]{1,0:T(8,128)(2,1)S(1)}, u32[]{:S(2)}, u32[]{:S(2)}) %collective-permute-start) | collective-permute-done | bytes 393248 | tf_op jit(solution)/shard_map/ppermute | solution.py:49
  14.9 1.3 %copy-done.8 = bf16[1536,256]{1,0:T(8,128)(2,1)S(1)} copy-done((bf16[1536,256]{1,0:T(8,128)(2,1)S(1)}, bf16[1536,256]{1,0:T(8,128)(2,1)}, u32[]{:S(2)}) %copy-start.8) | copy-done | bytes 786456
  16.2 1.0 copy-done.10
  17.2 0.7 copy-done.12
  17.9 0.7 project.2.refs_0_
  18.6 0.0 copy-start.7
  18.7 0.0 copy-start
  18.7 0.4 collective-permute-start.10
  19.1 4.2 %collective-permute-done.2.first.refs_2_ = bf16[128,1536]{1,0:T(8,128)(2,1)S(1)} collective-permute-done((bf16[128,1536]{1,0:T(8,128)(2,1)}, bf16[128,1536]{1,0:T(8,128)(2,1)S(1)}, u32[]{:S(2)}, u32[]{:S(2)}) %collective-permute-start.2) | collective-permute-done | bytes 393248 | tf_op jit(solution)/shard_map/ppermute | solution.py:49
  23.3 0.8 project.3.refs_1_
  24.1 0.0 copy-start.4
  24.1 0.1 collective-permute-start.14
  24.2 1.5 %collective-permute-start.4 = (bf16[128,512]{1,0:T(8,128)(2,1)S(1)}, bf16[128,512]{1,0:T(8,128)(2,1)S(1)}, u32[]{:S(2)}, u32[]{:S(2)}) collective-permute-start(bf16[128,512]{1,0:T(8,128)(2,1)S(1)} %get-tuple-element.61), channel_id=1, source_target_pairs={{0,2},{1,3},{2,0},{3,1},{4,6},{5,7},{6,4},{7,5},{8,10},{9,11},{10,... | collective-permute-start | bytes 393224 | tf_op jit(solution)/shard_map/ppermute | solution.py:49
  25.8 1.4 %collective-permute-start.5 = (bf16[128,512]{1,0:T(8,128)(2,1)S(1)}, bf16[128,512]{1,0:T(8,128)(2,1)S(1)}, u32[]{:S(2)}, u32[]{:S(2)}) collective-permute-start(bf16[128,512]{1,0:T(8,128)(2,1)S(1)} %get-tuple-element.60), channel_id=1, source_target_pairs={{0,4},{1,5},{2,6},{3,7},{4,0},{5,1},{6,2},{7,3},{8,12},{9,13},{10,... | collective-permute-start | bytes 393224 | tf_op jit(solution)/shard_map/ppermute | solution.py:49
  27.2 3.0 %collective-permute-done.4.by_x.refs_1_ = bf16[128,512]{1,0:T(8,128)(2,1)S(1)} collective-permute-done((bf16[128,512]{1,0:T(8,128)(2,1)S(1)}, bf16[128,512]{1,0:T(8,128)(2,1)S(1)}, u32[]{:S(2)}, u32[]{:S(2)}) %collective-permute-start.4) | collective-permute-done | bytes 131104 | tf_op jit(solution)/shard_map/ppermute | solution.py:49
  30.2 2.3 %collective-permute-start.6 = (bf16[128,512]{1,0:T(8,128)(2,1)S(1)}, bf16[128,512]{1,0:T(8,128)(2,1)S(1)}, u32[]{:S(2)}, u32[]{:S(2)}) collective-permute-start(bf16[128,512]{1,0:T(8,128)(2,1)S(1)} %get-tuple-element.58), channel_id=1, source_target_pairs={{0,6},{1,7},{2,4},{3,5},{4,2},{5,3},{6,0},{7,1},{8,14},{9,15},{10,... | collective-permute-start | bytes 393224 | tf_op jit(solution)/shard_map/ppermute | solution.py:49
  32.6 3.7 %collective-permute-done.6.by_xy.refs_3_ = bf16[128,512]{1,0:T(8,128)(2,1)S(1)} collective-permute-done((bf16[128,512]{1,0:T(8,128)(2,1)S(1)}, bf16[128,512]{1,0:T(8,128)(2,1)S(1)}, u32[]{:S(2)}, u32[]{:S(2)}) %collective-permute-start.6) | collective-permute-done | bytes 131104 | tf_op jit(solution)/shard_map/ppermute | solution.py:49
  36.2 1.5 %collective-permute-start.12 = (bf16[192,1536]{1,0:T(8,128)(2,1)S(1)}, bf16[192,1536]{1,0:T(8,128)(2,1)S(1)}, u32[]{:S(2)}, u32[]{:S(2)}) collective-permute-start(bf16[192,1536]{1,0:T(8,128)(2,1)S(1)} %bitcast.16), channel_id=1, source_target_pairs={{0,2},{1,3},{2,0},{3,1},{4,6},{5,7},{6,4},{7,5},{8,10},{9,11},{10,... | collective-permute-start | bytes 1769480 | tf_op jit(solution)/shard_map/ppermute | solution.py:49
  37.8 1.4 %collective-permute-start.13 = (bf16[192,1536]{1,0:T(8,128)(2,1)S(1)}, bf16[192,1536]{1,0:T(8,128)(2,1)S(1)}, u32[]{:S(2)}, u32[]{:S(2)}) collective-permute-start(bf16[192,1536]{1,0:T(8,128)(2,1)S(1)} %bitcast.17), channel_id=1, source_target_pairs={{0,4},{1,5},{2,6},{3,7},{4,0},{5,1},{6,2},{7,3},{8,12},{9,13},{10,... | collective-permute-start | bytes 1769480 | tf_op jit(solution)/shard_map/ppermute | solution.py:49
  39.2 2.1 %cache_pages.1 = bf16[4,128,512]{2,1,0:T(8,128)(2,1)S(1)} custom-call(s32[1,64]{1,0:T(1,128)S(1)} %copy-done.3, bf16[256,512]{1,0:T(8,128)(2,1)S(1)} %project.2.refs_0_, bf16[256,512]{1,0:T(8,128)(2,1)S(1)} %project.3.refs_1_, bf16[256,512]{1,0:T(8,128)(2,1)S(1)} %collective-permute-done.7.refs_2_, bf16[256,512]{1,0:T(8,128)(2,1)S(1)} %collective-permute-done.8.refs_3_), custom_call_target="tpu_custom_call" | custom-call | tf_op jit(solution)/shard_map/cache_pages/pallas_call | solution.py:422
  41.3 0.1 pack_kv.1.own.refs_4_
  41.4 3.5 %collective-permute-start.11 = (bf16[144,512]{1,0:T(8,128)(2,1)S(1)}, bf16[144,512]{1,0:T(8,128)(2,1)S(1)}, u32[]{:S(2)}, u32[]{:S(2)}) collective-permute-start(bf16[144,512]{1,0:T(8,128)(2,1)S(1)} %pack_kv.1.own.refs_4_), channel_id=1, source_target_pairs={{0,8},{8,16},{16,24},{1,9},{9,17},{17,25},{2,10},{10,18},{18,26},{... | collective-permute-start | bytes 442376 | tf_op jit(solution)/shard_map/ppermute | solution.py:497
  44.9 7.1 %collective-permute-done.12.refs_1_ = bf16[192,1536]{1,0:T(8,128)(2,1)S(1)} collective-permute-done((bf16[192,1536]{1,0:T(8,128)(2,1)S(1)}, bf16[192,1536]{1,0:T(8,128)(2,1)S(1)}, u32[]{:S(2)}, u32[]{:S(2)}) %collective-permute-start.12) | collective-permute-done | bytes 589856 | tf_op jit(solution)/shard_map/ppermute | solution.py:49
  52.0 1.2 collective-permute-done.13.refs_2_
  53.2 0.1 collective-permute-start.19
  53.3 0.1 choose_kv.1
  53.4 1.5 %collective-permute-start.16 = (bf16[144,512]{1,0:T(8,128)(2,1)S(1)}, bf16[144,512]{1,0:T(8,128)(2,1)S(1)}, u32[]{:S(2)}, u32[]{:S(2)}) collective-permute-start(bf16[144,512]{1,0:T(8,128)(2,1)S(1)} %get-tuple-element.38.refs_0_), channel_id=1, source_target_pairs={{0,2},{1,3},{2,0},{3,1},{4,6},{5,7},{6,4},{7,5},{8,10},{9,11},{10,... | collective-permute-start | bytes 442376 | tf_op jit(solution)/shard_map/ppermute | solution.py:49
  54.9 1.4 %collective-permute-start.17 = (bf16[144,512]{1,0:T(8,128)(2,1)S(1)}, bf16[144,512]{1,0:T(8,128)(2,1)S(1)}, u32[]{:S(2)}, u32[]{:S(2)}) collective-permute-start(bf16[144,512]{1,0:T(8,128)(2,1)S(1)} %get-tuple-element.39.refs_1_), channel_id=1, source_target_pairs={{0,4},{1,5},{2,6},{3,7},{4,0},{5,1},{6,2},{7,3},{8,12},{9,13},{10,... | collective-permute-start | bytes 442376 | tf_op jit(solution)/shard_map/ppermute | solution.py:49
  56.3 0.6 collective-permute-start.18
  57.0 0.6 collective-permute-start.25
  57.5 2.5 %collective-permute-done.16.refs_5_.refs_4_ = bf16[144,512]{1,0:T(8,128)(2,1)S(1)} collective-permute-done((bf16[144,512]{1,0:T(8,128)(2,1)S(1)}, bf16[144,512]{1,0:T(8,128)(2,1)S(1)}, u32[]{:S(2)}, u32[]{:S(2)}) %collective-permute-start.16) | collective-permute-done | bytes 147488 | tf_op jit(solution)/shard_map/ppermute | solution.py:49
  60.1 3.9 %collective-permute-done.17.refs_6_.refs_5_ = bf16[144,512]{1,0:T(8,128)(2,1)S(1)} collective-permute-done((bf16[144,512]{1,0:T(8,128)(2,1)S(1)}, bf16[144,512]{1,0:T(8,128)(2,1)S(1)}, u32[]{:S(2)}, u32[]{:S(2)}) %collective-permute-start.17) | collective-permute-done | bytes 147488 | tf_op jit(solution)/shard_map/ppermute | solution.py:49
  64.0 0.5 collective-permute-start.21
  64.5 0.1 collective-permute-start.22
  64.6 0.8 collective-permute-done.20.refs_10_
  65.3 1.4 %collective-permute-start.27 = (bf16[96,1536]{1,0:T(8,128)(2,1)S(1)}, bf16[96,1536]{1,0:T(8,128)(2,1)S(1)}, u32[]{:S(2)}, u32[]{:S(2)}) collective-permute-start(bf16[96,1536]{1,0:T(8,128)(2,1)S(1)} %hold.3), channel_id=1, source_target_pairs={{0,4},{1,5},{2,6},{3,7},{4,0},{5,1},{6,2},{7,3},{8,12},{9,13},{10,... | collective-permute-start | bytes 884744 | tf_op jit(solution)/shard_map/ppermute | solution.py:49
  66.8 0.6 collective-permute-start.26
  67.4 1.9 %attend.1.refs_0_ = bf16[128,1536]{1,0:T(8,128)(2,1)S(1)} custom-call(bf16[128,512]{1,0:T(8,128)(2,1)S(1)} %get-tuple-element.31.own.refs_0_, bf16[128,512]{1,0:T(8,128)(2,1)S(1)} %collective-permute-done.4.by_x.refs_1_, bf16[128,512]{1,0:T(8,128)(2,1)S(1)} %collective-permute-done.5.by_y.refs_2_, bf16[128,512]{1,0:T(8,128)(2,1)S(1)} %collective-permute-done.6.by_xy.refs_3_, ...), custom_call_target="tpu_custom_call" | custom-call | flops 20000000000 | bytes 1 | tf_op jit(solution)/shard_map/attend/pallas_call | solution.py:262
  69.3 0.0 copy-start.5
  69.3 5.1 %collective-permute-done.27.refs_4_ = bf16[96,1536]{1,0:T(8,128)(2,1)S(1)} collective-permute-done((bf16[96,1536]{1,0:T(8,128)(2,1)S(1)}, bf16[96,1536]{1,0:T(8,128)(2,1)S(1)}, u32[]{:S(2)}, u32[]{:S(2)}) %collective-permute-start.27) | collective-permute-done | bytes 294944 | tf_op jit(solution)/shard_map/ppermute | solution.py:49
  74.4 1.2 collective-permute-done.26.refs_3_
  75.6 0.7 collective-permute-start.28
  76.2 0.5 collective-permute-start.29
  76.8 1.4 %collective-permute-start.31 = (bf16[128,1536]{1,0:T(8,128)(2,1)S(1)}, bf16[128,1536]{1,0:T(8,128)(2,1)S(1)}, u32[]{:S(2)}, u32[]{:S(2)}) collective-permute-start(bf16[128,1536]{1,0:T(8,128)(2,1)S(1)} %attend.1.refs_0_), channel_id=1, source_target_pairs={{0,2},{1,3},{2,0},{3,1},{4,6},{5,7},{6,4},{7,5},{8,10},{9,11},{10,... | collective-permute-start | bytes 1179656 | tf_op jit(solution)/shard_map/ppermute | solution.py:49
  78.2 1.4 %collective-permute-start.32 = (bf16[128,1536]{1,0:T(8,128)(2,1)S(1)}, bf16[128,1536]{1,0:T(8,128)(2,1)S(1)}, u32[]{:S(2)}, u32[]{:S(2)}) collective-permute-start(bf16[128,1536]{1,0:T(8,128)(2,1)S(1)} %attend.1.refs_0_), channel_id=1, source_target_pairs={{0,4},{1,5},{2,6},{3,7},{4,0},{5,1},{6,2},{7,3},{8,12},{9,13},{10,... | collective-permute-start | bytes 1179656 | tf_op jit(solution)/shard_map/ppermute | solution.py:49
  79.6 0.3 assemble_w_out.1.refs_6_
  79.9 8.7 %collective-permute-done.28.refs_1_ = bf16[128,1536]{1,0:T(8,128)(2,1)S(1)} collective-permute-done((bf16[128,1536]{1,0:T(8,128)(2,1)S(1)}, bf16[128,1536]{1,0:T(8,128)(2,1)S(1)}, u32[]{:S(2)}, u32[]{:S(2)}) %collective-permute-start.28) | collective-permute-done | bytes 393248 | tf_op jit(solution)/shard_map/ppermute | solution.py:49
  88.6 5.4 %experts.2 = (f32[128,1536]{1,0:T(8,128)S(1)}, bf16[128,1536]{1,0:T(8,128)(2,1)S(1)}) custom-call(bf16[128,1536]{1,0:T(8,128)(2,1)S(1)} %attend.1.refs_0_, bf16[128,1536]{1,0:T(8,128)(2,1)S(1)} %collective-permute-done.28.refs_1_, bf16[128,1536]{1,0:T(8,128)(2,1)S(1)} %copy-done.11, bf16[128,1536]{1,0:T(8,128)(2,1)S(1)} %collective-permute-done.second.refs_3_, ...), custom_call_target="tpu_custom_call" | custom-call | flops 20000000000 | bytes 1 | tf_op jit(solution)/shard_map/experts/pallas_call | solution.py:359
  93.9 0.7 collective-permute-start.35
  94.7 0.8 collective-permute-done.31.refs_0_
  95.5 0.7 collective-permute-done.32.refs_1_
  96.2 5.3 %experts.3 = (bf16[128,1536]{1,0:T(8,128)(2,1)S(1)}, bf16[128,1536]{1,0:T(8,128)(2,1)S(1)}) custom-call(bf16[128,1536]{1,0:T(8,128)(2,1)S(1)} %collective-permute-done.31.refs_0_, bf16[128,1536]{1,0:T(8,128)(2,1)S(1)} %collective-permute-done.32.refs_1_, bf16[128,1536]{1,0:T(8,128)(2,1)S(1)} %collective-permute-done.2.first.refs_2_, ...), custom_call_target="tpu_custom_call" | custom-call | flops 20000000000 | bytes 1 | tf_op jit(solution)/shard_map/experts/pallas_call | solution.py:359
  101.5 0.7 collective-permute-start.33
  102.2 0.7 collective-permute-start.34
  102.9 0.7 collective-permute-start.36
  103.6 0.7 collective-permute-start.37
  104.3 1.3 %collective-permute-start.38 = (bf16[128,512]{1,0:T(8,128)(2,1)S(1)}, bf16[128,512]{1,0:T(8,128)(2,1)S(1)}, u32[]{:S(2)}, u32[]{:S(2)}) collective-permute-start(bf16[128,512]{1,0:T(8,128)(2,1)S(1)} %get-tuple-element.54), channel_id=1, source_target_pairs={{6,0},{7,1},{14,8},{15,9},{22,16},{23,17},{30,24},{31,25}} | collective-permute-start | bytes 393224 | tf_op jit(solution)/shard_map/ppermute | solution.py:518
  105.6 13.6 %collective-permute-done.38.refs_3_ = bf16[128,512]{1,0:T(8,128)(2,1)S(1)} collective-permute-done((bf16[128,512]{1,0:T(8,128)(2,1)S(1)}, bf16[128,512]{1,0:T(8,128)(2,1)S(1)}, u32[]{:S(2)}, u32[]{:S(2)}) %collective-permute-start.38) | collective-permute-done | bytes 131104 | tf_op jit(solution)/shard_map/ppermute | solution.py:518
  119.2 0.7 join_pages.1
  119.9 0.9 mix.1
  (60 shorter events, 0.3 us)
Async XLA Ops:
  0.6 14.3 %collective-permute-start.1 = (bf16[1536,256]{1,0:T(8,128)(2,1)}, bf16[1536,256]{1,0:T(8,128)(2,1)S(1)}, u32[]{:S(2)}, u32[]{:S(2)}) collective-permute-start(bf16[1536,256]{1,0:T(8,128)(2,1)} %w_own.3), channel_id=1, source_target_pairs={{0,1},{1,0},{2,3},{3,2},{4,5},{5,4},{6,7},{7,6},{8,9},{9,8},{10,11... | collective-permute-start | bytes 2359304 | tf_op jit(solution)/shard_map/ppermute | solution.py:49
  1.1 13.7 %collective-permute-start = (bf16[128,1536]{1,0:T(8,128)(2,1)}, bf16[128,1536]{1,0:T(8,128)(2,1)S(1)}, u32[]{:S(2)}, u32[]{:S(2)}) collective-permute-start(bf16[128,1536]{1,0:T(8,128)(2,1)} %refs_2_.1), channel_id=1, source_target_pairs={{0,6},{1,7},{2,4},{3,5},{4,2},{5,3},{6,0},{7,1},{8,14},{9,15},{10,... | collective-permute-start | bytes 1179656 | tf_op jit(solution)/shard_map/ppermute | solution.py:49
  4.7 18.7 %collective-permute-start.2 = (bf16[128,1536]{1,0:T(8,128)(2,1)}, bf16[128,1536]{1,0:T(8,128)(2,1)S(1)}, u32[]{:S(2)}, u32[]{:S(2)}) collective-permute-start(bf16[128,1536]{1,0:T(8,128)(2,1)} %refs_2_.1), channel_id=1, source_target_pairs={{0,2},{1,3},{2,0},{3,1},{4,6},{5,7},{6,4},{7,5},{8,10},{9,11},{10,... | collective-permute-start | bytes 1179656 | tf_op jit(solution)/shard_map/ppermute | solution.py:49
  5.2 18.1 %collective-permute-start.3 = (bf16[128,1536]{1,0:T(8,128)(2,1)}, bf16[128,1536]{1,0:T(8,128)(2,1)S(1)}, u32[]{:S(2)}, u32[]{:S(2)}) collective-permute-start(bf16[128,1536]{1,0:T(8,128)(2,1)} %refs_2_.1), channel_id=1, source_target_pairs={{0,4},{1,5},{2,6},{3,7},{4,0},{5,1},{6,2},{7,3},{8,12},{9,13},{10,... | collective-permute-start | bytes 1179656 | tf_op jit(solution)/shard_map/ppermute | solution.py:49
  14.9 3.7 %copy-start.6 = (bf16[1,1536,768]{2,1,0:T(8,128)(2,1)S(1)}, bf16[1,1536,768]{2,1,0:T(8,128)(2,1)}, u32[]{:S(2)}) copy-start(bf16[1,1536,768]{2,1,0:T(8,128)(2,1)} %param.22) | copy-start | bytes 7077892
  14.9 24.3 %collective-permute-start.9 = (bf16[1536,768]{1,0:T(8,128)(2,1)}, bf16[1536,768]{1,0:T(8,128)(2,1)S(1)}, u32[]{:S(2)}, u32[]{:S(2)}) collective-permute-start(bf16[1536,768]{1,0:T(8,128)(2,1)} %bitcast.23), channel_id=1, source_target_pairs={{0,1},{1,0},{2,3},{3,2},{4,5},{5,4},{6,7},{7,6},{8,9},{9,8},{10,11... | collective-permute-start | bytes 7077896 | tf_op jit(solution)/shard_map/ppermute | solution.py:49
  14.9 1.3 %copy-start.8 = (bf16[1536,256]{1,0:T(8,128)(2,1)S(1)}, bf16[1536,256]{1,0:T(8,128)(2,1)}, u32[]{:S(2)}) copy-start(bf16[1536,256]{1,0:T(8,128)(2,1)} %w_own.3) | copy-start | bytes 2359300
  16.2 1.0 copy-start.10
  17.2 0.7 copy-start.12
  17.9 5.5 %copy-start.9 = (bf16[1536,256]{1,0:T(8,128)(2,1)S(1)}, bf16[1536,256]{1,0:T(8,128)(2,1)}, u32[]{:S(2)}) copy-start(bf16[1536,256]{1,0:T(8,128)(2,1)} %w_own.3) | copy-start | bytes 2359300
  18.6 5.5 %copy-start.7 = (bf16[1,768,1536]{2,1,0:T(8,128)(2,1)S(1)}, bf16[1,768,1536]{2,1,0:T(8,128)(2,1)}, u32[]{:S(2)}) copy-start(bf16[1,768,1536]{2,1,0:T(8,128)(2,1)} %param.23) | copy-start | bytes 7077892
  18.7 17.6 %copy-start = (bf16[1536,192]{0,1:T(8,128)(2,1)S(1)}, bf16[1536,192]{0,1:T(8,128)(2,1)}, u32[]{:S(2)}) copy-start(bf16[1536,192]{0,1:T(8,128)(2,1)} %param.17) | copy-start | bytes 1769476
  18.7 20.5 %copy-start.3 = (s32[1,64]{1,0:T(1,128)S(1)}, s32[1,64]{1,0:T(1,128)}, u32[]{:S(2)}) copy-start(s32[1,64]{1,0:T(1,128)} %table_ref.1) | copy-start | bytes 772
  18.7 22.6 %collective-permute-start.10 = (bf16[1536,768]{1,0:T(8,128)(2,1)S(1)}, bf16[1536,768]{1,0:T(8,128)(2,1)S(1)}, u32[]{:S(2)}, u32[]{:S(2)}) collective-permute-start(bf16[1536,768]{1,0:T(8,128)(2,1)S(1)} %bitcast.26), channel_id=1, source_target_pairs={{0,1},{1,0},{2,3},{3,2},{4,5},{5,4},{6,7},{7,6},{8,9},{9,8},{10,11... | collective-permute-start | bytes 7077896 | tf_op jit(solution)/shard_map/ppermute | solution.py:49
  24.1 17.2 %copy-start.1 = (s32[128,4]{0,1:T(4,128)S(1)}, s32[128,4]{0,1:T(4,128)}, u32[]{:S(2)}) copy-start(s32[128,4]{0,1:T(4,128)} %param.19) | copy-start | bytes 6148
  24.1 17.2 %copy-start.2 = (f32[128,4]{0,1:T(4,128)S(1)}, f32[128,4]{0,1:T(4,128)}, u32[]{:S(2)}) copy-start(f32[128,4]{0,1:T(4,128)} %param.20) | copy-start | bytes 6148
  24.1 17.2 %copy-start.4 = (s32[128]{0:T(128)S(1)}, s32[128]{0:T(128)}, u32[]{:S(2)}) copy-start(s32[128]{0:T(128)} %param.13) | copy-start | bytes 1540
  24.1 29.1 %collective-permute-start.14 = (bf16[768,1536]{1,0:T(8,128)(2,1)S(1)}, bf16[768,1536]{1,0:T(8,128)(2,1)S(1)}, u32[]{:S(2)}, u32[]{:S(2)}) collective-permute-start(bf16[768,1536]{1,0:T(8,128)(2,1)S(1)} %bitcast.29), channel_id=1, source_target_pairs={{0,1},{1,0},{2,3},{3,2},{4,5},{5,4},{6,7},{7,6},{8,9},{9,8},{10,11... | collective-permute-start | bytes 7077896 | tf_op jit(solution)/shard_map/ppermute | solution.py:49
  24.2 6.0 %collective-permute-start.4 = (bf16[128,512]{1,0:T(8,128)(2,1)S(1)}, bf16[128,512]{1,0:T(8,128)(2,1)S(1)}, u32[]{:S(2)}, u32[]{:S(2)}) collective-permute-start(bf16[128,512]{1,0:T(8,128)(2,1)S(1)} %get-tuple-element.61), channel_id=1, source_target_pairs={{0,2},{1,3},{2,0},{3,1},{4,6},{5,7},{6,4},{7,5},{8,10},{9,11},{10,... | collective-permute-start | bytes 393224 | tf_op jit(solution)/shard_map/ppermute | solution.py:49
  25.8 6.8 %collective-permute-start.5 = (bf16[128,512]{1,0:T(8,128)(2,1)S(1)}, bf16[128,512]{1,0:T(8,128)(2,1)S(1)}, u32[]{:S(2)}, u32[]{:S(2)}) collective-permute-start(bf16[128,512]{1,0:T(8,128)(2,1)S(1)} %get-tuple-element.60), channel_id=1, source_target_pairs={{0,4},{1,5},{2,6},{3,7},{4,0},{5,1},{6,2},{7,3},{8,12},{9,13},{10,... | collective-permute-start | bytes 393224 | tf_op jit(solution)/shard_map/ppermute | solution.py:49
  30.2 6.0 %collective-permute-start.6 = (bf16[128,512]{1,0:T(8,128)(2,1)S(1)}, bf16[128,512]{1,0:T(8,128)(2,1)S(1)}, u32[]{:S(2)}, u32[]{:S(2)}) collective-permute-start(bf16[128,512]{1,0:T(8,128)(2,1)S(1)} %get-tuple-element.58), channel_id=1, source_target_pairs={{0,6},{1,7},{2,4},{3,5},{4,2},{5,3},{6,0},{7,1},{8,14},{9,15},{10,... | collective-permute-start | bytes 393224 | tf_op jit(solution)/shard_map/ppermute | solution.py:49
  32.5 3.7 %collective-permute-start.7 = (bf16[256,512]{1,0:T(8,128)(2,1)S(1)}, bf16[256,512]{1,0:T(8,128)(2,1)S(1)}, u32[]{:S(2)}, u32[]{:S(2)}) collective-permute-start(bf16[256,512]{1,0:T(8,128)(2,1)S(1)} %project.2.refs_0_), channel_id=1, source_target_pairs={{0,1},{1,0},{2,3},{3,2},{4,5},{5,4},{6,7},{7,6},{8,9},{9,8},{10,11... | collective-permute-start | bytes 786440 | tf_op jit(solution)/shard_map/ppermute | solution.py:49
  36.2 1.5 %collective-permute-start.8 = (bf16[256,512]{1,0:T(8,128)(2,1)S(1)}, bf16[256,512]{1,0:T(8,128)(2,1)S(1)}, u32[]{:S(2)}, u32[]{:S(2)}) collective-permute-start(bf16[256,512]{1,0:T(8,128)(2,1)S(1)} %project.3.refs_1_), channel_id=1, source_target_pairs={{0,1},{1,0},{2,3},{3,2},{4,5},{5,4},{6,7},{7,6},{8,9},{9,8},{10,11... | collective-permute-start | bytes 786440 | tf_op jit(solution)/shard_map/ppermute | solution.py:49
  36.2 15.7 %collective-permute-start.12 = (bf16[192,1536]{1,0:T(8,128)(2,1)S(1)}, bf16[192,1536]{1,0:T(8,128)(2,1)S(1)}, u32[]{:S(2)}, u32[]{:S(2)}) collective-permute-start(bf16[192,1536]{1,0:T(8,128)(2,1)S(1)} %bitcast.16), channel_id=1, source_target_pairs={{0,2},{1,3},{2,0},{3,1},{4,6},{5,7},{6,4},{7,5},{8,10},{9,11},{10,... | collective-permute-start | bytes 1769480 | tf_op jit(solution)/shard_map/ppermute | solution.py:49
  37.8 15.4 %collective-permute-start.13 = (bf16[192,1536]{1,0:T(8,128)(2,1)S(1)}, bf16[192,1536]{1,0:T(8,128)(2,1)S(1)}, u32[]{:S(2)}, u32[]{:S(2)}) collective-permute-start(bf16[192,1536]{1,0:T(8,128)(2,1)S(1)} %bitcast.17), channel_id=1, source_target_pairs={{0,4},{1,5},{2,6},{3,7},{4,0},{5,1},{6,2},{7,3},{8,12},{9,13},{10,... | collective-permute-start | bytes 1769480 | tf_op jit(solution)/shard_map/ppermute | solution.py:49
  39.2 14.1 %collective-permute-start.15 = (bf16[192,1536]{1,0:T(8,128)(2,1)S(1)}, bf16[192,1536]{1,0:T(8,128)(2,1)S(1)}, u32[]{:S(2)}, u32[]{:S(2)}) collective-permute-start(bf16[192,1536]{1,0:T(8,128)(2,1)S(1)} %bitcast.18), channel_id=1, source_target_pairs={{0,1},{1,0},{2,3},{3,2},{4,5},{5,4},{6,7},{7,6},{8,9},{9,8},{10,11... | collective-permute-start | bytes 1769480 | tf_op jit(solution)/shard_map/ppermute | solution.py:49
  41.4 11.9 %collective-permute-start.11 = (bf16[144,512]{1,0:T(8,128)(2,1)S(1)}, bf16[144,512]{1,0:T(8,128)(2,1)S(1)}, u32[]{:S(2)}, u32[]{:S(2)}) collective-permute-start(bf16[144,512]{1,0:T(8,128)(2,1)S(1)} %pack_kv.1.own.refs_4_), channel_id=1, source_target_pairs={{0,8},{8,16},{16,24},{1,9},{9,17},{17,25},{2,10},{10,18},{18,26},{... | collective-permute-start | bytes 442376 | tf_op jit(solution)/shard_map/ppermute | solution.py:497
  53.2 3.8 %collective-permute-start.19 = (bf16[144,512]{1,0:T(8,128)(2,1)S(1)}, bf16[144,512]{1,0:T(8,128)(2,1)S(1)}, u32[]{:S(2)}, u32[]{:S(2)}) collective-permute-start(bf16[144,512]{1,0:T(8,128)(2,1)S(1)} %pack_kv.1.own.refs_4_), channel_id=1, source_target_pairs={{0,1},{1,0},{2,3},{3,2},{4,5},{5,4},{6,7},{7,6},{8,9},{9,8},{10,11... | collective-permute-start | bytes 442376 | tf_op jit(solution)/shard_map/ppermute | solution.py:49
  53.4 6.7 %collective-permute-start.16 = (bf16[144,512]{1,0:T(8,128)(2,1)S(1)}, bf16[144,512]{1,0:T(8,128)(2,1)S(1)}, u32[]{:S(2)}, u32[]{:S(2)}) collective-permute-start(bf16[144,512]{1,0:T(8,128)(2,1)S(1)} %get-tuple-element.38.refs_0_), channel_id=1, source_target_pairs={{0,2},{1,3},{2,0},{3,1},{4,6},{5,7},{6,4},{7,5},{8,10},{9,11},{10,... | collective-permute-start | bytes 442376 | tf_op jit(solution)/shard_map/ppermute | solution.py:49
  54.9 9.1 %collective-permute-start.17 = (bf16[144,512]{1,0:T(8,128)(2,1)S(1)}, bf16[144,512]{1,0:T(8,128)(2,1)S(1)}, u32[]{:S(2)}, u32[]{:S(2)}) collective-permute-start(bf16[144,512]{1,0:T(8,128)(2,1)S(1)} %get-tuple-element.39.refs_1_), channel_id=1, source_target_pairs={{0,4},{1,5},{2,6},{3,7},{4,0},{5,1},{6,2},{7,3},{8,12},{9,13},{10,... | collective-permute-start | bytes 442376 | tf_op jit(solution)/shard_map/ppermute | solution.py:49
  56.3 7.7 %collective-permute-start.18 = (bf16[144,512]{1,0:T(8,128)(2,1)S(1)}, bf16[144,512]{1,0:T(8,128)(2,1)S(1)}, u32[]{:S(2)}, u32[]{:S(2)}) collective-permute-start(bf16[144,512]{1,0:T(8,128)(2,1)S(1)} %get-tuple-element.40.refs_2_), channel_id=1, source_target_pairs={{0,6},{1,7},{2,4},{3,5},{4,2},{5,3},{6,0},{7,1},{8,14},{9,15},{10,... | collective-permute-start | bytes 442376 | tf_op jit(solution)/shard_map/ppermute | solution.py:49
  56.9 7.6 %collective-permute-start.23 = (bf16[144,512]{1,0:T(8,128)(2,1)S(1)}, bf16[144,512]{1,0:T(8,128)(2,1)S(1)}, u32[]{:S(2)}, u32[]{:S(2)}) collective-permute-start(bf16[144,512]{1,0:T(8,128)(2,1)S(1)} %collective-permute-done.11.prev.refs_8_), channel_id=1, source_target_pairs={{0,1},{1,0},{2,3},{3,2},{4,5},{5,4},{6,7},{7,6},{8,9},{9,8},{10,11... | collective-permute-start | bytes 442376 | tf_op jit(solution)/shard_map/ppermute | solution.py:49
  57.0 10.4 %collective-permute-start.25 = (bf16[192,1536]{1,0:T(8,128)(2,1)S(1)}, bf16[192,1536]{1,0:T(8,128)(2,1)S(1)}, u32[]{:S(2)}, u32[]{:S(2)}) collective-permute-start(bf16[192,1536]{1,0:T(8,128)(2,1)S(1)} %collective-permute-done.13.refs_2_), channel_id=1, source_target_pairs={{0,1},{1,0},{2,3},{3,2},{4,5},{5,4},{6,7},{7,6},{8,9},{9,8},{10,11... | collective-permute-start | bytes 1769480 | tf_op jit(solution)/shard_map/ppermute | solution.py:49
  60.1 7.3 %collective-permute-start.24 = (bf16[192,1536]{1,0:T(8,128)(2,1)S(1)}, bf16[192,1536]{1,0:T(8,128)(2,1)S(1)}, u32[]{:S(2)}, u32[]{:S(2)}) collective-permute-start(bf16[192,1536]{1,0:T(8,128)(2,1)S(1)} %collective-permute-done.12.refs_1_), channel_id=1, source_target_pairs={{0,1},{1,0},{2,3},{3,2},{4,5},{5,4},{6,7},{7,6},{8,9},{9,8},{10,11... | collective-permute-start | bytes 1769480 | tf_op jit(solution)/shard_map/ppermute | solution.py:49
  64.0 1.4 %collective-permute-start.20 = (bf16[144,512]{1,0:T(8,128)(2,1)S(1)}, bf16[144,512]{1,0:T(8,128)(2,1)S(1)}, u32[]{:S(2)}, u32[]{:S(2)}) collective-permute-start(bf16[144,512]{1,0:T(8,128)(2,1)S(1)} %collective-permute-done.16.refs_5_.refs_4_), channel_id=1, source_target_pairs={{0,1},{1,0},{2,3},{3,2},{4,5},{5,4},{6,7},{7,6},{8,9},{9,8},{10,11... | collective-permute-start | bytes 442376 | tf_op jit(solution)/shard_map/ppermute | solution.py:49
  64.0 2.8 %collective-permute-start.21 = (bf16[144,512]{1,0:T(8,128)(2,1)S(1)}, bf16[144,512]{1,0:T(8,128)(2,1)S(1)}, u32[]{:S(2)}, u32[]{:S(2)}) collective-permute-start(bf16[144,512]{1,0:T(8,128)(2,1)S(1)} %collective-permute-done.17.refs_6_.refs_5_), channel_id=1, source_target_pairs={{0,1},{1,0},{2,3},{3,2},{4,5},{5,4},{6,7},{7,6},{8,9},{9,8},{10,11... | collective-permute-start | bytes 442376 | tf_op jit(solution)/shard_map/ppermute | solution.py:49
  64.5 2.9 %collective-permute-start.22 = (bf16[144,512]{1,0:T(8,128)(2,1)S(1)}, bf16[144,512]{1,0:T(8,128)(2,1)S(1)}, u32[]{:S(2)}, u32[]{:S(2)}) collective-permute-start(bf16[144,512]{1,0:T(8,128)(2,1)S(1)} %collective-permute-done.18.refs_7_.refs_5_), channel_id=1, source_target_pairs={{0,1},{1,0},{2,3},{3,2},{4,5},{5,4},{6,7},{7,6},{8,9},{9,8},{10,11... | collective-permute-start | bytes 442376 | tf_op jit(solution)/shard_map/ppermute | solution.py:49
  65.3 9.1 %collective-permute-start.27 = (bf16[96,1536]{1,0:T(8,128)(2,1)S(1)}, bf16[96,1536]{1,0:T(8,128)(2,1)S(1)}, u32[]{:S(2)}, u32[]{:S(2)}) collective-permute-start(bf16[96,1536]{1,0:T(8,128)(2,1)S(1)} %hold.3), channel_id=1, source_target_pairs={{0,4},{1,5},{2,6},{3,7},{4,0},{5,1},{6,2},{7,3},{8,12},{9,13},{10,... | collective-permute-start | bytes 884744 | tf_op jit(solution)/shard_map/ppermute | solution.py:49
  66.8 8.8 %collective-permute-start.26 = (bf16[96,1536]{1,0:T(8,128)(2,1)S(1)}, bf16[96,1536]{1,0:T(8,128)(2,1)S(1)}, u32[]{:S(2)}, u32[]{:S(2)}) collective-permute-start(bf16[96,1536]{1,0:T(8,128)(2,1)S(1)} %hold.2), channel_id=1, source_target_pairs={{0,2},{1,3},{2,0},{3,1},{4,6},{5,7},{6,4},{7,5},{8,10},{9,11},{10,... | collective-permute-start | bytes 884744 | tf_op jit(solution)/shard_map/ppermute | solution.py:49
  69.3 19.3 %copy-start.5 = (bf16[1,1536,768]{2,1,0:T(8,128)(2,1)S(1)}, bf16[1,1536,768]{2,1,0:T(8,128)(2,1)}, u32[]{:S(2)}) copy-start(bf16[1,1536,768]{2,1,0:T(8,128)(2,1)} %param.21) | copy-start | bytes 7077892
  69.3 19.3 %copy-start.11 = (bf16[128,1536]{1,0:T(8,128)(2,1)S(1)}, bf16[128,1536]{1,0:T(8,128)(2,1)}, u32[]{:S(2)}) copy-start(bf16[128,1536]{1,0:T(8,128)(2,1)} %refs_2_.1) | copy-start | bytes 1179652
  69.3 19.3 %copy-start.13 = (f32[1536]{0:T(1024)S(1)}, f32[1536]{0:T(1024)}, u32[]{:S(2)}) copy-start(f32[1536]{0:T(1024)} %refs_7_.3) | copy-start | bytes 18436
  75.6 13.0 %collective-permute-start.28 = (bf16[128,1536]{1,0:T(8,128)(2,1)S(1)}, bf16[128,1536]{1,0:T(8,128)(2,1)S(1)}, u32[]{:S(2)}, u32[]{:S(2)}) collective-permute-start(bf16[128,1536]{1,0:T(8,128)(2,1)S(1)} %attend.1.refs_0_), channel_id=1, source_target_pairs={{0,6},{1,7},{2,4},{3,5},{4,2},{5,3},{6,0},{7,1},{8,14},{9,15},{10,... | collective-permute-start | bytes 1179656 | tf_op jit(solution)/shard_map/ppermute | solution.py:49
  76.2 3.3 %collective-permute-start.30 = (bf16[96,1536]{1,0:T(8,128)(2,1)S(1)}, bf16[96,1536]{1,0:T(8,128)(2,1)S(1)}, u32[]{:S(2)}, u32[]{:S(2)}) collective-permute-start(bf16[96,1536]{1,0:T(8,128)(2,1)S(1)} %collective-permute-done.27.refs_4_), channel_id=1, source_target_pairs={{0,1},{1,0},{2,3},{3,2},{4,5},{5,4},{6,7},{7,6},{8,9},{9,8},{10,11... | collective-permute-start | bytes 884744 | tf_op jit(solution)/shard_map/ppermute | solution.py:49
  76.2 3.3 %collective-permute-start.29 = (bf16[96,1536]{1,0:T(8,128)(2,1)S(1)}, bf16[96,1536]{1,0:T(8,128)(2,1)S(1)}, u32[]{:S(2)}, u32[]{:S(2)}) collective-permute-start(bf16[96,1536]{1,0:T(8,128)(2,1)S(1)} %collective-permute-done.26.refs_3_), channel_id=1, source_target_pairs={{0,1},{1,0},{2,3},{3,2},{4,5},{5,4},{6,7},{7,6},{8,9},{9,8},{10,11... | collective-permute-start | bytes 884744 | tf_op jit(solution)/shard_map/ppermute | solution.py:49
  76.8 18.7 %collective-permute-start.31 = (bf16[128,1536]{1,0:T(8,128)(2,1)S(1)}, bf16[128,1536]{1,0:T(8,128)(2,1)S(1)}, u32[]{:S(2)}, u32[]{:S(2)}) collective-permute-start(bf16[128,1536]{1,0:T(8,128)(2,1)S(1)} %attend.1.refs_0_), channel_id=1, source_target_pairs={{0,2},{1,3},{2,0},{3,1},{4,6},{5,7},{6,4},{7,5},{8,10},{9,11},{10,... | collective-permute-start | bytes 1179656 | tf_op jit(solution)/shard_map/ppermute | solution.py:49
  78.2 18.0 %collective-permute-start.32 = (bf16[128,1536]{1,0:T(8,128)(2,1)S(1)}, bf16[128,1536]{1,0:T(8,128)(2,1)S(1)}, u32[]{:S(2)}, u32[]{:S(2)}) collective-permute-start(bf16[128,1536]{1,0:T(8,128)(2,1)S(1)} %attend.1.refs_0_), channel_id=1, source_target_pairs={{0,4},{1,5},{2,6},{3,7},{4,0},{5,1},{6,2},{7,3},{8,12},{9,13},{10,... | collective-permute-start | bytes 1179656 | tf_op jit(solution)/shard_map/ppermute | solution.py:49
  93.9 25.9 %collective-permute-start.35 = (bf16[128,1536]{1,0:T(8,128)(2,1)S(1)}, bf16[128,1536]{1,0:T(8,128)(2,1)S(1)}, u32[]{:S(2)}, u32[]{:S(2)}) collective-permute-start(bf16[128,1536]{1,0:T(8,128)(2,1)S(1)} %get-tuple-element.50.refs_14_), channel_id=1, source_target_pairs={{0,6},{1,7},{2,4},{3,5},{4,2},{5,3},{6,0},{7,1},{8,14},{9,15},{10,... | collective-permute-start | bytes 1179656 | tf_op jit(solution)/shard_map/ppermute | solution.py:49
  101.5 18.3 %collective-permute-start.33 = (bf16[128,1536]{1,0:T(8,128)(2,1)S(1)}, bf16[128,1536]{1,0:T(8,128)(2,1)S(1)}, u32[]{:S(2)}, u32[]{:S(2)}) collective-permute-start(bf16[128,1536]{1,0:T(8,128)(2,1)S(1)} %get-tuple-element.51), channel_id=1, source_target_pairs={{0,2},{1,3},{2,0},{3,1},{4,6},{5,7},{6,4},{7,5},{8,10},{9,11},{10,... | collective-permute-start | bytes 1179656 | tf_op jit(solution)/shard_map/ppermute | solution.py:49
  102.2 17.7 %collective-permute-start.34 = (bf16[128,1536]{1,0:T(8,128)(2,1)S(1)}, bf16[128,1536]{1,0:T(8,128)(2,1)S(1)}, u32[]{:S(2)}, u32[]{:S(2)}) collective-permute-start(bf16[128,1536]{1,0:T(8,128)(2,1)S(1)} %get-tuple-element.52), channel_id=1, source_target_pairs={{0,4},{1,5},{2,6},{3,7},{4,0},{5,1},{6,2},{7,3},{8,12},{9,13},{10,... | collective-permute-start | bytes 1179656 | tf_op jit(solution)/shard_map/ppermute | solution.py:49
  102.9 1.4 %collective-permute-start.36 = (bf16[128,512]{1,0:T(8,128)(2,1)S(1)}, bf16[128,512]{1,0:T(8,128)(2,1)S(1)}, u32[]{:S(2)}, u32[]{:S(2)}) collective-permute-start(bf16[128,512]{1,0:T(8,128)(2,1)S(1)} %get-tuple-element.56), channel_id=1, source_target_pairs={{6,4},{7,5},{14,12},{15,13},{22,20},{23,21},{30,28},{31,29}} | collective-permute-start | bytes 393224 | tf_op jit(solution)/shard_map/ppermute | solution.py:518
  103.6 2.0 %collective-permute-start.37 = (bf16[128,512]{1,0:T(8,128)(2,1)S(1)}, bf16[128,512]{1,0:T(8,128)(2,1)S(1)}, u32[]{:S(2)}, u32[]{:S(2)}) collective-permute-start(bf16[128,512]{1,0:T(8,128)(2,1)S(1)} %get-tuple-element.55), channel_id=1, source_target_pairs={{6,2},{7,3},{14,10},{15,11},{22,18},{23,19},{30,26},{31,27}} | collective-permute-start | bytes 393224 | tf_op jit(solution)/shard_map/ppermute | solution.py:518
  104.3 14.9 %collective-permute-start.38 = (bf16[128,512]{1,0:T(8,128)(2,1)S(1)}, bf16[128,512]{1,0:T(8,128)(2,1)S(1)}, u32[]{:S(2)}, u32[]{:S(2)}) collective-permute-start(bf16[128,512]{1,0:T(8,128)(2,1)S(1)} %get-tuple-element.54), channel_id=1, source_target_pairs={{6,0},{7,1},{14,8},{15,9},{22,16},{23,17},{30,24},{31,25}} | collective-permute-start | bytes 393224 | tf_op jit(solution)/shard_map/ppermute | solution.py:518

commit v3 on v2

--- a/solution.py
+++ b/solution.py
@@ -54,11 +54,16 @@
     return (wide * lax.rsqrt(mean_sq + epsilon) * gain_ref[...]).astype(jnp.bfloat16)
 
 
-def project_kernel(first, second, gain_ref, w_own, w_other, out_ref, rows_ref):
+def project_kernel(count, *refs):
+    pieces, (gain_ref, w_own, w_other) = refs[:count], refs[count : count + 3]
+    out_ref, rows_ref = refs[-2:]
     core = place()[1]
-    rows, cols = first.shape[0], w_own.shape[1]
-    rows_ref[:rows, :] = rms_rows(first[...].astype(jnp.float32), gain_ref)
-    rows_ref[rows:, :] = rms_rows(second[...].astype(jnp.float32), gain_ref)
+    cols = w_own.shape[1]
+    at = 0
+    for piece in pieces:
+        span = slice(at, at + piece.shape[0])
+        rows_ref[span, :] = rms_rows(piece[...].astype(jnp.float32), gain_ref)
+        at += piece.shape[0]
     for which, weights in ((core, w_own), (1 - core, w_other)):
         span = pl.ds(pl.multiple_of(which * cols, cols), cols)
         out_ref[:, span] = jnp.dot(
@@ -66,18 +71,18 @@
         ).astype(jnp.bfloat16)
 
 
-def project_call(first, second, gain, w_own, w_other):
-    rows, width = first.shape
-    return pl.pallas_call(
-        project_kernel,
-        out_shape=jax.ShapeDtypeStruct((2 * rows, CORES * w_own.shape[1]), jnp.bfloat16),
-        in_specs=[vmem()] * 5,
+def project_call(pieces, gain, w_own, w_other, *earlier):
+    rows, width = sum(p.shape[0] for p in pieces), pieces[0].shape[1]
+    return pl.pallas_call(
+        functools.partial(project_kernel, len(pieces)),
+        out_shape=jax.ShapeDtypeStruct((rows, CORES * w_own.shape[1]), jnp.bfloat16),
+        in_specs=[vmem()] * (len(pieces) + 3) + [anywhere()] * len(earlier),
         out_specs=vmem(),
-        scratch_shapes=[pltpu.VMEM((2 * rows, width), jnp.bfloat16)],
+        scratch_shapes=[pltpu.VMEM((rows, width), jnp.bfloat16)],
         cost_estimate=LONG,
         compiler_params=params(16),
         name="project",
-    )(first, second, gain, w_own, w_other)
+    )(*pieces, gain, w_own, w_other, *earlier)
 
 
 def pack_kernel(own, by_x, by_y, by_xy, segs_ref, routes_ref, shares_ref, out_ref):
@@ -271,7 +276,6 @@
             pltpu.VMEM((wide, rows), jnp.float32),
             pltpu.VMEM((wide, HEAD), jnp.float32),
         ],
-        cost_estimate=LONG,
         compiler_params=params(32),
         name="attend",
     )(*projected, *windows)
@@ -302,10 +306,9 @@
     )(*same, *other)
 
 
-def expert_kernel(tile, *refs):
-    context, tokens, tables = refs[:2], refs[2:4], refs[4:6]
-    w_ref, gain_ref = refs[6:8]
-    held, outs, (rows_ref, hidden_ref, total_ref) = refs[8:14], refs[-5:-3], refs[-3:]
+def expert_kernel(tile, count, *refs):
+    context, tables, (w_ref, gain_ref), held = refs[:2], refs[2:4], refs[4:6], refs[6:12]
+    tokens, outs, (rows_ref, hidden_ref, total_ref) = refs[12 : 12 + count], refs[-5:-3], refs[-3:]
     chip, core = place()
     rows, width = context[0].shape
     hidden = hidden_ref.shape[1]
@@ -315,7 +318,10 @@
     added = lax.dot_general(
         rows_ref[...], w_ref[...], (((1,), (1,)), ((), ())), preferred_element_type=jnp.float32
     )
-    for span, piece in zip(spans, tokens):
+    at = 0
+    for piece in tokens:
+        span = slice(at, at + piece.shape[0])
+        at += piece.shape[0]
         residual = (piece[...].astype(jnp.float32) + added[span]).astype(jnp.bfloat16)
         wide = residual.astype(jnp.float32)
         if outs[0].dtype == jnp.float32 and span.start == 0:
@@ -357,9 +363,9 @@
     rows, width = tokens[0].shape
     hidden = weights[0].shape[1]
     return pl.pallas_call(
-        functools.partial(expert_kernel, 256),
+        functools.partial(expert_kernel, 256, len(tokens)),
         out_shape=tuple(jax.ShapeDtypeStruct((rows, width), kind) for kind in kinds),
-        in_specs=[vmem()] * 14 + [anywhere()] * len(earlier),
+        in_specs=[vmem()] * (12 + len(tokens)) + [anywhere()] * len(earlier),
         out_specs=(vmem(), vmem()),
         scratch_shapes=[
             pltpu.VMEM((2 * rows, width), jnp.bfloat16),
@@ -369,7 +375,7 @@
         cost_estimate=LONG,
         compiler_params=params(32),
         name="experts",
-    )(*context, *tokens, *tables, w_all, gain, *weights, *earlier)
+    )(*context, *tables, w_all, gain, *weights, *tokens, *earlier)
 
 
 def mix_kernel(own, by_x, by_y, by_xy, out_ref):
@@ -425,6 +431,7 @@
         in_specs=[pl.BlockSpec(memory_space=pltpu.SMEM)] + [vmem()] * 4,
         out_specs=vmem(),
         scratch_shapes=[pltpu.VMEM((CORES * CHIPS, rows, width), jnp.bfloat16)],
+        cost_estimate=LONG,
         compiler_params=params(16),
         name="cache_pages",
     )(page_table, *same, *other)
@@ -445,6 +452,7 @@
         out_shape=jax.ShapeDtypeStruct(pieces[0].shape, pieces[0].dtype),
         in_specs=[vmem()] * CHIPS,
         out_specs=vmem(),
+        cost_estimate=LONG,
         compiler_params=params(16),
         name="join_pages",
     )(*pieces)
@@ -483,24 +491,33 @@
     gate, up, down = w_gate[0], w_up[0], w_down[0]
     w_own = w_out.T
 
-    tokens_xy, tokens_x, tokens_y = chips(tokens, 3), chips(tokens, 1), chips(tokens, 2)
-    w_qkv_other = hop(w_qkv, 1)
-    made = project_call(tokens, tokens_xy, attn_gain, w_qkv, w_qkv_other)
-    late = project_call(tokens_x, tokens_y, attn_gain, w_qkv, w_qkv_other)
+    tokens_x, tokens_y = chips(tokens, 1), chips(tokens, 2)
+    w_qkv_other, gate_other = hop(w_qkv, 1), hop(gate, 1)
+    tokens_xy = [chips(tokens_y[: rows // 2], 1), chips(tokens_x[rows // 2 :], 2)]
+    late = project_call((tokens_x, tokens_y), attn_gain, w_qkv, w_qkv_other)
+    made = project_call((tokens, *tokens_xy), attn_gain, w_qkv, w_qkv_other, late)
     projected = [made[:rows], chips(late[:rows], 1), chips(late[rows:], 2), chips(made[rows:], 3)]
-    gate_other, up_other = hop(after(gate, tokens_xy), 1), hop(after(up, made), 1)
-
-    paged = cache_call(page_table, (made, late), (hop(after(made, late), 1), hop(late, 1)))
+    up_other = hop(after(up, tokens_x), 1)
+
+    paged = cache_call(page_table, (made, late), (hop(made, 1), hop(after(late, made), 1)))
     own_kv = pack_call(
         after(projected, (paged, gate_other, up_other)), segment_ids, route_ids, route_weight
     )
     prev_kv = lax.ppermute(own_kv, "seq", [(i, i + 1) for i in range(seq_size - 1)])
-    w_going, down_going = after((w_own, down), late)
+    last = CHIPS - 1
+    pages = [paged[last]]
+    for by in (1, 2, 3):
+        pairs = [(last * CORES + k, (last ^ by) * CORES + k) for k in range(CORES)]
+        pages.append(lax.ppermute(paged[last ^ by], "tensor", pairs))
+    pages = join_call(pages)
+    w_going, down_going = after((w_own, down), own_kv)
     w_x, w_y = chips(w_going, 1), chips(w_going, 2)
     down_other, w_own_other = hop(down_going, 1), hop(w_going, 1)
 
-    sent = choose_call(own_kv, after(prev_kv, (w_x, w_y, down_other, w_own_other)))
+    done = (w_x, w_y, down_other, w_own_other, pages)
+    sent = choose_call(own_kv, after(prev_kv, done))
     kv_xy, kv_x, kv_y = chips(sent[2], 3), chips(sent[0], 1), chips(sent[1], 2)
+    kv_xy = hold_call(kv_xy)
     half = w_own.shape[0] // 2
     w_relayed = [hold_call(w_y[:half], *sent), hold_call(w_x[half:], *sent)]
     w_diagonal = [chips(w_relayed[0], 1), chips(w_relayed[1], 2)]
@@ -510,22 +527,15 @@
     windows_other = after(windows_other, (w_other, w_relayed))
     context = after(attend_call(projected, windows + windows_other), w_diagonal)
     context_xy, context_x, context_y = chips(context, 3), chips(context, 1), chips(context, 2)
-    last = CHIPS - 1
-    paged = after(paged, context)
-    pages = [paged[last]]
-    for by in (1, 2, 3):
-        pairs = [(last * CORES + k, (last ^ by) * CORES + k) for k in range(CORES)]
-        pages.append(lax.ppermute(paged[last ^ by], "tensor", pairs))
-    pages = join_call(pages)
     w_other += [hop(w, 1) for w in w_diagonal]
     w_all = assemble_call([w_own, w_x, w_y] + w_diagonal, w_other)
 
     weights = [gate, up, down, gate_other, up_other, down_other]
     out, out_xy = expert_call(
-        (context, context_xy), (tokens, tokens_xy), (own_kv, kv_xy), w_all, moe_gain, weights,
+        (context, context_xy), (tokens, *tokens_xy), (own_kv, kv_xy), w_all, moe_gain, weights,
         (jnp.float32, jnp.bfloat16),
     )
-    back_xy = chips(out_xy, 3)
+    back_xy = hold_call(chips(out_xy, 3))
     out_x, out_y = expert_call(
         (context_x, context_y), (tokens_x, tokens_y), (kv_x, kv_y), w_all, moe_gain, weights,
         (jnp.bfloat16, jnp.bfloat16), out_xy,

time: 121 us -> 115 us (0.950)
  waiting for transfers between devices: 66 us -> 53.6 us
  starting transfers between devices: 32.5 us -> 40.1 us
    ppermute x3, waiting for transfers between devices: 13.6 us -> 0.01 us  [chip_body(): pages.append(lax.ppermute(paged[last ^ by], 'tensor', pairs))]
    ppermute x35 -> x36, starting transfers between devices: 26.4 us -> 34 us  [hop(): return lax.ppermute(value, 'tensor', [(i, i ^ by) for i in range(length)])]
    unnamed x28 -> x26, local copies, waits for them, and re-layouts: 3.03 us -> 1.88 us
    ppermute x35 -> x36, waiting for transfers between devices: 52.4 us -> 53.5 us  [hop(): return lax.ppermute(value, 'tensor', [(i, i ^ by) for i in range(length)])]
  transfers between devices with their start and end apart: 39 -> 40, of which waited for: 15 -> 15; matrix products, arithmetic and copies ran while one was open for 0% -> 0% of each run, Pallas kernels for 14% -> 15%
where the time goes in v3:
time: 115 us
  waiting for transfers between devices  53.6 us (47%)
  starting transfers between devices  40.1 us (35%)
  Pallas kernels  18.2 us (16%)
  local copies, waits for them, and re-layouts  2.03 us (2%)
    ppermute x36, waiting for transfers between devices, hop(): return lax.ppermute(value, 'tensor', [(i, i ^ by) for i in range(length)])  53.5 us
    ppermute x36, starting transfers between devices, hop(): return lax.ppermute(value, 'tensor', [(i, i ^ by) for i in range(length)])  34 us
    pallas_call x2, Pallas kernels, expert_call(): pl.pallas_call(functools.partial(expert_kernel, 256, len(tokens)), out_sh...  10.7 us
    ppermute x1, starting transfers between devices, chip_body(): lax.ppermute(own_kv, 'seq', [(i, i + 1) for i in range(seq_size - 1)])  3.49 us
    ppermute x3, starting transfers between devices, chip_body(): pages.append(lax.ppermute(paged[last ^ by], 'tensor', pairs))  2.63 us
  transfers between devices with their start and end apart: 40, of which 15 were waited for; matrix products, arithmetic and copies ran while one was open for 0% of the time, Pallas kernels for 15%

profile of v3, /device:TPU:0, one launch (start us, length us, event | category | flops | bytes accessed | tf_op | source)
XLA Modules:
  0.0 114.9 jit_solution(16836917385792207033)
XLA Ops:
  0.6 0.5 collective-permute-start.4
  1.1 2.6 %collective-permute-start = (bf16[128,1536]{1,0:T(8,128)(2,1)}, bf16[128,1536]{1,0:T(8,128)(2,1)S(1)}, u32[]{:S(2)}, u32[]{:S(2)}) collective-permute-start(bf16[128,1536]{1,0:T(8,128)(2,1)} %refs_12_.1), channel_id=1, source_target_pairs={{0,4},{1,5},{2,6},{3,7},{4,0},{5,1},{6,2},{7,3},{8,12},{9,13},{10,... | collective-permute-start | bytes 1179656 | tf_op jit(solution)/shard_map/ppermute | solution.py:49
  3.7 1.5 %collective-permute-start.2 = (bf16[128,1536]{1,0:T(8,128)(2,1)}, bf16[128,1536]{1,0:T(8,128)(2,1)S(1)}, u32[]{:S(2)}, u32[]{:S(2)}) collective-permute-start(bf16[128,1536]{1,0:T(8,128)(2,1)} %refs_12_.1), channel_id=1, source_target_pairs={{0,2},{1,3},{2,0},{3,1},{4,6},{5,7},{6,4},{7,5},{8,10},{9,11},{10,... | collective-permute-start | bytes 1179656 | tf_op jit(solution)/shard_map/ppermute | solution.py:49
  5.2 8.4 %collective-permute-done.refs_1_.refs_13_ = bf16[128,1536]{1,0:T(8,128)(2,1)S(1)} collective-permute-done((bf16[128,1536]{1,0:T(8,128)(2,1)}, bf16[128,1536]{1,0:T(8,128)(2,1)S(1)}, u32[]{:S(2)}, u32[]{:S(2)}) %collective-permute-start) | collective-permute-done | bytes 393248 | tf_op jit(solution)/shard_map/ppermute | solution.py:49
  13.7 1.8 %collective-permute-start.1 = (bf16[64,1536]{1,0:T(8,128)(2,1)S(1)}, bf16[64,1536]{1,0:T(8,128)(2,1)S(1)}, u32[]{:S(2)}, u32[]{:S(2)}) collective-permute-start(bf16[64,1536]{1,0:T(8,128)(2,1)S(1)} %slice.48), channel_id=1, source_target_pairs={{0,2},{1,3},{2,0},{3,1},{4,6},{5,7},{6,4},{7,5},{8,10},{9,11},{10,... | collective-permute-start | bytes 589832 | tf_op jit(solution)/shard_map/ppermute | solution.py:49
  15.5 1.6 %collective-permute-start.3 = (bf16[64,1536]{1,0:T(8,128)(2,1)S(1)}, bf16[64,1536]{1,0:T(8,128)(2,1)S(1)}, u32[]{:S(2)}, u32[]{:S(2)}) collective-permute-start(bf16[64,1536]{1,0:T(8,128)(2,1)S(1)} %slice.49), channel_id=1, source_target_pairs={{0,4},{1,5},{2,6},{3,7},{4,0},{5,1},{6,2},{7,3},{8,12},{9,13},{10,... | collective-permute-start | bytes 589832 | tf_op jit(solution)/shard_map/ppermute | solution.py:49
  17.1 1.1 copy-done.7
  18.2 0.7 copy-done.10
  18.9 0.7 project.2.refs_6_.refs_1_
  19.7 0.0 copy-start.12
  19.7 0.7 collective-permute-done.1.refs_1_.refs_13_
  20.4 1.3 %collective-permute-done.3.refs_2_.refs_14_ = bf16[64,1536]{1,0:T(8,128)(2,1)S(1)} collective-permute-done((bf16[64,1536]{1,0:T(8,128)(2,1)S(1)}, bf16[64,1536]{1,0:T(8,128)(2,1)S(1)}, u32[]{:S(2)}, u32[]{:S(2)}) %collective-permute-start.3) | collective-permute-done | bytes 196640 | tf_op jit(solution)/shard_map/ppermute | solution.py:49
  21.8 0.7 project.3.refs_0_
  22.5 0.1 collective-permute-start.8
  22.6 0.5 collective-permute-start.9
  23.1 1.2 %collective-permute-start.5 = (bf16[128,512]{1,0:T(8,128)(2,1)S(1)}, bf16[128,512]{1,0:T(8,128)(2,1)S(1)}, u32[]{:S(2)}, u32[]{:S(2)}) collective-permute-start(bf16[128,512]{1,0:T(8,128)(2,1)S(1)} %get-tuple-element.57), channel_id=1, source_target_pairs={{0,2},{1,3},{2,0},{3,1},{4,6},{5,7},{6,4},{7,5},{8,10},{9,11},{10,... | collective-permute-start | bytes 393224 | tf_op jit(solution)/shard_map/ppermute | solution.py:49
  24.3 1.3 %collective-permute-start.6 = (bf16[128,512]{1,0:T(8,128)(2,1)S(1)}, bf16[128,512]{1,0:T(8,128)(2,1)S(1)}, u32[]{:S(2)}, u32[]{:S(2)}) collective-permute-start(bf16[128,512]{1,0:T(8,128)(2,1)S(1)} %get-tuple-element.56), channel_id=1, source_target_pairs={{0,4},{1,5},{2,6},{3,7},{4,0},{5,1},{6,2},{7,3},{8,12},{9,13},{10,... | collective-permute-start | bytes 393224 | tf_op jit(solution)/shard_map/ppermute | solution.py:49
  25.7 0.0 copy-start
  25.7 1.2 %collective-permute-start.7 = (bf16[128,512]{1,0:T(8,128)(2,1)S(1)}, bf16[128,512]{1,0:T(8,128)(2,1)S(1)}, u32[]{:S(2)}, u32[]{:S(2)}) collective-permute-start(bf16[128,512]{1,0:T(8,128)(2,1)S(1)} %get-tuple-element.54), channel_id=1, source_target_pairs={{0,6},{1,7},{2,4},{3,5},{4,2},{5,3},{6,0},{7,1},{8,14},{9,15},{10,... | collective-permute-start | bytes 393224 | tf_op jit(solution)/shard_map/ppermute | solution.py:49
  26.9 2.1 %cache_pages.1 = bf16[4,128,512]{2,1,0:T(8,128)(2,1)S(1)} custom-call(s32[1,64]{1,0:T(1,128)S(1)} %copy-done.12, bf16[256,512]{1,0:T(8,128)(2,1)S(1)} %project.3.refs_0_, bf16[256,512]{1,0:T(8,128)(2,1)S(1)} %project.2.refs_6_.refs_1_, bf16[256,512]{1,0:T(8,128)(2,1)S(1)} %collective-permute-done.8.refs_2_, bf16[256,512]{1,0:T(8,128)(2,1)S(1)} %collective-permute-done.9.refs_3_), custom_call_target="tpu_custom_call" | custom-call | flops 20000000000 | bytes 1 | tf_op jit(solution)/shard_map/cache_pages/pallas_call | solution.py:428
  28.9 0.0 collective-permute-done.5.by_x.refs_1_
  29.0 2.5 %collective-permute-done.6.by_y.refs_2_ = bf16[128,512]{1,0:T(8,128)(2,1)S(1)} collective-permute-done((bf16[128,512]{1,0:T(8,128)(2,1)S(1)}, bf16[128,512]{1,0:T(8,128)(2,1)S(1)}, u32[]{:S(2)}, u32[]{:S(2)}) %collective-permute-start.6) | collective-permute-done | bytes 131104 | tf_op jit(solution)/shard_map/ppermute | solution.py:49
  31.5 1.0 collective-permute-done.7.by_xy.refs_3_
  32.5 0.1 pack_kv.1.own.refs_4_.refs_2_
  32.6 0.1 collective-permute-start.15
  32.7 0.7 collective-permute-start.17
  33.4 0.7 collective-permute-start.18
  34.0 1.3 %collective-permute-start.19 = (bf16[128,512]{1,0:T(8,128)(2,1)S(1)}, bf16[128,512]{1,0:T(8,128)(2,1)S(1)}, u32[]{:S(2)}, u32[]{:S(2)}) collective-permute-start(bf16[128,512]{1,0:T(8,128)(2,1)S(1)} %get-tuple-element.50), channel_id=1, source_target_pairs={{6,0},{7,1},{14,8},{15,9},{22,16},{23,17},{30,24},{31,25}} | collective-permute-start | bytes 393224 | tf_op jit(solution)/shard_map/ppermute | solution.py:511
  35.3 3.5 %collective-permute-start.12 = (bf16[144,512]{1,0:T(8,128)(2,1)S(1)}, bf16[144,512]{1,0:T(8,128)(2,1)S(1)}, u32[]{:S(2)}, u32[]{:S(2)}) collective-permute-start(bf16[144,512]{1,0:T(8,128)(2,1)S(1)} %pack_kv.1.own.refs_4_.refs_2_), channel_id=1, source_target_pairs={{0,8},{8,16},{16,24},{1,9},{9,17},{17,25},{2,10},{10,18},{18,26},{... | collective-permute-start | bytes 442376 | tf_op jit(solution)/shard_map/ppermute | solution.py:506
  38.8 1.2 %collective-permute-start.13 = (bf16[192,1536]{1,0:T(8,128)(2,1)S(1)}, bf16[192,1536]{1,0:T(8,128)(2,1)S(1)}, u32[]{:S(2)}, u32[]{:S(2)}) collective-permute-start(bf16[192,1536]{1,0:T(8,128)(2,1)S(1)} %bitcast.16), channel_id=1, source_target_pairs={{0,2},{1,3},{2,0},{3,1},{4,6},{5,7},{6,4},{7,5},{8,10},{9,11},{10,... | collective-permute-start | bytes 1769480 | tf_op jit(solution)/shard_map/ppermute | solution.py:49
  40.0 4.3 %collective-permute-start.14 = (bf16[192,1536]{1,0:T(8,128)(2,1)S(1)}, bf16[192,1536]{1,0:T(8,128)(2,1)S(1)}, u32[]{:S(2)}, u32[]{:S(2)}) collective-permute-start(bf16[192,1536]{1,0:T(8,128)(2,1)S(1)} %bitcast.17), channel_id=1, source_target_pairs={{0,4},{1,5},{2,6},{3,7},{4,0},{5,1},{6,2},{7,3},{8,12},{9,13},{10,... | collective-permute-start | bytes 1769480 | tf_op jit(solution)/shard_map/ppermute | solution.py:49
  44.4 0.7 join_pages.1
  45.0 0.5 collective-permute-start.23
  45.5 12.0 %collective-permute-done.14.refs_2_ = bf16[192,1536]{1,0:T(8,128)(2,1)S(1)} collective-permute-done((bf16[192,1536]{1,0:T(8,128)(2,1)S(1)}, bf16[192,1536]{1,0:T(8,128)(2,1)S(1)}, u32[]{:S(2)}, u32[]{:S(2)}) %collective-permute-start.14) | collective-permute-done | bytes 589856 | tf_op jit(solution)/shard_map/ppermute | solution.py:49
  57.6 0.1 choose_kv.1
  57.6 0.8 collective-permute-start.20
  58.5 1.4 %collective-permute-start.21 = (bf16[144,512]{1,0:T(8,128)(2,1)S(1)}, bf16[144,512]{1,0:T(8,128)(2,1)S(1)}, u32[]{:S(2)}, u32[]{:S(2)}) collective-permute-start(bf16[144,512]{1,0:T(8,128)(2,1)S(1)} %get-tuple-element.36.refs_1_), channel_id=1, source_target_pairs={{0,4},{1,5},{2,6},{3,7},{4,0},{5,1},{6,2},{7,3},{8,12},{9,13},{10,... | collective-permute-start | bytes 442376 | tf_op jit(solution)/shard_map/ppermute | solution.py:49
  59.8 1.4 %collective-permute-start.22 = (bf16[144,512]{1,0:T(8,128)(2,1)S(1)}, bf16[144,512]{1,0:T(8,128)(2,1)S(1)}, u32[]{:S(2)}, u32[]{:S(2)}) collective-permute-start(bf16[144,512]{1,0:T(8,128)(2,1)S(1)} %get-tuple-element.37.refs_2_), channel_id=1, source_target_pairs={{0,6},{1,7},{2,4},{3,5},{4,2},{5,3},{6,0},{7,1},{8,14},{9,15},{10,... | collective-permute-start | bytes 442376 | tf_op jit(solution)/shard_map/ppermute | solution.py:49
  61.2 3.1 %collective-permute-done.20.refs_5_.refs_2_ = bf16[144,512]{1,0:T(8,128)(2,1)S(1)} collective-permute-done((bf16[144,512]{1,0:T(8,128)(2,1)S(1)}, bf16[144,512]{1,0:T(8,128)(2,1)S(1)}, u32[]{:S(2)}, u32[]{:S(2)}) %collective-permute-start.20) | collective-permute-done | bytes 147488 | tf_op jit(solution)/shard_map/ppermute | solution.py:49
  64.4 0.6 collective-permute-start.28
  65.0 0.1 collective-permute-start.29
  65.1 1.5 %collective-permute-done.21.refs_6_.refs_3_ = bf16[144,512]{1,0:T(8,128)(2,1)S(1)} collective-permute-done((bf16[144,512]{1,0:T(8,128)(2,1)S(1)}, bf16[144,512]{1,0:T(8,128)(2,1)S(1)}, u32[]{:S(2)}, u32[]{:S(2)}) %collective-permute-start.21) | collective-permute-done | bytes 147488 | tf_op jit(solution)/shard_map/ppermute | solution.py:49
  66.5 2.4 %collective-permute-start.30 = (bf16[96,1536]{1,0:T(8,128)(2,1)S(1)}, bf16[96,1536]{1,0:T(8,128)(2,1)S(1)}, u32[]{:S(2)}, u32[]{:S(2)}) collective-permute-start(bf16[96,1536]{1,0:T(8,128)(2,1)S(1)} %hold.5), channel_id=1, source_target_pairs={{0,2},{1,3},{2,0},{3,1},{4,6},{5,7},{6,4},{7,5},{8,10},{9,11},{10,... | collective-permute-start | bytes 884744 | tf_op jit(solution)/shard_map/ppermute | solution.py:49
  68.9 1.7 %collective-permute-start.31 = (bf16[96,1536]{1,0:T(8,128)(2,1)S(1)}, bf16[96,1536]{1,0:T(8,128)(2,1)S(1)}, u32[]{:S(2)}, u32[]{:S(2)}) collective-permute-start(bf16[96,1536]{1,0:T(8,128)(2,1)S(1)} %hold.6), channel_id=1, source_target_pairs={{0,4},{1,5},{2,6},{3,7},{4,0},{5,1},{6,2},{7,3},{8,12},{9,13},{10,... | collective-permute-start | bytes 884744 | tf_op jit(solution)/shard_map/ppermute | solution.py:49
  70.6 1.4 %collective-permute-done.25.refs_11_ = bf16[144,512]{1,0:T(8,128)(2,1)S(1)} collective-permute-done((bf16[144,512]{1,0:T(8,128)(2,1)S(1)}, bf16[144,512]{1,0:T(8,128)(2,1)S(1)}, u32[]{:S(2)}, u32[]{:S(2)}) %collective-permute-start.25) | collective-permute-done | bytes 147488 | tf_op jit(solution)/shard_map/ppermute | solution.py:49
  72.0 0.1 collective-permute-start.26
  72.2 1.2 %collective-permute-done.26.refs_12_ = bf16[144,512]{1,0:T(8,128)(2,1)S(1)} collective-permute-done((bf16[144,512]{1,0:T(8,128)(2,1)S(1)}, bf16[144,512]{1,0:T(8,128)(2,1)S(1)}, u32[]{:S(2)}, u32[]{:S(2)}) %collective-permute-start.26) | collective-permute-done | bytes 147488 | tf_op jit(solution)/shard_map/ppermute | solution.py:49
  73.4 1.9 %attend.1.refs_0_ = bf16[128,1536]{1,0:T(8,128)(2,1)S(1)} custom-call(bf16[128,512]{1,0:T(8,128)(2,1)S(1)} %get-tuple-element.28.own.refs_0_, bf16[128,512]{1,0:T(8,128)(2,1)S(1)} %collective-permute-done.5.by_x.refs_1_, bf16[128,512]{1,0:T(8,128)(2,1)S(1)} %collective-permute-done.6.by_y.refs_2_, bf16[128,512]{1,0:T(8,128)(2,1)S(1)} %collective-permute-done.7.by_xy.refs_3_, ...), custom_call_target="tpu_custom_call" | custom-call | tf_op jit(solution)/shard_map/attend/pallas_call | solution.py:267
  75.3 1.7 %collective-permute-done.31.refs_4_ = bf16[96,1536]{1,0:T(8,128)(2,1)S(1)} collective-permute-done((bf16[96,1536]{1,0:T(8,128)(2,1)S(1)}, bf16[96,1536]{1,0:T(8,128)(2,1)S(1)}, u32[]{:S(2)}, u32[]{:S(2)}) %collective-permute-start.31) | collective-permute-done | bytes 294944 | tf_op jit(solution)/shard_map/ppermute | solution.py:49
  77.0 1.4 %collective-permute-start.32 = (bf16[128,1536]{1,0:T(8,128)(2,1)S(1)}, bf16[128,1536]{1,0:T(8,128)(2,1)S(1)}, u32[]{:S(2)}, u32[]{:S(2)}) collective-permute-start(bf16[128,1536]{1,0:T(8,128)(2,1)S(1)} %attend.1.refs_0_), channel_id=1, source_target_pairs={{0,6},{1,7},{2,4},{3,5},{4,2},{5,3},{6,0},{7,1},{8,14},{9,15},{10,... | collective-permute-start | bytes 1179656 | tf_op jit(solution)/shard_map/ppermute | solution.py:49
  78.4 0.5 collective-permute-start.34
  78.9 1.7 %collective-permute-start.35 = (bf16[128,1536]{1,0:T(8,128)(2,1)S(1)}, bf16[128,1536]{1,0:T(8,128)(2,1)S(1)}, u32[]{:S(2)}, u32[]{:S(2)}) collective-permute-start(bf16[128,1536]{1,0:T(8,128)(2,1)S(1)} %attend.1.refs_0_), channel_id=1, source_target_pairs={{0,2},{1,3},{2,0},{3,1},{4,6},{5,7},{6,4},{7,5},{8,10},{9,11},{10,... | collective-permute-start | bytes 1179656 | tf_op jit(solution)/shard_map/ppermute | solution.py:49
  80.6 0.3 collective-permute-start.36
  81.0 0.3 assemble_w_out.1.refs_4_
  81.3 8.7 %collective-permute-done.32.refs_1_ = bf16[128,1536]{1,0:T(8,128)(2,1)S(1)} collective-permute-done((bf16[128,1536]{1,0:T(8,128)(2,1)S(1)}, bf16[128,1536]{1,0:T(8,128)(2,1)S(1)}, u32[]{:S(2)}, u32[]{:S(2)}) %collective-permute-start.32) | collective-permute-done | bytes 393248 | tf_op jit(solution)/shard_map/ppermute | solution.py:49
  90.0 5.4 %experts.2 = (f32[128,1536]{1,0:T(8,128)S(1)}, bf16[128,1536]{1,0:T(8,128)(2,1)S(1)}) custom-call(bf16[128,1536]{1,0:T(8,128)(2,1)S(1)} %attend.1.refs_0_, bf16[128,1536]{1,0:T(8,128)(2,1)S(1)} %collective-permute-done.32.refs_1_, bf16[144,512]{1,0:T(8,128)(2,1)S(1)} %pack_kv.1.own.refs_4_.refs_2_, bf16[144,512]{1,0:T(8,128)(2,1)S(1)} %hold.4.refs_7_.refs_3_, ...), custom_call_target="tpu_custom_call" | custom-call | flops 20000000000 | bytes 1 | tf_op jit(solution)/shard_map/experts/pallas_call | solution.py:365
  95.4 1.5 %collective-permute-start.39 = (bf16[128,1536]{1,0:T(8,128)(2,1)S(1)}, bf16[128,1536]{1,0:T(8,128)(2,1)S(1)}, u32[]{:S(2)}, u32[]{:S(2)}) collective-permute-start(bf16[128,1536]{1,0:T(8,128)(2,1)S(1)} %get-tuple-element.47.refs_14_), channel_id=1, source_target_pairs={{0,6},{1,7},{2,4},{3,5},{4,2},{5,3},{6,0},{7,1},{8,14},{9,15},{10,... | collective-permute-start | bytes 1179656 | tf_op jit(solution)/shard_map/ppermute | solution.py:49
  96.9 1.1 collective-permute-done.35.refs_0_
  97.9 5.3 %experts.3 = (bf16[128,1536]{1,0:T(8,128)(2,1)S(1)}, bf16[128,1536]{1,0:T(8,128)(2,1)S(1)}) custom-call(bf16[128,1536]{1,0:T(8,128)(2,1)S(1)} %collective-permute-done.35.refs_0_, bf16[128,1536]{1,0:T(8,128)(2,1)S(1)} %collective-permute-done.36.refs_1_, bf16[144,512]{1,0:T(8,128)(2,1)S(1)} %collective-permute-done.20.refs_5_.refs_2_, ...), custom_call_target="tpu_custom_call" | custom-call | flops 20000000000 | bytes 1 | tf_op jit(solution)/shard_map/experts/pallas_call | solution.py:365
  103.2 0.8 collective-permute-start.37
  104.0 1.0 collective-permute-start.38
  105.0 8.9 %collective-permute-done.37.by_x = bf16[128,1536]{1,0:T(8,128)(2,1)S(1)} collective-permute-done((bf16[128,1536]{1,0:T(8,128)(2,1)S(1)}, bf16[128,1536]{1,0:T(8,128)(2,1)S(1)}, u32[]{:S(2)}, u32[]{:S(2)}) %collective-permute-start.37) | collective-permute-done | bytes 393248 | tf_op jit(solution)/shard_map/ppermute | solution.py:49
  113.9 0.1 collective-permute-done.38.by_y
  114.0 0.9 mix.1
  (64 shorter events, 0.4 us)
Async XLA Ops:
  0.6 16.5 %collective-permute-start.4 = (bf16[1536,256]{1,0:T(8,128)(2,1)}, bf16[1536,256]{1,0:T(8,128)(2,1)S(1)}, u32[]{:S(2)}, u32[]{:S(2)}) collective-permute-start(bf16[1536,256]{1,0:T(8,128)(2,1)} %refs_4_.1), channel_id=1, source_target_pairs={{0,1},{1,0},{2,3},{3,2},{4,5},{5,4},{6,7},{7,6},{8,9},{9,8},{10,11... | collective-permute-start | bytes 2359304 | tf_op jit(solution)/shard_map/ppermute | solution.py:49
  1.1 12.5 %collective-permute-start = (bf16[128,1536]{1,0:T(8,128)(2,1)}, bf16[128,1536]{1,0:T(8,128)(2,1)S(1)}, u32[]{:S(2)}, u32[]{:S(2)}) collective-permute-start(bf16[128,1536]{1,0:T(8,128)(2,1)} %refs_12_.1), channel_id=1, source_target_pairs={{0,4},{1,5},{2,6},{3,7},{4,0},{5,1},{6,2},{7,3},{8,12},{9,13},{10,... | collective-permute-start | bytes 1179656 | tf_op jit(solution)/shard_map/ppermute | solution.py:49
  3.7 11.7 %collective-permute-start.2 = (bf16[128,1536]{1,0:T(8,128)(2,1)}, bf16[128,1536]{1,0:T(8,128)(2,1)S(1)}, u32[]{:S(2)}, u32[]{:S(2)}) collective-permute-start(bf16[128,1536]{1,0:T(8,128)(2,1)} %refs_12_.1), channel_id=1, source_target_pairs={{0,2},{1,3},{2,0},{3,1},{4,6},{5,7},{6,4},{7,5},{8,10},{9,11},{10,... | collective-permute-start | bytes 1179656 | tf_op jit(solution)/shard_map/ppermute | solution.py:49
  5.2 27.2 %collective-permute-start.10 = (bf16[1536,768]{1,0:T(8,128)(2,1)}, bf16[1536,768]{1,0:T(8,128)(2,1)S(1)}, u32[]{:S(2)}, u32[]{:S(2)}) collective-permute-start(bf16[1536,768]{1,0:T(8,128)(2,1)} %bitcast.23), channel_id=1, source_target_pairs={{0,1},{1,0},{2,3},{3,2},{4,5},{5,4},{6,7},{7,6},{8,9},{9,8},{10,11... | collective-permute-start | bytes 7077896 | tf_op jit(solution)/shard_map/ppermute | solution.py:49
  13.7 6.7 %collective-permute-start.1 = (bf16[64,1536]{1,0:T(8,128)(2,1)S(1)}, bf16[64,1536]{1,0:T(8,128)(2,1)S(1)}, u32[]{:S(2)}, u32[]{:S(2)}) collective-permute-start(bf16[64,1536]{1,0:T(8,128)(2,1)S(1)} %slice.48), channel_id=1, source_target_pairs={{0,2},{1,3},{2,0},{3,1},{4,6},{5,7},{6,4},{7,5},{8,10},{9,11},{10,... | collective-permute-start | bytes 589832 | tf_op jit(solution)/shard_map/ppermute | solution.py:49
  15.5 6.3 %collective-permute-start.3 = (bf16[64,1536]{1,0:T(8,128)(2,1)S(1)}, bf16[64,1536]{1,0:T(8,128)(2,1)S(1)}, u32[]{:S(2)}, u32[]{:S(2)}) collective-permute-start(bf16[64,1536]{1,0:T(8,128)(2,1)S(1)} %slice.49), channel_id=1, source_target_pairs={{0,4},{1,5},{2,6},{3,7},{4,0},{5,1},{6,2},{7,3},{8,12},{9,13},{10,... | collective-permute-start | bytes 589832 | tf_op jit(solution)/shard_map/ppermute | solution.py:49
  17.1 15.4 %collective-permute-start.11 = (bf16[1536,768]{1,0:T(8,128)(2,1)}, bf16[1536,768]{1,0:T(8,128)(2,1)S(1)}, u32[]{:S(2)}, u32[]{:S(2)}) collective-permute-start(bf16[1536,768]{1,0:T(8,128)(2,1)} %bitcast.26), channel_id=1, source_target_pairs={{0,1},{1,0},{2,3},{3,2},{4,5},{5,4},{6,7},{7,6},{8,9},{9,8},{10,11... | collective-permute-start | bytes 7077896 | tf_op jit(solution)/shard_map/ppermute | solution.py:49
  17.1 1.1 copy-start.7
  18.2 0.7 copy-start.10
  18.9 2.8 %copy-start.8 = (bf16[1536,256]{1,0:T(8,128)(2,1)S(1)}, bf16[1536,256]{1,0:T(8,128)(2,1)}, u32[]{:S(2)}) copy-start(bf16[1536,256]{1,0:T(8,128)(2,1)} %refs_4_.1) | copy-start | bytes 2359300
  18.9 2.8 %copy-start.9 = (bf16[128,1536]{1,0:T(8,128)(2,1)S(1)}, bf16[128,1536]{1,0:T(8,128)(2,1)}, u32[]{:S(2)}) copy-start(bf16[128,1536]{1,0:T(8,128)(2,1)} %refs_12_.1) | copy-start | bytes 1179652
  19.7 7.2 %copy-start.12 = (s32[1,64]{1,0:T(1,128)S(1)}, s32[1,64]{1,0:T(1,128)}, u32[]{:S(2)}) copy-start(s32[1,64]{1,0:T(1,128)} %table_ref.1) | copy-start | bytes 772
  22.5 1.8 %collective-permute-start.8 = (bf16[256,512]{1,0:T(8,128)(2,1)S(1)}, bf16[256,512]{1,0:T(8,128)(2,1)S(1)}, u32[]{:S(2)}, u32[]{:S(2)}) collective-permute-start(bf16[256,512]{1,0:T(8,128)(2,1)S(1)} %project.3.refs_0_), channel_id=1, source_target_pairs={{0,1},{1,0},{2,3},{3,2},{4,5},{5,4},{6,7},{7,6},{8,9},{9,8},{10,11... | collective-permute-start | bytes 786440 | tf_op jit(solution)/shard_map/ppermute | solution.py:49
  22.6 3.0 %collective-permute-start.9 = (bf16[256,512]{1,0:T(8,128)(2,1)S(1)}, bf16[256,512]{1,0:T(8,128)(2,1)S(1)}, u32[]{:S(2)}, u32[]{:S(2)}) collective-permute-start(bf16[256,512]{1,0:T(8,128)(2,1)S(1)} %project.2.refs_6_.refs_1_), channel_id=1, source_target_pairs={{0,1},{1,0},{2,3},{3,2},{4,5},{5,4},{6,7},{7,6},{8,9},{9,8},{10,11... | collective-permute-start | bytes 786440 | tf_op jit(solution)/shard_map/ppermute | solution.py:49
  23.1 5.9 %collective-permute-start.5 = (bf16[128,512]{1,0:T(8,128)(2,1)S(1)}, bf16[128,512]{1,0:T(8,128)(2,1)S(1)}, u32[]{:S(2)}, u32[]{:S(2)}) collective-permute-start(bf16[128,512]{1,0:T(8,128)(2,1)S(1)} %get-tuple-element.57), channel_id=1, source_target_pairs={{0,2},{1,3},{2,0},{3,1},{4,6},{5,7},{6,4},{7,5},{8,10},{9,11},{10,... | collective-permute-start | bytes 393224 | tf_op jit(solution)/shard_map/ppermute | solution.py:49
  24.3 7.2 %collective-permute-start.6 = (bf16[128,512]{1,0:T(8,128)(2,1)S(1)}, bf16[128,512]{1,0:T(8,128)(2,1)S(1)}, u32[]{:S(2)}, u32[]{:S(2)}) collective-permute-start(bf16[128,512]{1,0:T(8,128)(2,1)S(1)} %get-tuple-element.56), channel_id=1, source_target_pairs={{0,4},{1,5},{2,6},{3,7},{4,0},{5,1},{6,2},{7,3},{8,12},{9,13},{10,... | collective-permute-start | bytes 393224 | tf_op jit(solution)/shard_map/ppermute | solution.py:49
  25.6 6.8 %copy-start.1 = (s32[128,4]{0,1:T(4,128)S(1)}, s32[128,4]{0,1:T(4,128)}, u32[]{:S(2)}) copy-start(s32[128,4]{0,1:T(4,128)} %param.19) | copy-start | bytes 6148
  25.6 6.8 %copy-start.2 = (f32[128,4]{0,1:T(4,128)S(1)}, f32[128,4]{0,1:T(4,128)}, u32[]{:S(2)}) copy-start(f32[128,4]{0,1:T(4,128)} %param.20) | copy-start | bytes 6148
  25.6 6.8 %copy-start.3 = (s32[128]{0:T(128)S(1)}, s32[128]{0:T(128)}, u32[]{:S(2)}) copy-start(s32[128]{0:T(128)} %param.13) | copy-start | bytes 1540
  25.6 6.9 %copy-start.6 = (bf16[1,768,1536]{2,1,0:T(8,128)(2,1)S(1)}, bf16[1,768,1536]{2,1,0:T(8,128)(2,1)}, u32[]{:S(2)}) copy-start(bf16[1,768,1536]{2,1,0:T(8,128)(2,1)} %param.23) | copy-start | bytes 7077892
  25.7 13.2 %copy-start = (bf16[1536,192]{0,1:T(8,128)(2,1)S(1)}, bf16[1536,192]{0,1:T(8,128)(2,1)}, u32[]{:S(2)}) copy-start(bf16[1536,192]{0,1:T(8,128)(2,1)} %param.17) | copy-start | bytes 1769476
  25.7 6.8 %collective-permute-start.7 = (bf16[128,512]{1,0:T(8,128)(2,1)S(1)}, bf16[128,512]{1,0:T(8,128)(2,1)S(1)}, u32[]{:S(2)}, u32[]{:S(2)}) collective-permute-start(bf16[128,512]{1,0:T(8,128)(2,1)S(1)} %get-tuple-element.54), channel_id=1, source_target_pairs={{0,6},{1,7},{2,4},{3,5},{4,2},{5,3},{6,0},{7,1},{8,14},{9,15},{10,... | collective-permute-start | bytes 393224 | tf_op jit(solution)/shard_map/ppermute | solution.py:49
  32.6 25.0 %collective-permute-start.15 = (bf16[768,1536]{1,0:T(8,128)(2,1)S(1)}, bf16[768,1536]{1,0:T(8,128)(2,1)S(1)}, u32[]{:S(2)}, u32[]{:S(2)}) collective-permute-start(bf16[768,1536]{1,0:T(8,128)(2,1)S(1)} %bitcast.29), channel_id=1, source_target_pairs={{0,1},{1,0},{2,3},{3,2},{4,5},{5,4},{6,7},{7,6},{8,9},{9,8},{10,11... | collective-permute-start | bytes 7077896 | tf_op jit(solution)/shard_map/ppermute | solution.py:49
  32.7 6.2 %collective-permute-start.17 = (bf16[128,512]{1,0:T(8,128)(2,1)S(1)}, bf16[128,512]{1,0:T(8,128)(2,1)S(1)}, u32[]{:S(2)}, u32[]{:S(2)}) collective-permute-start(bf16[128,512]{1,0:T(8,128)(2,1)S(1)} %get-tuple-element.52), channel_id=1, source_target_pairs={{6,4},{7,5},{14,12},{15,13},{22,20},{23,21},{30,28},{31,29}} | collective-permute-start | bytes 393224 | tf_op jit(solution)/shard_map/ppermute | solution.py:511
  33.4 6.7 %collective-permute-start.18 = (bf16[128,512]{1,0:T(8,128)(2,1)S(1)}, bf16[128,512]{1,0:T(8,128)(2,1)S(1)}, u32[]{:S(2)}, u32[]{:S(2)}) collective-permute-start(bf16[128,512]{1,0:T(8,128)(2,1)S(1)} %get-tuple-element.51), channel_id=1, source_target_pairs={{6,2},{7,3},{14,10},{15,11},{22,18},{23,19},{30,26},{31,27}} | collective-permute-start | bytes 393224 | tf_op jit(solution)/shard_map/ppermute | solution.py:511
  34.0 10.3 %collective-permute-start.19 = (bf16[128,512]{1,0:T(8,128)(2,1)S(1)}, bf16[128,512]{1,0:T(8,128)(2,1)S(1)}, u32[]{:S(2)}, u32[]{:S(2)}) collective-permute-start(bf16[128,512]{1,0:T(8,128)(2,1)S(1)} %get-tuple-element.50), channel_id=1, source_target_pairs={{6,0},{7,1},{14,8},{15,9},{22,16},{23,17},{30,24},{31,25}} | collective-permute-start | bytes 393224 | tf_op jit(solution)/shard_map/ppermute | solution.py:511
  35.3 9.7 %collective-permute-start.12 = (bf16[144,512]{1,0:T(8,128)(2,1)S(1)}, bf16[144,512]{1,0:T(8,128)(2,1)S(1)}, u32[]{:S(2)}, u32[]{:S(2)}) collective-permute-start(bf16[144,512]{1,0:T(8,128)(2,1)S(1)} %pack_kv.1.own.refs_4_.refs_2_), channel_id=1, source_target_pairs={{0,8},{8,16},{16,24},{1,9},{9,17},{17,25},{2,10},{10,18},{18,26},{... | collective-permute-start | bytes 442376 | tf_op jit(solution)/shard_map/ppermute | solution.py:506
  38.8 18.7 %collective-permute-start.13 = (bf16[192,1536]{1,0:T(8,128)(2,1)S(1)}, bf16[192,1536]{1,0:T(8,128)(2,1)S(1)}, u32[]{:S(2)}, u32[]{:S(2)}) collective-permute-start(bf16[192,1536]{1,0:T(8,128)(2,1)S(1)} %bitcast.16), channel_id=1, source_target_pairs={{0,2},{1,3},{2,0},{3,1},{4,6},{5,7},{6,4},{7,5},{8,10},{9,11},{10,... | collective-permute-start | bytes 1769480 | tf_op jit(solution)/shard_map/ppermute | solution.py:49
  40.0 17.5 %collective-permute-start.14 = (bf16[192,1536]{1,0:T(8,128)(2,1)S(1)}, bf16[192,1536]{1,0:T(8,128)(2,1)S(1)}, u32[]{:S(2)}, u32[]{:S(2)}) collective-permute-start(bf16[192,1536]{1,0:T(8,128)(2,1)S(1)} %bitcast.17), channel_id=1, source_target_pairs={{0,4},{1,5},{2,6},{3,7},{4,0},{5,1},{6,2},{7,3},{8,12},{9,13},{10,... | collective-permute-start | bytes 1769480 | tf_op jit(solution)/shard_map/ppermute | solution.py:49
  44.4 13.2 %collective-permute-start.16 = (bf16[192,1536]{1,0:T(8,128)(2,1)S(1)}, bf16[192,1536]{1,0:T(8,128)(2,1)S(1)}, u32[]{:S(2)}, u32[]{:S(2)}) collective-permute-start(bf16[192,1536]{1,0:T(8,128)(2,1)S(1)} %bitcast.18), channel_id=1, source_target_pairs={{0,1},{1,0},{2,3},{3,2},{4,5},{5,4},{6,7},{7,6},{8,9},{9,8},{10,11... | collective-permute-start | bytes 1769480 | tf_op jit(solution)/shard_map/ppermute | solution.py:49
  45.0 19.4 %collective-permute-start.23 = (bf16[144,512]{1,0:T(8,128)(2,1)S(1)}, bf16[144,512]{1,0:T(8,128)(2,1)S(1)}, u32[]{:S(2)}, u32[]{:S(2)}) collective-permute-start(bf16[144,512]{1,0:T(8,128)(2,1)S(1)} %pack_kv.1.own.refs_4_.refs_2_), channel_id=1, source_target_pairs={{0,1},{1,0},{2,3},{3,2},{4,5},{5,4},{6,7},{7,6},{8,9},{9,8},{10,11... | collective-permute-start | bytes 442376 | tf_op jit(solution)/shard_map/ppermute | solution.py:49
  57.5 7.5 %collective-permute-start.27 = (bf16[144,512]{1,0:T(8,128)(2,1)S(1)}, bf16[144,512]{1,0:T(8,128)(2,1)S(1)}, u32[]{:S(2)}, u32[]{:S(2)}) collective-permute-start(bf16[144,512]{1,0:T(8,128)(2,1)S(1)} %collective-permute-done.12.prev.refs_8_), channel_id=1, source_target_pairs={{0,1},{1,0},{2,3},{3,2},{4,5},{5,4},{6,7},{7,6},{8,9},{9,8},{10,11... | collective-permute-start | bytes 442376 | tf_op jit(solution)/shard_map/ppermute | solution.py:49
  57.6 6.7 %collective-permute-start.20 = (bf16[144,512]{1,0:T(8,128)(2,1)S(1)}, bf16[144,512]{1,0:T(8,128)(2,1)S(1)}, u32[]{:S(2)}, u32[]{:S(2)}) collective-permute-start(bf16[144,512]{1,0:T(8,128)(2,1)S(1)} %get-tuple-element.35.refs_0_), channel_id=1, source_target_pairs={{0,2},{1,3},{2,0},{3,1},{4,6},{5,7},{6,4},{7,5},{8,10},{9,11},{10,... | collective-permute-start | bytes 442376 | tf_op jit(solution)/shard_map/ppermute | solution.py:49
  58.5 8.0 %collective-permute-start.21 = (bf16[144,512]{1,0:T(8,128)(2,1)S(1)}, bf16[144,512]{1,0:T(8,128)(2,1)S(1)}, u32[]{:S(2)}, u32[]{:S(2)}) collective-permute-start(bf16[144,512]{1,0:T(8,128)(2,1)S(1)} %get-tuple-element.36.refs_1_), channel_id=1, source_target_pairs={{0,4},{1,5},{2,6},{3,7},{4,0},{5,1},{6,2},{7,3},{8,12},{9,13},{10,... | collective-permute-start | bytes 442376 | tf_op jit(solution)/shard_map/ppermute | solution.py:49
  59.8 9.1 %collective-permute-start.22 = (bf16[144,512]{1,0:T(8,128)(2,1)S(1)}, bf16[144,512]{1,0:T(8,128)(2,1)S(1)}, u32[]{:S(2)}, u32[]{:S(2)}) collective-permute-start(bf16[144,512]{1,0:T(8,128)(2,1)S(1)} %get-tuple-element.37.refs_2_), channel_id=1, source_target_pairs={{0,6},{1,7},{2,4},{3,5},{4,2},{5,3},{6,0},{7,1},{8,14},{9,15},{10,... | collective-permute-start | bytes 442376 | tf_op jit(solution)/shard_map/ppermute | solution.py:49
  64.4 6.3 %collective-permute-start.24 = (bf16[144,512]{1,0:T(8,128)(2,1)S(1)}, bf16[144,512]{1,0:T(8,128)(2,1)S(1)}, u32[]{:S(2)}, u32[]{:S(2)}) collective-permute-start(bf16[144,512]{1,0:T(8,128)(2,1)S(1)} %collective-permute-done.20.refs_5_.refs_2_), channel_id=1, source_target_pairs={{0,1},{1,0},{2,3},{3,2},{4,5},{5,4},{6,7},{7,6},{8,9},{9,8},{10,11... | collective-permute-start | bytes 442376 | tf_op jit(solution)/shard_map/ppermute | solution.py:49
  64.4 9.0 %collective-permute-start.28 = (bf16[192,1536]{1,0:T(8,128)(2,1)S(1)}, bf16[192,1536]{1,0:T(8,128)(2,1)S(1)}, u32[]{:S(2)}, u32[]{:S(2)}) collective-permute-start(bf16[192,1536]{1,0:T(8,128)(2,1)S(1)} %collective-permute-done.13.refs_1_), channel_id=1, source_target_pairs={{0,1},{1,0},{2,3},{3,2},{4,5},{5,4},{6,7},{7,6},{8,9},{9,8},{10,11... | collective-permute-start | bytes 1769480 | tf_op jit(solution)/shard_map/ppermute | solution.py:49
  65.0 8.4 %collective-permute-start.29 = (bf16[192,1536]{1,0:T(8,128)(2,1)S(1)}, bf16[192,1536]{1,0:T(8,128)(2,1)S(1)}, u32[]{:S(2)}, u32[]{:S(2)}) collective-permute-start(bf16[192,1536]{1,0:T(8,128)(2,1)S(1)} %collective-permute-done.14.refs_2_), channel_id=1, source_target_pairs={{0,1},{1,0},{2,3},{3,2},{4,5},{5,4},{6,7},{7,6},{8,9},{9,8},{10,11... | collective-permute-start | bytes 1769480 | tf_op jit(solution)/shard_map/ppermute | solution.py:49
  66.5 8.8 %collective-permute-start.30 = (bf16[96,1536]{1,0:T(8,128)(2,1)S(1)}, bf16[96,1536]{1,0:T(8,128)(2,1)S(1)}, u32[]{:S(2)}, u32[]{:S(2)}) collective-permute-start(bf16[96,1536]{1,0:T(8,128)(2,1)S(1)} %hold.5), channel_id=1, source_target_pairs={{0,2},{1,3},{2,0},{3,1},{4,6},{5,7},{6,4},{7,5},{8,10},{9,11},{10,... | collective-permute-start | bytes 884744 | tf_op jit(solution)/shard_map/ppermute | solution.py:49
  68.9 8.1 %collective-permute-start.31 = (bf16[96,1536]{1,0:T(8,128)(2,1)S(1)}, bf16[96,1536]{1,0:T(8,128)(2,1)S(1)}, u32[]{:S(2)}, u32[]{:S(2)}) collective-permute-start(bf16[96,1536]{1,0:T(8,128)(2,1)S(1)} %hold.6), channel_id=1, source_target_pairs={{0,4},{1,5},{2,6},{3,7},{4,0},{5,1},{6,2},{7,3},{8,12},{9,13},{10,... | collective-permute-start | bytes 884744 | tf_op jit(solution)/shard_map/ppermute | solution.py:49
  70.6 1.4 %collective-permute-start.25 = (bf16[144,512]{1,0:T(8,128)(2,1)S(1)}, bf16[144,512]{1,0:T(8,128)(2,1)S(1)}, u32[]{:S(2)}, u32[]{:S(2)}) collective-permute-start(bf16[144,512]{1,0:T(8,128)(2,1)S(1)} %collective-permute-done.21.refs_6_.refs_3_), channel_id=1, source_target_pairs={{0,1},{1,0},{2,3},{3,2},{4,5},{5,4},{6,7},{7,6},{8,9},{9,8},{10,11... | collective-permute-start | bytes 442376 | tf_op jit(solution)/shard_map/ppermute | solution.py:49
  72.0 1.4 %collective-permute-start.26 = (bf16[144,512]{1,0:T(8,128)(2,1)S(1)}, bf16[144,512]{1,0:T(8,128)(2,1)S(1)}, u32[]{:S(2)}, u32[]{:S(2)}) collective-permute-start(bf16[144,512]{1,0:T(8,128)(2,1)S(1)} %hold.4.refs_7_.refs_3_), channel_id=1, source_target_pairs={{0,1},{1,0},{2,3},{3,2},{4,5},{5,4},{6,7},{7,6},{8,9},{9,8},{10,11... | collective-permute-start | bytes 442376 | tf_op jit(solution)/shard_map/ppermute | solution.py:49
  75.2 14.7 %copy-start.4 = (bf16[1,1536,768]{2,1,0:T(8,128)(2,1)S(1)}, bf16[1,1536,768]{2,1,0:T(8,128)(2,1)}, u32[]{:S(2)}) copy-start(bf16[1,1536,768]{2,1,0:T(8,128)(2,1)} %param.21) | copy-start | bytes 7077892
  75.3 14.7 %copy-start.5 = (bf16[1,1536,768]{2,1,0:T(8,128)(2,1)S(1)}, bf16[1,1536,768]{2,1,0:T(8,128)(2,1)}, u32[]{:S(2)}) copy-start(bf16[1,1536,768]{2,1,0:T(8,128)(2,1)} %param.22) | copy-start | bytes 7077892
  75.3 14.7 %copy-start.11 = (f32[1536]{0:T(1024)S(1)}, f32[1536]{0:T(1024)}, u32[]{:S(2)}) copy-start(f32[1536]{0:T(1024)} %refs_5_.3) | copy-start | bytes 18436
  77.0 13.0 %collective-permute-start.32 = (bf16[128,1536]{1,0:T(8,128)(2,1)S(1)}, bf16[128,1536]{1,0:T(8,128)(2,1)S(1)}, u32[]{:S(2)}, u32[]{:S(2)}) collective-permute-start(bf16[128,1536]{1,0:T(8,128)(2,1)S(1)} %attend.1.refs_0_), channel_id=1, source_target_pairs={{0,6},{1,7},{2,4},{3,5},{4,2},{5,3},{6,0},{7,1},{8,14},{9,15},{10,... | collective-permute-start | bytes 1179656 | tf_op jit(solution)/shard_map/ppermute | solution.py:49
  78.4 2.6 %collective-permute-start.33 = (bf16[96,1536]{1,0:T(8,128)(2,1)S(1)}, bf16[96,1536]{1,0:T(8,128)(2,1)S(1)}, u32[]{:S(2)}, u32[]{:S(2)}) collective-permute-start(bf16[96,1536]{1,0:T(8,128)(2,1)S(1)} %collective-permute-done.30.refs_3_), channel_id=1, source_target_pairs={{0,1},{1,0},{2,3},{3,2},{4,5},{5,4},{6,7},{7,6},{8,9},{9,8},{10,11... | collective-permute-start | bytes 884744 | tf_op jit(solution)/shard_map/ppermute | solution.py:49
  78.4 2.6 %collective-permute-start.34 = (bf16[96,1536]{1,0:T(8,128)(2,1)S(1)}, bf16[96,1536]{1,0:T(8,128)(2,1)S(1)}, u32[]{:S(2)}, u32[]{:S(2)}) collective-permute-start(bf16[96,1536]{1,0:T(8,128)(2,1)S(1)} %collective-permute-done.31.refs_4_), channel_id=1, source_target_pairs={{0,1},{1,0},{2,3},{3,2},{4,5},{5,4},{6,7},{7,6},{8,9},{9,8},{10,11... | collective-permute-start | bytes 884744 | tf_op jit(solution)/shard_map/ppermute | solution.py:49
  78.9 19.0 %collective-permute-start.35 = (bf16[128,1536]{1,0:T(8,128)(2,1)S(1)}, bf16[128,1536]{1,0:T(8,128)(2,1)S(1)}, u32[]{:S(2)}, u32[]{:S(2)}) collective-permute-start(bf16[128,1536]{1,0:T(8,128)(2,1)S(1)} %attend.1.refs_0_), channel_id=1, source_target_pairs={{0,2},{1,3},{2,0},{3,1},{4,6},{5,7},{6,4},{7,5},{8,10},{9,11},{10,... | collective-permute-start | bytes 1179656 | tf_op jit(solution)/shard_map/ppermute | solution.py:49
  80.6 17.3 %collective-permute-start.36 = (bf16[128,1536]{1,0:T(8,128)(2,1)S(1)}, bf16[128,1536]{1,0:T(8,128)(2,1)S(1)}, u32[]{:S(2)}, u32[]{:S(2)}) collective-permute-start(bf16[128,1536]{1,0:T(8,128)(2,1)S(1)} %attend.1.refs_0_), channel_id=1, source_target_pairs={{0,4},{1,5},{2,6},{3,7},{4,0},{5,1},{6,2},{7,3},{8,12},{9,13},{10,... | collective-permute-start | bytes 1179656 | tf_op jit(solution)/shard_map/ppermute | solution.py:49
  95.4 9.6 %collective-permute-start.39 = (bf16[128,1536]{1,0:T(8,128)(2,1)S(1)}, bf16[128,1536]{1,0:T(8,128)(2,1)S(1)}, u32[]{:S(2)}, u32[]{:S(2)}) collective-permute-start(bf16[128,1536]{1,0:T(8,128)(2,1)S(1)} %get-tuple-element.47.refs_14_), channel_id=1, source_target_pairs={{0,6},{1,7},{2,4},{3,5},{4,2},{5,3},{6,0},{7,1},{8,14},{9,15},{10,... | collective-permute-start | bytes 1179656 | tf_op jit(solution)/shard_map/ppermute | solution.py:49
  103.2 10.7 %collective-permute-start.37 = (bf16[128,1536]{1,0:T(8,128)(2,1)S(1)}, bf16[128,1536]{1,0:T(8,128)(2,1)S(1)}, u32[]{:S(2)}, u32[]{:S(2)}) collective-permute-start(bf16[128,1536]{1,0:T(8,128)(2,1)S(1)} %get-tuple-element.48), channel_id=1, source_target_pairs={{0,2},{1,3},{2,0},{3,1},{4,6},{5,7},{6,4},{7,5},{8,10},{9,11},{10,... | collective-permute-start | bytes 1179656 | tf_op jit(solution)/shard_map/ppermute | solution.py:49
  104.0 10.0 %collective-permute-start.38 = (bf16[128,1536]{1,0:T(8,128)(2,1)S(1)}, bf16[128,1536]{1,0:T(8,128)(2,1)S(1)}, u32[]{:S(2)}, u32[]{:S(2)}) collective-permute-start(bf16[128,1536]{1,0:T(8,128)(2,1)S(1)} %get-tuple-element.49), channel_id=1, source_target_pairs={{0,4},{1,5},{2,6},{3,7},{4,0},{5,1},{6,2},{7,3},{8,12},{9,13},{10,... | collective-permute-start | bytes 1179656 | tf_op jit(solution)/shard_map/ppermute | solution.py:49

commit v4 on v3

--- a/solution.py
+++ b/solution.py
@@ -306,15 +306,18 @@
     )(*same, *other)
 
 
-def expert_kernel(tile, count, *refs):
-    context, tables, (w_ref, gain_ref), held = refs[:2], refs[2:4], refs[4:6], refs[6:12]
-    tokens, outs, (rows_ref, hidden_ref, total_ref) = refs[12 : 12 + count], refs[-5:-3], refs[-3:]
+def expert_kernel(tile, pieces, count, *refs):
+    tables, (w_ref, gain_ref), held = refs[:2], refs[2:4], refs[4:10]
+    context, tokens = refs[10 : 10 + pieces], refs[10 + pieces : 10 + pieces + count]
+    outs, (rows_ref, hidden_ref, total_ref) = refs[-5:-3], refs[-3:]
     chip, core = place()
-    rows, width = context[0].shape
+    rows, width = outs[0].shape
     hidden = hidden_ref.shape[1]
     spans = [slice(i * rows, (i + 1) * rows) for i in range(2)]
-    for span, piece in zip(spans, context):
-        rows_ref[span, :] = piece[...]
+    at = 0
+    for piece in context:
+        rows_ref[at : at + piece.shape[0], :] = piece[...]
+        at += piece.shape[0]
     added = lax.dot_general(
         rows_ref[...], w_ref[...], (((1,), (1,)), ((), ())), preferred_element_type=jnp.float32
     )
@@ -363,9 +366,9 @@
     rows, width = tokens[0].shape
     hidden = weights[0].shape[1]
     return pl.pallas_call(
-        functools.partial(expert_kernel, 256, len(tokens)),
+        functools.partial(expert_kernel, 256, len(context), len(tokens)),
         out_shape=tuple(jax.ShapeDtypeStruct((rows, width), kind) for kind in kinds),
-        in_specs=[vmem()] * (12 + len(tokens)) + [anywhere()] * len(earlier),
+        in_specs=[vmem()] * (10 + len(context) + len(tokens)) + [anywhere()] * len(earlier),
         out_specs=(vmem(), vmem()),
         scratch_shapes=[
             pltpu.VMEM((2 * rows, width), jnp.bfloat16),
@@ -375,7 +378,7 @@
         cost_estimate=LONG,
         compiler_params=params(32),
         name="experts",
-    )(*context, *tables, w_all, gain, *weights, *tokens, *earlier)
+    )(*tables, w_all, gain, *weights, *context, *tokens, *earlier)
 
 
 def mix_kernel(own, by_x, by_y, by_xy, out_ref):
@@ -452,7 +455,6 @@
         out_shape=jax.ShapeDtypeStruct(pieces[0].shape, pieces[0].dtype),
         in_specs=[vmem()] * CHIPS,
         out_specs=vmem(),
-        cost_estimate=LONG,
         compiler_params=params(16),
         name="join_pages",
     )(*pieces)
@@ -504,18 +506,11 @@
         after(projected, (paged, gate_other, up_other)), segment_ids, route_ids, route_weight
     )
     prev_kv = lax.ppermute(own_kv, "seq", [(i, i + 1) for i in range(seq_size - 1)])
-    last = CHIPS - 1
-    pages = [paged[last]]
-    for by in (1, 2, 3):
-        pairs = [(last * CORES + k, (last ^ by) * CORES + k) for k in range(CORES)]
-        pages.append(lax.ppermute(paged[last ^ by], "tensor", pairs))
-    pages = join_call(pages)
     w_going, down_going = after((w_own, down), own_kv)
     w_x, w_y = chips(w_going, 1), chips(w_going, 2)
     down_other, w_own_other = hop(down_going, 1), hop(w_going, 1)
 
-    done = (w_x, w_y, down_other, w_own_other, pages)
-    sent = choose_call(own_kv, after(prev_kv, done))
+    sent = choose_call(own_kv, after(prev_kv, (w_x, w_y, down_other, w_own_other)))
     kv_xy, kv_x, kv_y = chips(sent[2], 3), chips(sent[0], 1), chips(sent[1], 2)
     kv_xy = hold_call(kv_xy)
     half = w_own.shape[0] // 2
@@ -526,21 +521,29 @@
     w_other = [w_own_other] + [hop(after(w, sent), 1) for w in (w_x, w_y)]
     windows_other = after(windows_other, (w_other, w_relayed))
     context = after(attend_call(projected, windows + windows_other), w_diagonal)
-    context_xy, context_x, context_y = chips(context, 3), chips(context, 1), chips(context, 2)
+    context_x, context_y = chips(context, 1), chips(context, 2)
+    context_xy = [chips(context_y[: rows // 2], 1), chips(context_x[rows // 2 :], 2)]
+    last = CHIPS - 1
+    paged = after(paged, (context_x, context_y))
+    pages = [paged[last]]
+    for by in (1, 2, 3):
+        pairs = [(last * CORES + k, (last ^ by) * CORES + k) for k in range(CORES)]
+        pages.append(lax.ppermute(paged[last ^ by], "tensor", pairs))
+    pages = join_call(pages)
     w_other += [hop(w, 1) for w in w_diagonal]
     w_all = assemble_call([w_own, w_x, w_y] + w_diagonal, w_other)
 
     weights = [gate, up, down, gate_other, up_other, down_other]
-    out, out_xy = expert_call(
-        (context, context_xy), (tokens, *tokens_xy), (own_kv, kv_xy), w_all, moe_gain, weights,
-        (jnp.float32, jnp.bfloat16),
-    )
-    back_xy = hold_call(chips(out_xy, 3))
     out_x, out_y = expert_call(
         (context_x, context_y), (tokens_x, tokens_y), (kv_x, kv_y), w_all, moe_gain, weights,
-        (jnp.bfloat16, jnp.bfloat16), out_xy,
-    )
-    back_x, back_y = chips(out_x, 1), chips(out_y, 2)
+        (jnp.bfloat16, jnp.bfloat16),
+    )
+    back_x, back_y = hold_call(chips(out_x, 1)), hold_call(chips(out_y, 2))
+    out, out_xy = expert_call(
+        (context, *context_xy), (tokens, *tokens_xy), (own_kv, kv_xy), w_all, moe_gain, weights,
+        (jnp.float32, jnp.bfloat16), out_x, pages,
+    )
+    back_xy = chips(out_xy, 3)
     mixed = mix_call((out, back_x, back_y, back_xy))
     return (mixed, pages.reshape(rows // PAGE, PAGE, pages.shape[1]))
 

time: 115 us -> 113 us (0.983)
  starting transfers between devices: 40.1 us -> 38 us
  waiting for transfers between devices: 53.6 us -> 52.4 us
    ppermute x36 -> x37, waiting for transfers between devices: 53.5 us -> 48.6 us  [hop(): return lax.ppermute(value, 'tensor', [(i, i ^ by) for i in range(length)])]
    ppermute x1, waiting for transfers between devices: 0.01 us -> 3.75 us  [chip_body(): lax.ppermute(own_kv, 'seq', [(i, i + 1) for i in range(seq_size - 1)])]
    ppermute x36 -> x37, starting transfers between devices: 34 us -> 31.7 us  [hop(): return lax.ppermute(value, 'tensor', [(i, i ^ by) for i in range(length)])]
    unnamed x26 -> x28, local copies, waits for them, and re-layouts: 1.88 us -> 2.79 us
  transfers between devices with their start and end apart: 40 -> 41, of which waited for: 15 -> 21; matrix products, arithmetic and copies ran while one was open for 0% -> 0% of each run, Pallas kernels for 15% -> 15%
where the time goes in v4:
time: 113 us; the launch traced here: 112 us
  waiting for transfers between devices  52.4 us (46%)
  starting transfers between devices  38 us (34%)
  Pallas kernels  18.1 us (16%)
  local copies, waits for them, and re-layouts  2.96 us (3%)
    ppermute x37, waiting for transfers between devices, hop(): return lax.ppermute(value, 'tensor', [(i, i ^ by) for i in range(length)])  48.6 us
    ppermute x37, starting transfers between devices, hop(): return lax.ppermute(value, 'tensor', [(i, i ^ by) for i in range(length)])  31.7 us
    pallas_call x2, Pallas kernels, expert_call(): pl.pallas_call(functools.partial(expert_kernel, 256, len(context), len(to...  10.7 us
    ppermute x1, waiting for transfers between devices, chip_body(): lax.ppermute(own_kv, 'seq', [(i, i + 1) for i in range(seq_size - 1)])  3.75 us
    ppermute x1, starting transfers between devices, chip_body(): lax.ppermute(own_kv, 'seq', [(i, i + 1) for i in range(seq_size - 1)])  3.46 us
    ppermute x3, starting transfers between devices, chip_body(): pages.append(lax.ppermute(paged[last ^ by], 'tensor', pairs))  2.81 us
    unnamed x28, local copies, waits for them, and re-layouts  2.79 us
  transfers between devices with their start and end apart: 41, of which 21 were waited for; matrix products, arithmetic and copies ran while one was open for 0% of the time, Pallas kernels for 15%

profile of v4, /device:TPU:0, one launch (start us, length us, event | category | flops | bytes accessed | tf_op | source)
XLA Modules:
  0.0 112.4 jit_solution(6827234099854873576)
XLA Ops:
  0.6 0.5 collective-permute-start.4
  1.1 2.6 %collective-permute-start.2 = (bf16[128,1536]{1,0:T(8,128)(2,1)}, bf16[128,1536]{1,0:T(8,128)(2,1)S(1)}, u32[]{:S(2)}, u32[]{:S(2)}) collective-permute-start(bf16[128,1536]{1,0:T(8,128)(2,1)} %refs_13_.1), channel_id=1, source_target_pairs={{0,2},{1,3},{2,0},{3,1},{4,6},{5,7},{6,4},{7,5},{8,10},{9,11},{10,... | collective-permute-start | bytes 1179656 | tf_op jit(solution)/shard_map/ppermute | solution.py:49
  3.7 1.5 %collective-permute-start = (bf16[128,1536]{1,0:T(8,128)(2,1)}, bf16[128,1536]{1,0:T(8,128)(2,1)S(1)}, u32[]{:S(2)}, u32[]{:S(2)}) collective-permute-start(bf16[128,1536]{1,0:T(8,128)(2,1)} %refs_13_.1), channel_id=1, source_target_pairs={{0,4},{1,5},{2,6},{3,7},{4,0},{5,1},{6,2},{7,3},{8,12},{9,13},{10,... | collective-permute-start | bytes 1179656 | tf_op jit(solution)/shard_map/ppermute | solution.py:49
  5.2 8.4 %collective-permute-done.2.refs_0_.refs_12_ = bf16[128,1536]{1,0:T(8,128)(2,1)S(1)} collective-permute-done((bf16[128,1536]{1,0:T(8,128)(2,1)}, bf16[128,1536]{1,0:T(8,128)(2,1)S(1)}, u32[]{:S(2)}, u32[]{:S(2)}) %collective-permute-start.2) | collective-permute-done | bytes 393248 | tf_op jit(solution)/shard_map/ppermute | solution.py:49
  13.6 1.9 %collective-permute-start.3 = (bf16[64,1536]{1,0:T(8,128)(2,1)S(1)}, bf16[64,1536]{1,0:T(8,128)(2,1)S(1)}, u32[]{:S(2)}, u32[]{:S(2)}) collective-permute-start(bf16[64,1536]{1,0:T(8,128)(2,1)S(1)} %slice.57), channel_id=1, source_target_pairs={{0,4},{1,5},{2,6},{3,7},{4,0},{5,1},{6,2},{7,3},{8,12},{9,13},{10,... | collective-permute-start | bytes 589832 | tf_op jit(solution)/shard_map/ppermute | solution.py:49
  15.5 1.6 %collective-permute-start.1 = (bf16[64,1536]{1,0:T(8,128)(2,1)S(1)}, bf16[64,1536]{1,0:T(8,128)(2,1)S(1)}, u32[]{:S(2)}, u32[]{:S(2)}) collective-permute-start(bf16[64,1536]{1,0:T(8,128)(2,1)S(1)} %slice.56), channel_id=1, source_target_pairs={{0,2},{1,3},{2,0},{3,1},{4,6},{5,7},{6,4},{7,5},{8,10},{9,11},{10,... | collective-permute-start | bytes 589832 | tf_op jit(solution)/shard_map/ppermute | solution.py:49
  17.1 1.1 %copy-done.8 = bf16[1536,256]{1,0:T(8,128)(2,1)S(1)} copy-done((bf16[1536,256]{1,0:T(8,128)(2,1)S(1)}, bf16[1536,256]{1,0:T(8,128)(2,1)}, u32[]{:S(2)}) %copy-start.8) | copy-done | bytes 786456
  18.2 0.7 copy-done.11
  18.9 0.7 project.2.refs_6_.refs_1_
  19.7 0.7 collective-permute-done.3.refs_2_.refs_15_
  20.4 1.4 %collective-permute-done.1.refs_1_.refs_14_ = bf16[64,1536]{1,0:T(8,128)(2,1)S(1)} collective-permute-done((bf16[64,1536]{1,0:T(8,128)(2,1)S(1)}, bf16[64,1536]{1,0:T(8,128)(2,1)S(1)}, u32[]{:S(2)}, u32[]{:S(2)}) %collective-permute-start.1) | collective-permute-done | bytes 196640 | tf_op jit(solution)/shard_map/ppermute | solution.py:49
  21.8 0.7 project.3.refs_0_
  22.5 0.1 collective-permute-start.8
  22.6 0.5 collective-permute-start.9
  23.1 1.5 %collective-permute-start.7 = (bf16[128,512]{1,0:T(8,128)(2,1)S(1)}, bf16[128,512]{1,0:T(8,128)(2,1)S(1)}, u32[]{:S(2)}, u32[]{:S(2)}) collective-permute-start(bf16[128,512]{1,0:T(8,128)(2,1)S(1)} %get-tuple-element.56), channel_id=1, source_target_pairs={{0,6},{1,7},{2,4},{3,5},{4,2},{5,3},{6,0},{7,1},{8,14},{9,15},{10,... | collective-permute-start | bytes 393224 | tf_op jit(solution)/shard_map/ppermute | solution.py:49
  24.6 1.4 %collective-permute-start.5 = (bf16[128,512]{1,0:T(8,128)(2,1)S(1)}, bf16[128,512]{1,0:T(8,128)(2,1)S(1)}, u32[]{:S(2)}, u32[]{:S(2)}) collective-permute-start(bf16[128,512]{1,0:T(8,128)(2,1)S(1)} %get-tuple-element.59), channel_id=1, source_target_pairs={{0,2},{1,3},{2,0},{3,1},{4,6},{5,7},{6,4},{7,5},{8,10},{9,11},{10,... | collective-permute-start | bytes 393224 | tf_op jit(solution)/shard_map/ppermute | solution.py:49
  26.0 0.8 collective-permute-start.6
  26.9 2.1 %cache_pages.1 = bf16[4,128,512]{2,1,0:T(8,128)(2,1)S(1)} custom-call(s32[1,64]{1,0:T(1,128)S(1)} %copy-done.13, bf16[256,512]{1,0:T(8,128)(2,1)S(1)} %project.3.refs_0_, bf16[256,512]{1,0:T(8,128)(2,1)S(1)} %project.2.refs_6_.refs_1_, bf16[256,512]{1,0:T(8,128)(2,1)S(1)} %collective-permute-done.8.refs_2_, bf16[256,512]{1,0:T(8,128)(2,1)S(1)} %collective-permute-done.9.refs_3_), custom_call_target="tpu_custom_call" | custom-call | flops 20000000000 | bytes 1 | tf_op jit(solution)/shard_map/cache_pages/pallas_call | solution.py:431
  28.9 1.5 %collective-permute-done.7.by_xy.refs_3_ = bf16[128,512]{1,0:T(8,128)(2,1)S(1)} collective-permute-done((bf16[128,512]{1,0:T(8,128)(2,1)S(1)}, bf16[128,512]{1,0:T(8,128)(2,1)S(1)}, u32[]{:S(2)}, u32[]{:S(2)}) %collective-permute-start.7) | collective-permute-done | bytes 131104 | tf_op jit(solution)/shard_map/ppermute | solution.py:49
  30.4 1.6 %collective-permute-done.5.by_x.refs_1_ = bf16[128,512]{1,0:T(8,128)(2,1)S(1)} collective-permute-done((bf16[128,512]{1,0:T(8,128)(2,1)S(1)}, bf16[128,512]{1,0:T(8,128)(2,1)S(1)}, u32[]{:S(2)}, u32[]{:S(2)}) %collective-permute-start.5) | collective-permute-done | bytes 131104 | tf_op jit(solution)/shard_map/ppermute | solution.py:49
  32.0 0.4 collective-permute-done.6.by_y.refs_2_
  32.6 1.6 %collective-permute-start.13 = (bf16[192,1536]{1,0:T(8,128)(2,1)S(1)}, bf16[192,1536]{1,0:T(8,128)(2,1)S(1)}, u32[]{:S(2)}, u32[]{:S(2)}) collective-permute-start(bf16[192,1536]{1,0:T(8,128)(2,1)S(1)} %bitcast.16), channel_id=1, source_target_pairs={{0,2},{1,3},{2,0},{3,1},{4,6},{5,7},{6,4},{7,5},{8,10},{9,11},{10,... | collective-permute-start | bytes 1769480 | tf_op jit(solution)/shard_map/ppermute | solution.py:49
  34.1 0.6 collective-permute-start.14
  34.7 3.5 %collective-permute-start.12 = (bf16[144,512]{1,0:T(8,128)(2,1)S(1)}, bf16[144,512]{1,0:T(8,128)(2,1)S(1)}, u32[]{:S(2)}, u32[]{:S(2)}) collective-permute-start(bf16[144,512]{1,0:T(8,128)(2,1)S(1)} %pack_kv.1.own.refs_4_.refs_0_), channel_id=1, source_target_pairs={{0,8},{8,16},{16,24},{1,9},{9,17},{17,25},{2,10},{10,18},{18,26},{... | collective-permute-start | bytes 442376 | tf_op jit(solution)/shard_map/ppermute | solution.py:508
  38.2 3.8 %collective-permute-done.12.prev.refs_8_ = bf16[144,512]{1,0:T(8,128)(2,1)S(1)} collective-permute-done((bf16[144,512]{1,0:T(8,128)(2,1)S(1)}, bf16[144,512]{1,0:T(8,128)(2,1)S(1)}, u32[]{:S(2)}, u32[]{:S(2)}) %collective-permute-start.12) | collective-permute-done | bytes 147488 | tf_op jit(solution)/shard_map/ppermute | solution.py:508
  41.9 6.4 %collective-permute-done.13.refs_1_ = bf16[192,1536]{1,0:T(8,128)(2,1)S(1)} collective-permute-done((bf16[192,1536]{1,0:T(8,128)(2,1)S(1)}, bf16[192,1536]{1,0:T(8,128)(2,1)S(1)}, u32[]{:S(2)}, u32[]{:S(2)}) %collective-permute-start.13) | collective-permute-done | bytes 589856 | tf_op jit(solution)/shard_map/ppermute | solution.py:49
  48.3 1.2 %collective-permute-done.14.refs_2_ = bf16[192,1536]{1,0:T(8,128)(2,1)S(1)} collective-permute-done((bf16[192,1536]{1,0:T(8,128)(2,1)S(1)}, bf16[192,1536]{1,0:T(8,128)(2,1)S(1)}, u32[]{:S(2)}, u32[]{:S(2)}) %collective-permute-start.14) | collective-permute-done | bytes 589856 | tf_op jit(solution)/shard_map/ppermute | solution.py:49
  49.6 1.1 collective-permute-start.17
  50.7 1.0 collective-permute-start.24
  51.7 1.5 %collective-permute-start.25 = (bf16[144,512]{1,0:T(8,128)(2,1)S(1)}, bf16[144,512]{1,0:T(8,128)(2,1)S(1)}, u32[]{:S(2)}, u32[]{:S(2)}) collective-permute-start(bf16[144,512]{1,0:T(8,128)(2,1)S(1)} %get-tuple-element.38.refs_1_), channel_id=1, source_target_pairs={{0,4},{1,5},{2,6},{3,7},{4,0},{5,1},{6,2},{7,3},{8,12},{9,13},{10,... | collective-permute-start | bytes 442376 | tf_op jit(solution)/shard_map/ppermute | solution.py:49
  53.2 4.1 %collective-permute-done.17.in_ref = bf16[144,512]{1,0:T(8,128)(2,1)S(1)} collective-permute-done((bf16[144,512]{1,0:T(8,128)(2,1)S(1)}, bf16[144,512]{1,0:T(8,128)(2,1)S(1)}, u32[]{:S(2)}, u32[]{:S(2)}) %collective-permute-start.17) | collective-permute-done | bytes 147488 | tf_op jit(solution)/shard_map/ppermute | solution.py:49
  57.3 0.6 collective-permute-start.20
  57.9 0.1 collective-permute-start.29
  58.0 0.5 collective-permute-done.24.refs_5_.refs_0_
  58.5 0.4 collective-permute-done.25.refs_6_.refs_1_
  58.9 1.1 collective-permute-start.19
  59.9 0.4 collective-permute-done.29.refs_12_
  60.3 0.7 collective-permute-start.18
  61.1 1.4 %collective-permute-done.28.refs_11_ = bf16[144,512]{1,0:T(8,128)(2,1)S(1)} collective-permute-done((bf16[144,512]{1,0:T(8,128)(2,1)S(1)}, bf16[144,512]{1,0:T(8,128)(2,1)S(1)}, u32[]{:S(2)}, u32[]{:S(2)}) %collective-permute-start.28) | collective-permute-done | bytes 147488 | tf_op jit(solution)/shard_map/ppermute | solution.py:49
  62.4 1.7 %attend.1.refs_10_ = bf16[128,1536]{1,0:T(8,128)(2,1)S(1)} custom-call(bf16[128,512]{1,0:T(8,128)(2,1)S(1)} %get-tuple-element.29.own.refs_0_, bf16[128,512]{1,0:T(8,128)(2,1)S(1)} %collective-permute-done.5.by_x.refs_1_, bf16[128,512]{1,0:T(8,128)(2,1)S(1)} %collective-permute-done.6.by_y.refs_2_, ...), custom_call_target="tpu_custom_call" | custom-call | tf_op jit(solution)/shard_map/attend/pallas_call | solution.py:267
  64.2 3.8 %collective-permute-done.19.refs_4_ = bf16[96,1536]{1,0:T(8,128)(2,1)S(1)} collective-permute-done((bf16[96,1536]{1,0:T(8,128)(2,1)S(1)}, bf16[96,1536]{1,0:T(8,128)(2,1)S(1)}, u32[]{:S(2)}, u32[]{:S(2)}) %collective-permute-start.19) | collective-permute-done | bytes 294944 | tf_op jit(solution)/shard_map/ppermute | solution.py:49
  68.0 1.4 %collective-permute-done.18.refs_3_ = bf16[96,1536]{1,0:T(8,128)(2,1)S(1)} collective-permute-done((bf16[96,1536]{1,0:T(8,128)(2,1)S(1)}, bf16[96,1536]{1,0:T(8,128)(2,1)S(1)}, u32[]{:S(2)}, u32[]{:S(2)}) %collective-permute-start.18) | collective-permute-done | bytes 294944 | tf_op jit(solution)/shard_map/ppermute | solution.py:49
  69.4 0.6 collective-permute-start.31
  70.0 1.0 collective-permute-start.33
  71.1 0.5 collective-permute-start.22
  71.6 1.1 collective-permute-done.23.refs_9_
  72.6 0.4 collective-permute-done.22.refs_8_
  73.1 0.3 assemble_w_out.1.refs_2_
  73.4 6.3 %collective-permute-done.31.refs_11_ = bf16[128,1536]{1,0:T(8,128)(2,1)S(1)} collective-permute-done((bf16[128,1536]{1,0:T(8,128)(2,1)S(1)}, bf16[128,1536]{1,0:T(8,128)(2,1)S(1)}, u32[]{:S(2)}, u32[]{:S(2)}) %collective-permute-start.31) | collective-permute-done | bytes 393248 | tf_op jit(solution)/shard_map/ppermute | solution.py:49
  79.7 0.4 collective-permute-done.33.refs_10_
  80.1 0.7 collective-permute-start.35
  80.8 0.7 collective-permute-start.36
  81.5 1.5 %collective-permute-start.37 = (bf16[128,512]{1,0:T(8,128)(2,1)S(1)}, bf16[128,512]{1,0:T(8,128)(2,1)S(1)}, u32[]{:S(2)}, u32[]{:S(2)}) collective-permute-start(bf16[128,512]{1,0:T(8,128)(2,1)S(1)} %get-tuple-element.52), channel_id=1, source_target_pairs={{6,0},{7,1},{14,8},{15,9},{22,16},{23,17},{30,24},{31,25}} | collective-permute-start | bytes 393224 | tf_op jit(solution)/shard_map/ppermute | solution.py:531
  83.0 0.9 collective-permute-start.32
  83.9 4.5 %collective-permute-start.34 = (bf16[64,1536]{1,0:T(8,128)(2,1)S(1)}, bf16[64,1536]{1,0:T(8,128)(2,1)S(1)}, u32[]{:S(2)}, u32[]{:S(2)}) collective-permute-start(bf16[64,1536]{1,0:T(8,128)(2,1)S(1)} %slice.65), channel_id=1, source_target_pairs={{0,4},{1,5},{2,6},{3,7},{4,0},{5,1},{6,2},{7,3},{8,12},{9,13},{10,... | collective-permute-start | bytes 589832 | tf_op jit(solution)/shard_map/ppermute | solution.py:49
  88.4 5.3 %experts.2 = (bf16[128,1536]{1,0:T(8,128)(2,1)S(1)}, bf16[128,1536]{1,0:T(8,128)(2,1)S(1)}) custom-call(bf16[144,512]{1,0:T(8,128)(2,1)S(1)} %collective-permute-done.24.refs_5_.refs_0_, bf16[144,512]{1,0:T(8,128)(2,1)S(1)} %collective-permute-done.25.refs_6_.refs_1_, bf16[1536,1536]{1,0:T(8,128)(2,1)S(1)} %assemble_w_out.1.refs_2_, f32[1536]{0:T(1024)S(1)} %copy-done.12, ...), custom_call_target="tpu_custom_call" | custom-call | flops 20000000000 | bytes 1 | tf_op jit(solution)/shard_map/experts/pallas_call | solution.py:368
  93.8 0.1 collective-permute-start.38
  93.9 0.1 collective-permute-start.39
  94.0 0.7 join_pages.1.refs_17_
  94.7 0.9 copy-done.1
  95.6 5.4 %experts.3 = (f32[128,1536]{1,0:T(8,128)S(1)}, bf16[128,1536]{1,0:T(8,128)(2,1)S(1)}) custom-call(bf16[144,512]{1,0:T(8,128)(2,1)S(1)} %pack_kv.1.own.refs_4_.refs_0_, bf16[144,512]{1,0:T(8,128)(2,1)S(1)} %hold.5.refs_7_.refs_1_, bf16[1536,1536]{1,0:T(8,128)(2,1)S(1)} %assemble_w_out.1.refs_2_, f32[1536]{0:T(1024)S(1)} %copy-done.12, ...), custom_call_target="tpu_custom_call" | custom-call | flops 20000000000 | bytes 1 | tf_op jit(solution)/shard_map/experts/pallas_call | solution.py:368
  100.9 3.4 %collective-permute-start.40 = (bf16[128,1536]{1,0:T(8,128)(2,1)S(1)}, bf16[128,1536]{1,0:T(8,128)(2,1)S(1)}, u32[]{:S(2)}, u32[]{:S(2)}) collective-permute-start(bf16[128,1536]{1,0:T(8,128)(2,1)S(1)} %get-tuple-element.51), channel_id=1, source_target_pairs={{0,6},{1,7},{2,4},{3,5},{4,2},{5,3},{6,0},{7,1},{8,14},{9,15},{10,... | collective-permute-start | bytes 1179656 | tf_op jit(solution)/shard_map/ppermute | solution.py:49
  104.5 7.0 %collective-permute-done.40.by_xy = bf16[128,1536]{1,0:T(8,128)(2,1)S(1)} collective-permute-done((bf16[128,1536]{1,0:T(8,128)(2,1)S(1)}, bf16[128,1536]{1,0:T(8,128)(2,1)S(1)}, u32[]{:S(2)}, u32[]{:S(2)}) %collective-permute-start.40) | collective-permute-done | bytes 393248 | tf_op jit(solution)/shard_map/ppermute | solution.py:49
  111.4 0.9 mix.1
  (71 shorter events, 0.6 us)
Async XLA Ops:
  0.6 16.5 %collective-permute-start.4 = (bf16[1536,256]{1,0:T(8,128)(2,1)}, bf16[1536,256]{1,0:T(8,128)(2,1)S(1)}, u32[]{:S(2)}, u32[]{:S(2)}) collective-permute-start(bf16[1536,256]{1,0:T(8,128)(2,1)} %refs_4_.1), channel_id=1, source_target_pairs={{0,1},{1,0},{2,3},{3,2},{4,5},{5,4},{6,7},{7,6},{8,9},{9,8},{10,11... | collective-permute-start | bytes 2359304 | tf_op jit(solution)/shard_map/ppermute | solution.py:49
  1.1 12.5 %collective-permute-start.2 = (bf16[128,1536]{1,0:T(8,128)(2,1)}, bf16[128,1536]{1,0:T(8,128)(2,1)S(1)}, u32[]{:S(2)}, u32[]{:S(2)}) collective-permute-start(bf16[128,1536]{1,0:T(8,128)(2,1)} %refs_13_.1), channel_id=1, source_target_pairs={{0,2},{1,3},{2,0},{3,1},{4,6},{5,7},{6,4},{7,5},{8,10},{9,11},{10,... | collective-permute-start | bytes 1179656 | tf_op jit(solution)/shard_map/ppermute | solution.py:49
  3.7 11.8 %collective-permute-start = (bf16[128,1536]{1,0:T(8,128)(2,1)}, bf16[128,1536]{1,0:T(8,128)(2,1)S(1)}, u32[]{:S(2)}, u32[]{:S(2)}) collective-permute-start(bf16[128,1536]{1,0:T(8,128)(2,1)} %refs_13_.1), channel_id=1, source_target_pairs={{0,4},{1,5},{2,6},{3,7},{4,0},{5,1},{6,2},{7,3},{8,12},{9,13},{10,... | collective-permute-start | bytes 1179656 | tf_op jit(solution)/shard_map/ppermute | solution.py:49
  5.2 27.1 %collective-permute-start.10 = (bf16[1536,768]{1,0:T(8,128)(2,1)}, bf16[1536,768]{1,0:T(8,128)(2,1)S(1)}, u32[]{:S(2)}, u32[]{:S(2)}) collective-permute-start(bf16[1536,768]{1,0:T(8,128)(2,1)} %bitcast.24), channel_id=1, source_target_pairs={{0,1},{1,0},{2,3},{3,2},{4,5},{5,4},{6,7},{7,6},{8,9},{9,8},{10,11... | collective-permute-start | bytes 7077896 | tf_op jit(solution)/shard_map/ppermute | solution.py:49
  13.6 6.7 %collective-permute-start.3 = (bf16[64,1536]{1,0:T(8,128)(2,1)S(1)}, bf16[64,1536]{1,0:T(8,128)(2,1)S(1)}, u32[]{:S(2)}, u32[]{:S(2)}) collective-permute-start(bf16[64,1536]{1,0:T(8,128)(2,1)S(1)} %slice.57), channel_id=1, source_target_pairs={{0,4},{1,5},{2,6},{3,7},{4,0},{5,1},{6,2},{7,3},{8,12},{9,13},{10,... | collective-permute-start | bytes 589832 | tf_op jit(solution)/shard_map/ppermute | solution.py:49
  15.5 6.3 %collective-permute-start.1 = (bf16[64,1536]{1,0:T(8,128)(2,1)S(1)}, bf16[64,1536]{1,0:T(8,128)(2,1)S(1)}, u32[]{:S(2)}, u32[]{:S(2)}) collective-permute-start(bf16[64,1536]{1,0:T(8,128)(2,1)S(1)} %slice.56), channel_id=1, source_target_pairs={{0,2},{1,3},{2,0},{3,1},{4,6},{5,7},{6,4},{7,5},{8,10},{9,11},{10,... | collective-permute-start | bytes 589832 | tf_op jit(solution)/shard_map/ppermute | solution.py:49
  17.1 15.3 %collective-permute-start.11 = (bf16[1536,768]{1,0:T(8,128)(2,1)}, bf16[1536,768]{1,0:T(8,128)(2,1)S(1)}, u32[]{:S(2)}, u32[]{:S(2)}) collective-permute-start(bf16[1536,768]{1,0:T(8,128)(2,1)} %bitcast.27), channel_id=1, source_target_pairs={{0,1},{1,0},{2,3},{3,2},{4,5},{5,4},{6,7},{7,6},{8,9},{9,8},{10,11... | collective-permute-start | bytes 7077896 | tf_op jit(solution)/shard_map/ppermute | solution.py:49
  17.1 1.1 %copy-start.8 = (bf16[1536,256]{1,0:T(8,128)(2,1)S(1)}, bf16[1536,256]{1,0:T(8,128)(2,1)}, u32[]{:S(2)}) copy-start(bf16[1536,256]{1,0:T(8,128)(2,1)} %refs_4_.1) | copy-start | bytes 2359300
  18.2 0.7 copy-start.11
  18.9 2.9 %copy-start.9 = (bf16[1536,256]{1,0:T(8,128)(2,1)S(1)}, bf16[1536,256]{1,0:T(8,128)(2,1)}, u32[]{:S(2)}) copy-start(bf16[1536,256]{1,0:T(8,128)(2,1)} %refs_4_.1) | copy-start | bytes 2359300
  18.9 2.9 %copy-start.10 = (bf16[128,1536]{1,0:T(8,128)(2,1)S(1)}, bf16[128,1536]{1,0:T(8,128)(2,1)}, u32[]{:S(2)}) copy-start(bf16[128,1536]{1,0:T(8,128)(2,1)} %refs_13_.1) | copy-start | bytes 1179652
  19.7 7.2 %copy-start.13 = (s32[1,64]{1,0:T(1,128)S(1)}, s32[1,64]{1,0:T(1,128)}, u32[]{:S(2)}) copy-start(s32[1,64]{1,0:T(1,128)} %table_ref.1) | copy-start | bytes 772
  22.5 3.5 %collective-permute-start.8 = (bf16[256,512]{1,0:T(8,128)(2,1)S(1)}, bf16[256,512]{1,0:T(8,128)(2,1)S(1)}, u32[]{:S(2)}, u32[]{:S(2)}) collective-permute-start(bf16[256,512]{1,0:T(8,128)(2,1)S(1)} %project.3.refs_0_), channel_id=1, source_target_pairs={{0,1},{1,0},{2,3},{3,2},{4,5},{5,4},{6,7},{7,6},{8,9},{9,8},{10,11... | collective-permute-start | bytes 786440 | tf_op jit(solution)/shard_map/ppermute | solution.py:49
  22.6 2.0 %collective-permute-start.9 = (bf16[256,512]{1,0:T(8,128)(2,1)S(1)}, bf16[256,512]{1,0:T(8,128)(2,1)S(1)}, u32[]{:S(2)}, u32[]{:S(2)}) collective-permute-start(bf16[256,512]{1,0:T(8,128)(2,1)S(1)} %project.2.refs_6_.refs_1_), channel_id=1, source_target_pairs={{0,1},{1,0},{2,3},{3,2},{4,5},{5,4},{6,7},{7,6},{8,9},{9,8},{10,11... | collective-permute-start | bytes 786440 | tf_op jit(solution)/shard_map/ppermute | solution.py:49
  23.1 7.3 %collective-permute-start.7 = (bf16[128,512]{1,0:T(8,128)(2,1)S(1)}, bf16[128,512]{1,0:T(8,128)(2,1)S(1)}, u32[]{:S(2)}, u32[]{:S(2)}) collective-permute-start(bf16[128,512]{1,0:T(8,128)(2,1)S(1)} %get-tuple-element.56), channel_id=1, source_target_pairs={{0,6},{1,7},{2,4},{3,5},{4,2},{5,3},{6,0},{7,1},{8,14},{9,15},{10,... | collective-permute-start | bytes 393224 | tf_op jit(solution)/shard_map/ppermute | solution.py:49
  24.6 7.3 %collective-permute-start.5 = (bf16[128,512]{1,0:T(8,128)(2,1)S(1)}, bf16[128,512]{1,0:T(8,128)(2,1)S(1)}, u32[]{:S(2)}, u32[]{:S(2)}) collective-permute-start(bf16[128,512]{1,0:T(8,128)(2,1)S(1)} %get-tuple-element.59), channel_id=1, source_target_pairs={{0,2},{1,3},{2,0},{3,1},{4,6},{5,7},{6,4},{7,5},{8,10},{9,11},{10,... | collective-permute-start | bytes 393224 | tf_op jit(solution)/shard_map/ppermute | solution.py:49
  26.0 6.4 %copy-start.2 = (s32[128,4]{0,1:T(4,128)S(1)}, s32[128,4]{0,1:T(4,128)}, u32[]{:S(2)}) copy-start(s32[128,4]{0,1:T(4,128)} %param.19) | copy-start | bytes 6148
  26.0 6.4 %copy-start.3 = (f32[128,4]{0,1:T(4,128)S(1)}, f32[128,4]{0,1:T(4,128)}, u32[]{:S(2)}) copy-start(f32[128,4]{0,1:T(4,128)} %param.20) | copy-start | bytes 6148
  26.0 6.4 %copy-start.4 = (s32[128]{0:T(128)S(1)}, s32[128]{0:T(128)}, u32[]{:S(2)}) copy-start(s32[128]{0:T(128)} %param.13) | copy-start | bytes 1540
  26.0 6.4 %copy-start.7 = (bf16[1,768,1536]{2,1,0:T(8,128)(2,1)S(1)}, bf16[1,768,1536]{2,1,0:T(8,128)(2,1)}, u32[]{:S(2)}) copy-start(bf16[1,768,1536]{2,1,0:T(8,128)(2,1)} %param.23) | copy-start | bytes 7077892
  26.0 6.5 %copy-start = (bf16[1536,192]{0,1:T(8,128)(2,1)S(1)}, bf16[1536,192]{0,1:T(8,128)(2,1)}, u32[]{:S(2)}) copy-start(bf16[1536,192]{0,1:T(8,128)(2,1)} %param.17) | copy-start | bytes 1769476
  26.0 6.3 %collective-permute-start.6 = (bf16[128,512]{1,0:T(8,128)(2,1)S(1)}, bf16[128,512]{1,0:T(8,128)(2,1)S(1)}, u32[]{:S(2)}, u32[]{:S(2)}) collective-permute-start(bf16[128,512]{1,0:T(8,128)(2,1)S(1)} %get-tuple-element.58), channel_id=1, source_target_pairs={{0,4},{1,5},{2,6},{3,7},{4,0},{5,1},{6,2},{7,3},{8,12},{9,13},{10,... | collective-permute-start | bytes 393224 | tf_op jit(solution)/shard_map/ppermute | solution.py:49
  32.5 17.1 %collective-permute-start.15 = (bf16[768,1536]{1,0:T(8,128)(2,1)S(1)}, bf16[768,1536]{1,0:T(8,128)(2,1)S(1)}, u32[]{:S(2)}, u32[]{:S(2)}) collective-permute-start(bf16[768,1536]{1,0:T(8,128)(2,1)S(1)} %bitcast.30), channel_id=1, source_target_pairs={{0,1},{1,0},{2,3},{3,2},{4,5},{5,4},{6,7},{7,6},{8,9},{9,8},{10,11... | collective-permute-start | bytes 7077896 | tf_op jit(solution)/shard_map/ppermute | solution.py:49
  32.6 15.7 %collective-permute-start.13 = (bf16[192,1536]{1,0:T(8,128)(2,1)S(1)}, bf16[192,1536]{1,0:T(8,128)(2,1)S(1)}, u32[]{:S(2)}, u32[]{:S(2)}) collective-permute-start(bf16[192,1536]{1,0:T(8,128)(2,1)S(1)} %bitcast.16), channel_id=1, source_target_pairs={{0,2},{1,3},{2,0},{3,1},{4,6},{5,7},{6,4},{7,5},{8,10},{9,11},{10,... | collective-permute-start | bytes 1769480 | tf_op jit(solution)/shard_map/ppermute | solution.py:49
  34.1 15.4 %collective-permute-start.14 = (bf16[192,1536]{1,0:T(8,128)(2,1)S(1)}, bf16[192,1536]{1,0:T(8,128)(2,1)S(1)}, u32[]{:S(2)}, u32[]{:S(2)}) collective-permute-start(bf16[192,1536]{1,0:T(8,128)(2,1)S(1)} %bitcast.17), channel_id=1, source_target_pairs={{0,4},{1,5},{2,6},{3,7},{4,0},{5,1},{6,2},{7,3},{8,12},{9,13},{10,... | collective-permute-start | bytes 1769480 | tf_op jit(solution)/shard_map/ppermute | solution.py:49
  34.7 14.8 %collective-permute-start.16 = (bf16[192,1536]{1,0:T(8,128)(2,1)S(1)}, bf16[192,1536]{1,0:T(8,128)(2,1)S(1)}, u32[]{:S(2)}, u32[]{:S(2)}) collective-permute-start(bf16[192,1536]{1,0:T(8,128)(2,1)S(1)} %bitcast.18), channel_id=1, source_target_pairs={{0,1},{1,0},{2,3},{3,2},{4,5},{5,4},{6,7},{7,6},{8,9},{9,8},{10,11... | collective-permute-start | bytes 1769480 | tf_op jit(solution)/shard_map/ppermute | solution.py:49
  34.7 7.2 %collective-permute-start.12 = (bf16[144,512]{1,0:T(8,128)(2,1)S(1)}, bf16[144,512]{1,0:T(8,128)(2,1)S(1)}, u32[]{:S(2)}, u32[]{:S(2)}) collective-permute-start(bf16[144,512]{1,0:T(8,128)(2,1)S(1)} %pack_kv.1.own.refs_4_.refs_0_), channel_id=1, source_target_pairs={{0,8},{8,16},{16,24},{1,9},{9,17},{17,25},{2,10},{10,18},{18,26},{... | collective-permute-start | bytes 442376 | tf_op jit(solution)/shard_map/ppermute | solution.py:508
  41.9 15.4 %collective-permute-start.26 = (bf16[144,512]{1,0:T(8,128)(2,1)S(1)}, bf16[144,512]{1,0:T(8,128)(2,1)S(1)}, u32[]{:S(2)}, u32[]{:S(2)}) collective-permute-start(bf16[144,512]{1,0:T(8,128)(2,1)S(1)} %pack_kv.1.own.refs_4_.refs_0_), channel_id=1, source_target_pairs={{0,1},{1,0},{2,3},{3,2},{4,5},{5,4},{6,7},{7,6},{8,9},{9,8},{10,11... | collective-permute-start | bytes 442376 | tf_op jit(solution)/shard_map/ppermute | solution.py:49
  48.3 9.6 %collective-permute-start.30 = (bf16[144,512]{1,0:T(8,128)(2,1)S(1)}, bf16[144,512]{1,0:T(8,128)(2,1)S(1)}, u32[]{:S(2)}, u32[]{:S(2)}) collective-permute-start(bf16[144,512]{1,0:T(8,128)(2,1)S(1)} %collective-permute-done.12.prev.refs_8_), channel_id=1, source_target_pairs={{0,1},{1,0},{2,3},{3,2},{4,5},{5,4},{6,7},{7,6},{8,9},{9,8},{10,11... | collective-permute-start | bytes 442376 | tf_op jit(solution)/shard_map/ppermute | solution.py:49
  49.6 7.6 %collective-permute-start.17 = (bf16[144,512]{1,0:T(8,128)(2,1)S(1)}, bf16[144,512]{1,0:T(8,128)(2,1)S(1)}, u32[]{:S(2)}, u32[]{:S(2)}) collective-permute-start(bf16[144,512]{1,0:T(8,128)(2,1)S(1)} %get-tuple-element.36.refs_2_), channel_id=1, source_target_pairs={{0,6},{1,7},{2,4},{3,5},{4,2},{5,3},{6,0},{7,1},{8,14},{9,15},{10,... | collective-permute-start | bytes 442376 | tf_op jit(solution)/shard_map/ppermute | solution.py:49
  50.7 7.7 %collective-permute-start.24 = (bf16[144,512]{1,0:T(8,128)(2,1)S(1)}, bf16[144,512]{1,0:T(8,128)(2,1)S(1)}, u32[]{:S(2)}, u32[]{:S(2)}) collective-permute-start(bf16[144,512]{1,0:T(8,128)(2,1)S(1)} %get-tuple-element.37.refs_0_), channel_id=1, source_target_pairs={{0,2},{1,3},{2,0},{3,1},{4,6},{5,7},{6,4},{7,5},{8,10},{9,11},{10,... | collective-permute-start | bytes 442376 | tf_op jit(solution)/shard_map/ppermute | solution.py:49
  51.7 7.1 %collective-permute-start.25 = (bf16[144,512]{1,0:T(8,128)(2,1)S(1)}, bf16[144,512]{1,0:T(8,128)(2,1)S(1)}, u32[]{:S(2)}, u32[]{:S(2)}) collective-permute-start(bf16[144,512]{1,0:T(8,128)(2,1)S(1)} %get-tuple-element.38.refs_1_), channel_id=1, source_target_pairs={{0,4},{1,5},{2,6},{3,7},{4,0},{5,1},{6,2},{7,3},{8,12},{9,13},{10,... | collective-permute-start | bytes 442376 | tf_op jit(solution)/shard_map/ppermute | solution.py:49
  57.3 5.2 %collective-permute-start.21 = (bf16[192,1536]{1,0:T(8,128)(2,1)S(1)}, bf16[192,1536]{1,0:T(8,128)(2,1)S(1)}, u32[]{:S(2)}, u32[]{:S(2)}) collective-permute-start(bf16[192,1536]{1,0:T(8,128)(2,1)S(1)} %collective-permute-done.14.refs_2_), channel_id=1, source_target_pairs={{0,1},{1,0},{2,3},{3,2},{4,5},{5,4},{6,7},{7,6},{8,9},{9,8},{10,11... | collective-permute-start | bytes 1769480 | tf_op jit(solution)/shard_map/ppermute | solution.py:49
  57.3 5.1 %collective-permute-start.20 = (bf16[192,1536]{1,0:T(8,128)(2,1)S(1)}, bf16[192,1536]{1,0:T(8,128)(2,1)S(1)}, u32[]{:S(2)}, u32[]{:S(2)}) collective-permute-start(bf16[192,1536]{1,0:T(8,128)(2,1)S(1)} %collective-permute-done.13.refs_1_), channel_id=1, source_target_pairs={{0,1},{1,0},{2,3},{3,2},{4,5},{5,4},{6,7},{7,6},{8,9},{9,8},{10,11... | collective-permute-start | bytes 1769480 | tf_op jit(solution)/shard_map/ppermute | solution.py:49
  57.9 2.5 %collective-permute-start.29 = (bf16[144,512]{1,0:T(8,128)(2,1)S(1)}, bf16[144,512]{1,0:T(8,128)(2,1)S(1)}, u32[]{:S(2)}, u32[]{:S(2)}) collective-permute-start(bf16[144,512]{1,0:T(8,128)(2,1)S(1)} %hold.5.refs_7_.refs_1_), channel_id=1, source_target_pairs={{0,1},{1,0},{2,3},{3,2},{4,5},{5,4},{6,7},{7,6},{8,9},{9,8},{10,11... | collective-permute-start | bytes 442376 | tf_op jit(solution)/shard_map/ppermute | solution.py:49
  58.5 2.6 %collective-permute-start.27 = (bf16[144,512]{1,0:T(8,128)(2,1)S(1)}, bf16[144,512]{1,0:T(8,128)(2,1)S(1)}, u32[]{:S(2)}, u32[]{:S(2)}) collective-permute-start(bf16[144,512]{1,0:T(8,128)(2,1)S(1)} %collective-permute-done.24.refs_5_.refs_0_), channel_id=1, source_target_pairs={{0,1},{1,0},{2,3},{3,2},{4,5},{5,4},{6,7},{7,6},{8,9},{9,8},{10,11... | collective-permute-start | bytes 442376 | tf_op jit(solution)/shard_map/ppermute | solution.py:49
  58.9 9.1 %collective-permute-start.19 = (bf16[96,1536]{1,0:T(8,128)(2,1)S(1)}, bf16[96,1536]{1,0:T(8,128)(2,1)S(1)}, u32[]{:S(2)}, u32[]{:S(2)}) collective-permute-start(bf16[96,1536]{1,0:T(8,128)(2,1)S(1)} %hold.7), channel_id=1, source_target_pairs={{0,4},{1,5},{2,6},{3,7},{4,0},{5,1},{6,2},{7,3},{8,12},{9,13},{10,... | collective-permute-start | bytes 884744 | tf_op jit(solution)/shard_map/ppermute | solution.py:49
  60.3 9.1 %collective-permute-start.18 = (bf16[96,1536]{1,0:T(8,128)(2,1)S(1)}, bf16[96,1536]{1,0:T(8,128)(2,1)S(1)}, u32[]{:S(2)}, u32[]{:S(2)}) collective-permute-start(bf16[96,1536]{1,0:T(8,128)(2,1)S(1)} %hold.6), channel_id=1, source_target_pairs={{0,2},{1,3},{2,0},{3,1},{4,6},{5,7},{6,4},{7,5},{8,10},{9,11},{10,... | collective-permute-start | bytes 884744 | tf_op jit(solution)/shard_map/ppermute | solution.py:49
  61.1 1.4 %collective-permute-start.28 = (bf16[144,512]{1,0:T(8,128)(2,1)S(1)}, bf16[144,512]{1,0:T(8,128)(2,1)S(1)}, u32[]{:S(2)}, u32[]{:S(2)}) collective-permute-start(bf16[144,512]{1,0:T(8,128)(2,1)S(1)} %collective-permute-done.25.refs_6_.refs_1_), channel_id=1, source_target_pairs={{0,1},{1,0},{2,3},{3,2},{4,5},{5,4},{6,7},{7,6},{8,9},{9,8},{10,11... | collective-permute-start | bytes 442376 | tf_op jit(solution)/shard_map/ppermute | solution.py:49
  64.1 24.3 %copy-start.5 = (bf16[1,1536,768]{2,1,0:T(8,128)(2,1)S(1)}, bf16[1,1536,768]{2,1,0:T(8,128)(2,1)}, u32[]{:S(2)}) copy-start(bf16[1,1536,768]{2,1,0:T(8,128)(2,1)} %param.21) | copy-start | bytes 7077892
  64.1 24.3 %copy-start.6 = (bf16[1,1536,768]{2,1,0:T(8,128)(2,1)S(1)}, bf16[1,1536,768]{2,1,0:T(8,128)(2,1)}, u32[]{:S(2)}) copy-start(bf16[1,1536,768]{2,1,0:T(8,128)(2,1)} %param.22) | copy-start | bytes 7077892
  64.1 24.3 %copy-start.12 = (f32[1536]{0:T(1024)S(1)}, f32[1536]{0:T(1024)}, u32[]{:S(2)}) copy-start(f32[1536]{0:T(1024)} %refs_3_.7) | copy-start | bytes 18436
  69.4 10.3 %collective-permute-start.31 = (bf16[128,1536]{1,0:T(8,128)(2,1)S(1)}, bf16[128,1536]{1,0:T(8,128)(2,1)S(1)}, u32[]{:S(2)}, u32[]{:S(2)}) collective-permute-start(bf16[128,1536]{1,0:T(8,128)(2,1)S(1)} %attend.1.refs_10_), channel_id=1, source_target_pairs={{0,4},{1,5},{2,6},{3,7},{4,0},{5,1},{6,2},{7,3},{8,12},{9,13},{10,... | collective-permute-start | bytes 1179656 | tf_op jit(solution)/shard_map/ppermute | solution.py:49
  70.0 10.0 %collective-permute-start.33 = (bf16[128,1536]{1,0:T(8,128)(2,1)S(1)}, bf16[128,1536]{1,0:T(8,128)(2,1)S(1)}, u32[]{:S(2)}, u32[]{:S(2)}) collective-permute-start(bf16[128,1536]{1,0:T(8,128)(2,1)S(1)} %attend.1.refs_10_), channel_id=1, source_target_pairs={{0,2},{1,3},{2,0},{3,1},{4,6},{5,7},{6,4},{7,5},{8,10},{9,11},{10,... | collective-permute-start | bytes 1179656 | tf_op jit(solution)/shard_map/ppermute | solution.py:49
  71.1 1.6 %collective-permute-start.23 = (bf16[96,1536]{1,0:T(8,128)(2,1)S(1)}, bf16[96,1536]{1,0:T(8,128)(2,1)S(1)}, u32[]{:S(2)}, u32[]{:S(2)}) collective-permute-start(bf16[96,1536]{1,0:T(8,128)(2,1)S(1)} %collective-permute-done.19.refs_4_), channel_id=1, source_target_pairs={{0,1},{1,0},{2,3},{3,2},{4,5},{5,4},{6,7},{7,6},{8,9},{9,8},{10,11... | collective-permute-start | bytes 884744 | tf_op jit(solution)/shard_map/ppermute | solution.py:49
  71.1 2.0 %collective-permute-start.22 = (bf16[96,1536]{1,0:T(8,128)(2,1)S(1)}, bf16[96,1536]{1,0:T(8,128)(2,1)S(1)}, u32[]{:S(2)}, u32[]{:S(2)}) collective-permute-start(bf16[96,1536]{1,0:T(8,128)(2,1)S(1)} %collective-permute-done.18.refs_3_), channel_id=1, source_target_pairs={{0,1},{1,0},{2,3},{3,2},{4,5},{5,4},{6,7},{7,6},{8,9},{9,8},{10,11... | collective-permute-start | bytes 884744 | tf_op jit(solution)/shard_map/ppermute | solution.py:49
  80.1 13.6 %collective-permute-start.35 = (bf16[128,512]{1,0:T(8,128)(2,1)S(1)}, bf16[128,512]{1,0:T(8,128)(2,1)S(1)}, u32[]{:S(2)}, u32[]{:S(2)}) collective-permute-start(bf16[128,512]{1,0:T(8,128)(2,1)S(1)} %get-tuple-element.54), channel_id=1, source_target_pairs={{6,4},{7,5},{14,12},{15,13},{22,20},{23,21},{30,28},{31,29}} | collective-permute-start | bytes 393224 | tf_op jit(solution)/shard_map/ppermute | solution.py:531
  80.8 13.1 %collective-permute-start.36 = (bf16[128,512]{1,0:T(8,128)(2,1)S(1)}, bf16[128,512]{1,0:T(8,128)(2,1)S(1)}, u32[]{:S(2)}, u32[]{:S(2)}) collective-permute-start(bf16[128,512]{1,0:T(8,128)(2,1)S(1)} %get-tuple-element.53), channel_id=1, source_target_pairs={{6,2},{7,3},{14,10},{15,11},{22,18},{23,19},{30,26},{31,27}} | collective-permute-start | bytes 393224 | tf_op jit(solution)/shard_map/ppermute | solution.py:531
  81.5 12.5 %collective-permute-start.37 = (bf16[128,512]{1,0:T(8,128)(2,1)S(1)}, bf16[128,512]{1,0:T(8,128)(2,1)S(1)}, u32[]{:S(2)}, u32[]{:S(2)}) collective-permute-start(bf16[128,512]{1,0:T(8,128)(2,1)S(1)} %get-tuple-element.52), channel_id=1, source_target_pairs={{6,0},{7,1},{14,8},{15,9},{22,16},{23,17},{30,24},{31,25}} | collective-permute-start | bytes 393224 | tf_op jit(solution)/shard_map/ppermute | solution.py:531
  83.0 11.7 %collective-permute-start.32 = (bf16[64,1536]{1,0:T(8,128)(2,1)S(1)}, bf16[64,1536]{1,0:T(8,128)(2,1)S(1)}, u32[]{:S(2)}, u32[]{:S(2)}) collective-permute-start(bf16[64,1536]{1,0:T(8,128)(2,1)S(1)} %slice.64), channel_id=1, source_target_pairs={{0,2},{1,3},{2,0},{3,1},{4,6},{5,7},{6,4},{7,5},{8,10},{9,11},{10,... | collective-permute-start | bytes 589832 | tf_op jit(solution)/shard_map/ppermute | solution.py:49
  83.9 10.7 %collective-permute-start.34 = (bf16[64,1536]{1,0:T(8,128)(2,1)S(1)}, bf16[64,1536]{1,0:T(8,128)(2,1)S(1)}, u32[]{:S(2)}, u32[]{:S(2)}) collective-permute-start(bf16[64,1536]{1,0:T(8,128)(2,1)S(1)} %slice.65), channel_id=1, source_target_pairs={{0,4},{1,5},{2,6},{3,7},{4,0},{5,1},{6,2},{7,3},{8,12},{9,13},{10,... | collective-permute-start | bytes 589832 | tf_op jit(solution)/shard_map/ppermute | solution.py:49
  93.8 10.6 %collective-permute-start.38 = (bf16[128,1536]{1,0:T(8,128)(2,1)S(1)}, bf16[128,1536]{1,0:T(8,128)(2,1)S(1)}, u32[]{:S(2)}, u32[]{:S(2)}) collective-permute-start(bf16[128,1536]{1,0:T(8,128)(2,1)S(1)} %get-tuple-element.47.refs_16_), channel_id=1, source_target_pairs={{0,2},{1,3},{2,0},{3,1},{4,6},{5,7},{6,4},{7,5},{8,10},{9,11},{10,... | collective-permute-start | bytes 1179656 | tf_op jit(solution)/shard_map/ppermute | solution.py:49
  93.9 10.6 %collective-permute-start.39 = (bf16[128,1536]{1,0:T(8,128)(2,1)S(1)}, bf16[128,1536]{1,0:T(8,128)(2,1)S(1)}, u32[]{:S(2)}, u32[]{:S(2)}) collective-permute-start(bf16[128,1536]{1,0:T(8,128)(2,1)S(1)} %get-tuple-element.50), channel_id=1, source_target_pairs={{0,4},{1,5},{2,6},{3,7},{4,0},{5,1},{6,2},{7,3},{8,12},{9,13},{10,... | collective-permute-start | bytes 1179656 | tf_op jit(solution)/shard_map/ppermute | solution.py:49
  94.7 0.9 copy-start.1
  100.9 10.5 %collective-permute-start.40 = (bf16[128,1536]{1,0:T(8,128)(2,1)S(1)}, bf16[128,1536]{1,0:T(8,128)(2,1)S(1)}, u32[]{:S(2)}, u32[]{:S(2)}) collective-permute-start(bf16[128,1536]{1,0:T(8,128)(2,1)S(1)} %get-tuple-element.51), channel_id=1, source_target_pairs={{0,6},{1,7},{2,4},{3,5},{4,2},{5,3},{6,0},{7,1},{8,14},{9,15},{10,... | collective-permute-start | bytes 1179656 | tf_op jit(solution)/shard_map/ppermute | solution.py:49

commit v5 on v4

--- a/solution.py
+++ b/solution.py
@@ -434,7 +434,6 @@
         in_specs=[pl.BlockSpec(memory_space=pltpu.SMEM)] + [vmem()] * 4,
         out_specs=vmem(),
         scratch_shapes=[pltpu.VMEM((CORES * CHIPS, rows, width), jnp.bfloat16)],
-        cost_estimate=LONG,
         compiler_params=params(16),
         name="cache_pages",
     )(page_table, *same, *other)
@@ -498,15 +497,21 @@
     tokens_xy = [chips(tokens_y[: rows // 2], 1), chips(tokens_x[rows // 2 :], 2)]
     late = project_call((tokens_x, tokens_y), attn_gain, w_qkv, w_qkv_other)
     made = project_call((tokens, *tokens_xy), attn_gain, w_qkv, w_qkv_other, late)
-    projected = [made[:rows], chips(late[:rows], 1), chips(late[rows:], 2), chips(made[rows:], 3)]
+    projected = [
+        made[:rows],
+        hold_call(chips(late[:rows], 1)),
+        hold_call(chips(late[rows:], 2)),
+        chips(made[rows:], 3),
+    ]
     up_other = hop(after(up, tokens_x), 1)
 
-    paged = cache_call(page_table, (made, late), (hop(made, 1), hop(after(late, made), 1)))
     own_kv = pack_call(
-        after(projected, (paged, gate_other, up_other)), segment_ids, route_ids, route_weight
+        after(projected, (gate_other, up_other)), segment_ids, route_ids, route_weight
     )
     prev_kv = lax.ppermute(own_kv, "seq", [(i, i + 1) for i in range(seq_size - 1)])
     w_going, down_going = after((w_own, down), own_kv)
+    mine = after((made, late), own_kv)
+    paged = cache_call(page_table, mine, [hop(kv, 1) for kv in mine])
     w_x, w_y = chips(w_going, 1), chips(w_going, 2)
     down_other, w_own_other = hop(down_going, 1), hop(w_going, 1)
 

time: 113 us -> 111 us (0.982)
  waiting for transfers between devices: 52.4 us -> 50.5 us
    ppermute x37, waiting for transfers between devices: 48.6 us -> 46.7 us  [hop(): return lax.ppermute(value, 'tensor', [(i, i ^ by) for i in range(length)])]
    unnamed x28 -> x30, local copies, waits for them, and re-layouts: 2.79 us -> 2.8 us
  transfers between devices with their start and end apart: 41 -> 41, of which waited for: 21 -> 17; matrix products, arithmetic and copies ran while one was open for 0% -> 0% of each run, Pallas kernels for 15% -> 15%
where the time goes in v5:
time: 111 us; the launch traced here: 110 us
  waiting for transfers between devices  50.5 us (45%)
  starting transfers between devices  37.8 us (34%)
  Pallas kernels  18.1 us (16%)
  local copies, waits for them, and re-layouts  2.97 us (3%)
    ppermute x37, waiting for transfers between devices, hop(): return lax.ppermute(value, 'tensor', [(i, i ^ by) for i in range(length)])  46.7 us
    ppermute x37, starting transfers between devices, hop(): return lax.ppermute(value, 'tensor', [(i, i ^ by) for i in range(length)])  31.5 us
    pallas_call x2, Pallas kernels, expert_call(): pl.pallas_call(functools.partial(expert_kernel, 256, len(context), len(to...  10.7 us
    ppermute x1, waiting for transfers between devices, chip_body(): lax.ppermute(own_kv, 'seq', [(i, i + 1) for i in range(seq_size - 1)])  3.75 us
    ppermute x1, starting transfers between devices, chip_body(): lax.ppermute(own_kv, 'seq', [(i, i + 1) for i in range(seq_size - 1)])  3.46 us
    ppermute x3, starting transfers between devices, chip_body(): pages.append(lax.ppermute(paged[last ^ by], 'tensor', pairs))  2.81 us
    unnamed x30, local copies, waits for them, and re-layouts  2.8 us
  transfers between devices with their start and end apart: 41, of which 17 were waited for; matrix products, arithmetic and copies ran while one was open for 0% of the time, Pallas kernels for 15%

profile of v5, /device:TPU:0, one launch (start us, length us, event | category | flops | bytes accessed | tf_op | source)
XLA Modules:
  0.0 110.4 jit_solution(15777286317058206162)
XLA Ops:
  0.6 0.5 collective-permute-start.4
  1.1 2.6 %collective-permute-start.2 = (bf16[128,1536]{1,0:T(8,128)(2,1)}, bf16[128,1536]{1,0:T(8,128)(2,1)S(1)}, u32[]{:S(2)}, u32[]{:S(2)}) collective-permute-start(bf16[128,1536]{1,0:T(8,128)(2,1)} %refs_13_.1), channel_id=1, source_target_pairs={{0,2},{1,3},{2,0},{3,1},{4,6},{5,7},{6,4},{7,5},{8,10},{9,11},{10,... | collective-permute-start | bytes 1179656 | tf_op jit(solution)/shard_map/ppermute | solution.py:49
  3.7 1.5 %collective-permute-start = (bf16[128,1536]{1,0:T(8,128)(2,1)}, bf16[128,1536]{1,0:T(8,128)(2,1)S(1)}, u32[]{:S(2)}, u32[]{:S(2)}) collective-permute-start(bf16[128,1536]{1,0:T(8,128)(2,1)} %refs_13_.1), channel_id=1, source_target_pairs={{0,4},{1,5},{2,6},{3,7},{4,0},{5,1},{6,2},{7,3},{8,12},{9,13},{10,... | collective-permute-start | bytes 1179656 | tf_op jit(solution)/shard_map/ppermute | solution.py:49
  5.2 8.4 %collective-permute-done.2.refs_0_.refs_12_ = bf16[128,1536]{1,0:T(8,128)(2,1)S(1)} collective-permute-done((bf16[128,1536]{1,0:T(8,128)(2,1)}, bf16[128,1536]{1,0:T(8,128)(2,1)S(1)}, u32[]{:S(2)}, u32[]{:S(2)}) %collective-permute-start.2) | collective-permute-done | bytes 393248 | tf_op jit(solution)/shard_map/ppermute | solution.py:49
  13.6 1.9 %collective-permute-start.3 = (bf16[64,1536]{1,0:T(8,128)(2,1)S(1)}, bf16[64,1536]{1,0:T(8,128)(2,1)S(1)}, u32[]{:S(2)}, u32[]{:S(2)}) collective-permute-start(bf16[64,1536]{1,0:T(8,128)(2,1)S(1)} %slice.57), channel_id=1, source_target_pairs={{0,4},{1,5},{2,6},{3,7},{4,0},{5,1},{6,2},{7,3},{8,12},{9,13},{10,... | collective-permute-start | bytes 589832 | tf_op jit(solution)/shard_map/ppermute | solution.py:49
  15.5 1.6 %collective-permute-start.1 = (bf16[64,1536]{1,0:T(8,128)(2,1)S(1)}, bf16[64,1536]{1,0:T(8,128)(2,1)S(1)}, u32[]{:S(2)}, u32[]{:S(2)}) collective-permute-start(bf16[64,1536]{1,0:T(8,128)(2,1)S(1)} %slice.56), channel_id=1, source_target_pairs={{0,2},{1,3},{2,0},{3,1},{4,6},{5,7},{6,4},{7,5},{8,10},{9,11},{10,... | collective-permute-start | bytes 589832 | tf_op jit(solution)/shard_map/ppermute | solution.py:49
  17.1 1.1 %copy-done.9 = bf16[1536,256]{1,0:T(8,128)(2,1)S(1)} copy-done((bf16[1536,256]{1,0:T(8,128)(2,1)S(1)}, bf16[1536,256]{1,0:T(8,128)(2,1)}, u32[]{:S(2)}) %copy-start.9) | copy-done | bytes 786456
  18.2 0.7 copy-done.12
  18.9 0.7 project.2.refs_6_.refs_1_
  19.7 0.6 collective-permute-start.5
  20.3 0.1 collective-permute-done.3.refs_2_.refs_15_
  20.4 1.4 %collective-permute-done.1.refs_1_.refs_14_ = bf16[64,1536]{1,0:T(8,128)(2,1)S(1)} collective-permute-done((bf16[64,1536]{1,0:T(8,128)(2,1)S(1)}, bf16[64,1536]{1,0:T(8,128)(2,1)S(1)}, u32[]{:S(2)}, u32[]{:S(2)}) %collective-permute-start.1) | collective-permute-done | bytes 196640 | tf_op jit(solution)/shard_map/ppermute | solution.py:49
  21.8 0.7 project.3.refs_0_
  22.6 1.5 %collective-permute-start.7 = (bf16[128,512]{1,0:T(8,128)(2,1)S(1)}, bf16[128,512]{1,0:T(8,128)(2,1)S(1)}, u32[]{:S(2)}, u32[]{:S(2)}) collective-permute-start(bf16[128,512]{1,0:T(8,128)(2,1)S(1)} %get-tuple-element.58), channel_id=1, source_target_pairs={{0,6},{1,7},{2,4},{3,5},{4,2},{5,3},{6,0},{7,1},{8,14},{9,15},{10,... | collective-permute-start | bytes 393224 | tf_op jit(solution)/shard_map/ppermute | solution.py:49
  24.1 1.5 %collective-permute-start.6 = (bf16[128,512]{1,0:T(8,128)(2,1)S(1)}, bf16[128,512]{1,0:T(8,128)(2,1)S(1)}, u32[]{:S(2)}, u32[]{:S(2)}) collective-permute-start(bf16[128,512]{1,0:T(8,128)(2,1)S(1)} %get-tuple-element.60), channel_id=1, source_target_pairs={{0,4},{1,5},{2,6},{3,7},{4,0},{5,1},{6,2},{7,3},{8,12},{9,13},{10,... | collective-permute-start | bytes 393224 | tf_op jit(solution)/shard_map/ppermute | solution.py:49
  25.6 0.5 collective-permute-done.5.in_ref
  26.1 0.0 copy-start.2
  26.1 0.0 copy-start.3
  26.1 4.6 %collective-permute-done.6.in_ref = bf16[128,512]{1,0:T(8,128)(2,1)S(1)} collective-permute-done((bf16[128,512]{1,0:T(8,128)(2,1)S(1)}, bf16[128,512]{1,0:T(8,128)(2,1)S(1)}, u32[]{:S(2)}, u32[]{:S(2)}) %collective-permute-start.6) | collective-permute-done | bytes 131104 | tf_op jit(solution)/shard_map/ppermute | solution.py:49
  30.8 0.1 pack_kv.1.own.refs_4_.refs_0_
  30.9 0.1 collective-permute-start.13
  31.0 1.2 %collective-permute-start.11 = (bf16[192,1536]{1,0:T(8,128)(2,1)S(1)}, bf16[192,1536]{1,0:T(8,128)(2,1)S(1)}, u32[]{:S(2)}, u32[]{:S(2)}) collective-permute-start(bf16[192,1536]{1,0:T(8,128)(2,1)S(1)} %bitcast.16), channel_id=1, source_target_pairs={{0,2},{1,3},{2,0},{3,1},{4,6},{5,7},{6,4},{7,5},{8,10},{9,11},{10,... | collective-permute-start | bytes 1769480 | tf_op jit(solution)/shard_map/ppermute | solution.py:49
  32.2 1.0 collective-permute-start.12
  33.2 3.5 %collective-permute-start.10 = (bf16[144,512]{1,0:T(8,128)(2,1)S(1)}, bf16[144,512]{1,0:T(8,128)(2,1)S(1)}, u32[]{:S(2)}, u32[]{:S(2)}) collective-permute-start(bf16[144,512]{1,0:T(8,128)(2,1)S(1)} %pack_kv.1.own.refs_4_.refs_0_), channel_id=1, source_target_pairs={{0,8},{8,16},{16,24},{1,9},{9,17},{17,25},{2,10},{10,18},{18,26},{... | collective-permute-start | bytes 442376 | tf_op jit(solution)/shard_map/ppermute | solution.py:511
  36.7 3.8 %collective-permute-done.10.prev.refs_8_ = bf16[144,512]{1,0:T(8,128)(2,1)S(1)} collective-permute-done((bf16[144,512]{1,0:T(8,128)(2,1)S(1)}, bf16[144,512]{1,0:T(8,128)(2,1)S(1)}, u32[]{:S(2)}, u32[]{:S(2)}) %collective-permute-start.10) | collective-permute-done | bytes 147488 | tf_op jit(solution)/shard_map/ppermute | solution.py:511
  40.5 6.3 %collective-permute-done.11.refs_1_ = bf16[192,1536]{1,0:T(8,128)(2,1)S(1)} collective-permute-done((bf16[192,1536]{1,0:T(8,128)(2,1)S(1)}, bf16[192,1536]{1,0:T(8,128)(2,1)S(1)}, u32[]{:S(2)}, u32[]{:S(2)}) %collective-permute-start.11) | collective-permute-done | bytes 589856 | tf_op jit(solution)/shard_map/ppermute | solution.py:49
  46.8 0.8 collective-permute-done.12.refs_2_
  47.7 0.1 choose_kv.1
  47.7 1.9 %collective-permute-start.15 = (bf16[144,512]{1,0:T(8,128)(2,1)S(1)}, bf16[144,512]{1,0:T(8,128)(2,1)S(1)}, u32[]{:S(2)}, u32[]{:S(2)}) collective-permute-start(bf16[144,512]{1,0:T(8,128)(2,1)S(1)} %get-tuple-element.36.refs_2_), channel_id=1, source_target_pairs={{0,6},{1,7},{2,4},{3,5},{4,2},{5,3},{6,0},{7,1},{8,14},{9,15},{10,... | collective-permute-start | bytes 442376 | tf_op jit(solution)/shard_map/ppermute | solution.py:49
  49.6 0.7 collective-permute-start.22
  50.3 1.0 collective-permute-start.23
  51.3 4.1 %collective-permute-done.15.in_ref = bf16[144,512]{1,0:T(8,128)(2,1)S(1)} collective-permute-done((bf16[144,512]{1,0:T(8,128)(2,1)S(1)}, bf16[144,512]{1,0:T(8,128)(2,1)S(1)}, u32[]{:S(2)}, u32[]{:S(2)}) %collective-permute-start.15) | collective-permute-done | bytes 147488 | tf_op jit(solution)/shard_map/ppermute | solution.py:49
  55.5 0.6 collective-permute-start.18
  56.1 0.1 collective-permute-start.27
  56.1 1.2 %collective-permute-done.22.refs_5_.refs_0_ = bf16[144,512]{1,0:T(8,128)(2,1)S(1)} collective-permute-done((bf16[144,512]{1,0:T(8,128)(2,1)S(1)}, bf16[144,512]{1,0:T(8,128)(2,1)S(1)}, u32[]{:S(2)}, u32[]{:S(2)}) %collective-permute-start.22) | collective-permute-done | bytes 147488 | tf_op jit(solution)/shard_map/ppermute | solution.py:49
  57.4 1.4 %collective-permute-start.17 = (bf16[96,1536]{1,0:T(8,128)(2,1)S(1)}, bf16[96,1536]{1,0:T(8,128)(2,1)S(1)}, u32[]{:S(2)}, u32[]{:S(2)}) collective-permute-start(bf16[96,1536]{1,0:T(8,128)(2,1)S(1)} %hold.11), channel_id=1, source_target_pairs={{0,4},{1,5},{2,6},{3,7},{4,0},{5,1},{6,2},{7,3},{8,12},{9,13},{10,... | collective-permute-start | bytes 884744 | tf_op jit(solution)/shard_map/ppermute | solution.py:49
  58.8 0.7 collective-permute-start.16
  59.5 1.4 %collective-permute-done.26.refs_11_ = bf16[144,512]{1,0:T(8,128)(2,1)S(1)} collective-permute-done((bf16[144,512]{1,0:T(8,128)(2,1)S(1)}, bf16[144,512]{1,0:T(8,128)(2,1)S(1)}, u32[]{:S(2)}, u32[]{:S(2)}) %collective-permute-start.26) | collective-permute-done | bytes 147488 | tf_op jit(solution)/shard_map/ppermute | solution.py:49
  60.8 0.1 collective-permute-start.33
  61.0 1.7 %attend.1.refs_10_ = bf16[128,1536]{1,0:T(8,128)(2,1)S(1)} custom-call(bf16[128,512]{1,0:T(8,128)(2,1)S(1)} %get-tuple-element.29.own.refs_0_, bf16[128,512]{1,0:T(8,128)(2,1)S(1)} %hold.7.by_x.refs_1_, bf16[128,512]{1,0:T(8,128)(2,1)S(1)} %hold.8.by_y.refs_2_, bf16[128,512]{1,0:T(8,128)(2,1)S(1)} %collective-permute-done.7.by_xy.refs_3_, ...), custom_call_target="tpu_custom_call" | custom-call | tf_op jit(solution)/shard_map/attend/pallas_call | solution.py:267
  62.7 4.2 %collective-permute-done.17.refs_4_ = bf16[96,1536]{1,0:T(8,128)(2,1)S(1)} collective-permute-done((bf16[96,1536]{1,0:T(8,128)(2,1)S(1)}, bf16[96,1536]{1,0:T(8,128)(2,1)S(1)}, u32[]{:S(2)}, u32[]{:S(2)}) %collective-permute-start.17) | collective-permute-done | bytes 294944 | tf_op jit(solution)/shard_map/ppermute | solution.py:49
  66.9 0.6 collective-permute-done.16.refs_3_
  67.6 1.1 collective-permute-start.29
  68.7 1.3 %collective-permute-start.31 = (bf16[128,1536]{1,0:T(8,128)(2,1)S(1)}, bf16[128,1536]{1,0:T(8,128)(2,1)S(1)}, u32[]{:S(2)}, u32[]{:S(2)}) collective-permute-start(bf16[128,1536]{1,0:T(8,128)(2,1)S(1)} %attend.1.refs_10_), channel_id=1, source_target_pairs={{0,2},{1,3},{2,0},{3,1},{4,6},{5,7},{6,4},{7,5},{8,10},{9,11},{10,... | collective-permute-start | bytes 1179656 | tf_op jit(solution)/shard_map/ppermute | solution.py:49
  70.0 0.5 collective-permute-start.20
  70.5 1.9 %collective-permute-done.34.refs_3_ = bf16[256,512]{1,0:T(8,128)(2,1)S(1)} collective-permute-done((bf16[256,512]{1,0:T(8,128)(2,1)S(1)}, bf16[256,512]{1,0:T(8,128)(2,1)S(1)}, u32[]{:S(2)}, u32[]{:S(2)}) %collective-permute-start.34) | collective-permute-done | bytes 262176 | tf_op jit(solution)/shard_map/ppermute | solution.py:49
  72.4 2.1 %cache_pages.1 = bf16[4,128,512]{2,1,0:T(8,128)(2,1)S(1)} custom-call(s32[1,64]{1,0:T(1,128)S(1)} %copy-done.5, bf16[256,512]{1,0:T(8,128)(2,1)S(1)} %project.3.refs_0_, bf16[256,512]{1,0:T(8,128)(2,1)S(1)} %project.2.refs_6_.refs_1_, bf16[256,512]{1,0:T(8,128)(2,1)S(1)} %collective-permute-done.33.refs_2_, bf16[256,512]{1,0:T(8,128)(2,1)S(1)} %collective-permute-done.34.refs_3_), custom_call_target="tpu_custom_call" | custom-call | tf_op jit(solution)/shard_map/cache_pages/pallas_call | solution.py:431
  74.5 0.3 assemble_w_out.1.refs_2_
  74.8 2.8 %collective-permute-done.29.refs_11_ = bf16[128,1536]{1,0:T(8,128)(2,1)S(1)} collective-permute-done((bf16[128,1536]{1,0:T(8,128)(2,1)S(1)}, bf16[128,1536]{1,0:T(8,128)(2,1)S(1)}, u32[]{:S(2)}, u32[]{:S(2)}) %collective-permute-start.29) | collective-permute-done | bytes 393248 | tf_op jit(solution)/shard_map/ppermute | solution.py:49
  77.7 1.1 %collective-permute-done.31.refs_10_ = bf16[128,1536]{1,0:T(8,128)(2,1)S(1)} collective-permute-done((bf16[128,1536]{1,0:T(8,128)(2,1)S(1)}, bf16[128,1536]{1,0:T(8,128)(2,1)S(1)}, u32[]{:S(2)}, u32[]{:S(2)}) %collective-permute-start.31) | collective-permute-done | bytes 393248 | tf_op jit(solution)/shard_map/ppermute | solution.py:49
  78.9 0.7 collective-permute-start.35
  79.5 0.7 collective-permute-start.36
  80.2 1.5 %collective-permute-start.37 = (bf16[128,512]{1,0:T(8,128)(2,1)S(1)}, bf16[128,512]{1,0:T(8,128)(2,1)S(1)}, u32[]{:S(2)}, u32[]{:S(2)}) collective-permute-start(bf16[128,512]{1,0:T(8,128)(2,1)S(1)} %get-tuple-element.54), channel_id=1, source_target_pairs={{6,0},{7,1},{14,8},{15,9},{22,16},{23,17},{30,24},{31,25}} | collective-permute-start | bytes 393224 | tf_op jit(solution)/shard_map/ppermute | solution.py:536
  81.7 1.3 %collective-permute-start.30 = (bf16[64,1536]{1,0:T(8,128)(2,1)S(1)}, bf16[64,1536]{1,0:T(8,128)(2,1)S(1)}, u32[]{:S(2)}, u32[]{:S(2)}) collective-permute-start(bf16[64,1536]{1,0:T(8,128)(2,1)S(1)} %slice.64), channel_id=1, source_target_pairs={{0,2},{1,3},{2,0},{3,1},{4,6},{5,7},{6,4},{7,5},{8,10},{9,11},{10,... | collective-permute-start | bytes 589832 | tf_op jit(solution)/shard_map/ppermute | solution.py:49
  83.0 3.3 %collective-permute-start.32 = (bf16[64,1536]{1,0:T(8,128)(2,1)S(1)}, bf16[64,1536]{1,0:T(8,128)(2,1)S(1)}, u32[]{:S(2)}, u32[]{:S(2)}) collective-permute-start(bf16[64,1536]{1,0:T(8,128)(2,1)S(1)} %slice.65), channel_id=1, source_target_pairs={{0,4},{1,5},{2,6},{3,7},{4,0},{5,1},{6,2},{7,3},{8,12},{9,13},{10,... | collective-permute-start | bytes 589832 | tf_op jit(solution)/shard_map/ppermute | solution.py:49
  86.4 5.3 %experts.2 = (bf16[128,1536]{1,0:T(8,128)(2,1)S(1)}, bf16[128,1536]{1,0:T(8,128)(2,1)S(1)}) custom-call(bf16[144,512]{1,0:T(8,128)(2,1)S(1)} %collective-permute-done.22.refs_5_.refs_0_, bf16[144,512]{1,0:T(8,128)(2,1)S(1)} %collective-permute-done.23.refs_6_.refs_1_, bf16[1536,1536]{1,0:T(8,128)(2,1)S(1)} %assemble_w_out.1.refs_2_, f32[1536]{0:T(1024)S(1)} %copy-done.14, ...), custom_call_target="tpu_custom_call" | custom-call | flops 20000000000 | bytes 1 | tf_op jit(solution)/shard_map/experts/pallas_call | solution.py:368
  91.7 0.1 collective-permute-start.38
  91.8 0.1 collective-permute-start.39
  91.9 0.7 join_pages.1.refs_17_
  92.6 0.9 copy-done.1
  93.5 5.4 %experts.3 = (f32[128,1536]{1,0:T(8,128)S(1)}, bf16[128,1536]{1,0:T(8,128)(2,1)S(1)}) custom-call(bf16[144,512]{1,0:T(8,128)(2,1)S(1)} %pack_kv.1.own.refs_4_.refs_0_, bf16[144,512]{1,0:T(8,128)(2,1)S(1)} %hold.9.refs_7_.refs_1_, bf16[1536,1536]{1,0:T(8,128)(2,1)S(1)} %assemble_w_out.1.refs_2_, f32[1536]{0:T(1024)S(1)} %copy-done.14, ...), custom_call_target="tpu_custom_call" | custom-call | flops 20000000000 | bytes 1 | tf_op jit(solution)/shard_map/experts/pallas_call | solution.py:368
  98.9 3.4 %collective-permute-start.40 = (bf16[128,1536]{1,0:T(8,128)(2,1)S(1)}, bf16[128,1536]{1,0:T(8,128)(2,1)S(1)}, u32[]{:S(2)}, u32[]{:S(2)}) collective-permute-start(bf16[128,1536]{1,0:T(8,128)(2,1)S(1)} %get-tuple-element.53), channel_id=1, source_target_pairs={{0,6},{1,7},{2,4},{3,5},{4,2},{5,3},{6,0},{7,1},{8,14},{9,15},{10,... | collective-permute-start | bytes 1179656 | tf_op jit(solution)/shard_map/ppermute | solution.py:49
  102.4 7.0 %collective-permute-done.40.by_xy = bf16[128,1536]{1,0:T(8,128)(2,1)S(1)} collective-permute-done((bf16[128,1536]{1,0:T(8,128)(2,1)S(1)}, bf16[128,1536]{1,0:T(8,128)(2,1)S(1)}, u32[]{:S(2)}, u32[]{:S(2)}) %collective-permute-start.40) | collective-permute-done | bytes 393248 | tf_op jit(solution)/shard_map/ppermute | solution.py:49
  109.4 0.9 mix.1
  (75 shorter events, 0.5 us)
Async XLA Ops:
  0.6 16.5 %collective-permute-start.4 = (bf16[1536,256]{1,0:T(8,128)(2,1)}, bf16[1536,256]{1,0:T(8,128)(2,1)S(1)}, u32[]{:S(2)}, u32[]{:S(2)}) collective-permute-start(bf16[1536,256]{1,0:T(8,128)(2,1)} %refs_4_.1), channel_id=1, source_target_pairs={{0,1},{1,0},{2,3},{3,2},{4,5},{5,4},{6,7},{7,6},{8,9},{9,8},{10,11... | collective-permute-start | bytes 2359304 | tf_op jit(solution)/shard_map/ppermute | solution.py:49
  1.1 12.5 %collective-permute-start.2 = (bf16[128,1536]{1,0:T(8,128)(2,1)}, bf16[128,1536]{1,0:T(8,128)(2,1)S(1)}, u32[]{:S(2)}, u32[]{:S(2)}) collective-permute-start(bf16[128,1536]{1,0:T(8,128)(2,1)} %refs_13_.1), channel_id=1, source_target_pairs={{0,2},{1,3},{2,0},{3,1},{4,6},{5,7},{6,4},{7,5},{8,10},{9,11},{10,... | collective-permute-start | bytes 1179656 | tf_op jit(solution)/shard_map/ppermute | solution.py:49
  3.7 11.8 %collective-permute-start = (bf16[128,1536]{1,0:T(8,128)(2,1)}, bf16[128,1536]{1,0:T(8,128)(2,1)S(1)}, u32[]{:S(2)}, u32[]{:S(2)}) collective-permute-start(bf16[128,1536]{1,0:T(8,128)(2,1)} %refs_13_.1), channel_id=1, source_target_pairs={{0,4},{1,5},{2,6},{3,7},{4,0},{5,1},{6,2},{7,3},{8,12},{9,13},{10,... | collective-permute-start | bytes 1179656 | tf_op jit(solution)/shard_map/ppermute | solution.py:49
  5.2 25.6 %collective-permute-start.8 = (bf16[1536,768]{1,0:T(8,128)(2,1)}, bf16[1536,768]{1,0:T(8,128)(2,1)S(1)}, u32[]{:S(2)}, u32[]{:S(2)}) collective-permute-start(bf16[1536,768]{1,0:T(8,128)(2,1)} %bitcast.24), channel_id=1, source_target_pairs={{0,1},{1,0},{2,3},{3,2},{4,5},{5,4},{6,7},{7,6},{8,9},{9,8},{10,11... | collective-permute-start | bytes 7077896 | tf_op jit(solution)/shard_map/ppermute | solution.py:49
  13.6 6.7 %collective-permute-start.3 = (bf16[64,1536]{1,0:T(8,128)(2,1)S(1)}, bf16[64,1536]{1,0:T(8,128)(2,1)S(1)}, u32[]{:S(2)}, u32[]{:S(2)}) collective-permute-start(bf16[64,1536]{1,0:T(8,128)(2,1)S(1)} %slice.57), channel_id=1, source_target_pairs={{0,4},{1,5},{2,6},{3,7},{4,0},{5,1},{6,2},{7,3},{8,12},{9,13},{10,... | collective-permute-start | bytes 589832 | tf_op jit(solution)/shard_map/ppermute | solution.py:49
  15.5 6.3 %collective-permute-start.1 = (bf16[64,1536]{1,0:T(8,128)(2,1)S(1)}, bf16[64,1536]{1,0:T(8,128)(2,1)S(1)}, u32[]{:S(2)}, u32[]{:S(2)}) collective-permute-start(bf16[64,1536]{1,0:T(8,128)(2,1)S(1)} %slice.56), channel_id=1, source_target_pairs={{0,2},{1,3},{2,0},{3,1},{4,6},{5,7},{6,4},{7,5},{8,10},{9,11},{10,... | collective-permute-start | bytes 589832 | tf_op jit(solution)/shard_map/ppermute | solution.py:49
  17.1 13.7 %collective-permute-start.9 = (bf16[1536,768]{1,0:T(8,128)(2,1)}, bf16[1536,768]{1,0:T(8,128)(2,1)S(1)}, u32[]{:S(2)}, u32[]{:S(2)}) collective-permute-start(bf16[1536,768]{1,0:T(8,128)(2,1)} %bitcast.27), channel_id=1, source_target_pairs={{0,1},{1,0},{2,3},{3,2},{4,5},{5,4},{6,7},{7,6},{8,9},{9,8},{10,11... | collective-permute-start | bytes 7077896 | tf_op jit(solution)/shard_map/ppermute | solution.py:49
  17.1 1.1 %copy-start.9 = (bf16[1536,256]{1,0:T(8,128)(2,1)S(1)}, bf16[1536,256]{1,0:T(8,128)(2,1)}, u32[]{:S(2)}) copy-start(bf16[1536,256]{1,0:T(8,128)(2,1)} %refs_4_.1) | copy-start | bytes 2359300
  18.2 0.7 copy-start.12
  18.9 2.9 %copy-start.10 = (bf16[1536,256]{1,0:T(8,128)(2,1)S(1)}, bf16[1536,256]{1,0:T(8,128)(2,1)}, u32[]{:S(2)}) copy-start(bf16[1536,256]{1,0:T(8,128)(2,1)} %refs_4_.1) | copy-start | bytes 2359300
  18.9 2.9 %copy-start.11 = (bf16[128,1536]{1,0:T(8,128)(2,1)S(1)}, bf16[128,1536]{1,0:T(8,128)(2,1)}, u32[]{:S(2)}) copy-start(bf16[128,1536]{1,0:T(8,128)(2,1)} %refs_13_.1) | copy-start | bytes 1179652
  18.9 2.9 %copy-start.13 = (f32[1536]{0:T(1024)S(1)}, f32[1536]{0:T(1024)}, u32[]{:S(2)}) copy-start(f32[1536]{0:T(1024)} %refs_3_.5) | copy-start | bytes 18436
  19.7 6.4 %collective-permute-start.5 = (bf16[128,512]{1,0:T(8,128)(2,1)S(1)}, bf16[128,512]{1,0:T(8,128)(2,1)S(1)}, u32[]{:S(2)}, u32[]{:S(2)}) collective-permute-start(bf16[128,512]{1,0:T(8,128)(2,1)S(1)} %get-tuple-element.61), channel_id=1, source_target_pairs={{0,2},{1,3},{2,0},{3,1},{4,6},{5,7},{6,4},{7,5},{8,10},{9,11},{10,... | collective-permute-start | bytes 393224 | tf_op jit(solution)/shard_map/ppermute | solution.py:49
  22.6 8.2 %collective-permute-start.7 = (bf16[128,512]{1,0:T(8,128)(2,1)S(1)}, bf16[128,512]{1,0:T(8,128)(2,1)S(1)}, u32[]{:S(2)}, u32[]{:S(2)}) collective-permute-start(bf16[128,512]{1,0:T(8,128)(2,1)S(1)} %get-tuple-element.58), channel_id=1, source_target_pairs={{0,6},{1,7},{2,4},{3,5},{4,2},{5,3},{6,0},{7,1},{8,14},{9,15},{10,... | collective-permute-start | bytes 393224 | tf_op jit(solution)/shard_map/ppermute | solution.py:49
  24.1 6.7 %collective-permute-start.6 = (bf16[128,512]{1,0:T(8,128)(2,1)S(1)}, bf16[128,512]{1,0:T(8,128)(2,1)S(1)}, u32[]{:S(2)}, u32[]{:S(2)}) collective-permute-start(bf16[128,512]{1,0:T(8,128)(2,1)S(1)} %get-tuple-element.60), channel_id=1, source_target_pairs={{0,4},{1,5},{2,6},{3,7},{4,0},{5,1},{6,2},{7,3},{8,12},{9,13},{10,... | collective-permute-start | bytes 393224 | tf_op jit(solution)/shard_map/ppermute | solution.py:49
  26.1 4.7 %copy-start.2 = (s32[128,4]{0,1:T(4,128)S(1)}, s32[128,4]{0,1:T(4,128)}, u32[]{:S(2)}) copy-start(s32[128,4]{0,1:T(4,128)} %param.19) | copy-start | bytes 6148
  26.1 4.7 %copy-start.3 = (f32[128,4]{0,1:T(4,128)S(1)}, f32[128,4]{0,1:T(4,128)}, u32[]{:S(2)}) copy-start(f32[128,4]{0,1:T(4,128)} %param.20) | copy-start | bytes 6148
  26.1 4.7 %copy-start.4 = (s32[128]{0:T(128)S(1)}, s32[128]{0:T(128)}, u32[]{:S(2)}) copy-start(s32[128]{0:T(128)} %param.13) | copy-start | bytes 1540
  26.1 4.8 %copy-start.8 = (bf16[1,768,1536]{2,1,0:T(8,128)(2,1)S(1)}, bf16[1,768,1536]{2,1,0:T(8,128)(2,1)}, u32[]{:S(2)}) copy-start(bf16[1,768,1536]{2,1,0:T(8,128)(2,1)} %param.23) | copy-start | bytes 7077892
  26.1 4.9 %copy-start = (bf16[1536,192]{0,1:T(8,128)(2,1)S(1)}, bf16[1536,192]{0,1:T(8,128)(2,1)}, u32[]{:S(2)}) copy-start(bf16[1536,192]{0,1:T(8,128)(2,1)} %param.17) | copy-start | bytes 1769476
  30.9 16.7 %collective-permute-start.13 = (bf16[768,1536]{1,0:T(8,128)(2,1)S(1)}, bf16[768,1536]{1,0:T(8,128)(2,1)S(1)}, u32[]{:S(2)}, u32[]{:S(2)}) collective-permute-start(bf16[768,1536]{1,0:T(8,128)(2,1)S(1)} %bitcast.30), channel_id=1, source_target_pairs={{0,1},{1,0},{2,3},{3,2},{4,5},{5,4},{6,7},{7,6},{8,9},{9,8},{10,11... | collective-permute-start | bytes 7077896 | tf_op jit(solution)/shard_map/ppermute | solution.py:49
  31.0 15.7 %collective-permute-start.11 = (bf16[192,1536]{1,0:T(8,128)(2,1)S(1)}, bf16[192,1536]{1,0:T(8,128)(2,1)S(1)}, u32[]{:S(2)}, u32[]{:S(2)}) collective-permute-start(bf16[192,1536]{1,0:T(8,128)(2,1)S(1)} %bitcast.16), channel_id=1, source_target_pairs={{0,2},{1,3},{2,0},{3,1},{4,6},{5,7},{6,4},{7,5},{8,10},{9,11},{10,... | collective-permute-start | bytes 1769480 | tf_op jit(solution)/shard_map/ppermute | solution.py:49
  32.2 15.4 %collective-permute-start.12 = (bf16[192,1536]{1,0:T(8,128)(2,1)S(1)}, bf16[192,1536]{1,0:T(8,128)(2,1)S(1)}, u32[]{:S(2)}, u32[]{:S(2)}) collective-permute-start(bf16[192,1536]{1,0:T(8,128)(2,1)S(1)} %bitcast.17), channel_id=1, source_target_pairs={{0,4},{1,5},{2,6},{3,7},{4,0},{5,1},{6,2},{7,3},{8,12},{9,13},{10,... | collective-permute-start | bytes 1769480 | tf_op jit(solution)/shard_map/ppermute | solution.py:49
  33.2 14.4 %collective-permute-start.14 = (bf16[192,1536]{1,0:T(8,128)(2,1)S(1)}, bf16[192,1536]{1,0:T(8,128)(2,1)S(1)}, u32[]{:S(2)}, u32[]{:S(2)}) collective-permute-start(bf16[192,1536]{1,0:T(8,128)(2,1)S(1)} %bitcast.18), channel_id=1, source_target_pairs={{0,1},{1,0},{2,3},{3,2},{4,5},{5,4},{6,7},{7,6},{8,9},{9,8},{10,11... | collective-permute-start | bytes 1769480 | tf_op jit(solution)/shard_map/ppermute | solution.py:49
  33.2 7.2 %collective-permute-start.10 = (bf16[144,512]{1,0:T(8,128)(2,1)S(1)}, bf16[144,512]{1,0:T(8,128)(2,1)S(1)}, u32[]{:S(2)}, u32[]{:S(2)}) collective-permute-start(bf16[144,512]{1,0:T(8,128)(2,1)S(1)} %pack_kv.1.own.refs_4_.refs_0_), channel_id=1, source_target_pairs={{0,8},{8,16},{16,24},{1,9},{9,17},{17,25},{2,10},{10,18},{18,26},{... | collective-permute-start | bytes 442376 | tf_op jit(solution)/shard_map/ppermute | solution.py:511
  40.5 15.0 %collective-permute-start.24 = (bf16[144,512]{1,0:T(8,128)(2,1)S(1)}, bf16[144,512]{1,0:T(8,128)(2,1)S(1)}, u32[]{:S(2)}, u32[]{:S(2)}) collective-permute-start(bf16[144,512]{1,0:T(8,128)(2,1)S(1)} %pack_kv.1.own.refs_4_.refs_0_), channel_id=1, source_target_pairs={{0,1},{1,0},{2,3},{3,2},{4,5},{5,4},{6,7},{7,6},{8,9},{9,8},{10,11... | collective-permute-start | bytes 442376 | tf_op jit(solution)/shard_map/ppermute | solution.py:49
  46.7 9.3 %collective-permute-start.28 = (bf16[144,512]{1,0:T(8,128)(2,1)S(1)}, bf16[144,512]{1,0:T(8,128)(2,1)S(1)}, u32[]{:S(2)}, u32[]{:S(2)}) collective-permute-start(bf16[144,512]{1,0:T(8,128)(2,1)S(1)} %collective-permute-done.10.prev.refs_8_), channel_id=1, source_target_pairs={{0,1},{1,0},{2,3},{3,2},{4,5},{5,4},{6,7},{7,6},{8,9},{9,8},{10,11... | collective-permute-start | bytes 442376 | tf_op jit(solution)/shard_map/ppermute | solution.py:49
  47.7 7.7 %collective-permute-start.15 = (bf16[144,512]{1,0:T(8,128)(2,1)S(1)}, bf16[144,512]{1,0:T(8,128)(2,1)S(1)}, u32[]{:S(2)}, u32[]{:S(2)}) collective-permute-start(bf16[144,512]{1,0:T(8,128)(2,1)S(1)} %get-tuple-element.36.refs_2_), channel_id=1, source_target_pairs={{0,6},{1,7},{2,4},{3,5},{4,2},{5,3},{6,0},{7,1},{8,14},{9,15},{10,... | collective-permute-start | bytes 442376 | tf_op jit(solution)/shard_map/ppermute | solution.py:49
  49.6 7.8 %collective-permute-start.22 = (bf16[144,512]{1,0:T(8,128)(2,1)S(1)}, bf16[144,512]{1,0:T(8,128)(2,1)S(1)}, u32[]{:S(2)}, u32[]{:S(2)}) collective-permute-start(bf16[144,512]{1,0:T(8,128)(2,1)S(1)} %get-tuple-element.37.refs_0_), channel_id=1, source_target_pairs={{0,2},{1,3},{2,0},{3,1},{4,6},{5,7},{6,4},{7,5},{8,10},{9,11},{10,... | collective-permute-start | bytes 442376 | tf_op jit(solution)/shard_map/ppermute | solution.py:49
  50.3 7.1 %collective-permute-start.23 = (bf16[144,512]{1,0:T(8,128)(2,1)S(1)}, bf16[144,512]{1,0:T(8,128)(2,1)S(1)}, u32[]{:S(2)}, u32[]{:S(2)}) collective-permute-start(bf16[144,512]{1,0:T(8,128)(2,1)S(1)} %get-tuple-element.38.refs_1_), channel_id=1, source_target_pairs={{0,4},{1,5},{2,6},{3,7},{4,0},{5,1},{6,2},{7,3},{8,12},{9,13},{10,... | collective-permute-start | bytes 442376 | tf_op jit(solution)/shard_map/ppermute | solution.py:49
  55.4 5.5 %collective-permute-start.19 = (bf16[192,1536]{1,0:T(8,128)(2,1)S(1)}, bf16[192,1536]{1,0:T(8,128)(2,1)S(1)}, u32[]{:S(2)}, u32[]{:S(2)}) collective-permute-start(bf16[192,1536]{1,0:T(8,128)(2,1)S(1)} %collective-permute-done.12.refs_2_), channel_id=1, source_target_pairs={{0,1},{1,0},{2,3},{3,2},{4,5},{5,4},{6,7},{7,6},{8,9},{9,8},{10,11... | collective-permute-start | bytes 1769480 | tf_op jit(solution)/shard_map/ppermute | solution.py:49
  55.5 5.5 %collective-permute-start.18 = (bf16[192,1536]{1,0:T(8,128)(2,1)S(1)}, bf16[192,1536]{1,0:T(8,128)(2,1)S(1)}, u32[]{:S(2)}, u32[]{:S(2)}) collective-permute-start(bf16[192,1536]{1,0:T(8,128)(2,1)S(1)} %collective-permute-done.11.refs_1_), channel_id=1, source_target_pairs={{0,1},{1,0},{2,3},{3,2},{4,5},{5,4},{6,7},{7,6},{8,9},{9,8},{10,11... | collective-permute-start | bytes 1769480 | tf_op jit(solution)/shard_map/ppermute | solution.py:49
  56.1 2.7 %collective-permute-start.27 = (bf16[144,512]{1,0:T(8,128)(2,1)S(1)}, bf16[144,512]{1,0:T(8,128)(2,1)S(1)}, u32[]{:S(2)}, u32[]{:S(2)}) collective-permute-start(bf16[144,512]{1,0:T(8,128)(2,1)S(1)} %hold.9.refs_7_.refs_1_), channel_id=1, source_target_pairs={{0,1},{1,0},{2,3},{3,2},{4,5},{5,4},{6,7},{7,6},{8,9},{9,8},{10,11... | collective-permute-start | bytes 442376 | tf_op jit(solution)/shard_map/ppermute | solution.py:49
  57.4 2.1 %collective-permute-start.25 = (bf16[144,512]{1,0:T(8,128)(2,1)S(1)}, bf16[144,512]{1,0:T(8,128)(2,1)S(1)}, u32[]{:S(2)}, u32[]{:S(2)}) collective-permute-start(bf16[144,512]{1,0:T(8,128)(2,1)S(1)} %collective-permute-done.22.refs_5_.refs_0_), channel_id=1, source_target_pairs={{0,1},{1,0},{2,3},{3,2},{4,5},{5,4},{6,7},{7,6},{8,9},{9,8},{10,11... | collective-permute-start | bytes 442376 | tf_op jit(solution)/shard_map/ppermute | solution.py:49
  57.4 15.0 %copy-start.5 = (s32[1,64]{1,0:T(1,128)S(1)}, s32[1,64]{1,0:T(1,128)}, u32[]{:S(2)}) copy-start(s32[1,64]{1,0:T(1,128)} %table_ref.1) | copy-start | bytes 772
  57.4 9.5 %collective-permute-start.17 = (bf16[96,1536]{1,0:T(8,128)(2,1)S(1)}, bf16[96,1536]{1,0:T(8,128)(2,1)S(1)}, u32[]{:S(2)}, u32[]{:S(2)}) collective-permute-start(bf16[96,1536]{1,0:T(8,128)(2,1)S(1)} %hold.11), channel_id=1, source_target_pairs={{0,4},{1,5},{2,6},{3,7},{4,0},{5,1},{6,2},{7,3},{8,12},{9,13},{10,... | collective-permute-start | bytes 884744 | tf_op jit(solution)/shard_map/ppermute | solution.py:49
  58.8 8.8 %collective-permute-start.16 = (bf16[96,1536]{1,0:T(8,128)(2,1)S(1)}, bf16[96,1536]{1,0:T(8,128)(2,1)S(1)}, u32[]{:S(2)}, u32[]{:S(2)}) collective-permute-start(bf16[96,1536]{1,0:T(8,128)(2,1)S(1)} %hold.10), channel_id=1, source_target_pairs={{0,2},{1,3},{2,0},{3,1},{4,6},{5,7},{6,4},{7,5},{8,10},{9,11},{10,... | collective-permute-start | bytes 884744 | tf_op jit(solution)/shard_map/ppermute | solution.py:49
  59.5 1.4 %collective-permute-start.26 = (bf16[144,512]{1,0:T(8,128)(2,1)S(1)}, bf16[144,512]{1,0:T(8,128)(2,1)S(1)}, u32[]{:S(2)}, u32[]{:S(2)}) collective-permute-start(bf16[144,512]{1,0:T(8,128)(2,1)S(1)} %collective-permute-done.23.refs_6_.refs_1_), channel_id=1, source_target_pairs={{0,1},{1,0},{2,3},{3,2},{4,5},{5,4},{6,7},{7,6},{8,9},{9,8},{10,11... | collective-permute-start | bytes 442376 | tf_op jit(solution)/shard_map/ppermute | solution.py:49
  60.8 9.7 %collective-permute-start.33 = (bf16[256,512]{1,0:T(8,128)(2,1)S(1)}, bf16[256,512]{1,0:T(8,128)(2,1)S(1)}, u32[]{:S(2)}, u32[]{:S(2)}) collective-permute-start(bf16[256,512]{1,0:T(8,128)(2,1)S(1)} %project.3.refs_0_), channel_id=1, source_target_pairs={{0,1},{1,0},{2,3},{3,2},{4,5},{5,4},{6,7},{7,6},{8,9},{9,8},{10,11... | collective-permute-start | bytes 786440 | tf_op jit(solution)/shard_map/ppermute | solution.py:49
  67.6 10.1 %collective-permute-start.29 = (bf16[128,1536]{1,0:T(8,128)(2,1)S(1)}, bf16[128,1536]{1,0:T(8,128)(2,1)S(1)}, u32[]{:S(2)}, u32[]{:S(2)}) collective-permute-start(bf16[128,1536]{1,0:T(8,128)(2,1)S(1)} %attend.1.refs_10_), channel_id=1, source_target_pairs={{0,4},{1,5},{2,6},{3,7},{4,0},{5,1},{6,2},{7,3},{8,12},{9,13},{10,... | collective-permute-start | bytes 1179656 | tf_op jit(solution)/shard_map/ppermute | solution.py:49
  68.7 10.1 %collective-permute-start.31 = (bf16[128,1536]{1,0:T(8,128)(2,1)S(1)}, bf16[128,1536]{1,0:T(8,128)(2,1)S(1)}, u32[]{:S(2)}, u32[]{:S(2)}) collective-permute-start(bf16[128,1536]{1,0:T(8,128)(2,1)S(1)} %attend.1.refs_10_), channel_id=1, source_target_pairs={{0,2},{1,3},{2,0},{3,1},{4,6},{5,7},{6,4},{7,5},{8,10},{9,11},{10,... | collective-permute-start | bytes 1179656 | tf_op jit(solution)/shard_map/ppermute | solution.py:49
  70.0 4.5 %collective-permute-start.21 = (bf16[96,1536]{1,0:T(8,128)(2,1)S(1)}, bf16[96,1536]{1,0:T(8,128)(2,1)S(1)}, u32[]{:S(2)}, u32[]{:S(2)}) collective-permute-start(bf16[96,1536]{1,0:T(8,128)(2,1)S(1)} %collective-permute-done.17.refs_4_), channel_id=1, source_target_pairs={{0,1},{1,0},{2,3},{3,2},{4,5},{5,4},{6,7},{7,6},{8,9},{9,8},{10,11... | collective-permute-start | bytes 884744 | tf_op jit(solution)/shard_map/ppermute | solution.py:49
  70.0 4.5 %collective-permute-start.20 = (bf16[96,1536]{1,0:T(8,128)(2,1)S(1)}, bf16[96,1536]{1,0:T(8,128)(2,1)S(1)}, u32[]{:S(2)}, u32[]{:S(2)}) collective-permute-start(bf16[96,1536]{1,0:T(8,128)(2,1)S(1)} %collective-permute-done.16.refs_3_), channel_id=1, source_target_pairs={{0,1},{1,0},{2,3},{3,2},{4,5},{5,4},{6,7},{7,6},{8,9},{9,8},{10,11... | collective-permute-start | bytes 884744 | tf_op jit(solution)/shard_map/ppermute | solution.py:49
  70.5 1.9 %collective-permute-start.34 = (bf16[256,512]{1,0:T(8,128)(2,1)S(1)}, bf16[256,512]{1,0:T(8,128)(2,1)S(1)}, u32[]{:S(2)}, u32[]{:S(2)}) collective-permute-start(bf16[256,512]{1,0:T(8,128)(2,1)S(1)} %project.2.refs_6_.refs_1_), channel_id=1, source_target_pairs={{0,1},{1,0},{2,3},{3,2},{4,5},{5,4},{6,7},{7,6},{8,9},{9,8},{10,11... | collective-permute-start | bytes 786440 | tf_op jit(solution)/shard_map/ppermute | solution.py:49
  74.4 11.9 %copy-start.6 = (bf16[1,1536,768]{2,1,0:T(8,128)(2,1)S(1)}, bf16[1,1536,768]{2,1,0:T(8,128)(2,1)}, u32[]{:S(2)}) copy-start(bf16[1,1536,768]{2,1,0:T(8,128)(2,1)} %param.21) | copy-start | bytes 7077892
  74.4 11.9 %copy-start.7 = (bf16[1,1536,768]{2,1,0:T(8,128)(2,1)S(1)}, bf16[1,1536,768]{2,1,0:T(8,128)(2,1)}, u32[]{:S(2)}) copy-start(bf16[1,1536,768]{2,1,0:T(8,128)(2,1)} %param.22) | copy-start | bytes 7077892
  74.4 11.9 %copy-start.14 = (f32[1536]{0:T(1024)S(1)}, f32[1536]{0:T(1024)}, u32[]{:S(2)}) copy-start(f32[1536]{0:T(1024)} %refs_3_.7) | copy-start | bytes 18436
  78.9 12.8 %collective-permute-start.35 = (bf16[128,512]{1,0:T(8,128)(2,1)S(1)}, bf16[128,512]{1,0:T(8,128)(2,1)S(1)}, u32[]{:S(2)}, u32[]{:S(2)}) collective-permute-start(bf16[128,512]{1,0:T(8,128)(2,1)S(1)} %get-tuple-element.56), channel_id=1, source_target_pairs={{6,4},{7,5},{14,12},{15,13},{22,20},{23,21},{30,28},{31,29}} | collective-permute-start | bytes 393224 | tf_op jit(solution)/shard_map/ppermute | solution.py:536
  79.5 12.3 %collective-permute-start.36 = (bf16[128,512]{1,0:T(8,128)(2,1)S(1)}, bf16[128,512]{1,0:T(8,128)(2,1)S(1)}, u32[]{:S(2)}, u32[]{:S(2)}) collective-permute-start(bf16[128,512]{1,0:T(8,128)(2,1)S(1)} %get-tuple-element.55), channel_id=1, source_target_pairs={{6,2},{7,3},{14,10},{15,11},{22,18},{23,19},{30,26},{31,27}} | collective-permute-start | bytes 393224 | tf_op jit(solution)/shard_map/ppermute | solution.py:536
  80.2 11.7 %collective-permute-start.37 = (bf16[128,512]{1,0:T(8,128)(2,1)S(1)}, bf16[128,512]{1,0:T(8,128)(2,1)S(1)}, u32[]{:S(2)}, u32[]{:S(2)}) collective-permute-start(bf16[128,512]{1,0:T(8,128)(2,1)S(1)} %get-tuple-element.54), channel_id=1, source_target_pairs={{6,0},{7,1},{14,8},{15,9},{22,16},{23,17},{30,24},{31,25}} | collective-permute-start | bytes 393224 | tf_op jit(solution)/shard_map/ppermute | solution.py:536
  81.7 10.9 %collective-permute-start.30 = (bf16[64,1536]{1,0:T(8,128)(2,1)S(1)}, bf16[64,1536]{1,0:T(8,128)(2,1)S(1)}, u32[]{:S(2)}, u32[]{:S(2)}) collective-permute-start(bf16[64,1536]{1,0:T(8,128)(2,1)S(1)} %slice.64), channel_id=1, source_target_pairs={{0,2},{1,3},{2,0},{3,1},{4,6},{5,7},{6,4},{7,5},{8,10},{9,11},{10,... | collective-permute-start | bytes 589832 | tf_op jit(solution)/shard_map/ppermute | solution.py:49
  83.0 9.6 %collective-permute-start.32 = (bf16[64,1536]{1,0:T(8,128)(2,1)S(1)}, bf16[64,1536]{1,0:T(8,128)(2,1)S(1)}, u32[]{:S(2)}, u32[]{:S(2)}) collective-permute-start(bf16[64,1536]{1,0:T(8,128)(2,1)S(1)} %slice.65), channel_id=1, source_target_pairs={{0,4},{1,5},{2,6},{3,7},{4,0},{5,1},{6,2},{7,3},{8,12},{9,13},{10,... | collective-permute-start | bytes 589832 | tf_op jit(solution)/shard_map/ppermute | solution.py:49
  91.7 10.6 %collective-permute-start.38 = (bf16[128,1536]{1,0:T(8,128)(2,1)S(1)}, bf16[128,1536]{1,0:T(8,128)(2,1)S(1)}, u32[]{:S(2)}, u32[]{:S(2)}) collective-permute-start(bf16[128,1536]{1,0:T(8,128)(2,1)S(1)} %get-tuple-element.47.refs_16_), channel_id=1, source_target_pairs={{0,2},{1,3},{2,0},{3,1},{4,6},{5,7},{6,4},{7,5},{8,10},{9,11},{10,... | collective-permute-start | bytes 1179656 | tf_op jit(solution)/shard_map/ppermute | solution.py:49
  91.8 10.6 %collective-permute-start.39 = (bf16[128,1536]{1,0:T(8,128)(2,1)S(1)}, bf16[128,1536]{1,0:T(8,128)(2,1)S(1)}, u32[]{:S(2)}, u32[]{:S(2)}) collective-permute-start(bf16[128,1536]{1,0:T(8,128)(2,1)S(1)} %get-tuple-element.52), channel_id=1, source_target_pairs={{0,4},{1,5},{2,6},{3,7},{4,0},{5,1},{6,2},{7,3},{8,12},{9,13},{10,... | collective-permute-start | bytes 1179656 | tf_op jit(solution)/shard_map/ppermute | solution.py:49
  92.6 0.9 copy-start.1
  98.9 10.6 %collective-permute-start.40 = (bf16[128,1536]{1,0:T(8,128)(2,1)S(1)}, bf16[128,1536]{1,0:T(8,128)(2,1)S(1)}, u32[]{:S(2)}, u32[]{:S(2)}) collective-permute-start(bf16[128,1536]{1,0:T(8,128)(2,1)S(1)} %get-tuple-element.53), channel_id=1, source_target_pairs={{0,6},{1,7},{2,4},{3,5},{4,2},{5,3},{6,0},{7,1},{8,14},{9,15},{10,... | collective-permute-start | bytes 1179656 | tf_op jit(solution)/shard_map/ppermute | solution.py:49

commit v6 on v5

--- a/solution.py
+++ b/solution.py
@@ -534,7 +534,6 @@
     for by in (1, 2, 3):
         pairs = [(last * CORES + k, (last ^ by) * CORES + k) for k in range(CORES)]
         pages.append(lax.ppermute(paged[last ^ by], "tensor", pairs))
-    pages = join_call(pages)
     w_other += [hop(w, 1) for w in w_diagonal]
     w_all = assemble_call([w_own, w_x, w_y] + w_diagonal, w_other)
 
@@ -546,9 +545,10 @@
     back_x, back_y = hold_call(chips(out_x, 1)), hold_call(chips(out_y, 2))
     out, out_xy = expert_call(
         (context, *context_xy), (tokens, *tokens_xy), (own_kv, kv_xy), w_all, moe_gain, weights,
-        (jnp.float32, jnp.bfloat16), out_x, pages,
+        (jnp.float32, jnp.bfloat16), out_x, *pages[1:],
     )
     back_xy = chips(out_xy, 3)
+    pages = join_call(after(pages, out_xy))
     mixed = mix_call((out, back_x, back_y, back_xy))
     return (mixed, pages.reshape(rows // PAGE, PAGE, pages.shape[1]))
 

time: 111 us -> 111 us (level)
    unnamed x30 -> x28, local copies, waits for them, and re-layouts: 2.8 us -> 1.9 us
  transfers between devices with their start and end apart: 41 -> 41, of which waited for: 17 -> 18; matrix products, arithmetic and copies ran while one was open for 0% -> 0% of each run, Pallas kernels for 15% -> 15%
where the time goes in v6:
time: 111 us; the launch traced here: 110 us
  waiting for transfers between devices  51.4 us (46%)
  starting transfers between devices  37.8 us (34%)
  Pallas kernels  18.1 us (16%)
  local copies, waits for them, and re-layouts  2.07 us (2%)
    ppermute x37, waiting for transfers between devices, hop(): return lax.ppermute(value, 'tensor', [(i, i ^ by) for i in range(length)])  47.6 us
    ppermute x37, starting transfers between devices, hop(): return lax.ppermute(value, 'tensor', [(i, i ^ by) for i in range(length)])  31.5 us
    pallas_call x2, Pallas kernels, expert_call(): pl.pallas_call(functools.partial(expert_kernel, 256, len(context), len(to...  10.7 us
    ppermute x1, waiting for transfers between devices, chip_body(): lax.ppermute(own_kv, 'seq', [(i, i + 1) for i in range(seq_size - 1)])  3.75 us
    ppermute x1, starting transfers between devices, chip_body(): lax.ppermute(own_kv, 'seq', [(i, i + 1) for i in range(seq_size - 1)])  3.46 us
    ppermute x3, starting transfers between devices, chip_body(): pages.append(lax.ppermute(paged[last ^ by], 'tensor', pairs))  2.81 us
  transfers between devices with their start and end apart: 41, of which 18 were waited for; matrix products, arithmetic and copies ran while one was open for 0% of the time, Pallas kernels for 15%

profile of v6, /device:TPU:0, one launch (start us, length us, event | category | flops | bytes accessed | tf_op | source)
XLA Modules:
  0.0 110.4 jit_solution(4273208754431847337)
XLA Ops:
  0.6 0.5 collective-permute-start.4
  1.1 2.6 %collective-permute-start.2 = (bf16[128,1536]{1,0:T(8,128)(2,1)}, bf16[128,1536]{1,0:T(8,128)(2,1)S(1)}, u32[]{:S(2)}, u32[]{:S(2)}) collective-permute-start(bf16[128,1536]{1,0:T(8,128)(2,1)} %refs_13_.1), channel_id=1, source_target_pairs={{0,2},{1,3},{2,0},{3,1},{4,6},{5,7},{6,4},{7,5},{8,10},{9,11},{10,... | collective-permute-start | bytes 1179656 | tf_op jit(solution)/shard_map/ppermute | solution.py:49
  3.7 1.5 %collective-permute-start = (bf16[128,1536]{1,0:T(8,128)(2,1)}, bf16[128,1536]{1,0:T(8,128)(2,1)S(1)}, u32[]{:S(2)}, u32[]{:S(2)}) collective-permute-start(bf16[128,1536]{1,0:T(8,128)(2,1)} %refs_13_.1), channel_id=1, source_target_pairs={{0,4},{1,5},{2,6},{3,7},{4,0},{5,1},{6,2},{7,3},{8,12},{9,13},{10,... | collective-permute-start | bytes 1179656 | tf_op jit(solution)/shard_map/ppermute | solution.py:49
  5.2 8.4 %collective-permute-done.2.refs_0_.refs_12_ = bf16[128,1536]{1,0:T(8,128)(2,1)S(1)} collective-permute-done((bf16[128,1536]{1,0:T(8,128)(2,1)}, bf16[128,1536]{1,0:T(8,128)(2,1)S(1)}, u32[]{:S(2)}, u32[]{:S(2)}) %collective-permute-start.2) | collective-permute-done | bytes 393248 | tf_op jit(solution)/shard_map/ppermute | solution.py:49
  13.6 1.9 %collective-permute-start.3 = (bf16[64,1536]{1,0:T(8,128)(2,1)S(1)}, bf16[64,1536]{1,0:T(8,128)(2,1)S(1)}, u32[]{:S(2)}, u32[]{:S(2)}) collective-permute-start(bf16[64,1536]{1,0:T(8,128)(2,1)S(1)} %slice.57), channel_id=1, source_target_pairs={{0,4},{1,5},{2,6},{3,7},{4,0},{5,1},{6,2},{7,3},{8,12},{9,13},{10,... | collective-permute-start | bytes 589832 | tf_op jit(solution)/shard_map/ppermute | solution.py:49
  15.5 1.6 %collective-permute-start.1 = (bf16[64,1536]{1,0:T(8,128)(2,1)S(1)}, bf16[64,1536]{1,0:T(8,128)(2,1)S(1)}, u32[]{:S(2)}, u32[]{:S(2)}) collective-permute-start(bf16[64,1536]{1,0:T(8,128)(2,1)S(1)} %slice.56), channel_id=1, source_target_pairs={{0,2},{1,3},{2,0},{3,1},{4,6},{5,7},{6,4},{7,5},{8,10},{9,11},{10,... | collective-permute-start | bytes 589832 | tf_op jit(solution)/shard_map/ppermute | solution.py:49
  17.1 1.1 %copy-done.8 = bf16[1536,256]{1,0:T(8,128)(2,1)S(1)} copy-done((bf16[1536,256]{1,0:T(8,128)(2,1)S(1)}, bf16[1536,256]{1,0:T(8,128)(2,1)}, u32[]{:S(2)}) %copy-start.8) | copy-done | bytes 786456
  18.2 0.7 copy-done.11
  18.9 0.7 project.2.refs_6_.refs_1_
  19.7 0.6 collective-permute-start.5
  20.3 0.1 collective-permute-done.3.refs_2_.refs_15_
  20.4 1.4 %collective-permute-done.1.refs_1_.refs_14_ = bf16[64,1536]{1,0:T(8,128)(2,1)S(1)} collective-permute-done((bf16[64,1536]{1,0:T(8,128)(2,1)S(1)}, bf16[64,1536]{1,0:T(8,128)(2,1)S(1)}, u32[]{:S(2)}, u32[]{:S(2)}) %collective-permute-start.1) | collective-permute-done | bytes 196640 | tf_op jit(solution)/shard_map/ppermute | solution.py:49
  21.8 0.7 project.3.refs_0_
  22.6 1.5 %collective-permute-start.7 = (bf16[128,512]{1,0:T(8,128)(2,1)S(1)}, bf16[128,512]{1,0:T(8,128)(2,1)S(1)}, u32[]{:S(2)}, u32[]{:S(2)}) collective-permute-start(bf16[128,512]{1,0:T(8,128)(2,1)S(1)} %get-tuple-element.66), channel_id=1, source_target_pairs={{0,6},{1,7},{2,4},{3,5},{4,2},{5,3},{6,0},{7,1},{8,14},{9,15},{10,... | collective-permute-start | bytes 393224 | tf_op jit(solution)/shard_map/ppermute | solution.py:49
  24.1 1.5 %collective-permute-start.6 = (bf16[128,512]{1,0:T(8,128)(2,1)S(1)}, bf16[128,512]{1,0:T(8,128)(2,1)S(1)}, u32[]{:S(2)}, u32[]{:S(2)}) collective-permute-start(bf16[128,512]{1,0:T(8,128)(2,1)S(1)} %get-tuple-element.68), channel_id=1, source_target_pairs={{0,4},{1,5},{2,6},{3,7},{4,0},{5,1},{6,2},{7,3},{8,12},{9,13},{10,... | collective-permute-start | bytes 393224 | tf_op jit(solution)/shard_map/ppermute | solution.py:49
  25.6 0.5 collective-permute-done.5.in_ref
  26.1 0.0 copy-start.1
  26.1 0.0 copy-start.2
  26.1 4.6 %collective-permute-done.6.in_ref = bf16[128,512]{1,0:T(8,128)(2,1)S(1)} collective-permute-done((bf16[128,512]{1,0:T(8,128)(2,1)S(1)}, bf16[128,512]{1,0:T(8,128)(2,1)S(1)}, u32[]{:S(2)}, u32[]{:S(2)}) %collective-permute-start.6) | collective-permute-done | bytes 131104 | tf_op jit(solution)/shard_map/ppermute | solution.py:49
  30.8 0.1 pack_kv.1.own.refs_4_.refs_0_
  30.9 0.1 collective-permute-start.13
  31.0 1.2 %collective-permute-start.11 = (bf16[192,1536]{1,0:T(8,128)(2,1)S(1)}, bf16[192,1536]{1,0:T(8,128)(2,1)S(1)}, u32[]{:S(2)}, u32[]{:S(2)}) collective-permute-start(bf16[192,1536]{1,0:T(8,128)(2,1)S(1)} %bitcast.16), channel_id=1, source_target_pairs={{0,2},{1,3},{2,0},{3,1},{4,6},{5,7},{6,4},{7,5},{8,10},{9,11},{10,... | collective-permute-start | bytes 1769480 | tf_op jit(solution)/shard_map/ppermute | solution.py:49
  32.2 1.0 collective-permute-start.12
  33.2 3.5 %collective-permute-start.10 = (bf16[144,512]{1,0:T(8,128)(2,1)S(1)}, bf16[144,512]{1,0:T(8,128)(2,1)S(1)}, u32[]{:S(2)}, u32[]{:S(2)}) collective-permute-start(bf16[144,512]{1,0:T(8,128)(2,1)S(1)} %pack_kv.1.own.refs_4_.refs_0_), channel_id=1, source_target_pairs={{0,8},{8,16},{16,24},{1,9},{9,17},{17,25},{2,10},{10,18},{18,26},{... | collective-permute-start | bytes 442376 | tf_op jit(solution)/shard_map/ppermute | solution.py:511
  36.7 3.8 %collective-permute-done.10.prev.refs_8_ = bf16[144,512]{1,0:T(8,128)(2,1)S(1)} collective-permute-done((bf16[144,512]{1,0:T(8,128)(2,1)S(1)}, bf16[144,512]{1,0:T(8,128)(2,1)S(1)}, u32[]{:S(2)}, u32[]{:S(2)}) %collective-permute-start.10) | collective-permute-done | bytes 147488 | tf_op jit(solution)/shard_map/ppermute | solution.py:511
  40.5 6.3 %collective-permute-done.11.refs_1_ = bf16[192,1536]{1,0:T(8,128)(2,1)S(1)} collective-permute-done((bf16[192,1536]{1,0:T(8,128)(2,1)S(1)}, bf16[192,1536]{1,0:T(8,128)(2,1)S(1)}, u32[]{:S(2)}, u32[]{:S(2)}) %collective-permute-start.11) | collective-permute-done | bytes 589856 | tf_op jit(solution)/shard_map/ppermute | solution.py:49
  46.8 0.8 collective-permute-done.12.refs_2_
  47.7 0.1 choose_kv.1
  47.7 1.9 %collective-permute-start.15 = (bf16[144,512]{1,0:T(8,128)(2,1)S(1)}, bf16[144,512]{1,0:T(8,128)(2,1)S(1)}, u32[]{:S(2)}, u32[]{:S(2)}) collective-permute-start(bf16[144,512]{1,0:T(8,128)(2,1)S(1)} %get-tuple-element.40.refs_2_), channel_id=1, source_target_pairs={{0,6},{1,7},{2,4},{3,5},{4,2},{5,3},{6,0},{7,1},{8,14},{9,15},{10,... | collective-permute-start | bytes 442376 | tf_op jit(solution)/shard_map/ppermute | solution.py:49
  49.6 0.7 collective-permute-start.22
  50.3 1.0 collective-permute-start.23
  51.3 4.1 %collective-permute-done.15.in_ref = bf16[144,512]{1,0:T(8,128)(2,1)S(1)} collective-permute-done((bf16[144,512]{1,0:T(8,128)(2,1)S(1)}, bf16[144,512]{1,0:T(8,128)(2,1)S(1)}, u32[]{:S(2)}, u32[]{:S(2)}) %collective-permute-start.15) | collective-permute-done | bytes 147488 | tf_op jit(solution)/shard_map/ppermute | solution.py:49
  55.5 0.6 collective-permute-start.18
  56.1 0.1 collective-permute-start.27
  56.1 1.2 %collective-permute-done.22.refs_5_.refs_0_ = bf16[144,512]{1,0:T(8,128)(2,1)S(1)} collective-permute-done((bf16[144,512]{1,0:T(8,128)(2,1)S(1)}, bf16[144,512]{1,0:T(8,128)(2,1)S(1)}, u32[]{:S(2)}, u32[]{:S(2)}) %collective-permute-start.22) | collective-permute-done | bytes 147488 | tf_op jit(solution)/shard_map/ppermute | solution.py:49
  57.4 1.4 %collective-permute-start.17 = (bf16[96,1536]{1,0:T(8,128)(2,1)S(1)}, bf16[96,1536]{1,0:T(8,128)(2,1)S(1)}, u32[]{:S(2)}, u32[]{:S(2)}) collective-permute-start(bf16[96,1536]{1,0:T(8,128)(2,1)S(1)} %hold.11), channel_id=1, source_target_pairs={{0,4},{1,5},{2,6},{3,7},{4,0},{5,1},{6,2},{7,3},{8,12},{9,13},{10,... | collective-permute-start | bytes 884744 | tf_op jit(solution)/shard_map/ppermute | solution.py:49
  58.8 0.7 collective-permute-start.16
  59.5 1.4 %collective-permute-done.26.refs_11_ = bf16[144,512]{1,0:T(8,128)(2,1)S(1)} collective-permute-done((bf16[144,512]{1,0:T(8,128)(2,1)S(1)}, bf16[144,512]{1,0:T(8,128)(2,1)S(1)}, u32[]{:S(2)}, u32[]{:S(2)}) %collective-permute-start.26) | collective-permute-done | bytes 147488 | tf_op jit(solution)/shard_map/ppermute | solution.py:49
  60.8 0.1 collective-permute-start.33
  61.0 1.7 %attend.1.refs_10_ = bf16[128,1536]{1,0:T(8,128)(2,1)S(1)} custom-call(bf16[128,512]{1,0:T(8,128)(2,1)S(1)} %get-tuple-element.33.own.refs_0_, bf16[128,512]{1,0:T(8,128)(2,1)S(1)} %hold.7.by_x.refs_1_, bf16[128,512]{1,0:T(8,128)(2,1)S(1)} %hold.8.by_y.refs_2_, bf16[128,512]{1,0:T(8,128)(2,1)S(1)} %collective-permute-done.7.by_xy.refs_3_, ...), custom_call_target="tpu_custom_call" | custom-call | tf_op jit(solution)/shard_map/attend/pallas_call | solution.py:267
  62.7 4.2 %collective-permute-done.17.refs_4_ = bf16[96,1536]{1,0:T(8,128)(2,1)S(1)} collective-permute-done((bf16[96,1536]{1,0:T(8,128)(2,1)S(1)}, bf16[96,1536]{1,0:T(8,128)(2,1)S(1)}, u32[]{:S(2)}, u32[]{:S(2)}) %collective-permute-start.17) | collective-permute-done | bytes 294944 | tf_op jit(solution)/shard_map/ppermute | solution.py:49
  66.9 0.6 collective-permute-done.16.refs_3_
  67.6 1.1 collective-permute-start.29
  68.7 1.3 %collective-permute-start.31 = (bf16[128,1536]{1,0:T(8,128)(2,1)S(1)}, bf16[128,1536]{1,0:T(8,128)(2,1)S(1)}, u32[]{:S(2)}, u32[]{:S(2)}) collective-permute-start(bf16[128,1536]{1,0:T(8,128)(2,1)S(1)} %attend.1.refs_10_), channel_id=1, source_target_pairs={{0,2},{1,3},{2,0},{3,1},{4,6},{5,7},{6,4},{7,5},{8,10},{9,11},{10,... | collective-permute-start | bytes 1179656 | tf_op jit(solution)/shard_map/ppermute | solution.py:49
  70.0 0.5 collective-permute-start.20
  70.5 1.9 %collective-permute-done.34.refs_3_ = bf16[256,512]{1,0:T(8,128)(2,1)S(1)} collective-permute-done((bf16[256,512]{1,0:T(8,128)(2,1)S(1)}, bf16[256,512]{1,0:T(8,128)(2,1)S(1)}, u32[]{:S(2)}, u32[]{:S(2)}) %collective-permute-start.34) | collective-permute-done | bytes 262176 | tf_op jit(solution)/shard_map/ppermute | solution.py:49
  72.4 2.1 %cache_pages.1 = bf16[4,128,512]{2,1,0:T(8,128)(2,1)S(1)} custom-call(s32[1,64]{1,0:T(1,128)S(1)} %copy-done.4, bf16[256,512]{1,0:T(8,128)(2,1)S(1)} %project.3.refs_0_, bf16[256,512]{1,0:T(8,128)(2,1)S(1)} %project.2.refs_6_.refs_1_, bf16[256,512]{1,0:T(8,128)(2,1)S(1)} %collective-permute-done.33.refs_2_, bf16[256,512]{1,0:T(8,128)(2,1)S(1)} %collective-permute-done.34.refs_3_), custom_call_target="tpu_custom_call" | custom-call | tf_op jit(solution)/shard_map/cache_pages/pallas_call | solution.py:431
  74.5 0.3 assemble_w_out.1.refs_2_
  74.8 2.8 %collective-permute-done.29.refs_11_ = bf16[128,1536]{1,0:T(8,128)(2,1)S(1)} collective-permute-done((bf16[128,1536]{1,0:T(8,128)(2,1)S(1)}, bf16[128,1536]{1,0:T(8,128)(2,1)S(1)}, u32[]{:S(2)}, u32[]{:S(2)}) %collective-permute-start.29) | collective-permute-done | bytes 393248 | tf_op jit(solution)/shard_map/ppermute | solution.py:49
  77.7 1.1 %collective-permute-done.31.refs_10_ = bf16[128,1536]{1,0:T(8,128)(2,1)S(1)} collective-permute-done((bf16[128,1536]{1,0:T(8,128)(2,1)S(1)}, bf16[128,1536]{1,0:T(8,128)(2,1)S(1)}, u32[]{:S(2)}, u32[]{:S(2)}) %collective-permute-start.31) | collective-permute-done | bytes 393248 | tf_op jit(solution)/shard_map/ppermute | solution.py:49
  78.8 0.7 collective-permute-start.35
  79.5 0.7 collective-permute-start.36
  80.2 1.5 %collective-permute-start.37 = (bf16[128,512]{1,0:T(8,128)(2,1)S(1)}, bf16[128,512]{1,0:T(8,128)(2,1)S(1)}, u32[]{:S(2)}, u32[]{:S(2)}) collective-permute-start(bf16[128,512]{1,0:T(8,128)(2,1)S(1)} %get-tuple-element.63), channel_id=1, source_target_pairs={{6,0},{7,1},{14,8},{15,9},{22,16},{23,17},{30,24},{31,25}} | collective-permute-start | bytes 393224 | tf_op jit(solution)/shard_map/ppermute | solution.py:536
  81.7 1.3 %collective-permute-start.30 = (bf16[64,1536]{1,0:T(8,128)(2,1)S(1)}, bf16[64,1536]{1,0:T(8,128)(2,1)S(1)}, u32[]{:S(2)}, u32[]{:S(2)}) collective-permute-start(bf16[64,1536]{1,0:T(8,128)(2,1)S(1)} %slice.64), channel_id=1, source_target_pairs={{0,2},{1,3},{2,0},{3,1},{4,6},{5,7},{6,4},{7,5},{8,10},{9,11},{10,... | collective-permute-start | bytes 589832 | tf_op jit(solution)/shard_map/ppermute | solution.py:49
  83.0 3.3 %collective-permute-start.32 = (bf16[64,1536]{1,0:T(8,128)(2,1)S(1)}, bf16[64,1536]{1,0:T(8,128)(2,1)S(1)}, u32[]{:S(2)}, u32[]{:S(2)}) collective-permute-start(bf16[64,1536]{1,0:T(8,128)(2,1)S(1)} %slice.65), channel_id=1, source_target_pairs={{0,4},{1,5},{2,6},{3,7},{4,0},{5,1},{6,2},{7,3},{8,12},{9,13},{10,... | collective-permute-start | bytes 589832 | tf_op jit(solution)/shard_map/ppermute | solution.py:49
  86.4 5.3 %experts.2 = (bf16[128,1536]{1,0:T(8,128)(2,1)S(1)}, bf16[128,1536]{1,0:T(8,128)(2,1)S(1)}) custom-call(bf16[144,512]{1,0:T(8,128)(2,1)S(1)} %collective-permute-done.22.refs_5_.refs_0_, bf16[144,512]{1,0:T(8,128)(2,1)S(1)} %collective-permute-done.23.refs_6_.refs_1_, bf16[1536,1536]{1,0:T(8,128)(2,1)S(1)} %assemble_w_out.1.refs_2_, f32[1536]{0:T(1024)S(1)} %copy-done.13, ...), custom_call_target="tpu_custom_call" | custom-call | flops 20000000000 | bytes 1 | tf_op jit(solution)/shard_map/experts/pallas_call | solution.py:368
  91.7 0.1 collective-permute-start.38
  91.8 0.1 collective-permute-start.39
  91.9 5.4 %experts.3 = (f32[128,1536]{1,0:T(8,128)S(1)}, bf16[128,1536]{1,0:T(8,128)(2,1)S(1)}) custom-call(bf16[144,512]{1,0:T(8,128)(2,1)S(1)} %pack_kv.1.own.refs_4_.refs_0_, bf16[144,512]{1,0:T(8,128)(2,1)S(1)} %hold.9.refs_7_.refs_1_, bf16[1536,1536]{1,0:T(8,128)(2,1)S(1)} %assemble_w_out.1.refs_2_, f32[1536]{0:T(1024)S(1)} %copy-done.13, ...), custom_call_target="tpu_custom_call" | custom-call | flops 20000000000 | bytes 1 | tf_op jit(solution)/shard_map/experts/pallas_call | solution.py:368
  97.3 3.4 %collective-permute-start.40 = (bf16[128,1536]{1,0:T(8,128)(2,1)S(1)}, bf16[128,1536]{1,0:T(8,128)(2,1)S(1)}, u32[]{:S(2)}, u32[]{:S(2)}) collective-permute-start(bf16[128,1536]{1,0:T(8,128)(2,1)S(1)} %get-tuple-element.57), channel_id=1, source_target_pairs={{0,6},{1,7},{2,4},{3,5},{4,2},{5,3},{6,0},{7,1},{8,14},{9,15},{10,... | collective-permute-start | bytes 1179656 | tf_op jit(solution)/shard_map/ppermute | solution.py:49
  100.7 0.7 join_pages.1
  101.4 0.3 collective-permute-done.39.in_ref
  101.7 7.7 %collective-permute-done.40.by_xy = bf16[128,1536]{1,0:T(8,128)(2,1)S(1)} collective-permute-done((bf16[128,1536]{1,0:T(8,128)(2,1)S(1)}, bf16[128,1536]{1,0:T(8,128)(2,1)S(1)}, u32[]{:S(2)}, u32[]{:S(2)}) %collective-permute-start.40) | collective-permute-done | bytes 393248 | tf_op jit(solution)/shard_map/ppermute | solution.py:49
  109.4 0.9 mix.1
  (73 shorter events, 0.4 us)
Async XLA Ops:
  0.6 16.5 %collective-permute-start.4 = (bf16[1536,256]{1,0:T(8,128)(2,1)}, bf16[1536,256]{1,0:T(8,128)(2,1)S(1)}, u32[]{:S(2)}, u32[]{:S(2)}) collective-permute-start(bf16[1536,256]{1,0:T(8,128)(2,1)} %refs_4_.1), channel_id=1, source_target_pairs={{0,1},{1,0},{2,3},{3,2},{4,5},{5,4},{6,7},{7,6},{8,9},{9,8},{10,11... | collective-permute-start | bytes 2359304 | tf_op jit(solution)/shard_map/ppermute | solution.py:49
  1.1 12.5 %collective-permute-start.2 = (bf16[128,1536]{1,0:T(8,128)(2,1)}, bf16[128,1536]{1,0:T(8,128)(2,1)S(1)}, u32[]{:S(2)}, u32[]{:S(2)}) collective-permute-start(bf16[128,1536]{1,0:T(8,128)(2,1)} %refs_13_.1), channel_id=1, source_target_pairs={{0,2},{1,3},{2,0},{3,1},{4,6},{5,7},{6,4},{7,5},{8,10},{9,11},{10,... | collective-permute-start | bytes 1179656 | tf_op jit(solution)/shard_map/ppermute | solution.py:49
  3.7 11.8 %collective-permute-start = (bf16[128,1536]{1,0:T(8,128)(2,1)}, bf16[128,1536]{1,0:T(8,128)(2,1)S(1)}, u32[]{:S(2)}, u32[]{:S(2)}) collective-permute-start(bf16[128,1536]{1,0:T(8,128)(2,1)} %refs_13_.1), channel_id=1, source_target_pairs={{0,4},{1,5},{2,6},{3,7},{4,0},{5,1},{6,2},{7,3},{8,12},{9,13},{10,... | collective-permute-start | bytes 1179656 | tf_op jit(solution)/shard_map/ppermute | solution.py:49
  5.2 25.6 %collective-permute-start.8 = (bf16[1536,768]{1,0:T(8,128)(2,1)}, bf16[1536,768]{1,0:T(8,128)(2,1)S(1)}, u32[]{:S(2)}, u32[]{:S(2)}) collective-permute-start(bf16[1536,768]{1,0:T(8,128)(2,1)} %bitcast.23), channel_id=1, source_target_pairs={{0,1},{1,0},{2,3},{3,2},{4,5},{5,4},{6,7},{7,6},{8,9},{9,8},{10,11... | collective-permute-start | bytes 7077896 | tf_op jit(solution)/shard_map/ppermute | solution.py:49
  13.6 6.7 %collective-permute-start.3 = (bf16[64,1536]{1,0:T(8,128)(2,1)S(1)}, bf16[64,1536]{1,0:T(8,128)(2,1)S(1)}, u32[]{:S(2)}, u32[]{:S(2)}) collective-permute-start(bf16[64,1536]{1,0:T(8,128)(2,1)S(1)} %slice.57), channel_id=1, source_target_pairs={{0,4},{1,5},{2,6},{3,7},{4,0},{5,1},{6,2},{7,3},{8,12},{9,13},{10,... | collective-permute-start | bytes 589832 | tf_op jit(solution)/shard_map/ppermute | solution.py:49
  15.5 6.3 %collective-permute-start.1 = (bf16[64,1536]{1,0:T(8,128)(2,1)S(1)}, bf16[64,1536]{1,0:T(8,128)(2,1)S(1)}, u32[]{:S(2)}, u32[]{:S(2)}) collective-permute-start(bf16[64,1536]{1,0:T(8,128)(2,1)S(1)} %slice.56), channel_id=1, source_target_pairs={{0,2},{1,3},{2,0},{3,1},{4,6},{5,7},{6,4},{7,5},{8,10},{9,11},{10,... | collective-permute-start | bytes 589832 | tf_op jit(solution)/shard_map/ppermute | solution.py:49
  17.1 13.7 %collective-permute-start.9 = (bf16[1536,768]{1,0:T(8,128)(2,1)}, bf16[1536,768]{1,0:T(8,128)(2,1)S(1)}, u32[]{:S(2)}, u32[]{:S(2)}) collective-permute-start(bf16[1536,768]{1,0:T(8,128)(2,1)} %bitcast.26), channel_id=1, source_target_pairs={{0,1},{1,0},{2,3},{3,2},{4,5},{5,4},{6,7},{7,6},{8,9},{9,8},{10,11... | collective-permute-start | bytes 7077896 | tf_op jit(solution)/shard_map/ppermute | solution.py:49
  17.1 1.1 %copy-start.8 = (bf16[1536,256]{1,0:T(8,128)(2,1)S(1)}, bf16[1536,256]{1,0:T(8,128)(2,1)}, u32[]{:S(2)}) copy-start(bf16[1536,256]{1,0:T(8,128)(2,1)} %refs_4_.1) | copy-start | bytes 2359300
  18.2 0.7 copy-start.11
  18.9 2.9 %copy-start.9 = (bf16[1536,256]{1,0:T(8,128)(2,1)S(1)}, bf16[1536,256]{1,0:T(8,128)(2,1)}, u32[]{:S(2)}) copy-start(bf16[1536,256]{1,0:T(8,128)(2,1)} %refs_4_.1) | copy-start | bytes 2359300
  18.9 2.9 %copy-start.10 = (bf16[128,1536]{1,0:T(8,128)(2,1)S(1)}, bf16[128,1536]{1,0:T(8,128)(2,1)}, u32[]{:S(2)}) copy-start(bf16[128,1536]{1,0:T(8,128)(2,1)} %refs_13_.1) | copy-start | bytes 1179652
  18.9 2.9 %copy-start.12 = (f32[1536]{0:T(1024)S(1)}, f32[1536]{0:T(1024)}, u32[]{:S(2)}) copy-start(f32[1536]{0:T(1024)} %refs_3_.5) | copy-start | bytes 18436
  19.7 6.4 %collective-permute-start.5 = (bf16[128,512]{1,0:T(8,128)(2,1)S(1)}, bf16[128,512]{1,0:T(8,128)(2,1)S(1)}, u32[]{:S(2)}, u32[]{:S(2)}) collective-permute-start(bf16[128,512]{1,0:T(8,128)(2,1)S(1)} %get-tuple-element.69), channel_id=1, source_target_pairs={{0,2},{1,3},{2,0},{3,1},{4,6},{5,7},{6,4},{7,5},{8,10},{9,11},{10,... | collective-permute-start | bytes 393224 | tf_op jit(solution)/shard_map/ppermute | solution.py:49
  22.6 8.2 %collective-permute-start.7 = (bf16[128,512]{1,0:T(8,128)(2,1)S(1)}, bf16[128,512]{1,0:T(8,128)(2,1)S(1)}, u32[]{:S(2)}, u32[]{:S(2)}) collective-permute-start(bf16[128,512]{1,0:T(8,128)(2,1)S(1)} %get-tuple-element.66), channel_id=1, source_target_pairs={{0,6},{1,7},{2,4},{3,5},{4,2},{5,3},{6,0},{7,1},{8,14},{9,15},{10,... | collective-permute-start | bytes 393224 | tf_op jit(solution)/shard_map/ppermute | solution.py:49
  24.1 6.7 %collective-permute-start.6 = (bf16[128,512]{1,0:T(8,128)(2,1)S(1)}, bf16[128,512]{1,0:T(8,128)(2,1)S(1)}, u32[]{:S(2)}, u32[]{:S(2)}) collective-permute-start(bf16[128,512]{1,0:T(8,128)(2,1)S(1)} %get-tuple-element.68), channel_id=1, source_target_pairs={{0,4},{1,5},{2,6},{3,7},{4,0},{5,1},{6,2},{7,3},{8,12},{9,13},{10,... | collective-permute-start | bytes 393224 | tf_op jit(solution)/shard_map/ppermute | solution.py:49
  26.1 4.7 %copy-start.1 = (s32[128,4]{0,1:T(4,128)S(1)}, s32[128,4]{0,1:T(4,128)}, u32[]{:S(2)}) copy-start(s32[128,4]{0,1:T(4,128)} %param.19) | copy-start | bytes 6148
  26.1 4.7 %copy-start.2 = (f32[128,4]{0,1:T(4,128)S(1)}, f32[128,4]{0,1:T(4,128)}, u32[]{:S(2)}) copy-start(f32[128,4]{0,1:T(4,128)} %param.20) | copy-start | bytes 6148
  26.1 4.7 %copy-start.3 = (s32[128]{0:T(128)S(1)}, s32[128]{0:T(128)}, u32[]{:S(2)}) copy-start(s32[128]{0:T(128)} %param.13) | copy-start | bytes 1540
  26.1 4.8 %copy-start.7 = (bf16[1,768,1536]{2,1,0:T(8,128)(2,1)S(1)}, bf16[1,768,1536]{2,1,0:T(8,128)(2,1)}, u32[]{:S(2)}) copy-start(bf16[1,768,1536]{2,1,0:T(8,128)(2,1)} %param.23) | copy-start | bytes 7077892
  26.1 4.9 %copy-start = (bf16[1536,192]{0,1:T(8,128)(2,1)S(1)}, bf16[1536,192]{0,1:T(8,128)(2,1)}, u32[]{:S(2)}) copy-start(bf16[1536,192]{0,1:T(8,128)(2,1)} %param.17) | copy-start | bytes 1769476
  30.9 16.7 %collective-permute-start.13 = (bf16[768,1536]{1,0:T(8,128)(2,1)S(1)}, bf16[768,1536]{1,0:T(8,128)(2,1)S(1)}, u32[]{:S(2)}, u32[]{:S(2)}) collective-permute-start(bf16[768,1536]{1,0:T(8,128)(2,1)S(1)} %bitcast.29), channel_id=1, source_target_pairs={{0,1},{1,0},{2,3},{3,2},{4,5},{5,4},{6,7},{7,6},{8,9},{9,8},{10,11... | collective-permute-start | bytes 7077896 | tf_op jit(solution)/shard_map/ppermute | solution.py:49
  31.0 15.7 %collective-permute-start.11 = (bf16[192,1536]{1,0:T(8,128)(2,1)S(1)}, bf16[192,1536]{1,0:T(8,128)(2,1)S(1)}, u32[]{:S(2)}, u32[]{:S(2)}) collective-permute-start(bf16[192,1536]{1,0:T(8,128)(2,1)S(1)} %bitcast.16), channel_id=1, source_target_pairs={{0,2},{1,3},{2,0},{3,1},{4,6},{5,7},{6,4},{7,5},{8,10},{9,11},{10,... | collective-permute-start | bytes 1769480 | tf_op jit(solution)/shard_map/ppermute | solution.py:49
  32.2 15.4 %collective-permute-start.12 = (bf16[192,1536]{1,0:T(8,128)(2,1)S(1)}, bf16[192,1536]{1,0:T(8,128)(2,1)S(1)}, u32[]{:S(2)}, u32[]{:S(2)}) collective-permute-start(bf16[192,1536]{1,0:T(8,128)(2,1)S(1)} %bitcast.17), channel_id=1, source_target_pairs={{0,4},{1,5},{2,6},{3,7},{4,0},{5,1},{6,2},{7,3},{8,12},{9,13},{10,... | collective-permute-start | bytes 1769480 | tf_op jit(solution)/shard_map/ppermute | solution.py:49
  33.2 14.4 %collective-permute-start.14 = (bf16[192,1536]{1,0:T(8,128)(2,1)S(1)}, bf16[192,1536]{1,0:T(8,128)(2,1)S(1)}, u32[]{:S(2)}, u32[]{:S(2)}) collective-permute-start(bf16[192,1536]{1,0:T(8,128)(2,1)S(1)} %bitcast.18), channel_id=1, source_target_pairs={{0,1},{1,0},{2,3},{3,2},{4,5},{5,4},{6,7},{7,6},{8,9},{9,8},{10,11... | collective-permute-start | bytes 1769480 | tf_op jit(solution)/shard_map/ppermute | solution.py:49
  33.2 7.2 %collective-permute-start.10 = (bf16[144,512]{1,0:T(8,128)(2,1)S(1)}, bf16[144,512]{1,0:T(8,128)(2,1)S(1)}, u32[]{:S(2)}, u32[]{:S(2)}) collective-permute-start(bf16[144,512]{1,0:T(8,128)(2,1)S(1)} %pack_kv.1.own.refs_4_.refs_0_), channel_id=1, source_target_pairs={{0,8},{8,16},{16,24},{1,9},{9,17},{17,25},{2,10},{10,18},{18,26},{... | collective-permute-start | bytes 442376 | tf_op jit(solution)/shard_map/ppermute | solution.py:511
  40.5 15.0 %collective-permute-start.24 = (bf16[144,512]{1,0:T(8,128)(2,1)S(1)}, bf16[144,512]{1,0:T(8,128)(2,1)S(1)}, u32[]{:S(2)}, u32[]{:S(2)}) collective-permute-start(bf16[144,512]{1,0:T(8,128)(2,1)S(1)} %pack_kv.1.own.refs_4_.refs_0_), channel_id=1, source_target_pairs={{0,1},{1,0},{2,3},{3,2},{4,5},{5,4},{6,7},{7,6},{8,9},{9,8},{10,11... | collective-permute-start | bytes 442376 | tf_op jit(solution)/shard_map/ppermute | solution.py:49
  46.7 9.3 %collective-permute-start.28 = (bf16[144,512]{1,0:T(8,128)(2,1)S(1)}, bf16[144,512]{1,0:T(8,128)(2,1)S(1)}, u32[]{:S(2)}, u32[]{:S(2)}) collective-permute-start(bf16[144,512]{1,0:T(8,128)(2,1)S(1)} %collective-permute-done.10.prev.refs_8_), channel_id=1, source_target_pairs={{0,1},{1,0},{2,3},{3,2},{4,5},{5,4},{6,7},{7,6},{8,9},{9,8},{10,11... | collective-permute-start | bytes 442376 | tf_op jit(solution)/shard_map/ppermute | solution.py:49
  47.7 7.7 %collective-permute-start.15 = (bf16[144,512]{1,0:T(8,128)(2,1)S(1)}, bf16[144,512]{1,0:T(8,128)(2,1)S(1)}, u32[]{:S(2)}, u32[]{:S(2)}) collective-permute-start(bf16[144,512]{1,0:T(8,128)(2,1)S(1)} %get-tuple-element.40.refs_2_), channel_id=1, source_target_pairs={{0,6},{1,7},{2,4},{3,5},{4,2},{5,3},{6,0},{7,1},{8,14},{9,15},{10,... | collective-permute-start | bytes 442376 | tf_op jit(solution)/shard_map/ppermute | solution.py:49
  49.6 7.8 %collective-permute-start.22 = (bf16[144,512]{1,0:T(8,128)(2,1)S(1)}, bf16[144,512]{1,0:T(8,128)(2,1)S(1)}, u32[]{:S(2)}, u32[]{:S(2)}) collective-permute-start(bf16[144,512]{1,0:T(8,128)(2,1)S(1)} %get-tuple-element.41.refs_0_), channel_id=1, source_target_pairs={{0,2},{1,3},{2,0},{3,1},{4,6},{5,7},{6,4},{7,5},{8,10},{9,11},{10,... | collective-permute-start | bytes 442376 | tf_op jit(solution)/shard_map/ppermute | solution.py:49
  50.3 7.1 %collective-permute-start.23 = (bf16[144,512]{1,0:T(8,128)(2,1)S(1)}, bf16[144,512]{1,0:T(8,128)(2,1)S(1)}, u32[]{:S(2)}, u32[]{:S(2)}) collective-permute-start(bf16[144,512]{1,0:T(8,128)(2,1)S(1)} %get-tuple-element.42.refs_1_), channel_id=1, source_target_pairs={{0,4},{1,5},{2,6},{3,7},{4,0},{5,1},{6,2},{7,3},{8,12},{9,13},{10,... | collective-permute-start | bytes 442376 | tf_op jit(solution)/shard_map/ppermute | solution.py:49
  55.4 5.5 %collective-permute-start.19 = (bf16[192,1536]{1,0:T(8,128)(2,1)S(1)}, bf16[192,1536]{1,0:T(8,128)(2,1)S(1)}, u32[]{:S(2)}, u32[]{:S(2)}) collective-permute-start(bf16[192,1536]{1,0:T(8,128)(2,1)S(1)} %collective-permute-done.12.refs_2_), channel_id=1, source_target_pairs={{0,1},{1,0},{2,3},{3,2},{4,5},{5,4},{6,7},{7,6},{8,9},{9,8},{10,11... | collective-permute-start | bytes 1769480 | tf_op jit(solution)/shard_map/ppermute | solution.py:49
  55.5 5.5 %collective-permute-start.18 = (bf16[192,1536]{1,0:T(8,128)(2,1)S(1)}, bf16[192,1536]{1,0:T(8,128)(2,1)S(1)}, u32[]{:S(2)}, u32[]{:S(2)}) collective-permute-start(bf16[192,1536]{1,0:T(8,128)(2,1)S(1)} %collective-permute-done.11.refs_1_), channel_id=1, source_target_pairs={{0,1},{1,0},{2,3},{3,2},{4,5},{5,4},{6,7},{7,6},{8,9},{9,8},{10,11... | collective-permute-start | bytes 1769480 | tf_op jit(solution)/shard_map/ppermute | solution.py:49
  56.1 2.7 %collective-permute-start.27 = (bf16[144,512]{1,0:T(8,128)(2,1)S(1)}, bf16[144,512]{1,0:T(8,128)(2,1)S(1)}, u32[]{:S(2)}, u32[]{:S(2)}) collective-permute-start(bf16[144,512]{1,0:T(8,128)(2,1)S(1)} %hold.9.refs_7_.refs_1_), channel_id=1, source_target_pairs={{0,1},{1,0},{2,3},{3,2},{4,5},{5,4},{6,7},{7,6},{8,9},{9,8},{10,11... | collective-permute-start | bytes 442376 | tf_op jit(solution)/shard_map/ppermute | solution.py:49
  57.4 2.1 %collective-permute-start.25 = (bf16[144,512]{1,0:T(8,128)(2,1)S(1)}, bf16[144,512]{1,0:T(8,128)(2,1)S(1)}, u32[]{:S(2)}, u32[]{:S(2)}) collective-permute-start(bf16[144,512]{1,0:T(8,128)(2,1)S(1)} %collective-permute-done.22.refs_5_.refs_0_), channel_id=1, source_target_pairs={{0,1},{1,0},{2,3},{3,2},{4,5},{5,4},{6,7},{7,6},{8,9},{9,8},{10,11... | collective-permute-start | bytes 442376 | tf_op jit(solution)/shard_map/ppermute | solution.py:49
  57.4 15.0 %copy-start.4 = (s32[1,64]{1,0:T(1,128)S(1)}, s32[1,64]{1,0:T(1,128)}, u32[]{:S(2)}) copy-start(s32[1,64]{1,0:T(1,128)} %table_ref.1) | copy-start | bytes 772
  57.4 9.5 %collective-permute-start.17 = (bf16[96,1536]{1,0:T(8,128)(2,1)S(1)}, bf16[96,1536]{1,0:T(8,128)(2,1)S(1)}, u32[]{:S(2)}, u32[]{:S(2)}) collective-permute-start(bf16[96,1536]{1,0:T(8,128)(2,1)S(1)} %hold.11), channel_id=1, source_target_pairs={{0,4},{1,5},{2,6},{3,7},{4,0},{5,1},{6,2},{7,3},{8,12},{9,13},{10,... | collective-permute-start | bytes 884744 | tf_op jit(solution)/shard_map/ppermute | solution.py:49
  58.8 8.8 %collective-permute-start.16 = (bf16[96,1536]{1,0:T(8,128)(2,1)S(1)}, bf16[96,1536]{1,0:T(8,128)(2,1)S(1)}, u32[]{:S(2)}, u32[]{:S(2)}) collective-permute-start(bf16[96,1536]{1,0:T(8,128)(2,1)S(1)} %hold.10), channel_id=1, source_target_pairs={{0,2},{1,3},{2,0},{3,1},{4,6},{5,7},{6,4},{7,5},{8,10},{9,11},{10,... | collective-permute-start | bytes 884744 | tf_op jit(solution)/shard_map/ppermute | solution.py:49
  59.5 1.4 %collective-permute-start.26 = (bf16[144,512]{1,0:T(8,128)(2,1)S(1)}, bf16[144,512]{1,0:T(8,128)(2,1)S(1)}, u32[]{:S(2)}, u32[]{:S(2)}) collective-permute-start(bf16[144,512]{1,0:T(8,128)(2,1)S(1)} %collective-permute-done.23.refs_6_.refs_1_), channel_id=1, source_target_pairs={{0,1},{1,0},{2,3},{3,2},{4,5},{5,4},{6,7},{7,6},{8,9},{9,8},{10,11... | collective-permute-start | bytes 442376 | tf_op jit(solution)/shard_map/ppermute | solution.py:49
  60.8 9.7 %collective-permute-start.33 = (bf16[256,512]{1,0:T(8,128)(2,1)S(1)}, bf16[256,512]{1,0:T(8,128)(2,1)S(1)}, u32[]{:S(2)}, u32[]{:S(2)}) collective-permute-start(bf16[256,512]{1,0:T(8,128)(2,1)S(1)} %project.3.refs_0_), channel_id=1, source_target_pairs={{0,1},{1,0},{2,3},{3,2},{4,5},{5,4},{6,7},{7,6},{8,9},{9,8},{10,11... | collective-permute-start | bytes 786440 | tf_op jit(solution)/shard_map/ppermute | solution.py:49
  67.6 10.1 %collective-permute-start.29 = (bf16[128,1536]{1,0:T(8,128)(2,1)S(1)}, bf16[128,1536]{1,0:T(8,128)(2,1)S(1)}, u32[]{:S(2)}, u32[]{:S(2)}) collective-permute-start(bf16[128,1536]{1,0:T(8,128)(2,1)S(1)} %attend.1.refs_10_), channel_id=1, source_target_pairs={{0,4},{1,5},{2,6},{3,7},{4,0},{5,1},{6,2},{7,3},{8,12},{9,13},{10,... | collective-permute-start | bytes 1179656 | tf_op jit(solution)/shard_map/ppermute | solution.py:49
  68.7 10.1 %collective-permute-start.31 = (bf16[128,1536]{1,0:T(8,128)(2,1)S(1)}, bf16[128,1536]{1,0:T(8,128)(2,1)S(1)}, u32[]{:S(2)}, u32[]{:S(2)}) collective-permute-start(bf16[128,1536]{1,0:T(8,128)(2,1)S(1)} %attend.1.refs_10_), channel_id=1, source_target_pairs={{0,2},{1,3},{2,0},{3,1},{4,6},{5,7},{6,4},{7,5},{8,10},{9,11},{10,... | collective-permute-start | bytes 1179656 | tf_op jit(solution)/shard_map/ppermute | solution.py:49
  70.0 4.5 %collective-permute-start.21 = (bf16[96,1536]{1,0:T(8,128)(2,1)S(1)}, bf16[96,1536]{1,0:T(8,128)(2,1)S(1)}, u32[]{:S(2)}, u32[]{:S(2)}) collective-permute-start(bf16[96,1536]{1,0:T(8,128)(2,1)S(1)} %collective-permute-done.17.refs_4_), channel_id=1, source_target_pairs={{0,1},{1,0},{2,3},{3,2},{4,5},{5,4},{6,7},{7,6},{8,9},{9,8},{10,11... | collective-permute-start | bytes 884744 | tf_op jit(solution)/shard_map/ppermute | solution.py:49
  70.0 4.5 %collective-permute-start.20 = (bf16[96,1536]{1,0:T(8,128)(2,1)S(1)}, bf16[96,1536]{1,0:T(8,128)(2,1)S(1)}, u32[]{:S(2)}, u32[]{:S(2)}) collective-permute-start(bf16[96,1536]{1,0:T(8,128)(2,1)S(1)} %collective-permute-done.16.refs_3_), channel_id=1, source_target_pairs={{0,1},{1,0},{2,3},{3,2},{4,5},{5,4},{6,7},{7,6},{8,9},{9,8},{10,11... | collective-permute-start | bytes 884744 | tf_op jit(solution)/shard_map/ppermute | solution.py:49
  70.5 1.9 %collective-permute-start.34 = (bf16[256,512]{1,0:T(8,128)(2,1)S(1)}, bf16[256,512]{1,0:T(8,128)(2,1)S(1)}, u32[]{:S(2)}, u32[]{:S(2)}) collective-permute-start(bf16[256,512]{1,0:T(8,128)(2,1)S(1)} %project.2.refs_6_.refs_1_), channel_id=1, source_target_pairs={{0,1},{1,0},{2,3},{3,2},{4,5},{5,4},{6,7},{7,6},{8,9},{9,8},{10,11... | collective-permute-start | bytes 786440 | tf_op jit(solution)/shard_map/ppermute | solution.py:49
  74.4 11.9 %copy-start.5 = (bf16[1,1536,768]{2,1,0:T(8,128)(2,1)S(1)}, bf16[1,1536,768]{2,1,0:T(8,128)(2,1)}, u32[]{:S(2)}) copy-start(bf16[1,1536,768]{2,1,0:T(8,128)(2,1)} %param.21) | copy-start | bytes 7077892
  74.4 11.9 %copy-start.6 = (bf16[1,1536,768]{2,1,0:T(8,128)(2,1)S(1)}, bf16[1,1536,768]{2,1,0:T(8,128)(2,1)}, u32[]{:S(2)}) copy-start(bf16[1,1536,768]{2,1,0:T(8,128)(2,1)} %param.22) | copy-start | bytes 7077892
  74.4 11.9 %copy-start.13 = (f32[1536]{0:T(1024)S(1)}, f32[1536]{0:T(1024)}, u32[]{:S(2)}) copy-start(f32[1536]{0:T(1024)} %refs_3_.7) | copy-start | bytes 18436
  78.8 12.8 %collective-permute-start.35 = (bf16[128,512]{1,0:T(8,128)(2,1)S(1)}, bf16[128,512]{1,0:T(8,128)(2,1)S(1)}, u32[]{:S(2)}, u32[]{:S(2)}) collective-permute-start(bf16[128,512]{1,0:T(8,128)(2,1)S(1)} %get-tuple-element.65), channel_id=1, source_target_pairs={{6,4},{7,5},{14,12},{15,13},{22,20},{23,21},{30,28},{31,29}} | collective-permute-start | bytes 393224 | tf_op jit(solution)/shard_map/ppermute | solution.py:536
  79.5 12.3 %collective-permute-start.36 = (bf16[128,512]{1,0:T(8,128)(2,1)S(1)}, bf16[128,512]{1,0:T(8,128)(2,1)S(1)}, u32[]{:S(2)}, u32[]{:S(2)}) collective-permute-start(bf16[128,512]{1,0:T(8,128)(2,1)S(1)} %get-tuple-element.64), channel_id=1, source_target_pairs={{6,2},{7,3},{14,10},{15,11},{22,18},{23,19},{30,26},{31,27}} | collective-permute-start | bytes 393224 | tf_op jit(solution)/shard_map/ppermute | solution.py:536
  80.2 11.7 %collective-permute-start.37 = (bf16[128,512]{1,0:T(8,128)(2,1)S(1)}, bf16[128,512]{1,0:T(8,128)(2,1)S(1)}, u32[]{:S(2)}, u32[]{:S(2)}) collective-permute-start(bf16[128,512]{1,0:T(8,128)(2,1)S(1)} %get-tuple-element.63), channel_id=1, source_target_pairs={{6,0},{7,1},{14,8},{15,9},{22,16},{23,17},{30,24},{31,25}} | collective-permute-start | bytes 393224 | tf_op jit(solution)/shard_map/ppermute | solution.py:536
  81.7 10.2 %collective-permute-start.30 = (bf16[64,1536]{1,0:T(8,128)(2,1)S(1)}, bf16[64,1536]{1,0:T(8,128)(2,1)S(1)}, u32[]{:S(2)}, u32[]{:S(2)}) collective-permute-start(bf16[64,1536]{1,0:T(8,128)(2,1)S(1)} %slice.64), channel_id=1, source_target_pairs={{0,2},{1,3},{2,0},{3,1},{4,6},{5,7},{6,4},{7,5},{8,10},{9,11},{10,... | collective-permute-start | bytes 589832 | tf_op jit(solution)/shard_map/ppermute | solution.py:49
  83.0 8.9 %collective-permute-start.32 = (bf16[64,1536]{1,0:T(8,128)(2,1)S(1)}, bf16[64,1536]{1,0:T(8,128)(2,1)S(1)}, u32[]{:S(2)}, u32[]{:S(2)}) collective-permute-start(bf16[64,1536]{1,0:T(8,128)(2,1)S(1)} %slice.65), channel_id=1, source_target_pairs={{0,4},{1,5},{2,6},{3,7},{4,0},{5,1},{6,2},{7,3},{8,12},{9,13},{10,... | collective-permute-start | bytes 589832 | tf_op jit(solution)/shard_map/ppermute | solution.py:49
  91.7 9.7 %collective-permute-start.38 = (bf16[128,1536]{1,0:T(8,128)(2,1)S(1)}, bf16[128,1536]{1,0:T(8,128)(2,1)S(1)}, u32[]{:S(2)}, u32[]{:S(2)}) collective-permute-start(bf16[128,1536]{1,0:T(8,128)(2,1)S(1)} %get-tuple-element.51.refs_16_), channel_id=1, source_target_pairs={{0,2},{1,3},{2,0},{3,1},{4,6},{5,7},{6,4},{7,5},{8,10},{9,11},{10,... | collective-permute-start | bytes 1179656 | tf_op jit(solution)/shard_map/ppermute | solution.py:49
  91.8 9.9 %collective-permute-start.39 = (bf16[128,1536]{1,0:T(8,128)(2,1)S(1)}, bf16[128,1536]{1,0:T(8,128)(2,1)S(1)}, u32[]{:S(2)}, u32[]{:S(2)}) collective-permute-start(bf16[128,1536]{1,0:T(8,128)(2,1)S(1)} %get-tuple-element.56), channel_id=1, source_target_pairs={{0,4},{1,5},{2,6},{3,7},{4,0},{5,1},{6,2},{7,3},{8,12},{9,13},{10,... | collective-permute-start | bytes 1179656 | tf_op jit(solution)/shard_map/ppermute | solution.py:49
  97.3 12.1 %collective-permute-start.40 = (bf16[128,1536]{1,0:T(8,128)(2,1)S(1)}, bf16[128,1536]{1,0:T(8,128)(2,1)S(1)}, u32[]{:S(2)}, u32[]{:S(2)}) collective-permute-start(bf16[128,1536]{1,0:T(8,128)(2,1)S(1)} %get-tuple-element.57), channel_id=1, source_target_pairs={{0,6},{1,7},{2,4},{3,5},{4,2},{5,3},{6,0},{7,1},{8,14},{9,15},{10,... | collective-permute-start | bytes 1179656 | tf_op jit(solution)/shard_map/ppermute | solution.py:49

commit v7 on v6

--- a/solution.py
+++ b/solution.py
@@ -545,10 +545,10 @@
     back_x, back_y = hold_call(chips(out_x, 1)), hold_call(chips(out_y, 2))
     out, out_xy = expert_call(
         (context, *context_xy), (tokens, *tokens_xy), (own_kv, kv_xy), w_all, moe_gain, weights,
-        (jnp.float32, jnp.bfloat16), out_x, *pages[1:],
+        (jnp.float32, jnp.bfloat16), out_x, *pages[1:3],
     )
     back_xy = chips(out_xy, 3)
-    pages = join_call(after(pages, out_xy))
+    pages = join_call(pages)
     mixed = mix_call((out, back_x, back_y, back_xy))
     return (mixed, pages.reshape(rows // PAGE, PAGE, pages.shape[1]))
 

time: 111 us -> 111 us (level)
  transfers between devices with their start and end apart: 41 -> 41, of which waited for: 18 -> 17; matrix products, arithmetic and copies ran while one was open for 0% -> 0% of each run, Pallas kernels for 15% -> 16%
where the time goes in v7:
time: 111 us; the launch traced here: 110 us
  waiting for transfers between devices  51.5 us (46%)
  starting transfers between devices  37.7 us (34%)
  Pallas kernels  18.1 us (16%)
  local copies, waits for them, and re-layouts  2.07 us (2%)
    ppermute x37, waiting for transfers between devices, hop(): return lax.ppermute(value, 'tensor', [(i, i ^ by) for i in range(length)])  47.7 us
    ppermute x37, starting transfers between devices, hop(): return lax.ppermute(value, 'tensor', [(i, i ^ by) for i in range(length)])  31.4 us
    pallas_call x2, Pallas kernels, expert_call(): pl.pallas_call(functools.partial(expert_kernel, 256, len(context), len(to...  10.7 us
    ppermute x1, waiting for transfers between devices, chip_body(): lax.ppermute(own_kv, 'seq', [(i, i + 1) for i in range(seq_size - 1)])  3.75 us
    ppermute x1, starting transfers between devices, chip_body(): lax.ppermute(own_kv, 'seq', [(i, i + 1) for i in range(seq_size - 1)])  3.48 us
    ppermute x3, starting transfers between devices, chip_body(): pages.append(lax.ppermute(paged[last ^ by], 'tensor', pairs))  2.81 us
  transfers between devices with their start and end apart: 41, of which 17 were waited for; matrix products, arithmetic and copies ran while one was open for 0% of the time, Pallas kernels for 16%

profile of v7, /device:TPU:0, one launch (start us, length us, event | category | flops | bytes accessed | tf_op | source)
XLA Modules:
  0.0 110.4 jit_solution(13512977735034324576)
XLA Ops:
  0.6 0.5 collective-permute-start.4
  1.1 2.6 %collective-permute-start.2 = (bf16[128,1536]{1,0:T(8,128)(2,1)}, bf16[128,1536]{1,0:T(8,128)(2,1)S(1)}, u32[]{:S(2)}, u32[]{:S(2)}) collective-permute-start(bf16[128,1536]{1,0:T(8,128)(2,1)} %refs_13_.1), channel_id=1, source_target_pairs={{0,2},{1,3},{2,0},{3,1},{4,6},{5,7},{6,4},{7,5},{8,10},{9,11},{10,... | collective-permute-start | bytes 1179656 | tf_op jit(solution)/shard_map/ppermute | solution.py:49
  3.7 1.5 %collective-permute-start = (bf16[128,1536]{1,0:T(8,128)(2,1)}, bf16[128,1536]{1,0:T(8,128)(2,1)S(1)}, u32[]{:S(2)}, u32[]{:S(2)}) collective-permute-start(bf16[128,1536]{1,0:T(8,128)(2,1)} %refs_13_.1), channel_id=1, source_target_pairs={{0,4},{1,5},{2,6},{3,7},{4,0},{5,1},{6,2},{7,3},{8,12},{9,13},{10,... | collective-permute-start | bytes 1179656 | tf_op jit(solution)/shard_map/ppermute | solution.py:49
  5.2 8.4 %collective-permute-done.2.refs_0_.refs_12_ = bf16[128,1536]{1,0:T(8,128)(2,1)S(1)} collective-permute-done((bf16[128,1536]{1,0:T(8,128)(2,1)}, bf16[128,1536]{1,0:T(8,128)(2,1)S(1)}, u32[]{:S(2)}, u32[]{:S(2)}) %collective-permute-start.2) | collective-permute-done | bytes 393248 | tf_op jit(solution)/shard_map/ppermute | solution.py:49
  13.6 1.9 %collective-permute-start.3 = (bf16[64,1536]{1,0:T(8,128)(2,1)S(1)}, bf16[64,1536]{1,0:T(8,128)(2,1)S(1)}, u32[]{:S(2)}, u32[]{:S(2)}) collective-permute-start(bf16[64,1536]{1,0:T(8,128)(2,1)S(1)} %slice.57), channel_id=1, source_target_pairs={{0,4},{1,5},{2,6},{3,7},{4,0},{5,1},{6,2},{7,3},{8,12},{9,13},{10,... | collective-permute-start | bytes 589832 | tf_op jit(solution)/shard_map/ppermute | solution.py:49
  15.5 1.6 %collective-permute-start.1 = (bf16[64,1536]{1,0:T(8,128)(2,1)S(1)}, bf16[64,1536]{1,0:T(8,128)(2,1)S(1)}, u32[]{:S(2)}, u32[]{:S(2)}) collective-permute-start(bf16[64,1536]{1,0:T(8,128)(2,1)S(1)} %slice.56), channel_id=1, source_target_pairs={{0,2},{1,3},{2,0},{3,1},{4,6},{5,7},{6,4},{7,5},{8,10},{9,11},{10,... | collective-permute-start | bytes 589832 | tf_op jit(solution)/shard_map/ppermute | solution.py:49
  17.1 1.1 %copy-done.8 = bf16[1536,256]{1,0:T(8,128)(2,1)S(1)} copy-done((bf16[1536,256]{1,0:T(8,128)(2,1)S(1)}, bf16[1536,256]{1,0:T(8,128)(2,1)}, u32[]{:S(2)}) %copy-start.8) | copy-done | bytes 786456
  18.2 0.7 copy-done.11
  18.9 0.7 project.2.refs_6_.refs_1_
  19.7 0.6 collective-permute-start.5
  20.3 0.1 collective-permute-done.3.refs_2_.refs_15_
  20.4 1.4 %collective-permute-done.1.refs_1_.refs_14_ = bf16[64,1536]{1,0:T(8,128)(2,1)S(1)} collective-permute-done((bf16[64,1536]{1,0:T(8,128)(2,1)S(1)}, bf16[64,1536]{1,0:T(8,128)(2,1)S(1)}, u32[]{:S(2)}, u32[]{:S(2)}) %collective-permute-start.1) | collective-permute-done | bytes 196640 | tf_op jit(solution)/shard_map/ppermute | solution.py:49
  21.8 0.8 project.3.refs_0_
  22.6 1.5 %collective-permute-start.7 = (bf16[128,512]{1,0:T(8,128)(2,1)S(1)}, bf16[128,512]{1,0:T(8,128)(2,1)S(1)}, u32[]{:S(2)}, u32[]{:S(2)}) collective-permute-start(bf16[128,512]{1,0:T(8,128)(2,1)S(1)} %get-tuple-element.58), channel_id=1, source_target_pairs={{0,6},{1,7},{2,4},{3,5},{4,2},{5,3},{6,0},{7,1},{8,14},{9,15},{10,... | collective-permute-start | bytes 393224 | tf_op jit(solution)/shard_map/ppermute | solution.py:49
  24.1 1.5 %collective-permute-start.6 = (bf16[128,512]{1,0:T(8,128)(2,1)S(1)}, bf16[128,512]{1,0:T(8,128)(2,1)S(1)}, u32[]{:S(2)}, u32[]{:S(2)}) collective-permute-start(bf16[128,512]{1,0:T(8,128)(2,1)S(1)} %get-tuple-element.60), channel_id=1, source_target_pairs={{0,4},{1,5},{2,6},{3,7},{4,0},{5,1},{6,2},{7,3},{8,12},{9,13},{10,... | collective-permute-start | bytes 393224 | tf_op jit(solution)/shard_map/ppermute | solution.py:49
  25.6 0.5 collective-permute-done.5.in_ref
  26.1 0.0 copy-start.3
  26.1 0.0 copy-start.7
  26.1 4.7 %collective-permute-done.6.in_ref = bf16[128,512]{1,0:T(8,128)(2,1)S(1)} collective-permute-done((bf16[128,512]{1,0:T(8,128)(2,1)S(1)}, bf16[128,512]{1,0:T(8,128)(2,1)S(1)}, u32[]{:S(2)}, u32[]{:S(2)}) %collective-permute-start.6) | collective-permute-done | bytes 131104 | tf_op jit(solution)/shard_map/ppermute | solution.py:49
  30.9 0.1 pack_kv.1.own.refs_4_.refs_0_
  30.9 0.1 collective-permute-start.13
  31.0 1.2 %collective-permute-start.11 = (bf16[192,1536]{1,0:T(8,128)(2,1)S(1)}, bf16[192,1536]{1,0:T(8,128)(2,1)S(1)}, u32[]{:S(2)}, u32[]{:S(2)}) collective-permute-start(bf16[192,1536]{1,0:T(8,128)(2,1)S(1)} %bitcast.16), channel_id=1, source_target_pairs={{0,2},{1,3},{2,0},{3,1},{4,6},{5,7},{6,4},{7,5},{8,10},{9,11},{10,... | collective-permute-start | bytes 1769480 | tf_op jit(solution)/shard_map/ppermute | solution.py:49
  32.2 1.0 collective-permute-start.12
  33.2 3.5 %collective-permute-start.10 = (bf16[144,512]{1,0:T(8,128)(2,1)S(1)}, bf16[144,512]{1,0:T(8,128)(2,1)S(1)}, u32[]{:S(2)}, u32[]{:S(2)}) collective-permute-start(bf16[144,512]{1,0:T(8,128)(2,1)S(1)} %pack_kv.1.own.refs_4_.refs_0_), channel_id=1, source_target_pairs={{0,8},{8,16},{16,24},{1,9},{9,17},{17,25},{2,10},{10,18},{18,26},{... | collective-permute-start | bytes 442376 | tf_op jit(solution)/shard_map/ppermute | solution.py:511
  36.7 3.8 %collective-permute-done.10.prev.refs_8_ = bf16[144,512]{1,0:T(8,128)(2,1)S(1)} collective-permute-done((bf16[144,512]{1,0:T(8,128)(2,1)S(1)}, bf16[144,512]{1,0:T(8,128)(2,1)S(1)}, u32[]{:S(2)}, u32[]{:S(2)}) %collective-permute-start.10) | collective-permute-done | bytes 147488 | tf_op jit(solution)/shard_map/ppermute | solution.py:511
  40.5 6.3 %collective-permute-done.11.refs_1_ = bf16[192,1536]{1,0:T(8,128)(2,1)S(1)} collective-permute-done((bf16[192,1536]{1,0:T(8,128)(2,1)S(1)}, bf16[192,1536]{1,0:T(8,128)(2,1)S(1)}, u32[]{:S(2)}, u32[]{:S(2)}) %collective-permute-start.11) | collective-permute-done | bytes 589856 | tf_op jit(solution)/shard_map/ppermute | solution.py:49
  46.8 0.8 collective-permute-done.12.refs_2_
  47.7 0.1 choose_kv.1
  47.7 1.9 %collective-permute-start.15 = (bf16[144,512]{1,0:T(8,128)(2,1)S(1)}, bf16[144,512]{1,0:T(8,128)(2,1)S(1)}, u32[]{:S(2)}, u32[]{:S(2)}) collective-permute-start(bf16[144,512]{1,0:T(8,128)(2,1)S(1)} %get-tuple-element.36.refs_2_), channel_id=1, source_target_pairs={{0,6},{1,7},{2,4},{3,5},{4,2},{5,3},{6,0},{7,1},{8,14},{9,15},{10,... | collective-permute-start | bytes 442376 | tf_op jit(solution)/shard_map/ppermute | solution.py:49
  49.6 0.6 collective-permute-start.22
  50.3 1.0 collective-permute-start.23
  51.3 4.1 %collective-permute-done.15.in_ref = bf16[144,512]{1,0:T(8,128)(2,1)S(1)} collective-permute-done((bf16[144,512]{1,0:T(8,128)(2,1)S(1)}, bf16[144,512]{1,0:T(8,128)(2,1)S(1)}, u32[]{:S(2)}, u32[]{:S(2)}) %collective-permute-start.15) | collective-permute-done | bytes 147488 | tf_op jit(solution)/shard_map/ppermute | solution.py:49
  55.5 0.6 collective-permute-start.18
  56.1 0.1 collective-permute-start.27
  56.2 1.2 %collective-permute-done.22.refs_5_.refs_0_ = bf16[144,512]{1,0:T(8,128)(2,1)S(1)} collective-permute-done((bf16[144,512]{1,0:T(8,128)(2,1)S(1)}, bf16[144,512]{1,0:T(8,128)(2,1)S(1)}, u32[]{:S(2)}, u32[]{:S(2)}) %collective-permute-start.22) | collective-permute-done | bytes 147488 | tf_op jit(solution)/shard_map/ppermute | solution.py:49
  57.5 1.4 %collective-permute-start.17 = (bf16[96,1536]{1,0:T(8,128)(2,1)S(1)}, bf16[96,1536]{1,0:T(8,128)(2,1)S(1)}, u32[]{:S(2)}, u32[]{:S(2)}) collective-permute-start(bf16[96,1536]{1,0:T(8,128)(2,1)S(1)} %hold.11), channel_id=1, source_target_pairs={{0,4},{1,5},{2,6},{3,7},{4,0},{5,1},{6,2},{7,3},{8,12},{9,13},{10,... | collective-permute-start | bytes 884744 | tf_op jit(solution)/shard_map/ppermute | solution.py:49
  58.8 0.6 collective-permute-start.16
  59.4 1.4 %collective-permute-done.26.refs_11_ = bf16[144,512]{1,0:T(8,128)(2,1)S(1)} collective-permute-done((bf16[144,512]{1,0:T(8,128)(2,1)S(1)}, bf16[144,512]{1,0:T(8,128)(2,1)S(1)}, u32[]{:S(2)}, u32[]{:S(2)}) %collective-permute-start.26) | collective-permute-done | bytes 147488 | tf_op jit(solution)/shard_map/ppermute | solution.py:49
  60.8 0.1 collective-permute-start.33
  61.0 1.7 %attend.1.refs_10_ = bf16[128,1536]{1,0:T(8,128)(2,1)S(1)} custom-call(bf16[128,512]{1,0:T(8,128)(2,1)S(1)} %get-tuple-element.29.own.refs_0_, bf16[128,512]{1,0:T(8,128)(2,1)S(1)} %hold.7.by_x.refs_1_, bf16[128,512]{1,0:T(8,128)(2,1)S(1)} %hold.8.by_y.refs_2_, bf16[128,512]{1,0:T(8,128)(2,1)S(1)} %collective-permute-done.7.by_xy.refs_3_, ...), custom_call_target="tpu_custom_call" | custom-call | tf_op jit(solution)/shard_map/attend/pallas_call | solution.py:267
  62.6 4.3 %collective-permute-done.17.refs_4_ = bf16[96,1536]{1,0:T(8,128)(2,1)S(1)} collective-permute-done((bf16[96,1536]{1,0:T(8,128)(2,1)S(1)}, bf16[96,1536]{1,0:T(8,128)(2,1)S(1)}, u32[]{:S(2)}, u32[]{:S(2)}) %collective-permute-start.17) | collective-permute-done | bytes 294944 | tf_op jit(solution)/shard_map/ppermute | solution.py:49
  66.9 0.6 collective-permute-done.16.refs_3_
  67.6 1.1 %collective-permute-start.29 = (bf16[128,1536]{1,0:T(8,128)(2,1)S(1)}, bf16[128,1536]{1,0:T(8,128)(2,1)S(1)}, u32[]{:S(2)}, u32[]{:S(2)}) collective-permute-start(bf16[128,1536]{1,0:T(8,128)(2,1)S(1)} %attend.1.refs_10_), channel_id=1, source_target_pairs={{0,4},{1,5},{2,6},{3,7},{4,0},{5,1},{6,2},{7,3},{8,12},{9,13},{10,... | collective-permute-start | bytes 1179656 | tf_op jit(solution)/shard_map/ppermute | solution.py:49
  68.7 1.3 %collective-permute-start.31 = (bf16[128,1536]{1,0:T(8,128)(2,1)S(1)}, bf16[128,1536]{1,0:T(8,128)(2,1)S(1)}, u32[]{:S(2)}, u32[]{:S(2)}) collective-permute-start(bf16[128,1536]{1,0:T(8,128)(2,1)S(1)} %attend.1.refs_10_), channel_id=1, source_target_pairs={{0,2},{1,3},{2,0},{3,1},{4,6},{5,7},{6,4},{7,5},{8,10},{9,11},{10,... | collective-permute-start | bytes 1179656 | tf_op jit(solution)/shard_map/ppermute | solution.py:49
  70.0 0.5 collective-permute-start.20
  70.5 1.9 %collective-permute-done.34.refs_3_ = bf16[256,512]{1,0:T(8,128)(2,1)S(1)} collective-permute-done((bf16[256,512]{1,0:T(8,128)(2,1)S(1)}, bf16[256,512]{1,0:T(8,128)(2,1)S(1)}, u32[]{:S(2)}, u32[]{:S(2)}) %collective-permute-start.34) | collective-permute-done | bytes 262176 | tf_op jit(solution)/shard_map/ppermute | solution.py:49
  72.3 2.1 %cache_pages.1 = bf16[4,128,512]{2,1,0:T(8,128)(2,1)S(1)} custom-call(s32[1,64]{1,0:T(1,128)S(1)} %copy-done.4, bf16[256,512]{1,0:T(8,128)(2,1)S(1)} %project.3.refs_0_, bf16[256,512]{1,0:T(8,128)(2,1)S(1)} %project.2.refs_6_.refs_1_, bf16[256,512]{1,0:T(8,128)(2,1)S(1)} %collective-permute-done.33.refs_2_, bf16[256,512]{1,0:T(8,128)(2,1)S(1)} %collective-permute-done.34.refs_3_), custom_call_target="tpu_custom_call" | custom-call | tf_op jit(solution)/shard_map/cache_pages/pallas_call | solution.py:431
  74.4 0.0 copy-start.6
  74.5 0.3 assemble_w_out.1.refs_2_
  74.8 2.9 %collective-permute-done.29.refs_11_ = bf16[128,1536]{1,0:T(8,128)(2,1)S(1)} collective-permute-done((bf16[128,1536]{1,0:T(8,128)(2,1)S(1)}, bf16[128,1536]{1,0:T(8,128)(2,1)S(1)}, u32[]{:S(2)}, u32[]{:S(2)}) %collective-permute-start.29) | collective-permute-done | bytes 393248 | tf_op jit(solution)/shard_map/ppermute | solution.py:49
  77.7 1.1 %collective-permute-done.31.refs_10_ = bf16[128,1536]{1,0:T(8,128)(2,1)S(1)} collective-permute-done((bf16[128,1536]{1,0:T(8,128)(2,1)S(1)}, bf16[128,1536]{1,0:T(8,128)(2,1)S(1)}, u32[]{:S(2)}, u32[]{:S(2)}) %collective-permute-start.31) | collective-permute-done | bytes 393248 | tf_op jit(solution)/shard_map/ppermute | solution.py:49
  78.9 0.7 collective-permute-start.35
  79.6 0.7 collective-permute-start.36
  80.2 1.5 %collective-permute-start.40 = (bf16[128,512]{1,0:T(8,128)(2,1)S(1)}, bf16[128,512]{1,0:T(8,128)(2,1)S(1)}, u32[]{:S(2)}, u32[]{:S(2)}) collective-permute-start(bf16[128,512]{1,0:T(8,128)(2,1)S(1)} %get-tuple-element.54), channel_id=1, source_target_pairs={{6,0},{7,1},{14,8},{15,9},{22,16},{23,17},{30,24},{31,25}} | collective-permute-start | bytes 393224 | tf_op jit(solution)/shard_map/ppermute | solution.py:536
  81.7 1.2 %collective-permute-start.30 = (bf16[64,1536]{1,0:T(8,128)(2,1)S(1)}, bf16[64,1536]{1,0:T(8,128)(2,1)S(1)}, u32[]{:S(2)}, u32[]{:S(2)}) collective-permute-start(bf16[64,1536]{1,0:T(8,128)(2,1)S(1)} %slice.64), channel_id=1, source_target_pairs={{0,2},{1,3},{2,0},{3,1},{4,6},{5,7},{6,4},{7,5},{8,10},{9,11},{10,... | collective-permute-start | bytes 589832 | tf_op jit(solution)/shard_map/ppermute | solution.py:49
  83.0 3.4 %collective-permute-start.32 = (bf16[64,1536]{1,0:T(8,128)(2,1)S(1)}, bf16[64,1536]{1,0:T(8,128)(2,1)S(1)}, u32[]{:S(2)}, u32[]{:S(2)}) collective-permute-start(bf16[64,1536]{1,0:T(8,128)(2,1)S(1)} %slice.65), channel_id=1, source_target_pairs={{0,4},{1,5},{2,6},{3,7},{4,0},{5,1},{6,2},{7,3},{8,12},{9,13},{10,... | collective-permute-start | bytes 589832 | tf_op jit(solution)/shard_map/ppermute | solution.py:49
  86.4 5.3 %experts.2 = (bf16[128,1536]{1,0:T(8,128)(2,1)S(1)}, bf16[128,1536]{1,0:T(8,128)(2,1)S(1)}) custom-call(bf16[144,512]{1,0:T(8,128)(2,1)S(1)} %collective-permute-done.22.refs_5_.refs_0_, bf16[144,512]{1,0:T(8,128)(2,1)S(1)} %collective-permute-done.23.refs_6_.refs_1_, bf16[1536,1536]{1,0:T(8,128)(2,1)S(1)} %assemble_w_out.1.refs_2_, f32[1536]{0:T(1024)S(1)} %copy-done.13, ...), custom_call_target="tpu_custom_call" | custom-call | flops 20000000000 | bytes 1 | tf_op jit(solution)/shard_map/experts/pallas_call | solution.py:368
  91.7 0.1 collective-permute-start.37
  91.8 0.1 collective-permute-start.38
  91.9 0.7 join_pages.1
  92.6 5.4 %experts.3 = (f32[128,1536]{1,0:T(8,128)S(1)}, bf16[128,1536]{1,0:T(8,128)(2,1)S(1)}) custom-call(bf16[144,512]{1,0:T(8,128)(2,1)S(1)} %pack_kv.1.own.refs_4_.refs_0_, bf16[144,512]{1,0:T(8,128)(2,1)S(1)} %hold.9.refs_7_.refs_1_, bf16[1536,1536]{1,0:T(8,128)(2,1)S(1)} %assemble_w_out.1.refs_2_, f32[1536]{0:T(1024)S(1)} %copy-done.13, ...), custom_call_target="tpu_custom_call" | custom-call | flops 20000000000 | bytes 1 | tf_op jit(solution)/shard_map/experts/pallas_call | solution.py:368
  98.0 3.4 %collective-permute-start.39 = (bf16[128,1536]{1,0:T(8,128)(2,1)S(1)}, bf16[128,1536]{1,0:T(8,128)(2,1)S(1)}, u32[]{:S(2)}, u32[]{:S(2)}) collective-permute-start(bf16[128,1536]{1,0:T(8,128)(2,1)S(1)} %get-tuple-element.53), channel_id=1, source_target_pairs={{0,6},{1,7},{2,4},{3,5},{4,2},{5,3},{6,0},{7,1},{8,14},{9,15},{10,... | collective-permute-start | bytes 1179656 | tf_op jit(solution)/shard_map/ppermute | solution.py:49
  101.5 7.9 %collective-permute-done.39.by_xy = bf16[128,1536]{1,0:T(8,128)(2,1)S(1)} collective-permute-done((bf16[128,1536]{1,0:T(8,128)(2,1)S(1)}, bf16[128,1536]{1,0:T(8,128)(2,1)S(1)}, u32[]{:S(2)}, u32[]{:S(2)}) %collective-permute-start.39) | collective-permute-done | bytes 393248 | tf_op jit(solution)/shard_map/ppermute | solution.py:49
  109.5 0.9 mix.1
  (73 shorter events, 0.4 us)
Async XLA Ops:
  0.6 16.5 %collective-permute-start.4 = (bf16[1536,256]{1,0:T(8,128)(2,1)}, bf16[1536,256]{1,0:T(8,128)(2,1)S(1)}, u32[]{:S(2)}, u32[]{:S(2)}) collective-permute-start(bf16[1536,256]{1,0:T(8,128)(2,1)} %refs_4_.1), channel_id=1, source_target_pairs={{0,1},{1,0},{2,3},{3,2},{4,5},{5,4},{6,7},{7,6},{8,9},{9,8},{10,11... | collective-permute-start | bytes 2359304 | tf_op jit(solution)/shard_map/ppermute | solution.py:49
  1.1 12.5 %collective-permute-start.2 = (bf16[128,1536]{1,0:T(8,128)(2,1)}, bf16[128,1536]{1,0:T(8,128)(2,1)S(1)}, u32[]{:S(2)}, u32[]{:S(2)}) collective-permute-start(bf16[128,1536]{1,0:T(8,128)(2,1)} %refs_13_.1), channel_id=1, source_target_pairs={{0,2},{1,3},{2,0},{3,1},{4,6},{5,7},{6,4},{7,5},{8,10},{9,11},{10,... | collective-permute-start | bytes 1179656 | tf_op jit(solution)/shard_map/ppermute | solution.py:49
  3.7 11.8 %collective-permute-start = (bf16[128,1536]{1,0:T(8,128)(2,1)}, bf16[128,1536]{1,0:T(8,128)(2,1)S(1)}, u32[]{:S(2)}, u32[]{:S(2)}) collective-permute-start(bf16[128,1536]{1,0:T(8,128)(2,1)} %refs_13_.1), channel_id=1, source_target_pairs={{0,4},{1,5},{2,6},{3,7},{4,0},{5,1},{6,2},{7,3},{8,12},{9,13},{10,... | collective-permute-start | bytes 1179656 | tf_op jit(solution)/shard_map/ppermute | solution.py:49
  5.2 25.6 %collective-permute-start.8 = (bf16[1536,768]{1,0:T(8,128)(2,1)}, bf16[1536,768]{1,0:T(8,128)(2,1)S(1)}, u32[]{:S(2)}, u32[]{:S(2)}) collective-permute-start(bf16[1536,768]{1,0:T(8,128)(2,1)} %bitcast.23), channel_id=1, source_target_pairs={{0,1},{1,0},{2,3},{3,2},{4,5},{5,4},{6,7},{7,6},{8,9},{9,8},{10,11... | collective-permute-start | bytes 7077896 | tf_op jit(solution)/shard_map/ppermute | solution.py:49
  13.6 6.7 %collective-permute-start.3 = (bf16[64,1536]{1,0:T(8,128)(2,1)S(1)}, bf16[64,1536]{1,0:T(8,128)(2,1)S(1)}, u32[]{:S(2)}, u32[]{:S(2)}) collective-permute-start(bf16[64,1536]{1,0:T(8,128)(2,1)S(1)} %slice.57), channel_id=1, source_target_pairs={{0,4},{1,5},{2,6},{3,7},{4,0},{5,1},{6,2},{7,3},{8,12},{9,13},{10,... | collective-permute-start | bytes 589832 | tf_op jit(solution)/shard_map/ppermute | solution.py:49
  15.5 6.3 %collective-permute-start.1 = (bf16[64,1536]{1,0:T(8,128)(2,1)S(1)}, bf16[64,1536]{1,0:T(8,128)(2,1)S(1)}, u32[]{:S(2)}, u32[]{:S(2)}) collective-permute-start(bf16[64,1536]{1,0:T(8,128)(2,1)S(1)} %slice.56), channel_id=1, source_target_pairs={{0,2},{1,3},{2,0},{3,1},{4,6},{5,7},{6,4},{7,5},{8,10},{9,11},{10,... | collective-permute-start | bytes 589832 | tf_op jit(solution)/shard_map/ppermute | solution.py:49
  17.1 13.7 %collective-permute-start.9 = (bf16[1536,768]{1,0:T(8,128)(2,1)}, bf16[1536,768]{1,0:T(8,128)(2,1)S(1)}, u32[]{:S(2)}, u32[]{:S(2)}) collective-permute-start(bf16[1536,768]{1,0:T(8,128)(2,1)} %bitcast.26), channel_id=1, source_target_pairs={{0,1},{1,0},{2,3},{3,2},{4,5},{5,4},{6,7},{7,6},{8,9},{9,8},{10,11... | collective-permute-start | bytes 7077896 | tf_op jit(solution)/shard_map/ppermute | solution.py:49
  17.1 1.1 %copy-start.8 = (bf16[1536,256]{1,0:T(8,128)(2,1)S(1)}, bf16[1536,256]{1,0:T(8,128)(2,1)}, u32[]{:S(2)}) copy-start(bf16[1536,256]{1,0:T(8,128)(2,1)} %refs_4_.1) | copy-start | bytes 2359300
  18.2 0.7 copy-start.11
  18.9 2.9 %copy-start.9 = (bf16[1536,256]{1,0:T(8,128)(2,1)S(1)}, bf16[1536,256]{1,0:T(8,128)(2,1)}, u32[]{:S(2)}) copy-start(bf16[1536,256]{1,0:T(8,128)(2,1)} %refs_4_.1) | copy-start | bytes 2359300
  18.9 2.9 %copy-start.10 = (bf16[128,1536]{1,0:T(8,128)(2,1)S(1)}, bf16[128,1536]{1,0:T(8,128)(2,1)}, u32[]{:S(2)}) copy-start(bf16[128,1536]{1,0:T(8,128)(2,1)} %refs_13_.1) | copy-start | bytes 1179652
  18.9 2.9 %copy-start.12 = (f32[1536]{0:T(1024)S(1)}, f32[1536]{0:T(1024)}, u32[]{:S(2)}) copy-start(f32[1536]{0:T(1024)} %refs_3_.5) | copy-start | bytes 18436
  19.7 6.4 %collective-permute-start.5 = (bf16[128,512]{1,0:T(8,128)(2,1)S(1)}, bf16[128,512]{1,0:T(8,128)(2,1)S(1)}, u32[]{:S(2)}, u32[]{:S(2)}) collective-permute-start(bf16[128,512]{1,0:T(8,128)(2,1)S(1)} %get-tuple-element.61), channel_id=1, source_target_pairs={{0,2},{1,3},{2,0},{3,1},{4,6},{5,7},{6,4},{7,5},{8,10},{9,11},{10,... | collective-permute-start | bytes 393224 | tf_op jit(solution)/shard_map/ppermute | solution.py:49
  22.6 8.2 %collective-permute-start.7 = (bf16[128,512]{1,0:T(8,128)(2,1)S(1)}, bf16[128,512]{1,0:T(8,128)(2,1)S(1)}, u32[]{:S(2)}, u32[]{:S(2)}) collective-permute-start(bf16[128,512]{1,0:T(8,128)(2,1)S(1)} %get-tuple-element.58), channel_id=1, source_target_pairs={{0,6},{1,7},{2,4},{3,5},{4,2},{5,3},{6,0},{7,1},{8,14},{9,15},{10,... | collective-permute-start | bytes 393224 | tf_op jit(solution)/shard_map/ppermute | solution.py:49
  24.1 6.7 %collective-permute-start.6 = (bf16[128,512]{1,0:T(8,128)(2,1)S(1)}, bf16[128,512]{1,0:T(8,128)(2,1)S(1)}, u32[]{:S(2)}, u32[]{:S(2)}) collective-permute-start(bf16[128,512]{1,0:T(8,128)(2,1)S(1)} %get-tuple-element.60), channel_id=1, source_target_pairs={{0,4},{1,5},{2,6},{3,7},{4,0},{5,1},{6,2},{7,3},{8,12},{9,13},{10,... | collective-permute-start | bytes 393224 | tf_op jit(solution)/shard_map/ppermute | solution.py:49
  26.1 4.8 %copy-start.1 = (s32[128,4]{0,1:T(4,128)S(1)}, s32[128,4]{0,1:T(4,128)}, u32[]{:S(2)}) copy-start(s32[128,4]{0,1:T(4,128)} %param.19) | copy-start | bytes 6148
  26.1 4.8 %copy-start.2 = (f32[128,4]{0,1:T(4,128)S(1)}, f32[128,4]{0,1:T(4,128)}, u32[]{:S(2)}) copy-start(f32[128,4]{0,1:T(4,128)} %param.20) | copy-start | bytes 6148
  26.1 4.8 %copy-start.3 = (s32[128]{0:T(128)S(1)}, s32[128]{0:T(128)}, u32[]{:S(2)}) copy-start(s32[128]{0:T(128)} %param.13) | copy-start | bytes 1540
  26.1 4.8 %copy-start.7 = (bf16[1,768,1536]{2,1,0:T(8,128)(2,1)S(1)}, bf16[1,768,1536]{2,1,0:T(8,128)(2,1)}, u32[]{:S(2)}) copy-start(bf16[1,768,1536]{2,1,0:T(8,128)(2,1)} %param.23) | copy-start | bytes 7077892
  26.1 4.9 %copy-start = (bf16[1536,192]{0,1:T(8,128)(2,1)S(1)}, bf16[1536,192]{0,1:T(8,128)(2,1)}, u32[]{:S(2)}) copy-start(bf16[1536,192]{0,1:T(8,128)(2,1)} %param.17) | copy-start | bytes 1769476
  30.9 16.7 %collective-permute-start.13 = (bf16[768,1536]{1,0:T(8,128)(2,1)S(1)}, bf16[768,1536]{1,0:T(8,128)(2,1)S(1)}, u32[]{:S(2)}, u32[]{:S(2)}) collective-permute-start(bf16[768,1536]{1,0:T(8,128)(2,1)S(1)} %bitcast.29), channel_id=1, source_target_pairs={{0,1},{1,0},{2,3},{3,2},{4,5},{5,4},{6,7},{7,6},{8,9},{9,8},{10,11... | collective-permute-start | bytes 7077896 | tf_op jit(solution)/shard_map/ppermute | solution.py:49
  31.0 15.7 %collective-permute-start.11 = (bf16[192,1536]{1,0:T(8,128)(2,1)S(1)}, bf16[192,1536]{1,0:T(8,128)(2,1)S(1)}, u32[]{:S(2)}, u32[]{:S(2)}) collective-permute-start(bf16[192,1536]{1,0:T(8,128)(2,1)S(1)} %bitcast.16), channel_id=1, source_target_pairs={{0,2},{1,3},{2,0},{3,1},{4,6},{5,7},{6,4},{7,5},{8,10},{9,11},{10,... | collective-permute-start | bytes 1769480 | tf_op jit(solution)/shard_map/ppermute | solution.py:49
  32.2 15.4 %collective-permute-start.12 = (bf16[192,1536]{1,0:T(8,128)(2,1)S(1)}, bf16[192,1536]{1,0:T(8,128)(2,1)S(1)}, u32[]{:S(2)}, u32[]{:S(2)}) collective-permute-start(bf16[192,1536]{1,0:T(8,128)(2,1)S(1)} %bitcast.17), channel_id=1, source_target_pairs={{0,4},{1,5},{2,6},{3,7},{4,0},{5,1},{6,2},{7,3},{8,12},{9,13},{10,... | collective-permute-start | bytes 1769480 | tf_op jit(solution)/shard_map/ppermute | solution.py:49
  33.2 14.4 %collective-permute-start.14 = (bf16[192,1536]{1,0:T(8,128)(2,1)S(1)}, bf16[192,1536]{1,0:T(8,128)(2,1)S(1)}, u32[]{:S(2)}, u32[]{:S(2)}) collective-permute-start(bf16[192,1536]{1,0:T(8,128)(2,1)S(1)} %bitcast.18), channel_id=1, source_target_pairs={{0,1},{1,0},{2,3},{3,2},{4,5},{5,4},{6,7},{7,6},{8,9},{9,8},{10,11... | collective-permute-start | bytes 1769480 | tf_op jit(solution)/shard_map/ppermute | solution.py:49
  33.2 7.2 %collective-permute-start.10 = (bf16[144,512]{1,0:T(8,128)(2,1)S(1)}, bf16[144,512]{1,0:T(8,128)(2,1)S(1)}, u32[]{:S(2)}, u32[]{:S(2)}) collective-permute-start(bf16[144,512]{1,0:T(8,128)(2,1)S(1)} %pack_kv.1.own.refs_4_.refs_0_), channel_id=1, source_target_pairs={{0,8},{8,16},{16,24},{1,9},{9,17},{17,25},{2,10},{10,18},{18,26},{... | collective-permute-start | bytes 442376 | tf_op jit(solution)/shard_map/ppermute | solution.py:511
  40.5 15.0 %collective-permute-start.24 = (bf16[144,512]{1,0:T(8,128)(2,1)S(1)}, bf16[144,512]{1,0:T(8,128)(2,1)S(1)}, u32[]{:S(2)}, u32[]{:S(2)}) collective-permute-start(bf16[144,512]{1,0:T(8,128)(2,1)S(1)} %pack_kv.1.own.refs_4_.refs_0_), channel_id=1, source_target_pairs={{0,1},{1,0},{2,3},{3,2},{4,5},{5,4},{6,7},{7,6},{8,9},{9,8},{10,11... | collective-permute-start | bytes 442376 | tf_op jit(solution)/shard_map/ppermute | solution.py:49
  46.8 9.3 %collective-permute-start.28 = (bf16[144,512]{1,0:T(8,128)(2,1)S(1)}, bf16[144,512]{1,0:T(8,128)(2,1)S(1)}, u32[]{:S(2)}, u32[]{:S(2)}) collective-permute-start(bf16[144,512]{1,0:T(8,128)(2,1)S(1)} %collective-permute-done.10.prev.refs_8_), channel_id=1, source_target_pairs={{0,1},{1,0},{2,3},{3,2},{4,5},{5,4},{6,7},{7,6},{8,9},{9,8},{10,11... | collective-permute-start | bytes 442376 | tf_op jit(solution)/shard_map/ppermute | solution.py:49
  47.7 7.7 %collective-permute-start.15 = (bf16[144,512]{1,0:T(8,128)(2,1)S(1)}, bf16[144,512]{1,0:T(8,128)(2,1)S(1)}, u32[]{:S(2)}, u32[]{:S(2)}) collective-permute-start(bf16[144,512]{1,0:T(8,128)(2,1)S(1)} %get-tuple-element.36.refs_2_), channel_id=1, source_target_pairs={{0,6},{1,7},{2,4},{3,5},{4,2},{5,3},{6,0},{7,1},{8,14},{9,15},{10,... | collective-permute-start | bytes 442376 | tf_op jit(solution)/shard_map/ppermute | solution.py:49
  49.6 7.8 %collective-permute-start.22 = (bf16[144,512]{1,0:T(8,128)(2,1)S(1)}, bf16[144,512]{1,0:T(8,128)(2,1)S(1)}, u32[]{:S(2)}, u32[]{:S(2)}) collective-permute-start(bf16[144,512]{1,0:T(8,128)(2,1)S(1)} %get-tuple-element.37.refs_0_), channel_id=1, source_target_pairs={{0,2},{1,3},{2,0},{3,1},{4,6},{5,7},{6,4},{7,5},{8,10},{9,11},{10,... | collective-permute-start | bytes 442376 | tf_op jit(solution)/shard_map/ppermute | solution.py:49
  50.3 7.2 %collective-permute-start.23 = (bf16[144,512]{1,0:T(8,128)(2,1)S(1)}, bf16[144,512]{1,0:T(8,128)(2,1)S(1)}, u32[]{:S(2)}, u32[]{:S(2)}) collective-permute-start(bf16[144,512]{1,0:T(8,128)(2,1)S(1)} %get-tuple-element.38.refs_1_), channel_id=1, source_target_pairs={{0,4},{1,5},{2,6},{3,7},{4,0},{5,1},{6,2},{7,3},{8,12},{9,13},{10,... | collective-permute-start | bytes 442376 | tf_op jit(solution)/shard_map/ppermute | solution.py:49
  55.5 5.5 %collective-permute-start.19 = (bf16[192,1536]{1,0:T(8,128)(2,1)S(1)}, bf16[192,1536]{1,0:T(8,128)(2,1)S(1)}, u32[]{:S(2)}, u32[]{:S(2)}) collective-permute-start(bf16[192,1536]{1,0:T(8,128)(2,1)S(1)} %collective-permute-done.12.refs_2_), channel_id=1, source_target_pairs={{0,1},{1,0},{2,3},{3,2},{4,5},{5,4},{6,7},{7,6},{8,9},{9,8},{10,11... | collective-permute-start | bytes 1769480 | tf_op jit(solution)/shard_map/ppermute | solution.py:49
  55.5 5.5 %collective-permute-start.18 = (bf16[192,1536]{1,0:T(8,128)(2,1)S(1)}, bf16[192,1536]{1,0:T(8,128)(2,1)S(1)}, u32[]{:S(2)}, u32[]{:S(2)}) collective-permute-start(bf16[192,1536]{1,0:T(8,128)(2,1)S(1)} %collective-permute-done.11.refs_1_), channel_id=1, source_target_pairs={{0,1},{1,0},{2,3},{3,2},{4,5},{5,4},{6,7},{7,6},{8,9},{9,8},{10,11... | collective-permute-start | bytes 1769480 | tf_op jit(solution)/shard_map/ppermute | solution.py:49
  56.1 2.7 %collective-permute-start.27 = (bf16[144,512]{1,0:T(8,128)(2,1)S(1)}, bf16[144,512]{1,0:T(8,128)(2,1)S(1)}, u32[]{:S(2)}, u32[]{:S(2)}) collective-permute-start(bf16[144,512]{1,0:T(8,128)(2,1)S(1)} %hold.9.refs_7_.refs_1_), channel_id=1, source_target_pairs={{0,1},{1,0},{2,3},{3,2},{4,5},{5,4},{6,7},{7,6},{8,9},{9,8},{10,11... | collective-permute-start | bytes 442376 | tf_op jit(solution)/shard_map/ppermute | solution.py:49
  57.4 2.0 %collective-permute-start.25 = (bf16[144,512]{1,0:T(8,128)(2,1)S(1)}, bf16[144,512]{1,0:T(8,128)(2,1)S(1)}, u32[]{:S(2)}, u32[]{:S(2)}) collective-permute-start(bf16[144,512]{1,0:T(8,128)(2,1)S(1)} %collective-permute-done.22.refs_5_.refs_0_), channel_id=1, source_target_pairs={{0,1},{1,0},{2,3},{3,2},{4,5},{5,4},{6,7},{7,6},{8,9},{9,8},{10,11... | collective-permute-start | bytes 442376 | tf_op jit(solution)/shard_map/ppermute | solution.py:49
  57.4 14.9 %copy-start.4 = (s32[1,64]{1,0:T(1,128)S(1)}, s32[1,64]{1,0:T(1,128)}, u32[]{:S(2)}) copy-start(s32[1,64]{1,0:T(1,128)} %table_ref.1) | copy-start | bytes 772
  57.5 9.5 %collective-permute-start.17 = (bf16[96,1536]{1,0:T(8,128)(2,1)S(1)}, bf16[96,1536]{1,0:T(8,128)(2,1)S(1)}, u32[]{:S(2)}, u32[]{:S(2)}) collective-permute-start(bf16[96,1536]{1,0:T(8,128)(2,1)S(1)} %hold.11), channel_id=1, source_target_pairs={{0,4},{1,5},{2,6},{3,7},{4,0},{5,1},{6,2},{7,3},{8,12},{9,13},{10,... | collective-permute-start | bytes 884744 | tf_op jit(solution)/shard_map/ppermute | solution.py:49
  58.8 8.8 %collective-permute-start.16 = (bf16[96,1536]{1,0:T(8,128)(2,1)S(1)}, bf16[96,1536]{1,0:T(8,128)(2,1)S(1)}, u32[]{:S(2)}, u32[]{:S(2)}) collective-permute-start(bf16[96,1536]{1,0:T(8,128)(2,1)S(1)} %hold.10), channel_id=1, source_target_pairs={{0,2},{1,3},{2,0},{3,1},{4,6},{5,7},{6,4},{7,5},{8,10},{9,11},{10,... | collective-permute-start | bytes 884744 | tf_op jit(solution)/shard_map/ppermute | solution.py:49
  59.4 1.4 %collective-permute-start.26 = (bf16[144,512]{1,0:T(8,128)(2,1)S(1)}, bf16[144,512]{1,0:T(8,128)(2,1)S(1)}, u32[]{:S(2)}, u32[]{:S(2)}) collective-permute-start(bf16[144,512]{1,0:T(8,128)(2,1)S(1)} %collective-permute-done.23.refs_6_.refs_1_), channel_id=1, source_target_pairs={{0,1},{1,0},{2,3},{3,2},{4,5},{5,4},{6,7},{7,6},{8,9},{9,8},{10,11... | collective-permute-start | bytes 442376 | tf_op jit(solution)/shard_map/ppermute | solution.py:49
  60.8 9.7 %collective-permute-start.33 = (bf16[256,512]{1,0:T(8,128)(2,1)S(1)}, bf16[256,512]{1,0:T(8,128)(2,1)S(1)}, u32[]{:S(2)}, u32[]{:S(2)}) collective-permute-start(bf16[256,512]{1,0:T(8,128)(2,1)S(1)} %project.3.refs_0_), channel_id=1, source_target_pairs={{0,1},{1,0},{2,3},{3,2},{4,5},{5,4},{6,7},{7,6},{8,9},{9,8},{10,11... | collective-permute-start | bytes 786440 | tf_op jit(solution)/shard_map/ppermute | solution.py:49
  67.6 10.1 %collective-permute-start.29 = (bf16[128,1536]{1,0:T(8,128)(2,1)S(1)}, bf16[128,1536]{1,0:T(8,128)(2,1)S(1)}, u32[]{:S(2)}, u32[]{:S(2)}) collective-permute-start(bf16[128,1536]{1,0:T(8,128)(2,1)S(1)} %attend.1.refs_10_), channel_id=1, source_target_pairs={{0,4},{1,5},{2,6},{3,7},{4,0},{5,1},{6,2},{7,3},{8,12},{9,13},{10,... | collective-permute-start | bytes 1179656 | tf_op jit(solution)/shard_map/ppermute | solution.py:49
  68.7 10.1 %collective-permute-start.31 = (bf16[128,1536]{1,0:T(8,128)(2,1)S(1)}, bf16[128,1536]{1,0:T(8,128)(2,1)S(1)}, u32[]{:S(2)}, u32[]{:S(2)}) collective-permute-start(bf16[128,1536]{1,0:T(8,128)(2,1)S(1)} %attend.1.refs_10_), channel_id=1, source_target_pairs={{0,2},{1,3},{2,0},{3,1},{4,6},{5,7},{6,4},{7,5},{8,10},{9,11},{10,... | collective-permute-start | bytes 1179656 | tf_op jit(solution)/shard_map/ppermute | solution.py:49
  70.0 4.5 %collective-permute-start.21 = (bf16[96,1536]{1,0:T(8,128)(2,1)S(1)}, bf16[96,1536]{1,0:T(8,128)(2,1)S(1)}, u32[]{:S(2)}, u32[]{:S(2)}) collective-permute-start(bf16[96,1536]{1,0:T(8,128)(2,1)S(1)} %collective-permute-done.17.refs_4_), channel_id=1, source_target_pairs={{0,1},{1,0},{2,3},{3,2},{4,5},{5,4},{6,7},{7,6},{8,9},{9,8},{10,11... | collective-permute-start | bytes 884744 | tf_op jit(solution)/shard_map/ppermute | solution.py:49
  70.0 4.5 %collective-permute-start.20 = (bf16[96,1536]{1,0:T(8,128)(2,1)S(1)}, bf16[96,1536]{1,0:T(8,128)(2,1)S(1)}, u32[]{:S(2)}, u32[]{:S(2)}) collective-permute-start(bf16[96,1536]{1,0:T(8,128)(2,1)S(1)} %collective-permute-done.16.refs_3_), channel_id=1, source_target_pairs={{0,1},{1,0},{2,3},{3,2},{4,5},{5,4},{6,7},{7,6},{8,9},{9,8},{10,11... | collective-permute-start | bytes 884744 | tf_op jit(solution)/shard_map/ppermute | solution.py:49
  70.5 1.9 %collective-permute-start.34 = (bf16[256,512]{1,0:T(8,128)(2,1)S(1)}, bf16[256,512]{1,0:T(8,128)(2,1)S(1)}, u32[]{:S(2)}, u32[]{:S(2)}) collective-permute-start(bf16[256,512]{1,0:T(8,128)(2,1)S(1)} %project.2.refs_6_.refs_1_), channel_id=1, source_target_pairs={{0,1},{1,0},{2,3},{3,2},{4,5},{5,4},{6,7},{7,6},{8,9},{9,8},{10,11... | collective-permute-start | bytes 786440 | tf_op jit(solution)/shard_map/ppermute | solution.py:49
  74.4 12.0 %copy-start.5 = (bf16[1,1536,768]{2,1,0:T(8,128)(2,1)S(1)}, bf16[1,1536,768]{2,1,0:T(8,128)(2,1)}, u32[]{:S(2)}) copy-start(bf16[1,1536,768]{2,1,0:T(8,128)(2,1)} %param.21) | copy-start | bytes 7077892
  74.4 12.0 %copy-start.6 = (bf16[1,1536,768]{2,1,0:T(8,128)(2,1)S(1)}, bf16[1,1536,768]{2,1,0:T(8,128)(2,1)}, u32[]{:S(2)}) copy-start(bf16[1,1536,768]{2,1,0:T(8,128)(2,1)} %param.22) | copy-start | bytes 7077892
  74.4 12.0 %copy-start.13 = (f32[1536]{0:T(1024)S(1)}, f32[1536]{0:T(1024)}, u32[]{:S(2)}) copy-start(f32[1536]{0:T(1024)} %refs_3_.7) | copy-start | bytes 18436
  78.9 12.8 %collective-permute-start.35 = (bf16[128,512]{1,0:T(8,128)(2,1)S(1)}, bf16[128,512]{1,0:T(8,128)(2,1)S(1)}, u32[]{:S(2)}, u32[]{:S(2)}) collective-permute-start(bf16[128,512]{1,0:T(8,128)(2,1)S(1)} %get-tuple-element.57), channel_id=1, source_target_pairs={{6,4},{7,5},{14,12},{15,13},{22,20},{23,21},{30,28},{31,29}} | collective-permute-start | bytes 393224 | tf_op jit(solution)/shard_map/ppermute | solution.py:536
  79.6 12.3 %collective-permute-start.36 = (bf16[128,512]{1,0:T(8,128)(2,1)S(1)}, bf16[128,512]{1,0:T(8,128)(2,1)S(1)}, u32[]{:S(2)}, u32[]{:S(2)}) collective-permute-start(bf16[128,512]{1,0:T(8,128)(2,1)S(1)} %get-tuple-element.56), channel_id=1, source_target_pairs={{6,2},{7,3},{14,10},{15,11},{22,18},{23,19},{30,26},{31,27}} | collective-permute-start | bytes 393224 | tf_op jit(solution)/shard_map/ppermute | solution.py:536
  80.2 11.7 %collective-permute-start.40 = (bf16[128,512]{1,0:T(8,128)(2,1)S(1)}, bf16[128,512]{1,0:T(8,128)(2,1)S(1)}, u32[]{:S(2)}, u32[]{:S(2)}) collective-permute-start(bf16[128,512]{1,0:T(8,128)(2,1)S(1)} %get-tuple-element.54), channel_id=1, source_target_pairs={{6,0},{7,1},{14,8},{15,9},{22,16},{23,17},{30,24},{31,25}} | collective-permute-start | bytes 393224 | tf_op jit(solution)/shard_map/ppermute | solution.py:536
  81.7 10.9 %collective-permute-start.30 = (bf16[64,1536]{1,0:T(8,128)(2,1)S(1)}, bf16[64,1536]{1,0:T(8,128)(2,1)S(1)}, u32[]{:S(2)}, u32[]{:S(2)}) collective-permute-start(bf16[64,1536]{1,0:T(8,128)(2,1)S(1)} %slice.64), channel_id=1, source_target_pairs={{0,2},{1,3},{2,0},{3,1},{4,6},{5,7},{6,4},{7,5},{8,10},{9,11},{10,... | collective-permute-start | bytes 589832 | tf_op jit(solution)/shard_map/ppermute | solution.py:49
  83.0 9.6 %collective-permute-start.32 = (bf16[64,1536]{1,0:T(8,128)(2,1)S(1)}, bf16[64,1536]{1,0:T(8,128)(2,1)S(1)}, u32[]{:S(2)}, u32[]{:S(2)}) collective-permute-start(bf16[64,1536]{1,0:T(8,128)(2,1)S(1)} %slice.65), channel_id=1, source_target_pairs={{0,4},{1,5},{2,6},{3,7},{4,0},{5,1},{6,2},{7,3},{8,12},{9,13},{10,... | collective-permute-start | bytes 589832 | tf_op jit(solution)/shard_map/ppermute | solution.py:49
  91.7 9.7 %collective-permute-start.37 = (bf16[128,1536]{1,0:T(8,128)(2,1)S(1)}, bf16[128,1536]{1,0:T(8,128)(2,1)S(1)}, u32[]{:S(2)}, u32[]{:S(2)}) collective-permute-start(bf16[128,1536]{1,0:T(8,128)(2,1)S(1)} %get-tuple-element.47.refs_16_), channel_id=1, source_target_pairs={{0,2},{1,3},{2,0},{3,1},{4,6},{5,7},{6,4},{7,5},{8,10},{9,11},{10,... | collective-permute-start | bytes 1179656 | tf_op jit(solution)/shard_map/ppermute | solution.py:49
  91.8 9.6 %collective-permute-start.38 = (bf16[128,1536]{1,0:T(8,128)(2,1)S(1)}, bf16[128,1536]{1,0:T(8,128)(2,1)S(1)}, u32[]{:S(2)}, u32[]{:S(2)}) collective-permute-start(bf16[128,1536]{1,0:T(8,128)(2,1)S(1)} %get-tuple-element.52), channel_id=1, source_target_pairs={{0,4},{1,5},{2,6},{3,7},{4,0},{5,1},{6,2},{7,3},{8,12},{9,13},{10,... | collective-permute-start | bytes 1179656 | tf_op jit(solution)/shard_map/ppermute | solution.py:49
  98.0 11.5 %collective-permute-start.39 = (bf16[128,1536]{1,0:T(8,128)(2,1)S(1)}, bf16[128,1536]{1,0:T(8,128)(2,1)S(1)}, u32[]{:S(2)}, u32[]{:S(2)}) collective-permute-start(bf16[128,1536]{1,0:T(8,128)(2,1)S(1)} %get-tuple-element.53), channel_id=1, source_target_pairs={{0,6},{1,7},{2,4},{3,5},{4,2},{5,3},{6,0},{7,1},{8,14},{9,15},{10,... | collective-permute-start | bytes 1179656 | tf_op jit(solution)/shard_map/ppermute | solution.py:49
